TPU v7x, 512 devices: a whole 4x8x8 slice. The times are simulated.
512 devices in a mesh: section: 16 (over z_lo, x), feat: 32 (over y, z_hi, core).
Axes of the slice: x: 4, y: 8, z: 8 (z_hi: 2, z_lo: 4; z = z_hi * 4 + z_lo), core: 2. Of those that a mesh axis runs over, the one named last changes fastest.
Arguments:
- decoders: bfloat16 [16, 4096, 4608], P('section', 'feat'), may hold values from -0.09375 to 0.09375
- encoders: bfloat16 [16, 4096, 4608], P('section', 'feat'), may hold values from -6 to 6
- out_proj: bfloat16 [16, 4096, 4608], P('section', 'feat'), may hold values from -0.09375 to 0.09375
- value_proj: bfloat16 [16, 4608, 4096], P('section', None, 'feat'), may hold values from -0.09375 to 0.09375
- attention: float32 [16, 32, 16, 16], P('section', 'feat'), may hold values from 0 to 1, as said below
- norm_scale: float32 [16, 16], P('section'), may hold values from 0.05 to 0.5
- act_ids: int32 [16, 4096], P('section'), may hold values from 0 to 4095, as said below
- act_values: float32 [16, 4096], P('section', 'feat'), may hold values from 0.1 to 10
- target_ids: int32 [64], P('section'), may hold values from 0 to 4095
- target_pos: int32 [64], P('section'), may hold values from 0 to 15
Outputs:
- edges: float32 [16, 64, 4096], P('section', None, 'feat')
Inputs may be any that keep to these rules, and one draw needn't show every extreme that they name: Every row attention[l, h, p, :] is nonnegative, zero at keys after p, and sums to one. `act_ids`: A feature id f is held by shard f // 128 of feat. In each aligned block of 128 entries of a layer (the entries of one device), at most 8 ids lie in one shard, and in every block some shard has exactly 8.
All inputs are finite; a program needn't handle non-finite values.
Results may differ from a plain program's by a relative error of at most 0.015.
Values may be sent and summed in bfloat16 or wider, within the bound.
No kernel may reach another device: no remote copies, remote signals or barrier semaphores. Data moves between devices by JAX's collectives and lax.ppermute only.
A program may use at most 64 MiB of HBM per device.

v0:
```python
import jax
import jax.numpy as jnp
from jax import lax
from jax.sharding import PartitionSpec as P

K_ACT = 256


def shifted(shard, axis, by):
    length = lax.axis_size(axis)
    pairs = [(i, i + by) for i in range(length) if 0 <= i + by < length]
    return lax.ppermute(shard, axis, pairs)


def per_device(
    decoders,
    encoders,
    out_proj,
    value_proj,
    attention,
    norm_scale,
    act_ids,
    act_values,
    target_ids,
    target_pos,
):
    feat_count = lax.axis_size("feat")
    section_count = lax.axis_size("section")
    feat_index = lax.axis_index("feat")
    section_index = lax.axis_index("section")
    dec_table = decoders[0]
    enc_table = encoders[0]
    out_weight = out_proj[0]
    value_weight = value_proj[0]
    mixing = attention[0, 0]
    scales = norm_scale[0]
    act_weights = act_values[0]
    feat_rows = dec_table.shape[0]
    model_width = dec_table.shape[1]
    head_width = out_weight.shape[0]
    seq_len = mixing.shape[0]
    batch_size = target_ids.shape[0]
    entries_dev = act_weights.shape[0]
    slot_count = 2 * entries_dev // feat_count
    rows_all = batch_size * seq_len
    rows_dev = rows_all // feat_count
    ids_blocks = act_ids[0].reshape(feat_count, entries_dev)
    owner_ids = ids_blocks // feat_rows
    local_ids = ids_blocks % feat_rows
    owned_mask = (owner_ids == feat_index).astype(jnp.int32)
    slot_rank = jnp.cumsum(owned_mask, axis=1) - 1
    slot_iota = jnp.arange(slot_count, dtype=jnp.int32)
    selected = owned_mask[:, None, :] * (slot_rank[:, None, :] == slot_iota[None, :, None]).astype(
        jnp.int32
    )
    source_row = jnp.sum(selected * local_ids[:, None, :], axis=2)
    is_filled = jnp.sum(selected, axis=2)
    entry_iota = jnp.arange(entries_dev, dtype=jnp.int32)
    outgoing = jnp.take(dec_table, source_row.reshape(-1), axis=0).reshape(
        feat_count, slot_count, model_width
    )
    outgoing = jnp.where(is_filled[:, :, None] > 0, outgoing, jnp.zeros_like(outgoing))
    own_owner = lax.dynamic_index_in_dim(owner_ids, feat_index, 0, keepdims=False)
    earlier = (entry_iota[None, :] < entry_iota[:, None]).astype(jnp.int32)
    same_owner = (own_owner[:, None] == own_owner[None, :]).astype(jnp.int32)
    own_rank = jnp.sum(earlier * same_owner, axis=1)
    flat_index = own_owner * slot_count + own_rank
    positions = jnp.arange(seq_len, dtype=jnp.int32)
    incoming = lax.all_to_all(outgoing, "feat", split_axis=0, concat_axis=0, tiled=True)
    partners = jnp.take(incoming.reshape(feat_count * slot_count, model_width), flat_index, axis=0)
    own_pos = (feat_index * entries_dev + entry_iota) // K_ACT
    edge_pick = (positions[:, None] == own_pos[None, :]).astype(jnp.float32)
    feat_iota = jnp.arange(feat_rows, dtype=jnp.int32)
    target_pick = ((target_ids - feat_index * feat_rows)[:, None] == feat_iota[None, :]).astype(
        jnp.bfloat16
    )
    enc_part = jnp.dot(target_pick, enc_table, preferred_element_type=jnp.float32)
    enc_full = lax.psum(enc_part.astype(jnp.bfloat16), "feat").astype(jnp.float32)
    row_iota = feat_index * rows_dev + jnp.arange(rows_dev, dtype=jnp.int32)
    row_target = row_iota // seq_len
    row_pos = row_iota % seq_len
    target_onehot = (
        row_target[:, None] == jnp.arange(batch_size, dtype=jnp.int32)[None, :]
    ).astype(jnp.float32)
    row_enc = jnp.dot(target_onehot, enc_full, precision=lax.Precision.HIGHEST)
    row_hit = jnp.sum(
        target_onehot * (row_pos[:, None] == target_pos[None, :]).astype(jnp.float32), axis=1
    )
    start_rows = row_enc * row_hit[:, None]
    scale_rows = jnp.tile(scales, batch_size)

    def produce(shard_rows):
        head_part = lax.dot_general(
            shard_rows, out_weight, (((1,), (1,)), ((), ())), preferred_element_type=jnp.float32
        )
        edge_part = lax.dot_general(
            shard_rows, partners, (((1,), (1,)), ((), ())), preferred_element_type=jnp.float32
        )
        return jnp.concatenate([head_part, edge_part], axis=1)

    def gathered_products(adjoint_rows):
        joined = produce(
            lax.all_gather(adjoint_rows.astype(jnp.bfloat16), "feat", axis=0, tiled=True)
        )
        return (joined[:, :head_width], joined[:, head_width:])

    def record(edges_out, edge_raw, step_num):
        edge_vals = jnp.sum(edge_raw.reshape(batch_size, seq_len, -1) * edge_pick[None], axis=1)
        edge_vals = edge_vals * act_weights[None, :]
        batch_num = section_index + step_num
        in_range = batch_num < section_count
        row_start = jnp.minimum(batch_num, section_count - 1) * batch_size
        current = lax.dynamic_slice_in_dim(edges_out, row_start, batch_size, 0)
        updated = jnp.where(in_range, edge_vals, current)
        return lax.dynamic_update_slice_in_dim(edges_out, updated, row_start, 0)

    def propagate(adjoint_rows, head_grad):
        mixed_rows = jnp.einsum(
            "pq,tph->tqh", mixing, head_grad.reshape(batch_size, seq_len, head_width)
        )
        mixed_rows = mixed_rows.astype(jnp.bfloat16).reshape(rows_all, head_width)
        head_term = lax.dot_general(
            mixed_rows, value_weight, (((1,), (1,)), ((), ())), preferred_element_type=jnp.float32
        )
        head_term = (head_term * scale_rows[:, None]).astype(jnp.bfloat16)
        head_parts = lax.all_to_all(
            head_term.reshape(feat_count, rows_dev, model_width),
            "feat",
            split_axis=0,
            concat_axis=0,
            tiled=True,
        )
        return adjoint_rows + jnp.sum(head_parts.astype(jnp.float32), axis=0)

    def one_hop(step_num, loop_state):
        adjoint_rows, edges_out = loop_state
        head_grad, edge_raw = gathered_products(adjoint_rows)
        edges_out = record(edges_out, edge_raw, step_num)
        adjoint_rows = propagate(adjoint_rows, head_grad)
        adjoint_rows = shifted(adjoint_rows, "section", -1)
        return (adjoint_rows, edges_out)

    blank_edges = jnp.zeros((batch_size * section_count, entries_dev), jnp.float32)
    adjoint_rows, edges_out = lax.fori_loop(
        0, section_count - 1, one_hop, (start_rows, blank_edges)
    )
    unused, edge_raw = gathered_products(adjoint_rows)
    edges_out = record(edges_out, edge_raw, section_count - 1)
    return edges_out[None]


def solution(mesh):
    in_specs = (
        P("section", "feat", None),
        P("section", "feat", None),
        P("section", "feat", None),
        P("section", None, "feat"),
        P("section", "feat", None, None),
        P("section", None),
        P("section", None),
        P("section", "feat"),
        P("section"),
        P("section"),
    )
    out_specs = P("section", None, "feat")
    return jax.shard_map(
        per_device, mesh=mesh, in_specs=in_specs, out_specs=out_specs, check_vma=False
    )
```

profile of v0, /device:TPU:7, one launch (start us, length us, event | category | flops | bytes accessed | tf_op | source)
XLA Modules:
  0.0 1709.8 jit_solution(6113719031879558442)
XLA Ops:
  7.6 16.5 all-to-all-start.1
  27.0 205.2 %psum.7 = bf16[4,4608]{1,0:T(4,128)(2,1)} all-reduce(bf16[4,4608]{1,0:T(4,128)(2,1)} %convolution_convert_fusion.1), channel_id=1, replica_groups=mesh['section'=16,'feat'=32] {'feat'}, use_global_device_ids=true, to_apply=%region_0.1 | all-reduce | flops 18432 | bytes 73728 | tf_op jit(solution)/shard_map/psum | solution.py:78
  243.0 1409.1 %while.16 = (s32[]{:T(128)}, f32[2,4608]{1,0:T(2,128)S(1)}, f32[64,128]{1,0:T(8,128)}, bf16[128,4608]{1,0:T(8,128)(2,1)}, bf16[16,16]{0,1:T(8,128)(2,1)S(1)}, /*...) while((s32[]{:T(128)}, f32[2,4608]{1,0:T(2,128)S(1)}, ...), condition=%wide.region_9.10_spmd.clone, body=%wide.region_6.9_spmd.clone.sunk | while | flops 227964416 | bytes 15944625 | solution.py:144
  243.6 57.1 %all-gather.4 = bf16[32,2,4608]{2,1,0:T(2,128)(2,1)S(1)} all-gather(bf16[1,2,4608]{2,1,0:T(2,128)(2,1)S(1)} %convert_bitcast_fusion.3), channel_id=1, replica_groups=mesh['section'=16,'feat'=32] {'feat'}, dimensions={0}, use_global_device_ids=true | all-gather | bytes 608256 | tf_op jit(solution)/shard_map/while/body/eval_jaxpr/all_gather | solution.py:103
  305.3 11.0 all-to-all-start
  317.4 19.1 %all-to-all-done = bf16[32,2,4608]{2,1,0:T(2,128)(2,1)S(1)} async-done(((bf16[32,2,4608]{2,1,0:T(2,128)(2,1)}), bf16[32,2,4608]{2,1,0:T(2,128)(2,1)S(1)}, u32[]{:S(2)}, u32[]{:S(2)}) %all-to-all-start) | async-done | bytes 589856 | tf_op jit(solution)/shard_map/while/body/eval_jaxpr/all_to_all | solution.py:126
  341.5 3.1 collective-permute-done
  345.2 53.4 %all-gather.4 = bf16[32,2,4608]{2,1,0:T(2,128)(2,1)S(1)} all-gather(bf16[1,2,4608]{2,1,0:T(2,128)(2,1)S(1)} %convert_bitcast_fusion.3), channel_id=1, replica_groups=mesh['section'=16,'feat'=32] {'feat'}, dimensions={0}, use_global_device_ids=true | all-gather | bytes 608256 | tf_op jit(solution)/shard_map/while/body/eval_jaxpr/all_gather | solution.py:103
  403.2 7.2 all-to-all-start
  411.5 18.7 %all-to-all-done = bf16[32,2,4608]{2,1,0:T(2,128)(2,1)S(1)} async-done(((bf16[32,2,4608]{2,1,0:T(2,128)(2,1)}), bf16[32,2,4608]{2,1,0:T(2,128)(2,1)S(1)}, u32[]{:S(2)}, u32[]{:S(2)}) %all-to-all-start) | async-done | bytes 589856 | tf_op jit(solution)/shard_map/while/body/eval_jaxpr/all_to_all | solution.py:126
  434.7 3.6 collective-permute-done
  438.9 54.1 %all-gather.4 = bf16[32,2,4608]{2,1,0:T(2,128)(2,1)S(1)} all-gather(bf16[1,2,4608]{2,1,0:T(2,128)(2,1)S(1)} %convert_bitcast_fusion.3), channel_id=1, replica_groups=mesh['section'=16,'feat'=32] {'feat'}, dimensions={0}, use_global_device_ids=true | all-gather | bytes 608256 | tf_op jit(solution)/shard_map/while/body/eval_jaxpr/all_gather | solution.py:103
  497.6 6.2 all-to-all-start
  504.9 18.7 %all-to-all-done = bf16[32,2,4608]{2,1,0:T(2,128)(2,1)S(1)} async-done(((bf16[32,2,4608]{2,1,0:T(2,128)(2,1)}), bf16[32,2,4608]{2,1,0:T(2,128)(2,1)S(1)}, u32[]{:S(2)}, u32[]{:S(2)}) %all-to-all-start) | async-done | bytes 589856 | tf_op jit(solution)/shard_map/while/body/eval_jaxpr/all_to_all | solution.py:126
  528.1 3.6 collective-permute-done
  532.3 54.1 %all-gather.4 = bf16[32,2,4608]{2,1,0:T(2,128)(2,1)S(1)} all-gather(bf16[1,2,4608]{2,1,0:T(2,128)(2,1)S(1)} %convert_bitcast_fusion.3), channel_id=1, replica_groups=mesh['section'=16,'feat'=32] {'feat'}, dimensions={0}, use_global_device_ids=true | all-gather | bytes 608256 | tf_op jit(solution)/shard_map/while/body/eval_jaxpr/all_gather | solution.py:103
  591.0 6.2 all-to-all-start
  598.3 18.7 %all-to-all-done = bf16[32,2,4608]{2,1,0:T(2,128)(2,1)S(1)} async-done(((bf16[32,2,4608]{2,1,0:T(2,128)(2,1)}), bf16[32,2,4608]{2,1,0:T(2,128)(2,1)S(1)}, u32[]{:S(2)}, u32[]{:S(2)}) %all-to-all-start) | async-done | bytes 589856 | tf_op jit(solution)/shard_map/while/body/eval_jaxpr/all_to_all | solution.py:126
  621.4 3.6 collective-permute-done
  625.7 54.2 %all-gather.4 = bf16[32,2,4608]{2,1,0:T(2,128)(2,1)S(1)} all-gather(bf16[1,2,4608]{2,1,0:T(2,128)(2,1)S(1)} %convert_bitcast_fusion.3), channel_id=1, replica_groups=mesh['section'=16,'feat'=32] {'feat'}, dimensions={0}, use_global_device_ids=true | all-gather | bytes 608256 | tf_op jit(solution)/shard_map/while/body/eval_jaxpr/all_gather | solution.py:103
  684.4 6.2 all-to-all-start
  691.7 18.7 %all-to-all-done = bf16[32,2,4608]{2,1,0:T(2,128)(2,1)S(1)} async-done(((bf16[32,2,4608]{2,1,0:T(2,128)(2,1)}), bf16[32,2,4608]{2,1,0:T(2,128)(2,1)S(1)}, u32[]{:S(2)}, u32[]{:S(2)}) %all-to-all-start) | async-done | bytes 589856 | tf_op jit(solution)/shard_map/while/body/eval_jaxpr/all_to_all | solution.py:126
  714.8 3.6 collective-permute-done
  719.0 54.2 %all-gather.4 = bf16[32,2,4608]{2,1,0:T(2,128)(2,1)S(1)} all-gather(bf16[1,2,4608]{2,1,0:T(2,128)(2,1)S(1)} %convert_bitcast_fusion.3), channel_id=1, replica_groups=mesh['section'=16,'feat'=32] {'feat'}, dimensions={0}, use_global_device_ids=true | all-gather | bytes 608256 | tf_op jit(solution)/shard_map/while/body/eval_jaxpr/all_gather | solution.py:103
  777.7 6.2 all-to-all-start
  785.1 18.7 %all-to-all-done = bf16[32,2,4608]{2,1,0:T(2,128)(2,1)S(1)} async-done(((bf16[32,2,4608]{2,1,0:T(2,128)(2,1)}), bf16[32,2,4608]{2,1,0:T(2,128)(2,1)S(1)}, u32[]{:S(2)}, u32[]{:S(2)}) %all-to-all-start) | async-done | bytes 589856 | tf_op jit(solution)/shard_map/while/body/eval_jaxpr/all_to_all | solution.py:126
  808.1 3.7 collective-permute-done
  812.4 54.2 %all-gather.4 = bf16[32,2,4608]{2,1,0:T(2,128)(2,1)S(1)} all-gather(bf16[1,2,4608]{2,1,0:T(2,128)(2,1)S(1)} %convert_bitcast_fusion.3), channel_id=1, replica_groups=mesh['section'=16,'feat'=32] {'feat'}, dimensions={0}, use_global_device_ids=true | all-gather | bytes 608256 | tf_op jit(solution)/shard_map/while/body/eval_jaxpr/all_gather | solution.py:103
  871.1 6.2 all-to-all-start
  878.4 18.7 %all-to-all-done = bf16[32,2,4608]{2,1,0:T(2,128)(2,1)S(1)} async-done(((bf16[32,2,4608]{2,1,0:T(2,128)(2,1)}), bf16[32,2,4608]{2,1,0:T(2,128)(2,1)S(1)}, u32[]{:S(2)}, u32[]{:S(2)}) %all-to-all-start) | async-done | bytes 589856 | tf_op jit(solution)/shard_map/while/body/eval_jaxpr/all_to_all | solution.py:126
  901.6 3.6 collective-permute-done
  905.8 54.2 %all-gather.4 = bf16[32,2,4608]{2,1,0:T(2,128)(2,1)S(1)} all-gather(bf16[1,2,4608]{2,1,0:T(2,128)(2,1)S(1)} %convert_bitcast_fusion.3), channel_id=1, replica_groups=mesh['section'=16,'feat'=32] {'feat'}, dimensions={0}, use_global_device_ids=true | all-gather | bytes 608256 | tf_op jit(solution)/shard_map/while/body/eval_jaxpr/all_gather | solution.py:103
  964.5 6.2 all-to-all-start
  971.8 18.7 %all-to-all-done = bf16[32,2,4608]{2,1,0:T(2,128)(2,1)S(1)} async-done(((bf16[32,2,4608]{2,1,0:T(2,128)(2,1)}), bf16[32,2,4608]{2,1,0:T(2,128)(2,1)S(1)}, u32[]{:S(2)}, u32[]{:S(2)}) %all-to-all-start) | async-done | bytes 589856 | tf_op jit(solution)/shard_map/while/body/eval_jaxpr/all_to_all | solution.py:126
  994.9 3.7 collective-permute-done
  999.2 54.2 %all-gather.4 = bf16[32,2,4608]{2,1,0:T(2,128)(2,1)S(1)} all-gather(bf16[1,2,4608]{2,1,0:T(2,128)(2,1)S(1)} %convert_bitcast_fusion.3), channel_id=1, replica_groups=mesh['section'=16,'feat'=32] {'feat'}, dimensions={0}, use_global_device_ids=true | all-gather | bytes 608256 | tf_op jit(solution)/shard_map/while/body/eval_jaxpr/all_gather | solution.py:103
  1057.9 6.2 all-to-all-start
  1065.2 18.7 %all-to-all-done = bf16[32,2,4608]{2,1,0:T(2,128)(2,1)S(1)} async-done(((bf16[32,2,4608]{2,1,0:T(2,128)(2,1)}), bf16[32,2,4608]{2,1,0:T(2,128)(2,1)S(1)}, u32[]{:S(2)}, u32[]{:S(2)}) %all-to-all-start) | async-done | bytes 589856 | tf_op jit(solution)/shard_map/while/body/eval_jaxpr/all_to_all | solution.py:126
  1088.3 3.6 collective-permute-done
  1092.5 54.2 %all-gather.4 = bf16[32,2,4608]{2,1,0:T(2,128)(2,1)S(1)} all-gather(bf16[1,2,4608]{2,1,0:T(2,128)(2,1)S(1)} %convert_bitcast_fusion.3), channel_id=1, replica_groups=mesh['section'=16,'feat'=32] {'feat'}, dimensions={0}, use_global_device_ids=true | all-gather | bytes 608256 | tf_op jit(solution)/shard_map/while/body/eval_jaxpr/all_gather | solution.py:103
  1151.2 6.2 all-to-all-start
  1158.5 18.7 %all-to-all-done = bf16[32,2,4608]{2,1,0:T(2,128)(2,1)S(1)} async-done(((bf16[32,2,4608]{2,1,0:T(2,128)(2,1)}), bf16[32,2,4608]{2,1,0:T(2,128)(2,1)S(1)}, u32[]{:S(2)}, u32[]{:S(2)}) %all-to-all-start) | async-done | bytes 589856 | tf_op jit(solution)/shard_map/while/body/eval_jaxpr/all_to_all | solution.py:126
  1181.7 3.6 collective-permute-done
  1185.9 54.2 %all-gather.4 = bf16[32,2,4608]{2,1,0:T(2,128)(2,1)S(1)} all-gather(bf16[1,2,4608]{2,1,0:T(2,128)(2,1)S(1)} %convert_bitcast_fusion.3), channel_id=1, replica_groups=mesh['section'=16,'feat'=32] {'feat'}, dimensions={0}, use_global_device_ids=true | all-gather | bytes 608256 | tf_op jit(solution)/shard_map/while/body/eval_jaxpr/all_gather | solution.py:103
  1244.6 6.2 all-to-all-start
  1251.9 18.7 %all-to-all-done = bf16[32,2,4608]{2,1,0:T(2,128)(2,1)S(1)} async-done(((bf16[32,2,4608]{2,1,0:T(2,128)(2,1)}), bf16[32,2,4608]{2,1,0:T(2,128)(2,1)S(1)}, u32[]{:S(2)}, u32[]{:S(2)}) %all-to-all-start) | async-done | bytes 589856 | tf_op jit(solution)/shard_map/while/body/eval_jaxpr/all_to_all | solution.py:126
  1275.1 3.6 collective-permute-done
  1279.3 54.2 %all-gather.4 = bf16[32,2,4608]{2,1,0:T(2,128)(2,1)S(1)} all-gather(bf16[1,2,4608]{2,1,0:T(2,128)(2,1)S(1)} %convert_bitcast_fusion.3), channel_id=1, replica_groups=mesh['section'=16,'feat'=32] {'feat'}, dimensions={0}, use_global_device_ids=true | all-gather | bytes 608256 | tf_op jit(solution)/shard_map/while/body/eval_jaxpr/all_gather | solution.py:103
  1338.0 6.2 all-to-all-start
  1345.3 18.7 %all-to-all-done = bf16[32,2,4608]{2,1,0:T(2,128)(2,1)S(1)} async-done(((bf16[32,2,4608]{2,1,0:T(2,128)(2,1)}), bf16[32,2,4608]{2,1,0:T(2,128)(2,1)S(1)}, u32[]{:S(2)}, u32[]{:S(2)}) %all-to-all-start) | async-done | bytes 589856 | tf_op jit(solution)/shard_map/while/body/eval_jaxpr/all_to_all | solution.py:126
  1368.5 3.6 collective-permute-done
  1372.7 54.2 %all-gather.4 = bf16[32,2,4608]{2,1,0:T(2,128)(2,1)S(1)} all-gather(bf16[1,2,4608]{2,1,0:T(2,128)(2,1)S(1)} %convert_bitcast_fusion.3), channel_id=1, replica_groups=mesh['section'=16,'feat'=32] {'feat'}, dimensions={0}, use_global_device_ids=true | all-gather | bytes 608256 | tf_op jit(solution)/shard_map/while/body/eval_jaxpr/all_gather | solution.py:103
  1431.4 6.2 all-to-all-start
  1438.7 18.7 %all-to-all-done = bf16[32,2,4608]{2,1,0:T(2,128)(2,1)S(1)} async-done(((bf16[32,2,4608]{2,1,0:T(2,128)(2,1)}), bf16[32,2,4608]{2,1,0:T(2,128)(2,1)S(1)}, u32[]{:S(2)}, u32[]{:S(2)}) %all-to-all-start) | async-done | bytes 589856 | tf_op jit(solution)/shard_map/while/body/eval_jaxpr/all_to_all | solution.py:126
  1461.8 3.6 collective-permute-done
  1466.0 54.2 %all-gather.4 = bf16[32,2,4608]{2,1,0:T(2,128)(2,1)S(1)} all-gather(bf16[1,2,4608]{2,1,0:T(2,128)(2,1)S(1)} %convert_bitcast_fusion.3), channel_id=1, replica_groups=mesh['section'=16,'feat'=32] {'feat'}, dimensions={0}, use_global_device_ids=true | all-gather | bytes 608256 | tf_op jit(solution)/shard_map/while/body/eval_jaxpr/all_gather | solution.py:103
  1524.7 6.2 all-to-all-start
  1532.0 18.7 %all-to-all-done = bf16[32,2,4608]{2,1,0:T(2,128)(2,1)S(1)} async-done(((bf16[32,2,4608]{2,1,0:T(2,128)(2,1)}), bf16[32,2,4608]{2,1,0:T(2,128)(2,1)S(1)}, u32[]{:S(2)}, u32[]{:S(2)}) %all-to-all-start) | async-done | bytes 589856 | tf_op jit(solution)/shard_map/while/body/eval_jaxpr/all_to_all | solution.py:126
  1555.2 3.6 collective-permute-done
  1559.4 54.2 %all-gather.4 = bf16[32,2,4608]{2,1,0:T(2,128)(2,1)S(1)} all-gather(bf16[1,2,4608]{2,1,0:T(2,128)(2,1)S(1)} %convert_bitcast_fusion.3), channel_id=1, replica_groups=mesh['section'=16,'feat'=32] {'feat'}, dimensions={0}, use_global_device_ids=true | all-gather | bytes 608256 | tf_op jit(solution)/shard_map/while/body/eval_jaxpr/all_gather | solution.py:103
  1618.1 6.2 all-to-all-start
  1625.4 18.7 %all-to-all-done = bf16[32,2,4608]{2,1,0:T(2,128)(2,1)S(1)} async-done(((bf16[32,2,4608]{2,1,0:T(2,128)(2,1)}), bf16[32,2,4608]{2,1,0:T(2,128)(2,1)S(1)}, u32[]{:S(2)}, u32[]{:S(2)}) %all-to-all-start) | async-done | bytes 589856 | tf_op jit(solution)/shard_map/while/body/eval_jaxpr/all_to_all | solution.py:126
  1648.6 3.6 collective-permute-done
  1652.2 54.2 %all-gather.1 = bf16[32,2,4608]{2,1,0:T(2,128)(2,1)S(1)} all-gather(bf16[1,2,4608]{2,1,0:T(2,128)(2,1)S(1)} %convert_bitcast_fusion.1), channel_id=1, replica_groups=mesh['section'=16,'feat'=32] {'feat'}, dimensions={0}, use_global_device_ids=true | all-gather | bytes 608256 | tf_op jit(solution)/shard_map/all_gather | solution.py:103
  (312 shorter events, 185.6 us)
Async XLA Ops:
  0.0 3.8 copy-start
  7.6 16.5 copy-start.5
  7.6 231.1 %all-to-all-start.1 = ((bf16[32,8,4608]{2,1,0:T(8,128)(2,1)}), bf16[32,8,4608]{2,1,0:T(8,128)(2,1)S(1)}, u32[]{:S(2)}, u32[]{:S(2)}) async-start(bf16[32,8,4608]{2,1,0:T(8,128)(2,1)} %fusion.7), calls=%async_computation.1 | async-start | bytes 4718592 | tf_op jit(solution)/shard_map/all_to_all | solution.py:69
  241.0 2.1 copy-start.2
  243.0 0.6 copy-start.3
  301.7 2.0 copy-start.1
  305.3 31.2 %all-to-all-start = ((bf16[32,2,4608]{2,1,0:T(2,128)(2,1)}), bf16[32,2,4608]{2,1,0:T(2,128)(2,1)S(1)}, u32[]{:S(2)}, u32[]{:S(2)}) async-start(bf16[32,2,4608]{2,1,0:T(2,128)(2,1)} %reshape.317), calls=%async_computation | async-start | bytes 1179648 | tf_op jit(solution)/shard_map/while/body/eval_jaxpr/all_to_all | solution.py:126
  337.8 6.8 collective-permute-start
  344.6 0.6 copy-start.3
  399.6 2.0 copy-start.1
  403.2 27.0 %all-to-all-start = ((bf16[32,2,4608]{2,1,0:T(2,128)(2,1)}), bf16[32,2,4608]{2,1,0:T(2,128)(2,1)S(1)}, u32[]{:S(2)}, u32[]{:S(2)}) async-start(bf16[32,2,4608]{2,1,0:T(2,128)(2,1)} %reshape.317), calls=%async_computation | async-start | bytes 1179648 | tf_op jit(solution)/shard_map/while/body/eval_jaxpr/all_to_all | solution.py:126
  431.5 6.8 collective-permute-start
  438.3 0.6 copy-start.3
  494.0 2.0 copy-start.1
  497.6 26.0 %all-to-all-start = ((bf16[32,2,4608]{2,1,0:T(2,128)(2,1)}), bf16[32,2,4608]{2,1,0:T(2,128)(2,1)S(1)}, u32[]{:S(2)}, u32[]{:S(2)}) async-start(bf16[32,2,4608]{2,1,0:T(2,128)(2,1)} %reshape.317), calls=%async_computation | async-start | bytes 1179648 | tf_op jit(solution)/shard_map/while/body/eval_jaxpr/all_to_all | solution.py:126
  524.9 6.8 collective-permute-start
  531.7 0.6 copy-start.3
  587.4 2.0 copy-start.1
  591.0 26.0 %all-to-all-start = ((bf16[32,2,4608]{2,1,0:T(2,128)(2,1)}), bf16[32,2,4608]{2,1,0:T(2,128)(2,1)S(1)}, u32[]{:S(2)}, u32[]{:S(2)}) async-start(bf16[32,2,4608]{2,1,0:T(2,128)(2,1)} %reshape.317), calls=%async_computation | async-start | bytes 1179648 | tf_op jit(solution)/shard_map/while/body/eval_jaxpr/all_to_all | solution.py:126
  618.3 6.8 collective-permute-start
  625.1 0.6 copy-start.3
  680.8 2.0 copy-start.1
  684.4 26.0 %all-to-all-start = ((bf16[32,2,4608]{2,1,0:T(2,128)(2,1)}), bf16[32,2,4608]{2,1,0:T(2,128)(2,1)S(1)}, u32[]{:S(2)}, u32[]{:S(2)}) async-start(bf16[32,2,4608]{2,1,0:T(2,128)(2,1)} %reshape.317), calls=%async_computation | async-start | bytes 1179648 | tf_op jit(solution)/shard_map/while/body/eval_jaxpr/all_to_all | solution.py:126
  711.6 6.8 collective-permute-start
  718.4 0.6 copy-start.3
  774.2 2.0 copy-start.1
  777.7 26.0 %all-to-all-start = ((bf16[32,2,4608]{2,1,0:T(2,128)(2,1)}), bf16[32,2,4608]{2,1,0:T(2,128)(2,1)S(1)}, u32[]{:S(2)}, u32[]{:S(2)}) async-start(bf16[32,2,4608]{2,1,0:T(2,128)(2,1)} %reshape.317), calls=%async_computation | async-start | bytes 1179648 | tf_op jit(solution)/shard_map/while/body/eval_jaxpr/all_to_all | solution.py:126
  805.0 6.8 collective-permute-start
  811.8 0.6 copy-start.3
  867.5 2.0 copy-start.1
  871.1 26.0 %all-to-all-start = ((bf16[32,2,4608]{2,1,0:T(2,128)(2,1)}), bf16[32,2,4608]{2,1,0:T(2,128)(2,1)S(1)}, u32[]{:S(2)}, u32[]{:S(2)}) async-start(bf16[32,2,4608]{2,1,0:T(2,128)(2,1)} %reshape.317), calls=%async_computation | async-start | bytes 1179648 | tf_op jit(solution)/shard_map/while/body/eval_jaxpr/all_to_all | solution.py:126
  898.4 6.8 collective-permute-start
  905.2 0.6 copy-start.3
  960.9 2.0 copy-start.1
  964.5 26.0 %all-to-all-start = ((bf16[32,2,4608]{2,1,0:T(2,128)(2,1)}), bf16[32,2,4608]{2,1,0:T(2,128)(2,1)S(1)}, u32[]{:S(2)}, u32[]{:S(2)}) async-start(bf16[32,2,4608]{2,1,0:T(2,128)(2,1)} %reshape.317), calls=%async_computation | async-start | bytes 1179648 | tf_op jit(solution)/shard_map/while/body/eval_jaxpr/all_to_all | solution.py:126
  991.7 6.8 collective-permute-start
  998.6 0.6 copy-start.3
  1054.3 2.0 copy-start.1
  1057.9 26.0 %all-to-all-start = ((bf16[32,2,4608]{2,1,0:T(2,128)(2,1)}), bf16[32,2,4608]{2,1,0:T(2,128)(2,1)S(1)}, u32[]{:S(2)}, u32[]{:S(2)}) async-start(bf16[32,2,4608]{2,1,0:T(2,128)(2,1)} %reshape.317), calls=%async_computation | async-start | bytes 1179648 | tf_op jit(solution)/shard_map/while/body/eval_jaxpr/all_to_all | solution.py:126
  1085.1 6.8 collective-permute-start
  1091.9 0.6 copy-start.3
  1147.7 2.0 copy-start.1
  1151.2 26.0 %all-to-all-start = ((bf16[32,2,4608]{2,1,0:T(2,128)(2,1)}), bf16[32,2,4608]{2,1,0:T(2,128)(2,1)S(1)}, u32[]{:S(2)}, u32[]{:S(2)}) async-start(bf16[32,2,4608]{2,1,0:T(2,128)(2,1)} %reshape.317), calls=%async_computation | async-start | bytes 1179648 | tf_op jit(solution)/shard_map/while/body/eval_jaxpr/all_to_all | solution.py:126
  1178.5 6.8 collective-permute-start
  1185.3 0.6 copy-start.3
  1241.0 2.0 copy-start.1
  1244.6 26.0 %all-to-all-start = ((bf16[32,2,4608]{2,1,0:T(2,128)(2,1)}), bf16[32,2,4608]{2,1,0:T(2,128)(2,1)S(1)}, u32[]{:S(2)}, u32[]{:S(2)}) async-start(bf16[32,2,4608]{2,1,0:T(2,128)(2,1)} %reshape.317), calls=%async_computation | async-start | bytes 1179648 | tf_op jit(solution)/shard_map/while/body/eval_jaxpr/all_to_all | solution.py:126
  1271.9 6.8 collective-permute-start
  1278.7 0.6 copy-start.3
  1334.4 2.0 copy-start.1
  1338.0 26.0 %all-to-all-start = ((bf16[32,2,4608]{2,1,0:T(2,128)(2,1)}), bf16[32,2,4608]{2,1,0:T(2,128)(2,1)S(1)}, u32[]{:S(2)}, u32[]{:S(2)}) async-start(bf16[32,2,4608]{2,1,0:T(2,128)(2,1)} %reshape.317), calls=%async_computation | async-start | bytes 1179648 | tf_op jit(solution)/shard_map/while/body/eval_jaxpr/all_to_all | solution.py:126
  1365.2 6.8 collective-permute-start
  1372.1 0.6 copy-start.3
  1427.8 2.0 copy-start.1
  1431.4 26.0 %all-to-all-start = ((bf16[32,2,4608]{2,1,0:T(2,128)(2,1)}), bf16[32,2,4608]{2,1,0:T(2,128)(2,1)S(1)}, u32[]{:S(2)}, u32[]{:S(2)}) async-start(bf16[32,2,4608]{2,1,0:T(2,128)(2,1)} %reshape.317), calls=%async_computation | async-start | bytes 1179648 | tf_op jit(solution)/shard_map/while/body/eval_jaxpr/all_to_all | solution.py:126
  1458.6 6.8 collective-permute-start
  1465.4 0.6 copy-start.3
  1521.2 2.0 copy-start.1
  1524.7 26.0 %all-to-all-start = ((bf16[32,2,4608]{2,1,0:T(2,128)(2,1)}), bf16[32,2,4608]{2,1,0:T(2,128)(2,1)S(1)}, u32[]{:S(2)}, u32[]{:S(2)}) async-start(bf16[32,2,4608]{2,1,0:T(2,128)(2,1)} %reshape.317), calls=%async_computation | async-start | bytes 1179648 | tf_op jit(solution)/shard_map/while/body/eval_jaxpr/all_to_all | solution.py:126
  1552.0 6.8 collective-permute-start
  1614.5 2.0 copy-start.1
  1618.1 26.0 %all-to-all-start = ((bf16[32,2,4608]{2,1,0:T(2,128)(2,1)}), bf16[32,2,4608]{2,1,0:T(2,128)(2,1)S(1)}, u32[]{:S(2)}, u32[]{:S(2)}) async-start(bf16[32,2,4608]{2,1,0:T(2,128)(2,1)} %reshape.317), calls=%async_computation | async-start | bytes 1179648 | tf_op jit(solution)/shard_map/while/body/eval_jaxpr/all_to_all | solution.py:126
  1645.4 6.8 collective-permute-start
  1706.6 1.9 copy-start.4
  (1 other events, 0.6 us)
where the time goes:
time: 1710 us
  blocking collectives  1070 us (63%)
  waiting for transfers between devices  334 us (20%)
  starting transfers between devices  144 us (8%)
  other arithmetic  60.3 us (4%)
  matrix products  49.9 us (3%)
  local copies, waits for them, and re-layouts  46 us (3%)
    all_gather x16, blocking collectives, gathered_products(): lax.all_gather(adjoint_rows.astype(jnp.bfloat16), 'feat', axis=0, tiled=T...  869 us
    all_to_all x15, waiting for transfers between devices, propagate(): lax.all_to_all(head_term.reshape(feat_count, rows_dev, model_width), 'fea...  281 us
    psum x1, blocking collectives, per_device(): lax.psum(enc_part.astype(jnp.bfloat16), 'feat').astype(jnp.float32)  205 us
    all_to_all x15, starting transfers between devices, propagate(): lax.all_to_all(head_term.reshape(feat_count, rows_dev, model_width), 'fea...  98.3 us
    ppermute x15, waiting for transfers between devices, shifted(): return lax.ppermute(shard, axis, pairs)  53.8 us
  transfers between devices with their start and end apart: 31, of which 30 were waited for; matrix products, arithmetic and copies ran while one was open for 3% of the time, Pallas kernels for 0%

commit v1 on v0

v1 whole, which is shorter than its diff:
```python
import jax
import jax.numpy as jnp
from jax import lax
from jax.sharding import Mesh, PartitionSpec as P

K_ACT = 256
BF = jnp.bfloat16
F32 = jnp.float32
FEAT = ("y2", "par", "zh", "core")
CHIPS = ("y2", "par", "zh")
QUADS = 4
SWAP = [(0, 1), (1, 0)]


def neighbour_heads(shard):
    pairs = []
    for y in range(8):
        pairs.append((2 * y, 2 * ((y - 1) % 8)))
        pairs.append((2 * y + 1, 2 * ((y + 1) % 8) + 1))
    split = [(y * 2 + core) for y in range(8) for core in range(2)]
    assert len(split) == len(pairs)
    return lax.ppermute(shard, ("y2", "par", "core"), pairs)


def send_down(shard, step, by, sections):
    pairs = []
    for section in range(1, sections - step):
        for i in range(QUADS):
            pairs.append((section * QUADS + i, (section - 1) * QUADS + (i + by) % QUADS))
    return lax.ppermute(shard, ("section", "y2"), pairs)


def decoder_panel(dec_table, act_ids, entries_dev, feat_index, feat_count):
    feat_rows, model_width = dec_table.shape
    slot_count = 2 * entries_dev // feat_count
    ids_blocks = act_ids.reshape(feat_count, entries_dev)
    owner_ids = ids_blocks // feat_rows
    local_ids = ids_blocks % feat_rows
    owned_mask = owner_ids == feat_index
    entry_iota = jnp.arange(entries_dev, dtype=jnp.int32)
    before = (entry_iota[:, None] < entry_iota[None, :]).astype(BF)
    slot_rank = jnp.dot(owned_mask.astype(BF), before, preferred_element_type=F32).astype(jnp.int32)
    slot_iota = jnp.arange(slot_count, dtype=jnp.int32)
    selected = (
        owned_mask[:, None, :] & (slot_rank[:, None, :] == slot_iota[None, :, None])
    ).astype(jnp.int32)
    source_row = jnp.sum(selected * local_ids[:, None, :], axis=2)
    outgoing = jnp.take(dec_table, source_row.reshape(-1), axis=0).reshape(
        feat_count, slot_count, model_width
    )
    own_owner = lax.dynamic_index_in_dim(owner_ids, feat_index, 0, keepdims=False)
    earlier = (entry_iota[None, :] < entry_iota[:, None]).astype(jnp.int32)
    same_owner = (own_owner[:, None] == own_owner[None, :]).astype(jnp.int32)
    own_rank = jnp.sum(earlier * same_owner, axis=1)
    flat_index = own_owner * slot_count + own_rank
    incoming = lax.all_to_all(outgoing, FEAT, split_axis=0, concat_axis=0, tiled=True)
    return jnp.take(incoming.reshape(feat_count * slot_count, model_width), flat_index, axis=0)


def per_device(
    decoders,
    encoders,
    out_proj,
    value_proj,
    attention,
    norm_scale,
    act_ids,
    act_values,
    target_ids,
    target_pos,
):
    sections = lax.axis_size("section")
    section_index = lax.axis_index("section")
    feat_index = lax.axis_index(FEAT)
    feat_count = lax.axis_size(FEAT)
    model_width = decoders.shape[2]
    half = model_width // 2
    feat_rows = decoders.shape[1]
    seq_len = attention.shape[2]
    head_width = out_proj.shape[1]
    entries_dev = act_values.shape[1]
    targets = target_ids.shape[0]

    own = (out_proj[0], value_proj[0], attention[0, 0])
    beyond = tuple(lax.ppermute(a, "zh", SWAP) for a in own)
    near = tuple(neighbour_heads(a) for a in own)

    feat_iota = jnp.arange(feat_rows, dtype=jnp.int32)
    target_pick = (
        (target_ids - feat_index * feat_rows)[:, None] == feat_iota[None, :]
    ).astype(BF)
    enc_rows = jnp.dot(target_pick, encoders[0], preferred_element_type=F32).astype(BF)
    enc_send = jnp.broadcast_to(
        enc_rows.reshape(1, targets, 2, half), (QUADS, targets, 2, half)
    ).reshape(feat_count, half)
    enc_got = lax.all_to_all(enc_send, FEAT, split_axis=0, concat_axis=0, tiled=True)
    enc_row = jnp.sum(enc_got.astype(F32), axis=0)
    own_target = lax.axis_index(("par", "zh"))
    own_pos = lax.dynamic_index_in_dim(target_pos, own_target, 0, keepdims=False)
    positions = jnp.arange(seq_len, dtype=jnp.int32)
    rows = jnp.where((positions == own_pos)[:, None], enc_row[None, :], 0.0)

    far = tuple(neighbour_heads(a) for a in beyond)
    out_parts, value_parts, mix_parts = [], [], []
    for out_head, value_head, mix_head in (own, near, beyond, far):
        out_parts.append(
            lax.all_to_all(
                out_head.reshape(head_width, 2, half).transpose(1, 0, 2),
                "core",
                split_axis=0,
                concat_axis=0,
                tiled=True,
            ).reshape(2 * head_width, half)
        )
        got = lax.all_to_all(
            value_head.reshape(2, half, head_width), "core", split_axis=0, concat_axis=0, tiled=True
        )
        value_parts += [got[0], got[1]]
        mix_parts.append(lax.all_gather(mix_head, "core", axis=0))
    out_weight = jnp.concatenate(out_parts, axis=0)
    value_weight = jnp.concatenate(value_parts, axis=1)
    mixing = jnp.concatenate(mix_parts, axis=0)
    heads = mixing.shape[0]
    mix_wide = jnp.broadcast_to(
        mixing.transpose(1, 2, 0)[..., None], (seq_len, seq_len, heads, head_width)
    ).reshape(seq_len, seq_len, heads * head_width)
    scales = norm_scale[0][:, None]

    history = [rows.astype(BF)]
    for step in range(sections - 1):
        grad_part = lax.dot_general(
            history[-1], out_weight, (((1,), (1,)), ((), ())), preferred_element_type=F32
        )
        grads = jnp.sum(lax.all_gather(grad_part, "core", axis=0), axis=0)
        mixed = jnp.sum(mix_wide * grads[:, None, :], axis=0).astype(BF)
        term = lax.dot_general(
            mixed, value_weight, (((1,), (1,)), ((), ())), preferred_element_type=F32
        )
        share = (rows * (1.0 / QUADS) + term * scales).astype(BF)
        arrived = [send_down(share, step, by, sections) for by in range(QUADS)]
        rows = sum(a.astype(F32) for a in arrived)
        history.append(rows.astype(BF))

    panel = decoder_panel(decoders[0], act_ids[0], entries_dev, feat_index, feat_count)

    steps_each = sections // QUADS
    held = jnp.stack(history)
    first = lax.axis_index("y2") * steps_each
    held = lax.dynamic_slice_in_dim(held, first, steps_each, 0).transpose(1, 0, 2)
    got = lax.all_to_all(held, CHIPS, split_axis=0, concat_axis=0, tiled=True)
    got = lax.all_gather(got.reshape(-1, half), "core", axis=0)
    raw = sum(
        lax.dot_general(
            got[core],
            panel[:, core * half : (core + 1) * half],
            (((1,), (1,)), ((), ())),
            preferred_element_type=F32,
        )
        for core in range(2)
    )
    edges = raw.reshape(QUADS, targets, steps_each, entries_dev).transpose(0, 2, 1, 3)
    edges = edges.reshape(sections * targets, entries_dev) * act_values[0][None, :]
    padded = jnp.concatenate([jnp.zeros_like(edges), edges], axis=0)
    edges = lax.dynamic_slice_in_dim(
        padded, (sections - section_index) * targets, sections * targets, 0
    )
    return edges[None]


def solution(mesh):
    sections = mesh.shape["section"]
    fine = Mesh(mesh.devices.reshape(sections, 4, 2, 2, 2), ("section", *FEAT))
    in_specs = (
        P("section", FEAT, None),
        P("section", FEAT, None),
        P("section", FEAT, None),
        P("section", None, FEAT),
        P("section", FEAT, None, None),
        P("section", None),
        P("section", None),
        P("section", FEAT),
        P("section"),
        P("section"),
    )
    return jax.shard_map(
        per_device, mesh=fine, in_specs=in_specs, out_specs=P("section", None, FEAT), check_vma=False
    )
```

time: 1710 us -> 1130 us (0.66)
  the two profiles are of different devices: /device:TPU:7 before, /device:TPU:1 now
where the time goes in v1:
time: 1130 us; the launch traced here: 1110 us
  starting transfers between devices  679 us (60%)
  waiting for transfers between devices  190 us (17%)
  matrix products  111 us (10%)
  blocking collectives  53.7 us (5%)
  local copies, waits for them, and re-layouts  46.2 us (4%)
  other arithmetic  31.8 us (3%)
    ppermute x60, starting transfers between devices, send_down(): return lax.ppermute(shard, ('section', 'y2'), pairs)  540 us
    ppermute x60, waiting for transfers between devices, send_down(): return lax.ppermute(shard, ('section', 'y2'), pairs)  110 us
    dot_general x15, matrix products, per_device(): lax.dot_general(mixed, value_weight, (((1,), (1,)), ((), ())), preferred_...  55.6 us
    dot_general x15, matrix products, per_device(): lax.dot_general(history[-1], out_weight, (((1,), (1,)), ((), ())), prefer...  50 us
    ppermute x3, starting transfers between devices, per_device(): beyond = tuple((lax.ppermute(a, 'zh', SWAP) for a in own))  48 us
    all_to_all x1, waiting for transfers between devices, decoder_panel(): lax.all_to_all(outgoing, FEAT, split_axis=0, concat_axis=0, tiled=True)  47.4 us
    all_gather x15, blocking collectives, per_device(): grads = jnp.sum(lax.all_gather(grad_part, 'core', axis=0), axis=0)  36.5 us
    all_to_all x4, starting transfers between devices, per_device(): lax.all_to_all(out_head.reshape(head_width, 2, half).transpose(1, 0, 2),...  23.4 us
  transfers between devices with their start and end apart: 80, of which 40 were waited for; matrix products, arithmetic and copies ran while one was open for 5% of the time, Pallas kernels for 0%

profile of v1, /device:TPU:1, one launch (start us, length us, event | category | flops | bytes accessed | tf_op | source)
XLA Modules:
  0.0 1112.2 jit_solution(1589773920571421733)
XLA Ops:
  0.0 4.2 collective-permute-start.6
  4.2 18.0 %collective-permute-start.7 = (bf16[4608,128]{1,0:T(8,128)(2,1)}, bf16[4608,128]{1,0:T(8,128)(2,1)}, u32[]{:S(2)}, u32[]{:S(2)}) collective-permute-start(bf16[4608,128]{1,0:T(8,128)(2,1)} %bitcast.289), channel_id=1, source_target_pairs={{0,2},{2,0},{1,3},{3,1},{4,6},{6,4},{5,7},{7,5},{8,10},{10,8},{9,1... | collective-permute-start | bytes 3538952 | tf_op jit(solution)/shard_map/ppermute | solution.py:85
  22.2 16.7 %collective-permute-start.1 = (f32[16,16]{1,0:T(8,128)}, f32[16,16]{1,0:T(8,128)S(1)}, u32[]{:S(2)}, u32[]{:S(2)}) collective-permute-start(f32[16,16]{1,0:T(8,128)} %bitcast.375), channel_id=1, source_target_pairs={{0,2},{2,0},{1,3},{3,1},{4,6},{6,4},{5,7},{7,5},{8,10},{10,8},{9,1... | collective-permute-start | bytes 3080 | tf_op jit(solution)/shard_map/ppermute | solution.py:85
  42.2 6.4 all-to-all-start.5
  51.0 13.2 %collective-permute-start.4 = (bf16[128,4608]{0,1:T(8,128)(2,1)}, bf16[128,4608]{0,1:T(8,128)(2,1)}, u32[]{:S(2)}, u32[]{:S(2)}) collective-permute-start(bf16[128,4608]{0,1:T(8,128)(2,1)} %bitcast.11), channel_id=1, source_target_pairs={{0,2},{2,0},{1,3},{3,1},{4,6},{6,4},{5,7},{7,5},{8,10},{10,8},{9,1... | collective-permute-start | bytes 3538952 | tf_op jit(solution)/shard_map/ppermute | solution.py:85
  64.8 7.9 all-to-all-start.1
  86.0 10.4 all-to-all-start
  103.2 6.5 collective-permute-done.1
  112.9 4.7 all-gather.2
  124.9 10.8 all-to-all-done
  137.4 5.0 all-to-all-start.6
  148.7 6.5 all-to-all-start.3
  159.2 4.5 all-to-all-start.2
  166.1 4.5 all-to-all-start.7
  177.0 4.5 all-to-all-start.4
  183.4 4.8 all-to-all-start.8
  207.0 7.5 collective-permute-start.12
  214.5 16.7 %collective-permute-start.11 = (bf16[16,2304]{1,0:T(8,128)(2,1)S(1)}, bf16[16,2304]{1,0:T(8,128)(2,1)S(1)}, u32[]{:S(2)}, u32[]{:S(2)}) collective-permute-start(bf16[16,2304]{1,0:T(8,128)(2,1)S(1)} %fusion.1), channel_id=1, source_target_pairs={{32,16},{40,24},{48,0},{56,8},{64,48},{72,56},{80,32},{88,40},{96,... | collective-permute-start | bytes 221192 | tf_op jit(solution)/shard_map/ppermute | solution.py:30
  231.2 16.7 %collective-permute-start.10 = (bf16[16,2304]{1,0:T(8,128)(2,1)S(1)}, bf16[16,2304]{1,0:T(8,128)(2,1)S(1)}, u32[]{:S(2)}, u32[]{:S(2)}) collective-permute-start(bf16[16,2304]{1,0:T(8,128)(2,1)S(1)} %fusion.1), channel_id=1, source_target_pairs={{32,8},{40,16},{48,24},{56,0},{64,40},{72,48},{80,56},{88,32},{96,... | collective-permute-start | bytes 221192 | tf_op jit(solution)/shard_map/ppermute | solution.py:30
  248.0 16.7 %collective-permute-start.9 = (bf16[16,2304]{1,0:T(8,128)(2,1)S(1)}, bf16[16,2304]{1,0:T(8,128)(2,1)S(1)}, u32[]{:S(2)}, u32[]{:S(2)}) collective-permute-start(bf16[16,2304]{1,0:T(8,128)(2,1)S(1)} %fusion.1), channel_id=1, source_target_pairs={{32,0},{40,8},{48,16},{56,24},{64,32},{72,40},{80,48},{88,56},{96,... | collective-permute-start | bytes 221192 | tf_op jit(solution)/shard_map/ppermute | solution.py:30
  277.5 15.6 %collective-permute-start.16 = (bf16[16,2304]{1,0:T(8,128)(2,1)S(1)}, bf16[16,2304]{1,0:T(8,128)(2,1)S(1)}, u32[]{:S(2)}, u32[]{:S(2)}) collective-permute-start(bf16[16,2304]{1,0:T(8,128)(2,1)S(1)} %add_convert_fusion.14), channel_id=1, source_target_pairs={{32,24},{40,0},{48,8},{56,16},{64,56},{72,32},{80,40},{88,48},{96,... | collective-permute-start | bytes 221192 | tf_op jit(solution)/shard_map/ppermute | solution.py:30
  293.1 16.7 %collective-permute-start.15 = (bf16[16,2304]{1,0:T(8,128)(2,1)S(1)}, bf16[16,2304]{1,0:T(8,128)(2,1)S(1)}, u32[]{:S(2)}, u32[]{:S(2)}) collective-permute-start(bf16[16,2304]{1,0:T(8,128)(2,1)S(1)} %add_convert_fusion.14), channel_id=1, source_target_pairs={{32,16},{40,24},{48,0},{56,8},{64,48},{72,56},{80,32},{88,40},{96,... | collective-permute-start | bytes 221192 | tf_op jit(solution)/shard_map/ppermute | solution.py:30
  309.9 16.7 %collective-permute-start.14 = (bf16[16,2304]{1,0:T(8,128)(2,1)S(1)}, bf16[16,2304]{1,0:T(8,128)(2,1)S(1)}, u32[]{:S(2)}, u32[]{:S(2)}) collective-permute-start(bf16[16,2304]{1,0:T(8,128)(2,1)S(1)} %add_convert_fusion.14), channel_id=1, source_target_pairs={{32,8},{40,16},{48,24},{56,0},{64,40},{72,48},{80,56},{88,32},{96,... | collective-permute-start | bytes 221192 | tf_op jit(solution)/shard_map/ppermute | solution.py:30
  326.6 17.2 %collective-permute-start.13 = (bf16[16,2304]{1,0:T(8,128)(2,1)S(1)}, bf16[16,2304]{1,0:T(8,128)(2,1)S(1)}, u32[]{:S(2)}, u32[]{:S(2)}) collective-permute-start(bf16[16,2304]{1,0:T(8,128)(2,1)S(1)} %add_convert_fusion.14), channel_id=1, source_target_pairs={{32,0},{40,8},{48,16},{56,24},{64,32},{72,40},{80,48},{88,56},{96,... | collective-permute-start | bytes 221192 | tf_op jit(solution)/shard_map/ppermute | solution.py:30
  343.8 3.9 collective-permute-done.13
  358.5 15.6 %collective-permute-start.20 = (bf16[16,2304]{1,0:T(8,128)(2,1)S(1)}, bf16[16,2304]{1,0:T(8,128)(2,1)S(1)}, u32[]{:S(2)}, u32[]{:S(2)}) collective-permute-start(bf16[16,2304]{1,0:T(8,128)(2,1)S(1)} %add_convert_fusion.13), channel_id=1, source_target_pairs={{32,24},{40,0},{48,8},{56,16},{64,56},{72,32},{80,40},{88,48},{96,... | collective-permute-start | bytes 221192 | tf_op jit(solution)/shard_map/ppermute | solution.py:30
  374.1 16.7 %collective-permute-start.19 = (bf16[16,2304]{1,0:T(8,128)(2,1)S(1)}, bf16[16,2304]{1,0:T(8,128)(2,1)S(1)}, u32[]{:S(2)}, u32[]{:S(2)}) collective-permute-start(bf16[16,2304]{1,0:T(8,128)(2,1)S(1)} %add_convert_fusion.13), channel_id=1, source_target_pairs={{32,16},{40,24},{48,0},{56,8},{64,48},{72,56},{80,32},{88,40},{96,... | collective-permute-start | bytes 221192 | tf_op jit(solution)/shard_map/ppermute | solution.py:30
  390.9 16.7 %collective-permute-start.18 = (bf16[16,2304]{1,0:T(8,128)(2,1)S(1)}, bf16[16,2304]{1,0:T(8,128)(2,1)S(1)}, u32[]{:S(2)}, u32[]{:S(2)}) collective-permute-start(bf16[16,2304]{1,0:T(8,128)(2,1)S(1)} %add_convert_fusion.13), channel_id=1, source_target_pairs={{32,8},{40,16},{48,24},{56,0},{64,40},{72,48},{80,56},{88,32},{96,... | collective-permute-start | bytes 221192 | tf_op jit(solution)/shard_map/ppermute | solution.py:30
  407.6 16.7 %collective-permute-start.17 = (bf16[16,2304]{1,0:T(8,128)(2,1)S(1)}, bf16[16,2304]{1,0:T(8,128)(2,1)S(1)}, u32[]{:S(2)}, u32[]{:S(2)}) collective-permute-start(bf16[16,2304]{1,0:T(8,128)(2,1)S(1)} %add_convert_fusion.13), channel_id=1, source_target_pairs={{32,0},{40,8},{48,16},{56,24},{64,32},{72,40},{80,48},{88,56},{96,... | collective-permute-start | bytes 221192 | tf_op jit(solution)/shard_map/ppermute | solution.py:30
  424.4 4.3 collective-permute-done.17
  439.5 15.6 %collective-permute-start.24 = (bf16[16,2304]{1,0:T(8,128)(2,1)S(1)}, bf16[16,2304]{1,0:T(8,128)(2,1)S(1)}, u32[]{:S(2)}, u32[]{:S(2)}) collective-permute-start(bf16[16,2304]{1,0:T(8,128)(2,1)S(1)} %add_convert_fusion.12), channel_id=1, source_target_pairs={{32,24},{40,0},{48,8},{56,16},{64,56},{72,32},{80,40},{88,48},{96,... | collective-permute-start | bytes 221192 | tf_op jit(solution)/shard_map/ppermute | solution.py:30
  455.1 16.7 %collective-permute-start.23 = (bf16[16,2304]{1,0:T(8,128)(2,1)S(1)}, bf16[16,2304]{1,0:T(8,128)(2,1)S(1)}, u32[]{:S(2)}, u32[]{:S(2)}) collective-permute-start(bf16[16,2304]{1,0:T(8,128)(2,1)S(1)} %add_convert_fusion.12), channel_id=1, source_target_pairs={{32,16},{40,24},{48,0},{56,8},{64,48},{72,56},{80,32},{88,40},{96,... | collective-permute-start | bytes 221192 | tf_op jit(solution)/shard_map/ppermute | solution.py:30
  471.8 16.7 %collective-permute-start.22 = (bf16[16,2304]{1,0:T(8,128)(2,1)S(1)}, bf16[16,2304]{1,0:T(8,128)(2,1)S(1)}, u32[]{:S(2)}, u32[]{:S(2)}) collective-permute-start(bf16[16,2304]{1,0:T(8,128)(2,1)S(1)} %add_convert_fusion.12), channel_id=1, source_target_pairs={{32,8},{40,16},{48,24},{56,0},{64,40},{72,48},{80,56},{88,32},{96,... | collective-permute-start | bytes 221192 | tf_op jit(solution)/shard_map/ppermute | solution.py:30
  488.6 16.7 %collective-permute-start.21 = (bf16[16,2304]{1,0:T(8,128)(2,1)S(1)}, bf16[16,2304]{1,0:T(8,128)(2,1)S(1)}, u32[]{:S(2)}, u32[]{:S(2)}) collective-permute-start(bf16[16,2304]{1,0:T(8,128)(2,1)S(1)} %add_convert_fusion.12), channel_id=1, source_target_pairs={{32,0},{40,8},{48,16},{56,24},{64,32},{72,40},{80,48},{88,56},{96,... | collective-permute-start | bytes 221192 | tf_op jit(solution)/shard_map/ppermute | solution.py:30
  505.3 4.3 collective-permute-done.21
  520.5 15.6 %collective-permute-start.28 = (bf16[16,2304]{1,0:T(8,128)(2,1)S(1)}, bf16[16,2304]{1,0:T(8,128)(2,1)S(1)}, u32[]{:S(2)}, u32[]{:S(2)}) collective-permute-start(bf16[16,2304]{1,0:T(8,128)(2,1)S(1)} %add_convert_fusion.11), channel_id=1, source_target_pairs={{32,24},{40,0},{48,8},{56,16},{64,56},{72,32},{80,40},{88,48},{96,... | collective-permute-start | bytes 221192 | tf_op jit(solution)/shard_map/ppermute | solution.py:30
  536.1 16.7 %collective-permute-start.27 = (bf16[16,2304]{1,0:T(8,128)(2,1)S(1)}, bf16[16,2304]{1,0:T(8,128)(2,1)S(1)}, u32[]{:S(2)}, u32[]{:S(2)}) collective-permute-start(bf16[16,2304]{1,0:T(8,128)(2,1)S(1)} %add_convert_fusion.11), channel_id=1, source_target_pairs={{32,16},{40,24},{48,0},{56,8},{64,48},{72,56},{80,32},{88,40},{96,... | collective-permute-start | bytes 221192 | tf_op jit(solution)/shard_map/ppermute | solution.py:30
  552.8 16.7 %collective-permute-start.26 = (bf16[16,2304]{1,0:T(8,128)(2,1)S(1)}, bf16[16,2304]{1,0:T(8,128)(2,1)S(1)}, u32[]{:S(2)}, u32[]{:S(2)}) collective-permute-start(bf16[16,2304]{1,0:T(8,128)(2,1)S(1)} %add_convert_fusion.11), channel_id=1, source_target_pairs={{32,8},{40,16},{48,24},{56,0},{64,40},{72,48},{80,56},{88,32},{96,... | collective-permute-start | bytes 221192 | tf_op jit(solution)/shard_map/ppermute | solution.py:30
  569.6 16.7 %collective-permute-start.25 = (bf16[16,2304]{1,0:T(8,128)(2,1)S(1)}, bf16[16,2304]{1,0:T(8,128)(2,1)S(1)}, u32[]{:S(2)}, u32[]{:S(2)}) collective-permute-start(bf16[16,2304]{1,0:T(8,128)(2,1)S(1)} %add_convert_fusion.11), channel_id=1, source_target_pairs={{32,0},{40,8},{48,16},{56,24},{64,32},{72,40},{80,48},{88,56},{96,... | collective-permute-start | bytes 221192 | tf_op jit(solution)/shard_map/ppermute | solution.py:30
  586.3 4.3 collective-permute-done.25
  601.5 15.6 %collective-permute-start.32 = (bf16[16,2304]{1,0:T(8,128)(2,1)S(1)}, bf16[16,2304]{1,0:T(8,128)(2,1)S(1)}, u32[]{:S(2)}, u32[]{:S(2)}) collective-permute-start(bf16[16,2304]{1,0:T(8,128)(2,1)S(1)} %add_convert_fusion.10), channel_id=1, source_target_pairs={{32,24},{40,0},{48,8},{56,16},{64,56},{72,32},{80,40},{88,48},{96,... | collective-permute-start | bytes 221192 | tf_op jit(solution)/shard_map/ppermute | solution.py:30
  617.1 16.7 %collective-permute-start.31 = (bf16[16,2304]{1,0:T(8,128)(2,1)S(1)}, bf16[16,2304]{1,0:T(8,128)(2,1)S(1)}, u32[]{:S(2)}, u32[]{:S(2)}) collective-permute-start(bf16[16,2304]{1,0:T(8,128)(2,1)S(1)} %add_convert_fusion.10), channel_id=1, source_target_pairs={{32,16},{40,24},{48,0},{56,8},{64,48},{72,56},{80,32},{88,40},{96,... | collective-permute-start | bytes 221192 | tf_op jit(solution)/shard_map/ppermute | solution.py:30
  633.8 16.7 %collective-permute-start.30 = (bf16[16,2304]{1,0:T(8,128)(2,1)S(1)}, bf16[16,2304]{1,0:T(8,128)(2,1)S(1)}, u32[]{:S(2)}, u32[]{:S(2)}) collective-permute-start(bf16[16,2304]{1,0:T(8,128)(2,1)S(1)} %add_convert_fusion.10), channel_id=1, source_target_pairs={{32,8},{40,16},{48,24},{56,0},{64,40},{72,48},{80,56},{88,32},{96,... | collective-permute-start | bytes 221192 | tf_op jit(solution)/shard_map/ppermute | solution.py:30
  650.6 16.7 %collective-permute-start.29 = (bf16[16,2304]{1,0:T(8,128)(2,1)S(1)}, bf16[16,2304]{1,0:T(8,128)(2,1)S(1)}, u32[]{:S(2)}, u32[]{:S(2)}) collective-permute-start(bf16[16,2304]{1,0:T(8,128)(2,1)S(1)} %add_convert_fusion.10), channel_id=1, source_target_pairs={{32,0},{40,8},{48,16},{56,24},{64,32},{72,40},{80,48},{88,56},{96,... | collective-permute-start | bytes 221192 | tf_op jit(solution)/shard_map/ppermute | solution.py:30
  667.3 4.3 collective-permute-done.29
  682.5 15.6 %collective-permute-start.36 = (bf16[16,2304]{1,0:T(8,128)(2,1)S(1)}, bf16[16,2304]{1,0:T(8,128)(2,1)S(1)}, u32[]{:S(2)}, u32[]{:S(2)}) collective-permute-start(bf16[16,2304]{1,0:T(8,128)(2,1)S(1)} %add_convert_fusion.9), channel_id=1, source_target_pairs={{32,24},{40,0},{48,8},{56,16},{64,56},{72,32},{80,40},{88,48},{96,... | collective-permute-start | bytes 221192 | tf_op jit(solution)/shard_map/ppermute | solution.py:30
  698.1 16.7 %collective-permute-start.35 = (bf16[16,2304]{1,0:T(8,128)(2,1)S(1)}, bf16[16,2304]{1,0:T(8,128)(2,1)S(1)}, u32[]{:S(2)}, u32[]{:S(2)}) collective-permute-start(bf16[16,2304]{1,0:T(8,128)(2,1)S(1)} %add_convert_fusion.9), channel_id=1, source_target_pairs={{32,16},{40,24},{48,0},{56,8},{64,48},{72,56},{80,32},{88,40},{96,... | collective-permute-start | bytes 221192 | tf_op jit(solution)/shard_map/ppermute | solution.py:30
  714.8 16.7 %collective-permute-start.34 = (bf16[16,2304]{1,0:T(8,128)(2,1)S(1)}, bf16[16,2304]{1,0:T(8,128)(2,1)S(1)}, u32[]{:S(2)}, u32[]{:S(2)}) collective-permute-start(bf16[16,2304]{1,0:T(8,128)(2,1)S(1)} %add_convert_fusion.9), channel_id=1, source_target_pairs={{32,8},{40,16},{48,24},{56,0},{64,40},{72,48},{80,56},{88,32},{96,... | collective-permute-start | bytes 221192 | tf_op jit(solution)/shard_map/ppermute | solution.py:30
  731.6 16.7 %collective-permute-start.33 = (bf16[16,2304]{1,0:T(8,128)(2,1)S(1)}, bf16[16,2304]{1,0:T(8,128)(2,1)S(1)}, u32[]{:S(2)}, u32[]{:S(2)}) collective-permute-start(bf16[16,2304]{1,0:T(8,128)(2,1)S(1)} %add_convert_fusion.9), channel_id=1, source_target_pairs={{32,0},{40,8},{48,16},{56,24},{64,32},{72,40},{80,48},{88,56},{96,... | collective-permute-start | bytes 221192 | tf_op jit(solution)/shard_map/ppermute | solution.py:30
  748.3 4.3 collective-permute-done.33
  763.6 15.6 %collective-permute-start.40 = (bf16[16,2304]{1,0:T(8,128)(2,1)S(1)}, bf16[16,2304]{1,0:T(8,128)(2,1)S(1)}, u32[]{:S(2)}, u32[]{:S(2)}) collective-permute-start(bf16[16,2304]{1,0:T(8,128)(2,1)S(1)} %add_convert_fusion.8), channel_id=1, source_target_pairs={{32,24},{40,0},{48,8},{56,16},{64,56},{72,32},{80,40},{88,48},{96,... | collective-permute-start | bytes 221192 | tf_op jit(solution)/shard_map/ppermute | solution.py:30
  779.2 16.7 %collective-permute-start.39 = (bf16[16,2304]{1,0:T(8,128)(2,1)S(1)}, bf16[16,2304]{1,0:T(8,128)(2,1)S(1)}, u32[]{:S(2)}, u32[]{:S(2)}) collective-permute-start(bf16[16,2304]{1,0:T(8,128)(2,1)S(1)} %add_convert_fusion.8), channel_id=1, source_target_pairs={{32,16},{40,24},{48,0},{56,8},{64,48},{72,56},{80,32},{88,40},{96,... | collective-permute-start | bytes 221192 | tf_op jit(solution)/shard_map/ppermute | solution.py:30
  796.0 16.7 %collective-permute-start.38 = (bf16[16,2304]{1,0:T(8,128)(2,1)S(1)}, bf16[16,2304]{1,0:T(8,128)(2,1)S(1)}, u32[]{:S(2)}, u32[]{:S(2)}) collective-permute-start(bf16[16,2304]{1,0:T(8,128)(2,1)S(1)} %add_convert_fusion.8), channel_id=1, source_target_pairs={{32,8},{40,16},{48,24},{56,0},{64,40},{72,48},{80,56},{88,32},{96,... | collective-permute-start | bytes 221192 | tf_op jit(solution)/shard_map/ppermute | solution.py:30
  814.0 7.3 collective-permute-done.38
  840.1 4.4 collective-permute-done.43
  893.6 3.9 collective-permute-done.51
  971.1 5.5 collective-permute-done.64
  976.5 3.8 collective-permute-done.63
  990.8 4.3 add_convert_fusion.1
  1015.7 11.6 %all-to-all-start.9 = ((bf16[16,4,2304]{2,1,0:T(4,128)(2,1)}), bf16[16,4,2304]{2,1,0:T(4,128)(2,1)}, u32[]{:S(2)}, u32[]{:S(2)}) async-start(bf16[16,4,2304]{2,1,0:T(4,128)(2,1)} %copy.51), calls=%async_computation.9 | async-start | bytes 589824 | tf_op jit(solution)/shard_map/all_to_all | solution.py:150
  1029.7 12.7 %all-to-all-done.9 = bf16[16,4,2304]{2,1,0:T(4,128)(2,1)} async-done(((bf16[16,4,2304]{2,1,0:T(4,128)(2,1)}), bf16[16,4,2304]{2,1,0:T(4,128)(2,1)}, u32[]{:S(2)}, u32[]{:S(2)}) %all-to-all-start.9) | async-done | bytes 294944 | tf_op jit(solution)/shard_map/all_to_all | solution.py:150
  1042.5 6.2 all-to-all-start.10
  1051.8 5.5 all_gather.151
  1057.3 47.4 %all-to-all-done.10 = bf16[32,8,4608]{2,1,0:T(8,128)(2,1)S(1)} async-done(((bf16[32,8,4608]{2,1,0:T(8,128)(2,1)}), bf16[32,8,4608]{2,1,0:T(8,128)(2,1)S(1)}, u32[]{:S(2)}, u32[]{:S(2)}) %all-to-all-start.10) | async-done | bytes 2359328 | tf_op jit(solution)/shard_map/all_to_all | solution.py:56
  (282 shorter events, 341.8 us)
Async XLA Ops:
  0.0 137.4 %collective-permute-start.6 = (bf16[4608,128]{1,0:T(8,128)(2,1)}, bf16[4608,128]{1,0:T(8,128)(2,1)}, u32[]{:S(2)}, u32[]{:S(2)}) collective-permute-start(bf16[4608,128]{1,0:T(8,128)(2,1)} %bitcast.288), channel_id=1, source_target_pairs={{0,28},{1,5},{4,0},{5,9},{8,4},{9,13},{12,8},{13,17},{16,12},{17,2... | collective-permute-start | bytes 3538952 | tf_op jit(solution)/shard_map/ppermute | solution.py:22
  4.2 138.2 %collective-permute-start.7 = (bf16[4608,128]{1,0:T(8,128)(2,1)}, bf16[4608,128]{1,0:T(8,128)(2,1)}, u32[]{:S(2)}, u32[]{:S(2)}) collective-permute-start(bf16[4608,128]{1,0:T(8,128)(2,1)} %bitcast.289), channel_id=1, source_target_pairs={{0,2},{2,0},{1,3},{3,1},{4,6},{6,4},{5,7},{7,5},{8,10},{10,8},{9,1... | collective-permute-start | bytes 3538952 | tf_op jit(solution)/shard_map/ppermute | solution.py:85
  22.2 87.5 %collective-permute-start.1 = (f32[16,16]{1,0:T(8,128)}, f32[16,16]{1,0:T(8,128)S(1)}, u32[]{:S(2)}, u32[]{:S(2)}) collective-permute-start(f32[16,16]{1,0:T(8,128)} %bitcast.375), channel_id=1, source_target_pairs={{0,2},{2,0},{1,3},{3,1},{4,6},{6,4},{5,7},{7,5},{8,10},{10,8},{9,1... | collective-permute-start | bytes 3080 | tf_op jit(solution)/shard_map/ppermute | solution.py:85
  38.9 78.7 %collective-permute-start = (f32[16,16]{1,0:T(8,128)}, f32[16,16]{1,0:T(8,128)}, u32[]{:S(2)}, u32[]{:S(2)}) collective-permute-start(f32[16,16]{1,0:T(8,128)} %bitcast.376), channel_id=1, source_target_pairs={{0,28},{1,5},{4,0},{5,9},{8,4},{9,13},{12,8},{13,17},{16,12},{17,2... | collective-permute-start | bytes 3080 | tf_op jit(solution)/shard_map/ppermute | solution.py:22
  42.2 22.5 %all-to-all-start.5 = ((bf16[2,2304,128]{2,1,0:T(8,128)(2,1)}), bf16[2,2304,128]{2,1,0:T(8,128)(2,1)S(1)}, u32[]{:S(2)}, u32[]{:S(2)}) async-start(bf16[2,2304,128]{2,1,0:T(8,128)(2,1)} %bitcast.290), calls=%async_computation.5 | async-start | bytes 2359296 | tf_op jit(solution)/shard_map/all_to_all | solution.py:115
  51.0 94.5 %collective-permute-start.4 = (bf16[128,4608]{0,1:T(8,128)(2,1)}, bf16[128,4608]{0,1:T(8,128)(2,1)}, u32[]{:S(2)}, u32[]{:S(2)}) collective-permute-start(bf16[128,4608]{0,1:T(8,128)(2,1)} %bitcast.11), channel_id=1, source_target_pairs={{0,2},{2,0},{1,3},{3,1},{4,6},{6,4},{5,7},{7,5},{8,10},{10,8},{9,1... | collective-permute-start | bytes 3538952 | tf_op jit(solution)/shard_map/ppermute | solution.py:85
  64.8 21.2 %all-to-all-start.1 = ((bf16[2,128,2304]{1,2,0:T(8,128)(2,1)}), bf16[2,128,2304]{1,2,0:T(8,128)(2,1)S(1)}, u32[]{:S(2)}, u32[]{:S(2)}) async-start(bf16[2,128,2304]{1,2,0:T(8,128)(2,1)} %bitcast.9), calls=%async_computation.1 | async-start | bytes 2359296 | tf_op jit(solution)/shard_map/all_to_all | solution.py:107
  86.0 49.7 %all-to-all-start = ((bf16[32,2,1152]{2,1,0:T(2,128)(2,1)}), bf16[32,2,1152]{2,1,0:T(2,128)(2,1)}, u32[]{:S(2)}, u32[]{:S(2)}) async-start(bf16[32,2,1152]{2,1,0:T(2,128)(2,1)} %reshape.356), calls=%async_computation | async-start | bytes 294912 | tf_op jit(solution)/shard_map/all_to_all | solution.py:96
  109.7 13.3 %collective-permute-start.2 = (f32[16,16]{1,0:T(8,128)S(1)}, f32[16,16]{1,0:T(8,128)S(1)}, u32[]{:S(2)}, u32[]{:S(2)}) collective-permute-start(f32[16,16]{1,0:T(8,128)S(1)} %collective-permute-done.1), channel_id=1, source_target_pairs={{0,28},{1,5},{4,0},{5,9},{8,4},{9,13},{12,8},{13,17},{16,12},{17,2... | collective-permute-start | bytes 3080 | tf_op jit(solution)/shard_map/ppermute | solution.py:22
  117.6 41.6 %collective-permute-start.3 = (bf16[128,4608]{0,1:T(8,128)(2,1)}, bf16[128,4608]{0,1:T(8,128)(2,1)}, u32[]{:S(2)}, u32[]{:S(2)}) collective-permute-start(bf16[128,4608]{0,1:T(8,128)(2,1)} %bitcast.11), channel_id=1, source_target_pairs={{0,28},{1,5},{4,0},{5,9},{8,4},{9,13},{12,8},{13,17},{16,12},{17,2... | collective-permute-start | bytes 3538952 | tf_op jit(solution)/shard_map/ppermute | solution.py:22
  137.4 11.3 %all-to-all-start.6 = ((bf16[2,2304,128]{2,1,0:T(8,128)(2,1)}), bf16[2,2304,128]{2,1,0:T(8,128)(2,1)}, u32[]{:S(2)}, u32[]{:S(2)}) async-start(bf16[2,2304,128]{2,1,0:T(8,128)(2,1)} %bitcast.26), calls=%async_computation.6 | async-start | bytes 2359296 | tf_op jit(solution)/shard_map/all_to_all | solution.py:115
  142.4 39.1 %collective-permute-start.8 = (bf16[4608,128]{1,0:T(8,128)(2,1)}, bf16[4608,128]{1,0:T(8,128)(2,1)}, u32[]{:S(2)}, u32[]{:S(2)}) collective-permute-start(bf16[4608,128]{1,0:T(8,128)(2,1)} %collective-permute-done.7), channel_id=1, source_target_pairs={{0,28},{1,5},{4,0},{5,9},{8,4},{9,13},{12,8},{13,17},{16,12},{17,2... | collective-permute-start | bytes 3538952 | tf_op jit(solution)/shard_map/ppermute | solution.py:22
  145.5 31.5 %collective-permute-start.5 = (bf16[128,4608]{0,1:T(8,128)(2,1)}, bf16[128,4608]{0,1:T(8,128)(2,1)}, u32[]{:S(2)}, u32[]{:S(2)}) collective-permute-start(bf16[128,4608]{0,1:T(8,128)(2,1)} %collective-permute-done.4), channel_id=1, source_target_pairs={{0,28},{1,5},{4,0},{5,9},{8,4},{9,13},{12,8},{13,17},{16,12},{17,2... | collective-permute-start | bytes 3538952 | tf_op jit(solution)/shard_map/ppermute | solution.py:22
  183.4 15.7 %all-to-all-start.8 = ((bf16[2,2304,128]{2,1,0:T(8,128)(2,1)}), bf16[2,2304,128]{2,1,0:T(8,128)(2,1)}, u32[]{:S(2)}, u32[]{:S(2)}) async-start(bf16[2,2304,128]{2,1,0:T(8,128)(2,1)} %bitcast.32), calls=%async_computation.8 | async-start | bytes 2359296 | tf_op jit(solution)/shard_map/all_to_all | solution.py:115
  207.0 58.5 %collective-permute-start.12 = (bf16[16,2304]{1,0:T(8,128)(2,1)S(1)}, bf16[16,2304]{1,0:T(8,128)(2,1)S(1)}, u32[]{:S(2)}, u32[]{:S(2)}) collective-permute-start(bf16[16,2304]{1,0:T(8,128)(2,1)S(1)} %fusion.1), channel_id=1, source_target_pairs={{32,24},{40,0},{48,8},{56,16},{64,56},{72,32},{80,40},{88,48},{96,... | collective-permute-start | bytes 221192 | tf_op jit(solution)/shard_map/ppermute | solution.py:30
  214.5 51.0 %collective-permute-start.11 = (bf16[16,2304]{1,0:T(8,128)(2,1)S(1)}, bf16[16,2304]{1,0:T(8,128)(2,1)S(1)}, u32[]{:S(2)}, u32[]{:S(2)}) collective-permute-start(bf16[16,2304]{1,0:T(8,128)(2,1)S(1)} %fusion.1), channel_id=1, source_target_pairs={{32,16},{40,24},{48,0},{56,8},{64,48},{72,56},{80,32},{88,40},{96,... | collective-permute-start | bytes 221192 | tf_op jit(solution)/shard_map/ppermute | solution.py:30
  231.2 34.2 %collective-permute-start.10 = (bf16[16,2304]{1,0:T(8,128)(2,1)S(1)}, bf16[16,2304]{1,0:T(8,128)(2,1)S(1)}, u32[]{:S(2)}, u32[]{:S(2)}) collective-permute-start(bf16[16,2304]{1,0:T(8,128)(2,1)S(1)} %fusion.1), channel_id=1, source_target_pairs={{32,8},{40,16},{48,24},{56,0},{64,40},{72,48},{80,56},{88,32},{96,... | collective-permute-start | bytes 221192 | tf_op jit(solution)/shard_map/ppermute | solution.py:30
  248.0 21.1 %collective-permute-start.9 = (bf16[16,2304]{1,0:T(8,128)(2,1)S(1)}, bf16[16,2304]{1,0:T(8,128)(2,1)S(1)}, u32[]{:S(2)}, u32[]{:S(2)}) collective-permute-start(bf16[16,2304]{1,0:T(8,128)(2,1)S(1)} %fusion.1), channel_id=1, source_target_pairs={{32,0},{40,8},{48,16},{56,24},{64,32},{72,40},{80,48},{88,56},{96,... | collective-permute-start | bytes 221192 | tf_op jit(solution)/shard_map/ppermute | solution.py:30
  277.5 66.3 %collective-permute-start.16 = (bf16[16,2304]{1,0:T(8,128)(2,1)S(1)}, bf16[16,2304]{1,0:T(8,128)(2,1)S(1)}, u32[]{:S(2)}, u32[]{:S(2)}) collective-permute-start(bf16[16,2304]{1,0:T(8,128)(2,1)S(1)} %add_convert_fusion.14), channel_id=1, source_target_pairs={{32,24},{40,0},{48,8},{56,16},{64,56},{72,32},{80,40},{88,48},{96,... | collective-permute-start | bytes 221192 | tf_op jit(solution)/shard_map/ppermute | solution.py:30
  293.1 50.7 %collective-permute-start.15 = (bf16[16,2304]{1,0:T(8,128)(2,1)S(1)}, bf16[16,2304]{1,0:T(8,128)(2,1)S(1)}, u32[]{:S(2)}, u32[]{:S(2)}) collective-permute-start(bf16[16,2304]{1,0:T(8,128)(2,1)S(1)} %add_convert_fusion.14), channel_id=1, source_target_pairs={{32,16},{40,24},{48,0},{56,8},{64,48},{72,56},{80,32},{88,40},{96,... | collective-permute-start | bytes 221192 | tf_op jit(solution)/shard_map/ppermute | solution.py:30
  309.9 34.0 %collective-permute-start.14 = (bf16[16,2304]{1,0:T(8,128)(2,1)S(1)}, bf16[16,2304]{1,0:T(8,128)(2,1)S(1)}, u32[]{:S(2)}, u32[]{:S(2)}) collective-permute-start(bf16[16,2304]{1,0:T(8,128)(2,1)S(1)} %add_convert_fusion.14), channel_id=1, source_target_pairs={{32,8},{40,16},{48,24},{56,0},{64,40},{72,48},{80,56},{88,32},{96,... | collective-permute-start | bytes 221192 | tf_op jit(solution)/shard_map/ppermute | solution.py:30
  326.6 21.1 %collective-permute-start.13 = (bf16[16,2304]{1,0:T(8,128)(2,1)S(1)}, bf16[16,2304]{1,0:T(8,128)(2,1)S(1)}, u32[]{:S(2)}, u32[]{:S(2)}) collective-permute-start(bf16[16,2304]{1,0:T(8,128)(2,1)S(1)} %add_convert_fusion.14), channel_id=1, source_target_pairs={{32,0},{40,8},{48,16},{56,24},{64,32},{72,40},{80,48},{88,56},{96,... | collective-permute-start | bytes 221192 | tf_op jit(solution)/shard_map/ppermute | solution.py:30
  358.5 65.8 %collective-permute-start.20 = (bf16[16,2304]{1,0:T(8,128)(2,1)S(1)}, bf16[16,2304]{1,0:T(8,128)(2,1)S(1)}, u32[]{:S(2)}, u32[]{:S(2)}) collective-permute-start(bf16[16,2304]{1,0:T(8,128)(2,1)S(1)} %add_convert_fusion.13), channel_id=1, source_target_pairs={{32,24},{40,0},{48,8},{56,16},{64,56},{72,32},{80,40},{88,48},{96,... | collective-permute-start | bytes 221192 | tf_op jit(solution)/shard_map/ppermute | solution.py:30
  374.1 50.2 %collective-permute-start.19 = (bf16[16,2304]{1,0:T(8,128)(2,1)S(1)}, bf16[16,2304]{1,0:T(8,128)(2,1)S(1)}, u32[]{:S(2)}, u32[]{:S(2)}) collective-permute-start(bf16[16,2304]{1,0:T(8,128)(2,1)S(1)} %add_convert_fusion.13), channel_id=1, source_target_pairs={{32,16},{40,24},{48,0},{56,8},{64,48},{72,56},{80,32},{88,40},{96,... | collective-permute-start | bytes 221192 | tf_op jit(solution)/shard_map/ppermute | solution.py:30
  390.9 33.5 %collective-permute-start.18 = (bf16[16,2304]{1,0:T(8,128)(2,1)S(1)}, bf16[16,2304]{1,0:T(8,128)(2,1)S(1)}, u32[]{:S(2)}, u32[]{:S(2)}) collective-permute-start(bf16[16,2304]{1,0:T(8,128)(2,1)S(1)} %add_convert_fusion.13), channel_id=1, source_target_pairs={{32,8},{40,16},{48,24},{56,0},{64,40},{72,48},{80,56},{88,32},{96,... | collective-permute-start | bytes 221192 | tf_op jit(solution)/shard_map/ppermute | solution.py:30
  407.6 21.1 %collective-permute-start.17 = (bf16[16,2304]{1,0:T(8,128)(2,1)S(1)}, bf16[16,2304]{1,0:T(8,128)(2,1)S(1)}, u32[]{:S(2)}, u32[]{:S(2)}) collective-permute-start(bf16[16,2304]{1,0:T(8,128)(2,1)S(1)} %add_convert_fusion.13), channel_id=1, source_target_pairs={{32,0},{40,8},{48,16},{56,24},{64,32},{72,40},{80,48},{88,56},{96,... | collective-permute-start | bytes 221192 | tf_op jit(solution)/shard_map/ppermute | solution.py:30
  439.5 65.8 %collective-permute-start.24 = (bf16[16,2304]{1,0:T(8,128)(2,1)S(1)}, bf16[16,2304]{1,0:T(8,128)(2,1)S(1)}, u32[]{:S(2)}, u32[]{:S(2)}) collective-permute-start(bf16[16,2304]{1,0:T(8,128)(2,1)S(1)} %add_convert_fusion.12), channel_id=1, source_target_pairs={{32,24},{40,0},{48,8},{56,16},{64,56},{72,32},{80,40},{88,48},{96,... | collective-permute-start | bytes 221192 | tf_op jit(solution)/shard_map/ppermute | solution.py:30
  455.1 50.2 %collective-permute-start.23 = (bf16[16,2304]{1,0:T(8,128)(2,1)S(1)}, bf16[16,2304]{1,0:T(8,128)(2,1)S(1)}, u32[]{:S(2)}, u32[]{:S(2)}) collective-permute-start(bf16[16,2304]{1,0:T(8,128)(2,1)S(1)} %add_convert_fusion.12), channel_id=1, source_target_pairs={{32,16},{40,24},{48,0},{56,8},{64,48},{72,56},{80,32},{88,40},{96,... | collective-permute-start | bytes 221192 | tf_op jit(solution)/shard_map/ppermute | solution.py:30
  471.8 33.5 %collective-permute-start.22 = (bf16[16,2304]{1,0:T(8,128)(2,1)S(1)}, bf16[16,2304]{1,0:T(8,128)(2,1)S(1)}, u32[]{:S(2)}, u32[]{:S(2)}) collective-permute-start(bf16[16,2304]{1,0:T(8,128)(2,1)S(1)} %add_convert_fusion.12), channel_id=1, source_target_pairs={{32,8},{40,16},{48,24},{56,0},{64,40},{72,48},{80,56},{88,32},{96,... | collective-permute-start | bytes 221192 | tf_op jit(solution)/shard_map/ppermute | solution.py:30
  488.6 21.1 %collective-permute-start.21 = (bf16[16,2304]{1,0:T(8,128)(2,1)S(1)}, bf16[16,2304]{1,0:T(8,128)(2,1)S(1)}, u32[]{:S(2)}, u32[]{:S(2)}) collective-permute-start(bf16[16,2304]{1,0:T(8,128)(2,1)S(1)} %add_convert_fusion.12), channel_id=1, source_target_pairs={{32,0},{40,8},{48,16},{56,24},{64,32},{72,40},{80,48},{88,56},{96,... | collective-permute-start | bytes 221192 | tf_op jit(solution)/shard_map/ppermute | solution.py:30
  520.5 65.8 %collective-permute-start.28 = (bf16[16,2304]{1,0:T(8,128)(2,1)S(1)}, bf16[16,2304]{1,0:T(8,128)(2,1)S(1)}, u32[]{:S(2)}, u32[]{:S(2)}) collective-permute-start(bf16[16,2304]{1,0:T(8,128)(2,1)S(1)} %add_convert_fusion.11), channel_id=1, source_target_pairs={{32,24},{40,0},{48,8},{56,16},{64,56},{72,32},{80,40},{88,48},{96,... | collective-permute-start | bytes 221192 | tf_op jit(solution)/shard_map/ppermute | solution.py:30
  536.1 50.2 %collective-permute-start.27 = (bf16[16,2304]{1,0:T(8,128)(2,1)S(1)}, bf16[16,2304]{1,0:T(8,128)(2,1)S(1)}, u32[]{:S(2)}, u32[]{:S(2)}) collective-permute-start(bf16[16,2304]{1,0:T(8,128)(2,1)S(1)} %add_convert_fusion.11), channel_id=1, source_target_pairs={{32,16},{40,24},{48,0},{56,8},{64,48},{72,56},{80,32},{88,40},{96,... | collective-permute-start | bytes 221192 | tf_op jit(solution)/shard_map/ppermute | solution.py:30
  552.8 33.5 %collective-permute-start.26 = (bf16[16,2304]{1,0:T(8,128)(2,1)S(1)}, bf16[16,2304]{1,0:T(8,128)(2,1)S(1)}, u32[]{:S(2)}, u32[]{:S(2)}) collective-permute-start(bf16[16,2304]{1,0:T(8,128)(2,1)S(1)} %add_convert_fusion.11), channel_id=1, source_target_pairs={{32,8},{40,16},{48,24},{56,0},{64,40},{72,48},{80,56},{88,32},{96,... | collective-permute-start | bytes 221192 | tf_op jit(solution)/shard_map/ppermute | solution.py:30
  569.6 21.1 %collective-permute-start.25 = (bf16[16,2304]{1,0:T(8,128)(2,1)S(1)}, bf16[16,2304]{1,0:T(8,128)(2,1)S(1)}, u32[]{:S(2)}, u32[]{:S(2)}) collective-permute-start(bf16[16,2304]{1,0:T(8,128)(2,1)S(1)} %add_convert_fusion.11), channel_id=1, source_target_pairs={{32,0},{40,8},{48,16},{56,24},{64,32},{72,40},{80,48},{88,56},{96,... | collective-permute-start | bytes 221192 | tf_op jit(solution)/shard_map/ppermute | solution.py:30
  601.5 65.8 %collective-permute-start.32 = (bf16[16,2304]{1,0:T(8,128)(2,1)S(1)}, bf16[16,2304]{1,0:T(8,128)(2,1)S(1)}, u32[]{:S(2)}, u32[]{:S(2)}) collective-permute-start(bf16[16,2304]{1,0:T(8,128)(2,1)S(1)} %add_convert_fusion.10), channel_id=1, source_target_pairs={{32,24},{40,0},{48,8},{56,16},{64,56},{72,32},{80,40},{88,48},{96,... | collective-permute-start | bytes 221192 | tf_op jit(solution)/shard_map/ppermute | solution.py:30
  617.1 50.2 %collective-permute-start.31 = (bf16[16,2304]{1,0:T(8,128)(2,1)S(1)}, bf16[16,2304]{1,0:T(8,128)(2,1)S(1)}, u32[]{:S(2)}, u32[]{:S(2)}) collective-permute-start(bf16[16,2304]{1,0:T(8,128)(2,1)S(1)} %add_convert_fusion.10), channel_id=1, source_target_pairs={{32,16},{40,24},{48,0},{56,8},{64,48},{72,56},{80,32},{88,40},{96,... | collective-permute-start | bytes 221192 | tf_op jit(solution)/shard_map/ppermute | solution.py:30
  633.8 33.5 %collective-permute-start.30 = (bf16[16,2304]{1,0:T(8,128)(2,1)S(1)}, bf16[16,2304]{1,0:T(8,128)(2,1)S(1)}, u32[]{:S(2)}, u32[]{:S(2)}) collective-permute-start(bf16[16,2304]{1,0:T(8,128)(2,1)S(1)} %add_convert_fusion.10), channel_id=1, source_target_pairs={{32,8},{40,16},{48,24},{56,0},{64,40},{72,48},{80,56},{88,32},{96,... | collective-permute-start | bytes 221192 | tf_op jit(solution)/shard_map/ppermute | solution.py:30
  650.6 21.1 %collective-permute-start.29 = (bf16[16,2304]{1,0:T(8,128)(2,1)S(1)}, bf16[16,2304]{1,0:T(8,128)(2,1)S(1)}, u32[]{:S(2)}, u32[]{:S(2)}) collective-permute-start(bf16[16,2304]{1,0:T(8,128)(2,1)S(1)} %add_convert_fusion.10), channel_id=1, source_target_pairs={{32,0},{40,8},{48,16},{56,24},{64,32},{72,40},{80,48},{88,56},{96,... | collective-permute-start | bytes 221192 | tf_op jit(solution)/shard_map/ppermute | solution.py:30
  682.5 65.8 %collective-permute-start.36 = (bf16[16,2304]{1,0:T(8,128)(2,1)S(1)}, bf16[16,2304]{1,0:T(8,128)(2,1)S(1)}, u32[]{:S(2)}, u32[]{:S(2)}) collective-permute-start(bf16[16,2304]{1,0:T(8,128)(2,1)S(1)} %add_convert_fusion.9), channel_id=1, source_target_pairs={{32,24},{40,0},{48,8},{56,16},{64,56},{72,32},{80,40},{88,48},{96,... | collective-permute-start | bytes 221192 | tf_op jit(solution)/shard_map/ppermute | solution.py:30
  698.1 50.2 %collective-permute-start.35 = (bf16[16,2304]{1,0:T(8,128)(2,1)S(1)}, bf16[16,2304]{1,0:T(8,128)(2,1)S(1)}, u32[]{:S(2)}, u32[]{:S(2)}) collective-permute-start(bf16[16,2304]{1,0:T(8,128)(2,1)S(1)} %add_convert_fusion.9), channel_id=1, source_target_pairs={{32,16},{40,24},{48,0},{56,8},{64,48},{72,56},{80,32},{88,40},{96,... | collective-permute-start | bytes 221192 | tf_op jit(solution)/shard_map/ppermute | solution.py:30
  714.8 33.5 %collective-permute-start.34 = (bf16[16,2304]{1,0:T(8,128)(2,1)S(1)}, bf16[16,2304]{1,0:T(8,128)(2,1)S(1)}, u32[]{:S(2)}, u32[]{:S(2)}) collective-permute-start(bf16[16,2304]{1,0:T(8,128)(2,1)S(1)} %add_convert_fusion.9), channel_id=1, source_target_pairs={{32,8},{40,16},{48,24},{56,0},{64,40},{72,48},{80,56},{88,32},{96,... | collective-permute-start | bytes 221192 | tf_op jit(solution)/shard_map/ppermute | solution.py:30
  731.6 21.1 %collective-permute-start.33 = (bf16[16,2304]{1,0:T(8,128)(2,1)S(1)}, bf16[16,2304]{1,0:T(8,128)(2,1)S(1)}, u32[]{:S(2)}, u32[]{:S(2)}) collective-permute-start(bf16[16,2304]{1,0:T(8,128)(2,1)S(1)} %add_convert_fusion.9), channel_id=1, source_target_pairs={{32,0},{40,8},{48,16},{56,24},{64,32},{72,40},{80,48},{88,56},{96,... | collective-permute-start | bytes 221192 | tf_op jit(solution)/shard_map/ppermute | solution.py:30
  763.6 50.4 %collective-permute-start.40 = (bf16[16,2304]{1,0:T(8,128)(2,1)S(1)}, bf16[16,2304]{1,0:T(8,128)(2,1)S(1)}, u32[]{:S(2)}, u32[]{:S(2)}) collective-permute-start(bf16[16,2304]{1,0:T(8,128)(2,1)S(1)} %add_convert_fusion.8), channel_id=1, source_target_pairs={{32,24},{40,0},{48,8},{56,16},{64,56},{72,32},{80,40},{88,48},{96,... | collective-permute-start | bytes 221192 | tf_op jit(solution)/shard_map/ppermute | solution.py:30
  779.2 34.8 %collective-permute-start.39 = (bf16[16,2304]{1,0:T(8,128)(2,1)S(1)}, bf16[16,2304]{1,0:T(8,128)(2,1)S(1)}, u32[]{:S(2)}, u32[]{:S(2)}) collective-permute-start(bf16[16,2304]{1,0:T(8,128)(2,1)S(1)} %add_convert_fusion.8), channel_id=1, source_target_pairs={{32,16},{40,24},{48,0},{56,8},{64,48},{72,56},{80,32},{88,40},{96,... | collective-permute-start | bytes 221192 | tf_op jit(solution)/shard_map/ppermute | solution.py:30
  796.0 25.3 %collective-permute-start.38 = (bf16[16,2304]{1,0:T(8,128)(2,1)S(1)}, bf16[16,2304]{1,0:T(8,128)(2,1)S(1)}, u32[]{:S(2)}, u32[]{:S(2)}) collective-permute-start(bf16[16,2304]{1,0:T(8,128)(2,1)S(1)} %add_convert_fusion.8), channel_id=1, source_target_pairs={{32,8},{40,16},{48,24},{56,0},{64,40},{72,48},{80,56},{88,32},{96,... | collective-permute-start | bytes 221192 | tf_op jit(solution)/shard_map/ppermute | solution.py:30
  837.0 11.1 collective-permute-start.41
  861.1 12.9 %collective-permute-start.46 = (bf16[16,2304]{1,0:T(8,128)(2,1)S(1)}, bf16[16,2304]{1,0:T(8,128)(2,1)S(1)}, u32[]{:S(2)}, u32[]{:S(2)}) collective-permute-start(bf16[16,2304]{1,0:T(8,128)(2,1)S(1)} %add_convert_fusion.6), channel_id=1, source_target_pairs={{32,8},{40,16},{48,24},{56,0},{64,40},{72,48},{80,56},{88,32},{96,... | collective-permute-start | bytes 221192 | tf_op jit(solution)/shard_map/ppermute | solution.py:30
  862.4 11.6 %collective-permute-start.45 = (bf16[16,2304]{1,0:T(8,128)(2,1)S(1)}, bf16[16,2304]{1,0:T(8,128)(2,1)S(1)}, u32[]{:S(2)}, u32[]{:S(2)}) collective-permute-start(bf16[16,2304]{1,0:T(8,128)(2,1)S(1)} %add_convert_fusion.6), channel_id=1, source_target_pairs={{32,0},{40,8},{48,16},{56,24},{64,32},{72,40},{80,48},{88,56},{96,... | collective-permute-start | bytes 221192 | tf_op jit(solution)/shard_map/ppermute | solution.py:30
  887.8 12.3 %collective-permute-start.50 = (bf16[16,2304]{1,0:T(8,128)(2,1)S(1)}, bf16[16,2304]{1,0:T(8,128)(2,1)S(1)}, u32[]{:S(2)}, u32[]{:S(2)}) collective-permute-start(bf16[16,2304]{1,0:T(8,128)(2,1)S(1)} %add_convert_fusion.5), channel_id=1, source_target_pairs={{32,8},{40,16},{48,24},{56,0},{64,40},{72,48},{80,56},{88,32},{96,... | collective-permute-start | bytes 221192 | tf_op jit(solution)/shard_map/ppermute | solution.py:30
  889.1 12.0 %collective-permute-start.49 = (bf16[16,2304]{1,0:T(8,128)(2,1)S(1)}, bf16[16,2304]{1,0:T(8,128)(2,1)S(1)}, u32[]{:S(2)}, u32[]{:S(2)}) collective-permute-start(bf16[16,2304]{1,0:T(8,128)(2,1)S(1)} %add_convert_fusion.5), channel_id=1, source_target_pairs={{32,0},{40,8},{48,16},{56,24},{64,32},{72,40},{80,48},{88,56},{96,... | collective-permute-start | bytes 221192 | tf_op jit(solution)/shard_map/ppermute | solution.py:30
  913.0 11.1 collective-permute-start.55
  914.3 12.1 %collective-permute-start.54 = (bf16[16,2304]{1,0:T(8,128)(2,1)S(1)}, bf16[16,2304]{1,0:T(8,128)(2,1)S(1)}, u32[]{:S(2)}, u32[]{:S(2)}) collective-permute-start(bf16[16,2304]{1,0:T(8,128)(2,1)S(1)} %add_convert_fusion.4), channel_id=1, source_target_pairs={{32,8},{40,16},{48,24},{56,0},{64,40},{72,48},{80,56},{88,32},{96,... | collective-permute-start | bytes 221192 | tf_op jit(solution)/shard_map/ppermute | solution.py:30
  915.6 12.0 %collective-permute-start.53 = (bf16[16,2304]{1,0:T(8,128)(2,1)S(1)}, bf16[16,2304]{1,0:T(8,128)(2,1)S(1)}, u32[]{:S(2)}, u32[]{:S(2)}) collective-permute-start(bf16[16,2304]{1,0:T(8,128)(2,1)S(1)} %add_convert_fusion.4), channel_id=1, source_target_pairs={{32,0},{40,8},{48,16},{56,24},{64,32},{72,40},{80,48},{88,56},{96,... | collective-permute-start | bytes 221192 | tf_op jit(solution)/shard_map/ppermute | solution.py:30
  939.7 11.8 %collective-permute-start.59 = (bf16[16,2304]{1,0:T(8,128)(2,1)S(1)}, bf16[16,2304]{1,0:T(8,128)(2,1)S(1)}, u32[]{:S(2)}, u32[]{:S(2)}) collective-permute-start(bf16[16,2304]{1,0:T(8,128)(2,1)S(1)} %add_convert_fusion.3), channel_id=1, source_target_pairs={{32,16},{40,24},{48,0},{56,8},{64,48},{72,56},{80,32},{88,40},{96,... | collective-permute-start | bytes 221192 | tf_op jit(solution)/shard_map/ppermute | solution.py:30
  941.0 13.0 %collective-permute-start.58 = (bf16[16,2304]{1,0:T(8,128)(2,1)S(1)}, bf16[16,2304]{1,0:T(8,128)(2,1)S(1)}, u32[]{:S(2)}, u32[]{:S(2)}) collective-permute-start(bf16[16,2304]{1,0:T(8,128)(2,1)S(1)} %add_convert_fusion.3), channel_id=1, source_target_pairs={{32,8},{40,16},{48,24},{56,0},{64,40},{72,48},{80,56},{88,32},{96,... | collective-permute-start | bytes 221192 | tf_op jit(solution)/shard_map/ppermute | solution.py:30
  942.3 13.0 %collective-permute-start.57 = (bf16[16,2304]{1,0:T(8,128)(2,1)S(1)}, bf16[16,2304]{1,0:T(8,128)(2,1)S(1)}, u32[]{:S(2)}, u32[]{:S(2)}) collective-permute-start(bf16[16,2304]{1,0:T(8,128)(2,1)S(1)} %add_convert_fusion.3), channel_id=1, source_target_pairs={{32,0},{40,8},{48,16},{56,24},{64,32},{72,40},{80,48},{88,56},{96,... | collective-permute-start | bytes 221192 | tf_op jit(solution)/shard_map/ppermute | solution.py:30
  967.1 13.2 %collective-permute-start.63 = (bf16[16,2304]{1,0:T(8,128)(2,1)S(1)}, bf16[16,2304]{1,0:T(8,128)(2,1)S(1)}, u32[]{:S(2)}, u32[]{:S(2)}) collective-permute-start(bf16[16,2304]{1,0:T(8,128)(2,1)S(1)} %add_convert_fusion.2), channel_id=1, source_target_pairs={{32,16},{40,24},{48,0},{56,8},{64,48},{72,56},{80,32},{88,40},{33,... | collective-permute-start | bytes 221192 | tf_op jit(solution)/shard_map/ppermute | solution.py:30
  968.4 13.9 %collective-permute-start.62 = (bf16[16,2304]{1,0:T(8,128)(2,1)S(1)}, bf16[16,2304]{1,0:T(8,128)(2,1)S(1)}, u32[]{:S(2)}, u32[]{:S(2)}) collective-permute-start(bf16[16,2304]{1,0:T(8,128)(2,1)S(1)} %add_convert_fusion.2), channel_id=1, source_target_pairs={{32,8},{40,16},{48,24},{56,0},{64,40},{72,48},{80,56},{88,32},{33,... | collective-permute-start | bytes 221192 | tf_op jit(solution)/shard_map/ppermute | solution.py:30
  969.7 14.2 %collective-permute-start.61 = (bf16[16,2304]{1,0:T(8,128)(2,1)S(1)}, bf16[16,2304]{1,0:T(8,128)(2,1)S(1)}, u32[]{:S(2)}, u32[]{:S(2)}) collective-permute-start(bf16[16,2304]{1,0:T(8,128)(2,1)S(1)} %add_convert_fusion.2), channel_id=1, source_target_pairs={{32,0},{40,8},{48,16},{56,24},{64,32},{72,40},{80,48},{88,56},{33,... | collective-permute-start | bytes 221192 | tf_op jit(solution)/shard_map/ppermute | solution.py:30
  996.4 12.2 %collective-permute-start.67 = (bf16[16,2304]{1,0:T(8,128)(2,1)}, bf16[16,2304]{1,0:T(8,128)(2,1)}, u32[]{:S(2)}, u32[]{:S(2)}) collective-permute-start(bf16[16,2304]{1,0:T(8,128)(2,1)} %add_convert_fusion.1), channel_id=1, source_target_pairs={{32,16},{40,24},{48,0},{56,8},{33,17},{41,25},{49,1},{57,9},{34,18... | collective-permute-start | bytes 221192 | tf_op jit(solution)/shard_map/ppermute | solution.py:30
  997.7 13.2 %collective-permute-start.66 = (bf16[16,2304]{1,0:T(8,128)(2,1)}, bf16[16,2304]{1,0:T(8,128)(2,1)}, u32[]{:S(2)}, u32[]{:S(2)}) collective-permute-start(bf16[16,2304]{1,0:T(8,128)(2,1)} %add_convert_fusion.1), channel_id=1, source_target_pairs={{32,8},{40,16},{48,24},{56,0},{33,9},{41,17},{49,25},{57,1},{34,10... | collective-permute-start | bytes 221192 | tf_op jit(solution)/shard_map/ppermute | solution.py:30
  999.0 13.1 %collective-permute-start.65 = (bf16[16,2304]{1,0:T(8,128)(2,1)}, bf16[16,2304]{1,0:T(8,128)(2,1)}, u32[]{:S(2)}, u32[]{:S(2)}) collective-permute-start(bf16[16,2304]{1,0:T(8,128)(2,1)} %add_convert_fusion.1), channel_id=1, source_target_pairs={{32,0},{40,8},{48,16},{56,24},{33,1},{41,9},{49,17},{57,25},{34,2}... | collective-permute-start | bytes 221192 | tf_op jit(solution)/shard_map/ppermute | solution.py:30
  1015.7 26.8 %all-to-all-start.9 = ((bf16[16,4,2304]{2,1,0:T(4,128)(2,1)}), bf16[16,4,2304]{2,1,0:T(4,128)(2,1)}, u32[]{:S(2)}, u32[]{:S(2)}) async-start(bf16[16,4,2304]{2,1,0:T(4,128)(2,1)} %copy.51), calls=%async_computation.9 | async-start | bytes 589824 | tf_op jit(solution)/shard_map/all_to_all | solution.py:150
  1042.5 62.2 %all-to-all-start.10 = ((bf16[32,8,4608]{2,1,0:T(8,128)(2,1)}), bf16[32,8,4608]{2,1,0:T(8,128)(2,1)S(1)}, u32[]{:S(2)}, u32[]{:S(2)}) async-start(bf16[32,8,4608]{2,1,0:T(8,128)(2,1)} %bitcast_select_fusion), calls=%async_computation.10 | async-start | bytes 4718592 | tf_op jit(solution)/shard_map/all_to_all | solution.py:56
  (27 other events, 1368.9 us)

commit v2 on v1

--- a/solution.py
+++ b/solution.py
@@ -1,6 +1,8 @@
 import jax
 import jax.numpy as jnp
 from jax import lax
+from jax.experimental import pallas as pl
+from jax.experimental.pallas import tpu as pltpu
 from jax.sharding import Mesh, PartitionSpec as P
 
 K_ACT = 256
@@ -22,12 +24,84 @@
     return lax.ppermute(shard, ("y2", "par", "core"), pairs)
 
 
-def send_down(shard, step, by, sections):
+def send_down(shard, by, sections):
     pairs = []
-    for section in range(1, sections - step):
+    for section in range(1, sections):
         for i in range(QUADS):
             pairs.append((section * QUADS + i, (section - 1) * QUADS + (i + by) % QUADS))
     return lax.ppermute(shard, ("section", "y2"), pairs)
+
+
+def grads_kernel(*refs):
+    *in_refs, rows_ref, rounded_ref, grads_ref = refs
+    arrived, outs = in_refs[:QUADS], in_refs[QUADS:]
+    rows = arrived[0][...].astype(F32)
+    for ref in arrived[1:]:
+        rows = rows + ref[...].astype(F32)
+    rows_ref[...] = rows
+    rounded = rows.astype(BF)
+    rounded_ref[...] = rounded
+    wide = outs[0].shape[0]
+    for k, ref in enumerate(outs):
+        grads_ref[:, k * wide : (k + 1) * wide] = lax.dot_general(
+            rounded, ref[...], (((1,), (1,)), ((), ())), preferred_element_type=F32
+        )
+
+
+def terms_kernel(grads_ref, mix_ref, rows_ref, scales_ref, *refs):
+    *values, share_ref = refs
+    grads = grads_ref[0] + grads_ref[1]
+    mixed = mix_ref[0] * grads[0:1, :]
+    for p in range(1, grads.shape[0]):
+        mixed = mixed + mix_ref[p] * grads[p : p + 1, :]
+    mixed = mixed.astype(BF)
+    wide = values[0].shape[1]
+    term = None
+    for k, ref in enumerate(values):
+        part = lax.dot_general(
+            mixed[:, k * wide : (k + 1) * wide],
+            ref[...],
+            (((1,), (1,)), ((), ())),
+            preferred_element_type=F32,
+        )
+        term = part if term is None else term + part
+    share_ref[...] = (rows_ref[...] * (1.0 / QUADS) + term * scales_ref[...]).astype(BF)
+
+
+def keep(array):
+    return pltpu.with_memory_space_constraint(array, pltpu.VMEM)
+
+
+def whole():
+    return pl.BlockSpec(memory_space=pltpu.VMEM)
+
+
+def head_grads(arrived, outs):
+    seq_len, half = arrived[0].shape
+    heads_wide = sum(w.shape[0] for w in outs)
+    return pl.pallas_call(
+        grads_kernel,
+        out_shape=(
+            jax.ShapeDtypeStruct((seq_len, half), F32),
+            jax.ShapeDtypeStruct((seq_len, half), BF),
+            jax.ShapeDtypeStruct((seq_len, heads_wide), F32),
+        ),
+        in_specs=[whole()] * (len(arrived) + len(outs)),
+        out_specs=(whole(),) * 3,
+        compiler_params=pltpu.CompilerParams(vmem_limit_bytes=24 << 20),
+        name="head_grads",
+    )(*arrived, *outs)
+
+
+def head_terms(grads, mix_wide, values, rows, scales):
+    return pl.pallas_call(
+        terms_kernel,
+        out_shape=jax.ShapeDtypeStruct(rows.shape, BF),
+        in_specs=[whole()] * (4 + len(values)),
+        out_specs=whole(),
+        compiler_params=pltpu.CompilerParams(vmem_limit_bytes=24 << 20),
+        name="head_terms",
+    )(grads, mix_wide, rows, scales, *values)
 
 
 def decoder_panel(dec_table, act_ids, entries_dev, feat_index, feat_count):
@@ -100,25 +174,22 @@
     positions = jnp.arange(seq_len, dtype=jnp.int32)
     rows = jnp.where((positions == own_pos)[:, None], enc_row[None, :], 0.0)
 
+    panel = decoder_panel(decoders[0], act_ids[0], entries_dev, feat_index, feat_count)
+    rows, panel = lax.optimization_barrier((rows, panel))
     far = tuple(neighbour_heads(a) for a in beyond)
-    out_parts, value_parts, mix_parts = [], [], []
+    outs, values, mix_parts = [], [], []
     for out_head, value_head, mix_head in (own, near, beyond, far):
-        out_parts.append(
-            lax.all_to_all(
-                out_head.reshape(head_width, 2, half).transpose(1, 0, 2),
-                "core",
-                split_axis=0,
-                concat_axis=0,
-                tiled=True,
-            ).reshape(2 * head_width, half)
+        halves = jnp.stack([out_head[:, :half], out_head[:, half:]])
+        outs.append(
+            lax.all_to_all(halves, "core", split_axis=0, concat_axis=0, tiled=True).reshape(
+                2 * head_width, half
+            )
         )
         got = lax.all_to_all(
             value_head.reshape(2, half, head_width), "core", split_axis=0, concat_axis=0, tiled=True
         )
-        value_parts += [got[0], got[1]]
+        values.append(jnp.concatenate([got[0], got[1]], axis=1))
         mix_parts.append(lax.all_gather(mix_head, "core", axis=0))
-    out_weight = jnp.concatenate(out_parts, axis=0)
-    value_weight = jnp.concatenate(value_parts, axis=1)
     mixing = jnp.concatenate(mix_parts, axis=0)
     heads = mixing.shape[0]
     mix_wide = jnp.broadcast_to(
@@ -126,22 +197,18 @@
     ).reshape(seq_len, seq_len, heads * head_width)
     scales = norm_scale[0][:, None]
 
-    history = [rows.astype(BF)]
+    outs, values = [keep(w) for w in outs], [keep(w) for w in values]
+    mix_wide = keep(mix_wide)
+    arrived = [rows.astype(BF)] + [jnp.zeros((seq_len, half), BF)] * (QUADS - 1)
+    history = [arrived[0]]
     for step in range(sections - 1):
-        grad_part = lax.dot_general(
-            history[-1], out_weight, (((1,), (1,)), ((), ())), preferred_element_type=F32
-        )
-        grads = jnp.sum(lax.all_gather(grad_part, "core", axis=0), axis=0)
-        mixed = jnp.sum(mix_wide * grads[:, None, :], axis=0).astype(BF)
-        term = lax.dot_general(
-            mixed, value_weight, (((1,), (1,)), ((), ())), preferred_element_type=F32
-        )
-        share = (rows * (1.0 / QUADS) + term * scales).astype(BF)
-        arrived = [send_down(share, step, by, sections) for by in range(QUADS)]
-        rows = sum(a.astype(F32) for a in arrived)
-        history.append(rows.astype(BF))
-
-    panel = decoder_panel(decoders[0], act_ids[0], entries_dev, feat_index, feat_count)
+        rows, rounded, grad_part = head_grads(arrived, outs)
+        if step:
+            history.append(rounded)
+        grads = lax.all_gather(grad_part, "core", axis=0)
+        share = head_terms(grads, mix_wide, values, rows, scales)
+        arrived = [send_down(share, by, sections) for by in range(QUADS)]
+    history.append(sum(a.astype(F32) for a in arrived).astype(BF))
 
     steps_each = sections // QUADS
     held = jnp.stack(history)

time: 1130 us -> 680 us (0.60)
  the two profiles are of different devices: /device:TPU:1 before, /device:TPU:197 now
where the time goes in v2:
time: 680 us; the launch traced here: 668 us
  starting transfers between devices  307 us (45%)
  waiting for transfers between devices  169 us (25%)
  blocking collectives  104 us (15%)
  local copies, waits for them, and re-layouts  42.5 us (6%)
  Pallas kernels  21.5 us (3%)
  other arithmetic  21.1 us (3%)
    ppermute x60, starting transfers between devices, send_down(): return lax.ppermute(shard, ('section', 'y2'), pairs)  225 us
    ppermute x6, waiting for transfers between devices, neighbour_heads(): return lax.ppermute(shard, ('y2', 'par', 'core'), pairs)  63.5 us
    ppermute x60, waiting for transfers between devices, send_down(): return lax.ppermute(shard, ('section', 'y2'), pairs)  61.2 us
    all_gather x15, blocking collectives, per_device(): grads = lax.all_gather(grad_part, 'core', axis=0)  52.5 us
    all_to_all x1, waiting for transfers between devices, per_device(): lax.all_to_all(enc_send, FEAT, split_axis=0, concat_axis=0, tiled=True)  30.7 us
    ppermute x6, starting transfers between devices, neighbour_heads(): return lax.ppermute(shard, ('y2', 'par', 'core'), pairs)  20.6 us
    pallas_call x15, Pallas kernels, head_terms(): pl.pallas_call(terms_kernel, out_shape=jax.ShapeDtypeStruct(rows.shape, B...  20.2 us
    all_to_all x2, blocking collectives, per_device(): lax.all_to_all(value_head.reshape(2, half, head_width), 'core', split_axi...  19.4 us
  transfers between devices with their start and end apart: 75, of which 32 were waited for; matrix products, arithmetic and copies ran while one was open for 6% of the time, Pallas kernels for 0%

profile of v2, /device:TPU:197, one launch (start us, length us, event | category | flops | bytes accessed | tf_op | source)
XLA Modules:
  0.0 668.0 jit_solution(12230005780347823729)
XLA Ops:
  0.0 8.1 %collective-permute-start.1 = (bf16[128,4608]{1,0:T(8,128)(2,1)}, bf16[128,4608]{1,0:T(8,128)(2,1)}, u32[]{:S(2)}, u32[]{:S(2)}) collective-permute-start(bf16[128,4608]{1,0:T(8,128)(2,1)} %bitcast.216), channel_id=1, source_target_pairs={{0,2},{2,0},{1,3},{3,1},{4,6},{6,4},{5,7},{7,5},{8,10},{10,8},{9,1... | collective-permute-start | bytes 3538952 | tf_op jit(solution)/shard_map/ppermute | solution.py:159
  16.4 7.3 %collective-permute-start.7 = (bf16[4608,128]{1,0:T(8,128)(2,1)}, bf16[4608,128]{1,0:T(8,128)(2,1)}, u32[]{:S(2)}, u32[]{:S(2)}) collective-permute-start(bf16[4608,128]{1,0:T(8,128)(2,1)} %bitcast.219), channel_id=1, source_target_pairs={{0,2},{2,0},{1,3},{3,1},{4,6},{6,4},{5,7},{7,5},{8,10},{10,8},{9,1... | collective-permute-start | bytes 3538952 | tf_op jit(solution)/shard_map/ppermute | solution.py:159
  23.8 8.4 %all-to-all-start.6 = ((bf16[2,2304,128]{2,1,0:T(8,128)(2,1)}), bf16[2,2304,128]{2,1,0:T(8,128)(2,1)}, u32[]{:S(2)}, u32[]{:S(2)}) async-start(bf16[2,2304,128]{2,1,0:T(8,128)(2,1)} %bitcast.220), calls=%async_computation.6 | async-start | bytes 2359296 | tf_op jit(solution)/shard_map/all_to_all | solution.py:188
  47.9 3.7 all-to-all-start
  57.9 3.3 collective-permute-start.5
  61.2 3.6 all-gather.3
  66.7 3.5 all-gather.2
  73.6 30.7 %all-to-all-done = bf16[32,2,1152]{2,1,0:T(2,128)(2,1)S(1)} async-done(((bf16[32,2,1152]{2,1,0:T(2,128)(2,1)}), bf16[32,2,1152]{2,1,0:T(2,128)(2,1)S(1)}, u32[]{:S(2)}, u32[]{:S(2)}) %all-to-all-start) | async-done | bytes 147488 | tf_op jit(solution)/shard_map/all_to_all | solution.py:170
  105.4 4.4 all-to-all-start.8
  109.8 5.7 collective-permute-start.8
  119.2 12.7 %all_to_all.60 = bf16[2,2304,128]{2,1,0:T(8,128)(2,1)S(1)} all-to-all(bf16[2,2304,128]{2,1,0:T(8,128)(2,1)} %bitcast.37), channel_id=1, replica_groups=mesh['section'=16,'y2'=4,'par'=2,'zh'=2,'core'=2] {'core'}, dimensions={0} | all-to-all | bytes 2359296 | tf_op jit(solution)/shard_map/all_to_all | solution.py:188
  131.9 4.4 collective-permute-done.8
  136.3 6.8 %all_to_all.61 = bf16[2,2304,128]{2,1,0:T(8,128)(2,1)} all-to-all(bf16[2,2304,128]{2,1,0:T(8,128)(2,1)} %bitcast.43), channel_id=1, replica_groups=mesh['section'=16,'y2'=4,'par'=2,'zh'=2,'core'=2] {'core'}, dimensions={0} | all-to-all | bytes 2359296 | tf_op jit(solution)/shard_map/all_to_all | solution.py:188
  143.1 12.7 %all-to-all-start.1 = ((bf16[32,8,4608]{2,1,0:T(8,128)(2,1)}), bf16[32,8,4608]{2,1,0:T(8,128)(2,1)}, u32[]{:S(2)}, u32[]{:S(2)}) async-start(bf16[32,8,4608]{2,1,0:T(8,128)(2,1)} %bitcast_select_fusion), calls=%async_computation.1 | async-start | bytes 4718592 | tf_op jit(solution)/shard_map/all_to_all | solution.py:130
  158.2 3.3 collective-permute-start.2
  163.5 59.1 %collective-permute-done.2 = bf16[128,4608]{1,0:T(8,128)(2,1)S(1)} collective-permute-done((bf16[128,4608]{1,0:T(8,128)(2,1)}, bf16[128,4608]{1,0:T(8,128)(2,1)S(1)}, u32[]{:S(2)}, u32[]{:S(2)}) %collective-permute-start.2) | collective-permute-done | bytes 1179680 | tf_op jit(solution)/shard_map/ppermute | solution.py:24
  226.2 4.0 all-to-all-start.2
  230.1 5.4 gather_fusion.1
  238.1 5.6 all_to_all.62
  243.7 4.8 all_to_all.63
  248.5 5.0 all_to_all.64
  258.1 4.5 collective-permute-start.10
  262.6 6.2 collective-permute-start.11
  268.8 3.5 collective-permute-start.12
  289.4 7.5 %collective-permute-start.15 = (bf16[16,2304]{1,0:T(8,128)(2,1)S(1)}, bf16[16,2304]{1,0:T(8,128)(2,1)S(1)}, u32[]{:S(2)}, u32[]{:S(2)}) collective-permute-start(bf16[16,2304]{1,0:T(8,128)(2,1)S(1)} %head_terms.16), channel_id=1, source_target_pairs={{32,16},{40,24},{48,0},{56,8},{64,48},{72,56},{80,32},{88,40},{96,... | collective-permute-start | bytes 221192 | tf_op jit(solution)/shard_map/ppermute | solution.py:32
  296.9 4.7 collective-permute-start.16
  305.3 4.4 all-gather.6
  311.1 5.6 collective-permute-start.17
  316.7 5.0 collective-permute-start.18
  321.8 6.2 collective-permute-start.19
  328.0 4.9 collective-permute-start.20
  341.4 3.5 collective-permute-start.21
  345.0 5.9 collective-permute-start.22
  350.9 6.7 collective-permute-start.23
  366.3 3.9 all-gather.8
  371.5 3.6 collective-permute-start.25
  375.1 4.7 collective-permute-start.26
  379.8 6.1 collective-permute-start.27
  386.0 3.7 collective-permute-start.28
  389.8 4.8 collective-permute-done.28
  405.2 5.9 collective-permute-start.31
  411.1 3.6 collective-permute-start.32
  415.2 3.6 collective-permute-done.32
  430.7 5.2 collective-permute-start.35
  435.9 3.3 collective-permute-start.36
  444.9 3.3 all-gather.11
  454.8 6.0 collective-permute-start.39
  469.1 3.8 all-gather.12
  479.1 5.6 collective-permute-start.43
  492.9 3.9 all-gather.13
  503.1 5.1 collective-permute-start.47
  516.4 3.9 all-gather.14
  526.4 5.5 collective-permute-start.51
  540.2 3.9 all-gather.15
  550.2 5.5 collective-permute-start.55
  564.0 3.9 all-gather.16
  574.0 5.2 collective-permute-start.59
  587.4 3.9 all-gather.17
  597.5 5.1 collective-permute-start.63
  610.8 3.9 all-gather.18
  620.9 5.3 collective-permute-start.67
  635.6 10.9 %all-to-all-start.10 = ((bf16[16,4,2304]{2,1,0:T(4,128)(2,1)}), bf16[16,4,2304]{2,1,0:T(4,128)(2,1)S(1)}, u32[]{:S(2)}, u32[]{:S(2)}) async-start(bf16[16,4,2304]{2,1,0:T(4,128)(2,1)} %copy.99), calls=%async_computation.10 | async-start | bytes 589824 | tf_op jit(solution)/shard_map/all_to_all | solution.py:217
  646.5 13.8 %all-to-all-done.10 = bf16[16,4,2304]{2,1,0:T(4,128)(2,1)S(1)} async-done(((bf16[16,4,2304]{2,1,0:T(4,128)(2,1)}), bf16[16,4,2304]{2,1,0:T(4,128)(2,1)S(1)}, u32[]{:S(2)}, u32[]{:S(2)}) %all-to-all-start.10) | async-done | bytes 294944 | tf_op jit(solution)/shard_map/all_to_all | solution.py:217
  660.5 5.8 all_gather.151
  (255 shorter events, 242.7 us)
Async XLA Ops:
  0.0 115.5 %collective-permute-start.1 = (bf16[128,4608]{1,0:T(8,128)(2,1)}, bf16[128,4608]{1,0:T(8,128)(2,1)}, u32[]{:S(2)}, u32[]{:S(2)}) collective-permute-start(bf16[128,4608]{1,0:T(8,128)(2,1)} %bitcast.216), channel_id=1, source_target_pairs={{0,2},{2,0},{1,3},{3,1},{4,6},{6,4},{5,7},{7,5},{8,10},{10,8},{9,1... | collective-permute-start | bytes 3538952 | tf_op jit(solution)/shard_map/ppermute | solution.py:159
  8.1 109.8 %collective-permute-start = (bf16[128,4608]{1,0:T(8,128)(2,1)}, bf16[128,4608]{1,0:T(8,128)(2,1)}, u32[]{:S(2)}, u32[]{:S(2)}) collective-permute-start(bf16[128,4608]{1,0:T(8,128)(2,1)} %bitcast.217), channel_id=1, source_target_pairs={{0,28},{1,5},{4,0},{5,9},{8,4},{9,13},{12,8},{13,17},{16,12},{17,2... | collective-permute-start | bytes 3538952 | tf_op jit(solution)/shard_map/ppermute | solution.py:24
  11.3 46.6 %collective-permute-start.4 = (f32[16,16]{1,0:T(8,128)}, f32[16,16]{1,0:T(8,128)}, u32[]{:S(2)}, u32[]{:S(2)}) collective-permute-start(f32[16,16]{1,0:T(8,128)} %bitcast.231), channel_id=1, source_target_pairs={{0,2},{2,0},{1,3},{3,1},{4,6},{6,4},{5,7},{7,5},{8,10},{10,8},{9,1... | collective-permute-start | bytes 3080 | tf_op jit(solution)/shard_map/ppermute | solution.py:159
  13.2 51.6 %collective-permute-start.3 = (f32[16,16]{1,0:T(8,128)}, f32[16,16]{1,0:T(8,128)}, u32[]{:S(2)}, u32[]{:S(2)}) collective-permute-start(f32[16,16]{1,0:T(8,128)} %bitcast.232), channel_id=1, source_target_pairs={{0,28},{1,5},{4,0},{5,9},{8,4},{9,13},{12,8},{13,17},{16,12},{17,2... | collective-permute-start | bytes 3080 | tf_op jit(solution)/shard_map/ppermute | solution.py:24
  16.4 89.0 %collective-permute-start.7 = (bf16[4608,128]{1,0:T(8,128)(2,1)}, bf16[4608,128]{1,0:T(8,128)(2,1)}, u32[]{:S(2)}, u32[]{:S(2)}) collective-permute-start(bf16[4608,128]{1,0:T(8,128)(2,1)} %bitcast.219), channel_id=1, source_target_pairs={{0,2},{2,0},{1,3},{3,1},{4,6},{6,4},{5,7},{7,5},{8,10},{10,8},{9,1... | collective-permute-start | bytes 3538952 | tf_op jit(solution)/shard_map/ppermute | solution.py:159
  23.8 24.2 %all-to-all-start.6 = ((bf16[2,2304,128]{2,1,0:T(8,128)(2,1)}), bf16[2,2304,128]{2,1,0:T(8,128)(2,1)}, u32[]{:S(2)}, u32[]{:S(2)}) async-start(bf16[2,2304,128]{2,1,0:T(8,128)(2,1)} %bitcast.220), calls=%async_computation.6 | async-start | bytes 2359296 | tf_op jit(solution)/shard_map/all_to_all | solution.py:188
  47.9 56.4 %all-to-all-start = ((bf16[32,2,1152]{2,1,0:T(2,128)(2,1)}), bf16[32,2,1152]{2,1,0:T(2,128)(2,1)S(1)}, u32[]{:S(2)}, u32[]{:S(2)}) async-start(bf16[32,2,1152]{2,1,0:T(2,128)(2,1)} %reshape.225), calls=%async_computation | async-start | bytes 294912 | tf_op jit(solution)/shard_map/all_to_all | solution.py:170
  57.9 12.3 %collective-permute-start.5 = (f32[16,16]{1,0:T(8,128)}, f32[16,16]{1,0:T(8,128)S(1)}, u32[]{:S(2)}, u32[]{:S(2)}) collective-permute-start(f32[16,16]{1,0:T(8,128)} %collective-permute-done.4), channel_id=1, source_target_pairs={{0,28},{1,5},{4,0},{5,9},{8,4},{9,13},{12,8},{13,17},{16,12},{17,2... | collective-permute-start | bytes 3080 | tf_op jit(solution)/shard_map/ppermute | solution.py:24
  64.8 54.4 %collective-permute-start.6 = (bf16[4608,128]{1,0:T(8,128)(2,1)S(1)}, bf16[4608,128]{1,0:T(8,128)(2,1)}, u32[]{:S(2)}, u32[]{:S(2)}) collective-permute-start(bf16[4608,128]{1,0:T(8,128)(2,1)S(1)} %bitcast.221), channel_id=1, source_target_pairs={{0,28},{1,5},{4,0},{5,9},{8,4},{9,13},{12,8},{13,17},{16,12},{17,2... | collective-permute-start | bytes 3538952 | tf_op jit(solution)/shard_map/ppermute | solution.py:24
  105.4 13.7 %all-to-all-start.8 = ((bf16[2,2304,128]{2,1,0:T(8,128)(2,1)}), bf16[2,2304,128]{2,1,0:T(8,128)(2,1)S(1)}, u32[]{:S(2)}, u32[]{:S(2)}) async-start(bf16[2,2304,128]{2,1,0:T(8,128)(2,1)} %bitcast.40), calls=%async_computation.8 | async-start | bytes 2359296 | tf_op jit(solution)/shard_map/all_to_all | solution.py:188
  109.8 26.5 %collective-permute-start.8 = (bf16[4608,128]{1,0:T(8,128)(2,1)}, bf16[4608,128]{1,0:T(8,128)(2,1)}, u32[]{:S(2)}, u32[]{:S(2)}) collective-permute-start(bf16[4608,128]{1,0:T(8,128)(2,1)} %collective-permute-done.7), channel_id=1, source_target_pairs={{0,28},{1,5},{4,0},{5,9},{8,4},{9,13},{12,8},{13,17},{16,12},{17,2... | collective-permute-start | bytes 3538952 | tf_op jit(solution)/shard_map/ppermute | solution.py:24
  143.1 83.1 %all-to-all-start.1 = ((bf16[32,8,4608]{2,1,0:T(8,128)(2,1)}), bf16[32,8,4608]{2,1,0:T(8,128)(2,1)}, u32[]{:S(2)}, u32[]{:S(2)}) async-start(bf16[32,8,4608]{2,1,0:T(8,128)(2,1)} %bitcast_select_fusion), calls=%async_computation.1 | async-start | bytes 4718592 | tf_op jit(solution)/shard_map/all_to_all | solution.py:130
  158.2 64.5 %collective-permute-start.2 = (bf16[128,4608]{1,0:T(8,128)(2,1)}, bf16[128,4608]{1,0:T(8,128)(2,1)S(1)}, u32[]{:S(2)}, u32[]{:S(2)}) collective-permute-start(bf16[128,4608]{1,0:T(8,128)(2,1)} %collective-permute-done.1), channel_id=1, source_target_pairs={{0,28},{1,5},{4,0},{5,9},{8,4},{9,13},{12,8},{13,17},{16,12},{17,2... | collective-permute-start | bytes 3538952 | tf_op jit(solution)/shard_map/ppermute | solution.py:24
  226.2 11.9 %all-to-all-start.2 = ((bf16[2,128,2304]{2,1,0:T(8,128)(2,1)}), bf16[2,128,2304]{2,1,0:T(8,128)(2,1)S(1)}, u32[]{:S(2)}, u32[]{:S(2)}) async-start(bf16[2,128,2304]{2,1,0:T(8,128)(2,1)} %pad_maximum_fusion), calls=%async_computation.2 | async-start | bytes 2359296 | tf_op jit(solution)/shard_map/all_to_all | solution.py:184
  258.1 16.7 %collective-permute-start.10 = (bf16[16,2304]{1,0:T(8,128)(2,1)S(1)}, bf16[16,2304]{1,0:T(8,128)(2,1)S(1)}, u32[]{:S(2)}, u32[]{:S(2)}) collective-permute-start(bf16[16,2304]{1,0:T(8,128)(2,1)S(1)} %head_terms.15), channel_id=1, source_target_pairs={{32,8},{40,16},{48,24},{56,0},{64,40},{72,48},{80,56},{88,32},{96,... | collective-permute-start | bytes 221192 | tf_op jit(solution)/shard_map/ppermute | solution.py:32
  262.6 13.6 %collective-permute-start.11 = (bf16[16,2304]{1,0:T(8,128)(2,1)S(1)}, bf16[16,2304]{1,0:T(8,128)(2,1)S(1)}, u32[]{:S(2)}, u32[]{:S(2)}) collective-permute-start(bf16[16,2304]{1,0:T(8,128)(2,1)S(1)} %head_terms.15), channel_id=1, source_target_pairs={{32,16},{40,24},{48,0},{56,8},{64,48},{72,56},{80,32},{88,40},{96,... | collective-permute-start | bytes 221192 | tf_op jit(solution)/shard_map/ppermute | solution.py:32
  268.8 9.8 %collective-permute-start.12 = (bf16[16,2304]{1,0:T(8,128)(2,1)S(1)}, bf16[16,2304]{1,0:T(8,128)(2,1)S(1)}, u32[]{:S(2)}, u32[]{:S(2)}) collective-permute-start(bf16[16,2304]{1,0:T(8,128)(2,1)S(1)} %head_terms.15), channel_id=1, source_target_pairs={{32,24},{40,0},{48,8},{56,16},{64,56},{72,32},{80,40},{88,48},{96,... | collective-permute-start | bytes 221192 | tf_op jit(solution)/shard_map/ppermute | solution.py:32
  284.5 17.1 %collective-permute-start.13 = (bf16[16,2304]{1,0:T(8,128)(2,1)S(1)}, bf16[16,2304]{1,0:T(8,128)(2,1)S(1)}, u32[]{:S(2)}, u32[]{:S(2)}) collective-permute-start(bf16[16,2304]{1,0:T(8,128)(2,1)S(1)} %head_terms.16), channel_id=1, source_target_pairs={{32,0},{40,8},{48,16},{56,24},{64,32},{72,40},{80,48},{88,56},{96,... | collective-permute-start | bytes 221192 | tf_op jit(solution)/shard_map/ppermute | solution.py:32
  286.7 15.0 %collective-permute-start.14 = (bf16[16,2304]{1,0:T(8,128)(2,1)S(1)}, bf16[16,2304]{1,0:T(8,128)(2,1)S(1)}, u32[]{:S(2)}, u32[]{:S(2)}) collective-permute-start(bf16[16,2304]{1,0:T(8,128)(2,1)S(1)} %head_terms.16), channel_id=1, source_target_pairs={{32,8},{40,16},{48,24},{56,0},{64,40},{72,48},{80,56},{88,32},{96,... | collective-permute-start | bytes 221192 | tf_op jit(solution)/shard_map/ppermute | solution.py:32
  289.4 12.3 %collective-permute-start.15 = (bf16[16,2304]{1,0:T(8,128)(2,1)S(1)}, bf16[16,2304]{1,0:T(8,128)(2,1)S(1)}, u32[]{:S(2)}, u32[]{:S(2)}) collective-permute-start(bf16[16,2304]{1,0:T(8,128)(2,1)S(1)} %head_terms.16), channel_id=1, source_target_pairs={{32,16},{40,24},{48,0},{56,8},{64,48},{72,56},{80,32},{88,40},{96,... | collective-permute-start | bytes 221192 | tf_op jit(solution)/shard_map/ppermute | solution.py:32
  311.1 21.7 %collective-permute-start.17 = (bf16[16,2304]{1,0:T(8,128)(2,1)S(1)}, bf16[16,2304]{1,0:T(8,128)(2,1)S(1)}, u32[]{:S(2)}, u32[]{:S(2)}) collective-permute-start(bf16[16,2304]{1,0:T(8,128)(2,1)S(1)} %head_terms.17), channel_id=1, source_target_pairs={{32,0},{40,8},{48,16},{56,24},{64,32},{72,40},{80,48},{88,56},{96,... | collective-permute-start | bytes 221192 | tf_op jit(solution)/shard_map/ppermute | solution.py:32
  316.7 16.1 %collective-permute-start.18 = (bf16[16,2304]{1,0:T(8,128)(2,1)S(1)}, bf16[16,2304]{1,0:T(8,128)(2,1)S(1)}, u32[]{:S(2)}, u32[]{:S(2)}) collective-permute-start(bf16[16,2304]{1,0:T(8,128)(2,1)S(1)} %head_terms.17), channel_id=1, source_target_pairs={{32,8},{40,16},{48,24},{56,0},{64,40},{72,48},{80,56},{88,32},{96,... | collective-permute-start | bytes 221192 | tf_op jit(solution)/shard_map/ppermute | solution.py:32
  321.8 11.1 %collective-permute-start.19 = (bf16[16,2304]{1,0:T(8,128)(2,1)S(1)}, bf16[16,2304]{1,0:T(8,128)(2,1)S(1)}, u32[]{:S(2)}, u32[]{:S(2)}) collective-permute-start(bf16[16,2304]{1,0:T(8,128)(2,1)S(1)} %head_terms.17), channel_id=1, source_target_pairs={{32,16},{40,24},{48,0},{56,8},{64,48},{72,56},{80,32},{88,40},{96,... | collective-permute-start | bytes 221192 | tf_op jit(solution)/shard_map/ppermute | solution.py:32
  328.0 7.7 %collective-permute-start.20 = (bf16[16,2304]{1,0:T(8,128)(2,1)S(1)}, bf16[16,2304]{1,0:T(8,128)(2,1)S(1)}, u32[]{:S(2)}, u32[]{:S(2)}) collective-permute-start(bf16[16,2304]{1,0:T(8,128)(2,1)S(1)} %head_terms.17), channel_id=1, source_target_pairs={{32,24},{40,0},{48,8},{56,16},{64,56},{72,32},{80,40},{88,48},{96,... | collective-permute-start | bytes 221192 | tf_op jit(solution)/shard_map/ppermute | solution.py:32
  341.4 19.2 %collective-permute-start.21 = (bf16[16,2304]{1,0:T(8,128)(2,1)S(1)}, bf16[16,2304]{1,0:T(8,128)(2,1)S(1)}, u32[]{:S(2)}, u32[]{:S(2)}) collective-permute-start(bf16[16,2304]{1,0:T(8,128)(2,1)S(1)} %head_terms.18), channel_id=1, source_target_pairs={{32,0},{40,8},{48,16},{56,24},{64,32},{72,40},{80,48},{88,56},{96,... | collective-permute-start | bytes 221192 | tf_op jit(solution)/shard_map/ppermute | solution.py:32
  345.0 15.6 %collective-permute-start.22 = (bf16[16,2304]{1,0:T(8,128)(2,1)S(1)}, bf16[16,2304]{1,0:T(8,128)(2,1)S(1)}, u32[]{:S(2)}, u32[]{:S(2)}) collective-permute-start(bf16[16,2304]{1,0:T(8,128)(2,1)S(1)} %head_terms.18), channel_id=1, source_target_pairs={{32,8},{40,16},{48,24},{56,0},{64,40},{72,48},{80,56},{88,32},{96,... | collective-permute-start | bytes 221192 | tf_op jit(solution)/shard_map/ppermute | solution.py:32
  350.9 11.1 %collective-permute-start.23 = (bf16[16,2304]{1,0:T(8,128)(2,1)S(1)}, bf16[16,2304]{1,0:T(8,128)(2,1)S(1)}, u32[]{:S(2)}, u32[]{:S(2)}) collective-permute-start(bf16[16,2304]{1,0:T(8,128)(2,1)S(1)} %head_terms.18), channel_id=1, source_target_pairs={{32,16},{40,24},{48,0},{56,8},{64,48},{72,56},{80,32},{88,40},{96,... | collective-permute-start | bytes 221192 | tf_op jit(solution)/shard_map/ppermute | solution.py:32
  371.5 18.2 %collective-permute-start.25 = (bf16[16,2304]{1,0:T(8,128)(2,1)S(1)}, bf16[16,2304]{1,0:T(8,128)(2,1)S(1)}, u32[]{:S(2)}, u32[]{:S(2)}) collective-permute-start(bf16[16,2304]{1,0:T(8,128)(2,1)S(1)} %head_terms.19), channel_id=1, source_target_pairs={{32,0},{40,8},{48,16},{56,24},{64,32},{72,40},{80,48},{88,56},{96,... | collective-permute-start | bytes 221192 | tf_op jit(solution)/shard_map/ppermute | solution.py:32
  375.1 14.6 %collective-permute-start.26 = (bf16[16,2304]{1,0:T(8,128)(2,1)S(1)}, bf16[16,2304]{1,0:T(8,128)(2,1)S(1)}, u32[]{:S(2)}, u32[]{:S(2)}) collective-permute-start(bf16[16,2304]{1,0:T(8,128)(2,1)S(1)} %head_terms.19), channel_id=1, source_target_pairs={{32,8},{40,16},{48,24},{56,0},{64,40},{72,48},{80,56},{88,32},{96,... | collective-permute-start | bytes 221192 | tf_op jit(solution)/shard_map/ppermute | solution.py:32
  379.8 10.0 %collective-permute-start.27 = (bf16[16,2304]{1,0:T(8,128)(2,1)S(1)}, bf16[16,2304]{1,0:T(8,128)(2,1)S(1)}, u32[]{:S(2)}, u32[]{:S(2)}) collective-permute-start(bf16[16,2304]{1,0:T(8,128)(2,1)S(1)} %head_terms.19), channel_id=1, source_target_pairs={{32,16},{40,24},{48,0},{56,8},{64,48},{72,56},{80,32},{88,40},{96,... | collective-permute-start | bytes 221192 | tf_op jit(solution)/shard_map/ppermute | solution.py:32
  386.0 8.7 %collective-permute-start.28 = (bf16[16,2304]{1,0:T(8,128)(2,1)S(1)}, bf16[16,2304]{1,0:T(8,128)(2,1)S(1)}, u32[]{:S(2)}, u32[]{:S(2)}) collective-permute-start(bf16[16,2304]{1,0:T(8,128)(2,1)S(1)} %head_terms.19), channel_id=1, source_target_pairs={{32,24},{40,0},{48,8},{56,16},{64,56},{72,32},{80,40},{88,48},{96,... | collective-permute-start | bytes 221192 | tf_op jit(solution)/shard_map/ppermute | solution.py:32
  399.8 14.9 %collective-permute-start.29 = (bf16[16,2304]{1,0:T(8,128)(2,1)S(1)}, bf16[16,2304]{1,0:T(8,128)(2,1)S(1)}, u32[]{:S(2)}, u32[]{:S(2)}) collective-permute-start(bf16[16,2304]{1,0:T(8,128)(2,1)S(1)} %head_terms.20), channel_id=1, source_target_pairs={{32,0},{40,8},{48,16},{56,24},{64,32},{72,40},{80,48},{88,56},{96,... | collective-permute-start | bytes 221192 | tf_op jit(solution)/shard_map/ppermute | solution.py:32
  402.1 12.7 %collective-permute-start.30 = (bf16[16,2304]{1,0:T(8,128)(2,1)S(1)}, bf16[16,2304]{1,0:T(8,128)(2,1)S(1)}, u32[]{:S(2)}, u32[]{:S(2)}) collective-permute-start(bf16[16,2304]{1,0:T(8,128)(2,1)S(1)} %head_terms.20), channel_id=1, source_target_pairs={{32,8},{40,16},{48,24},{56,0},{64,40},{72,48},{80,56},{88,32},{96,... | collective-permute-start | bytes 221192 | tf_op jit(solution)/shard_map/ppermute | solution.py:32
  405.2 10.0 %collective-permute-start.31 = (bf16[16,2304]{1,0:T(8,128)(2,1)S(1)}, bf16[16,2304]{1,0:T(8,128)(2,1)S(1)}, u32[]{:S(2)}, u32[]{:S(2)}) collective-permute-start(bf16[16,2304]{1,0:T(8,128)(2,1)S(1)} %head_terms.20), channel_id=1, source_target_pairs={{32,16},{40,24},{48,0},{56,8},{64,48},{72,56},{80,32},{88,40},{96,... | collective-permute-start | bytes 221192 | tf_op jit(solution)/shard_map/ppermute | solution.py:32
  411.1 7.7 %collective-permute-start.32 = (bf16[16,2304]{1,0:T(8,128)(2,1)S(1)}, bf16[16,2304]{1,0:T(8,128)(2,1)S(1)}, u32[]{:S(2)}, u32[]{:S(2)}) collective-permute-start(bf16[16,2304]{1,0:T(8,128)(2,1)S(1)} %head_terms.20), channel_id=1, source_target_pairs={{32,24},{40,0},{48,8},{56,16},{64,56},{72,32},{80,40},{88,48},{96,... | collective-permute-start | bytes 221192 | tf_op jit(solution)/shard_map/ppermute | solution.py:32
  424.6 14.6 %collective-permute-start.33 = (bf16[16,2304]{1,0:T(8,128)(2,1)S(1)}, bf16[16,2304]{1,0:T(8,128)(2,1)S(1)}, u32[]{:S(2)}, u32[]{:S(2)}) collective-permute-start(bf16[16,2304]{1,0:T(8,128)(2,1)S(1)} %head_terms.21), channel_id=1, source_target_pairs={{32,0},{40,8},{48,16},{56,24},{64,32},{72,40},{80,48},{88,56},{96,... | collective-permute-start | bytes 221192 | tf_op jit(solution)/shard_map/ppermute | solution.py:32
  427.4 11.8 %collective-permute-start.34 = (bf16[16,2304]{1,0:T(8,128)(2,1)S(1)}, bf16[16,2304]{1,0:T(8,128)(2,1)S(1)}, u32[]{:S(2)}, u32[]{:S(2)}) collective-permute-start(bf16[16,2304]{1,0:T(8,128)(2,1)S(1)} %head_terms.21), channel_id=1, source_target_pairs={{32,8},{40,16},{48,24},{56,0},{64,40},{72,48},{80,56},{88,32},{96,... | collective-permute-start | bytes 221192 | tf_op jit(solution)/shard_map/ppermute | solution.py:32
  430.7 10.0 %collective-permute-start.35 = (bf16[16,2304]{1,0:T(8,128)(2,1)S(1)}, bf16[16,2304]{1,0:T(8,128)(2,1)S(1)}, u32[]{:S(2)}, u32[]{:S(2)}) collective-permute-start(bf16[16,2304]{1,0:T(8,128)(2,1)S(1)} %head_terms.21), channel_id=1, source_target_pairs={{32,16},{40,24},{48,0},{56,8},{64,48},{72,56},{80,32},{88,40},{96,... | collective-permute-start | bytes 221192 | tf_op jit(solution)/shard_map/ppermute | solution.py:32
  435.9 7.7 %collective-permute-start.36 = (bf16[16,2304]{1,0:T(8,128)(2,1)S(1)}, bf16[16,2304]{1,0:T(8,128)(2,1)S(1)}, u32[]{:S(2)}, u32[]{:S(2)}) collective-permute-start(bf16[16,2304]{1,0:T(8,128)(2,1)S(1)} %head_terms.21), channel_id=1, source_target_pairs={{32,24},{40,0},{48,8},{56,16},{64,56},{72,32},{80,40},{88,48},{96,... | collective-permute-start | bytes 221192 | tf_op jit(solution)/shard_map/ppermute | solution.py:32
  449.5 13.5 %collective-permute-start.37 = (bf16[16,2304]{1,0:T(8,128)(2,1)S(1)}, bf16[16,2304]{1,0:T(8,128)(2,1)S(1)}, u32[]{:S(2)}, u32[]{:S(2)}) collective-permute-start(bf16[16,2304]{1,0:T(8,128)(2,1)S(1)} %head_terms.22), channel_id=1, source_target_pairs={{32,0},{40,8},{48,16},{56,24},{64,32},{72,40},{80,48},{88,56},{96,... | collective-permute-start | bytes 221192 | tf_op jit(solution)/shard_map/ppermute | solution.py:32
  451.9 11.2 %collective-permute-start.38 = (bf16[16,2304]{1,0:T(8,128)(2,1)S(1)}, bf16[16,2304]{1,0:T(8,128)(2,1)S(1)}, u32[]{:S(2)}, u32[]{:S(2)}) collective-permute-start(bf16[16,2304]{1,0:T(8,128)(2,1)S(1)} %head_terms.22), channel_id=1, source_target_pairs={{32,8},{40,16},{48,24},{56,0},{64,40},{72,48},{80,56},{88,32},{96,... | collective-permute-start | bytes 221192 | tf_op jit(solution)/shard_map/ppermute | solution.py:32
  454.8 10.0 %collective-permute-start.39 = (bf16[16,2304]{1,0:T(8,128)(2,1)S(1)}, bf16[16,2304]{1,0:T(8,128)(2,1)S(1)}, u32[]{:S(2)}, u32[]{:S(2)}) collective-permute-start(bf16[16,2304]{1,0:T(8,128)(2,1)S(1)} %head_terms.22), channel_id=1, source_target_pairs={{32,16},{40,24},{48,0},{56,8},{64,48},{72,56},{80,32},{88,40},{96,... | collective-permute-start | bytes 221192 | tf_op jit(solution)/shard_map/ppermute | solution.py:32
  474.2 12.9 %collective-permute-start.41 = (bf16[16,2304]{1,0:T(8,128)(2,1)S(1)}, bf16[16,2304]{1,0:T(8,128)(2,1)S(1)}, u32[]{:S(2)}, u32[]{:S(2)}) collective-permute-start(bf16[16,2304]{1,0:T(8,128)(2,1)S(1)} %head_terms.23), channel_id=1, source_target_pairs={{32,0},{40,8},{48,16},{56,24},{64,32},{72,40},{80,48},{88,56},{96,... | collective-permute-start | bytes 221192 | tf_op jit(solution)/shard_map/ppermute | solution.py:32
  476.2 11.0 %collective-permute-start.42 = (bf16[16,2304]{1,0:T(8,128)(2,1)S(1)}, bf16[16,2304]{1,0:T(8,128)(2,1)S(1)}, u32[]{:S(2)}, u32[]{:S(2)}) collective-permute-start(bf16[16,2304]{1,0:T(8,128)(2,1)S(1)} %head_terms.23), channel_id=1, source_target_pairs={{32,8},{40,16},{48,24},{56,0},{64,40},{72,48},{80,56},{88,32},{96,... | collective-permute-start | bytes 221192 | tf_op jit(solution)/shard_map/ppermute | solution.py:32
  479.1 10.0 %collective-permute-start.43 = (bf16[16,2304]{1,0:T(8,128)(2,1)S(1)}, bf16[16,2304]{1,0:T(8,128)(2,1)S(1)}, u32[]{:S(2)}, u32[]{:S(2)}) collective-permute-start(bf16[16,2304]{1,0:T(8,128)(2,1)S(1)} %head_terms.23), channel_id=1, source_target_pairs={{32,16},{40,24},{48,0},{56,8},{64,48},{72,56},{80,32},{88,40},{96,... | collective-permute-start | bytes 221192 | tf_op jit(solution)/shard_map/ppermute | solution.py:32
  498.1 13.0 %collective-permute-start.45 = (bf16[16,2304]{1,0:T(8,128)(2,1)S(1)}, bf16[16,2304]{1,0:T(8,128)(2,1)S(1)}, u32[]{:S(2)}, u32[]{:S(2)}) collective-permute-start(bf16[16,2304]{1,0:T(8,128)(2,1)S(1)} %head_terms.24), channel_id=1, source_target_pairs={{32,0},{40,8},{48,16},{56,24},{64,32},{72,40},{80,48},{88,56},{96,... | collective-permute-start | bytes 221192 | tf_op jit(solution)/shard_map/ppermute | solution.py:32
  500.1 11.1 %collective-permute-start.46 = (bf16[16,2304]{1,0:T(8,128)(2,1)S(1)}, bf16[16,2304]{1,0:T(8,128)(2,1)S(1)}, u32[]{:S(2)}, u32[]{:S(2)}) collective-permute-start(bf16[16,2304]{1,0:T(8,128)(2,1)S(1)} %head_terms.24), channel_id=1, source_target_pairs={{32,8},{40,16},{48,24},{56,0},{64,40},{72,48},{80,56},{88,32},{96,... | collective-permute-start | bytes 221192 | tf_op jit(solution)/shard_map/ppermute | solution.py:32
  503.1 10.0 %collective-permute-start.47 = (bf16[16,2304]{1,0:T(8,128)(2,1)S(1)}, bf16[16,2304]{1,0:T(8,128)(2,1)S(1)}, u32[]{:S(2)}, u32[]{:S(2)}) collective-permute-start(bf16[16,2304]{1,0:T(8,128)(2,1)S(1)} %head_terms.24), channel_id=1, source_target_pairs={{32,16},{40,24},{48,0},{56,8},{64,48},{72,56},{80,32},{88,40},{96,... | collective-permute-start | bytes 221192 | tf_op jit(solution)/shard_map/ppermute | solution.py:32
  521.6 13.1 %collective-permute-start.49 = (bf16[16,2304]{1,0:T(8,128)(2,1)S(1)}, bf16[16,2304]{1,0:T(8,128)(2,1)S(1)}, u32[]{:S(2)}, u32[]{:S(2)}) collective-permute-start(bf16[16,2304]{1,0:T(8,128)(2,1)S(1)} %head_terms.25), channel_id=1, source_target_pairs={{32,0},{40,8},{48,16},{56,24},{64,32},{72,40},{80,48},{88,56},{96,... | collective-permute-start | bytes 221192 | tf_op jit(solution)/shard_map/ppermute | solution.py:32
  524.0 10.7 %collective-permute-start.50 = (bf16[16,2304]{1,0:T(8,128)(2,1)S(1)}, bf16[16,2304]{1,0:T(8,128)(2,1)S(1)}, u32[]{:S(2)}, u32[]{:S(2)}) collective-permute-start(bf16[16,2304]{1,0:T(8,128)(2,1)S(1)} %head_terms.25), channel_id=1, source_target_pairs={{32,8},{40,16},{48,24},{56,0},{64,40},{72,48},{80,56},{88,32},{96,... | collective-permute-start | bytes 221192 | tf_op jit(solution)/shard_map/ppermute | solution.py:32
  526.4 10.0 %collective-permute-start.51 = (bf16[16,2304]{1,0:T(8,128)(2,1)S(1)}, bf16[16,2304]{1,0:T(8,128)(2,1)S(1)}, u32[]{:S(2)}, u32[]{:S(2)}) collective-permute-start(bf16[16,2304]{1,0:T(8,128)(2,1)S(1)} %head_terms.25), channel_id=1, source_target_pairs={{32,16},{40,24},{48,0},{56,8},{64,48},{72,56},{80,32},{88,40},{96,... | collective-permute-start | bytes 221192 | tf_op jit(solution)/shard_map/ppermute | solution.py:32
  545.4 12.7 %collective-permute-start.53 = (bf16[16,2304]{1,0:T(8,128)(2,1)S(1)}, bf16[16,2304]{1,0:T(8,128)(2,1)S(1)}, u32[]{:S(2)}, u32[]{:S(2)}) collective-permute-start(bf16[16,2304]{1,0:T(8,128)(2,1)S(1)} %head_terms.26), channel_id=1, source_target_pairs={{32,0},{40,8},{48,16},{56,24},{64,32},{72,40},{80,48},{88,56},{96,... | collective-permute-start | bytes 221192 | tf_op jit(solution)/shard_map/ppermute | solution.py:32
  547.4 10.7 %collective-permute-start.54 = (bf16[16,2304]{1,0:T(8,128)(2,1)S(1)}, bf16[16,2304]{1,0:T(8,128)(2,1)S(1)}, u32[]{:S(2)}, u32[]{:S(2)}) collective-permute-start(bf16[16,2304]{1,0:T(8,128)(2,1)S(1)} %head_terms.26), channel_id=1, source_target_pairs={{32,8},{40,16},{48,24},{56,0},{64,40},{72,48},{80,56},{88,32},{96,... | collective-permute-start | bytes 221192 | tf_op jit(solution)/shard_map/ppermute | solution.py:32
  550.2 10.0 %collective-permute-start.55 = (bf16[16,2304]{1,0:T(8,128)(2,1)S(1)}, bf16[16,2304]{1,0:T(8,128)(2,1)S(1)}, u32[]{:S(2)}, u32[]{:S(2)}) collective-permute-start(bf16[16,2304]{1,0:T(8,128)(2,1)S(1)} %head_terms.26), channel_id=1, source_target_pairs={{32,16},{40,24},{48,0},{56,8},{64,48},{72,56},{80,32},{88,40},{96,... | collective-permute-start | bytes 221192 | tf_op jit(solution)/shard_map/ppermute | solution.py:32
  569.2 12.4 %collective-permute-start.57 = (bf16[16,2304]{1,0:T(8,128)(2,1)S(1)}, bf16[16,2304]{1,0:T(8,128)(2,1)S(1)}, u32[]{:S(2)}, u32[]{:S(2)}) collective-permute-start(bf16[16,2304]{1,0:T(8,128)(2,1)S(1)} %head_terms.27), channel_id=1, source_target_pairs={{32,0},{40,8},{48,16},{56,24},{64,32},{72,40},{80,48},{88,56},{96,... | collective-permute-start | bytes 221192 | tf_op jit(solution)/shard_map/ppermute | solution.py:32
  571.1 10.5 %collective-permute-start.58 = (bf16[16,2304]{1,0:T(8,128)(2,1)S(1)}, bf16[16,2304]{1,0:T(8,128)(2,1)S(1)}, u32[]{:S(2)}, u32[]{:S(2)}) collective-permute-start(bf16[16,2304]{1,0:T(8,128)(2,1)S(1)} %head_terms.27), channel_id=1, source_target_pairs={{32,8},{40,16},{48,24},{56,0},{64,40},{72,48},{80,56},{88,32},{96,... | collective-permute-start | bytes 221192 | tf_op jit(solution)/shard_map/ppermute | solution.py:32
  574.0 10.0 %collective-permute-start.59 = (bf16[16,2304]{1,0:T(8,128)(2,1)S(1)}, bf16[16,2304]{1,0:T(8,128)(2,1)S(1)}, u32[]{:S(2)}, u32[]{:S(2)}) collective-permute-start(bf16[16,2304]{1,0:T(8,128)(2,1)S(1)} %head_terms.27), channel_id=1, source_target_pairs={{32,16},{40,24},{48,0},{56,8},{64,48},{72,56},{80,32},{88,40},{96,... | collective-permute-start | bytes 221192 | tf_op jit(solution)/shard_map/ppermute | solution.py:32
  592.6 12.8 %collective-permute-start.61 = (bf16[16,2304]{1,0:T(8,128)(2,1)S(1)}, bf16[16,2304]{1,0:T(8,128)(2,1)S(1)}, u32[]{:S(2)}, u32[]{:S(2)}) collective-permute-start(bf16[16,2304]{1,0:T(8,128)(2,1)S(1)} %head_terms.28), channel_id=1, source_target_pairs={{32,0},{40,8},{48,16},{56,24},{64,32},{72,40},{80,48},{88,56},{96,... | collective-permute-start | bytes 221192 | tf_op jit(solution)/shard_map/ppermute | solution.py:32
  594.5 10.9 %collective-permute-start.62 = (bf16[16,2304]{1,0:T(8,128)(2,1)S(1)}, bf16[16,2304]{1,0:T(8,128)(2,1)S(1)}, u32[]{:S(2)}, u32[]{:S(2)}) collective-permute-start(bf16[16,2304]{1,0:T(8,128)(2,1)S(1)} %head_terms.28), channel_id=1, source_target_pairs={{32,8},{40,16},{48,24},{56,0},{64,40},{72,48},{80,56},{88,32},{96,... | collective-permute-start | bytes 221192 | tf_op jit(solution)/shard_map/ppermute | solution.py:32
  597.5 10.0 %collective-permute-start.63 = (bf16[16,2304]{1,0:T(8,128)(2,1)S(1)}, bf16[16,2304]{1,0:T(8,128)(2,1)S(1)}, u32[]{:S(2)}, u32[]{:S(2)}) collective-permute-start(bf16[16,2304]{1,0:T(8,128)(2,1)S(1)} %head_terms.28), channel_id=1, source_target_pairs={{32,16},{40,24},{48,0},{56,8},{64,48},{72,56},{80,32},{88,40},{96,... | collective-permute-start | bytes 221192 | tf_op jit(solution)/shard_map/ppermute | solution.py:32
  616.1 12.8 %collective-permute-start.65 = (bf16[16,2304]{1,0:T(8,128)(2,1)S(1)}, bf16[16,2304]{1,0:T(8,128)(2,1)S(1)}, u32[]{:S(2)}, u32[]{:S(2)}) collective-permute-start(bf16[16,2304]{1,0:T(8,128)(2,1)S(1)} %head_terms.29), channel_id=1, source_target_pairs={{32,0},{40,8},{48,16},{56,24},{64,32},{72,40},{80,48},{88,56},{96,... | collective-permute-start | bytes 221192 | tf_op jit(solution)/shard_map/ppermute | solution.py:32
  618.2 10.7 %collective-permute-start.66 = (bf16[16,2304]{1,0:T(8,128)(2,1)S(1)}, bf16[16,2304]{1,0:T(8,128)(2,1)S(1)}, u32[]{:S(2)}, u32[]{:S(2)}) collective-permute-start(bf16[16,2304]{1,0:T(8,128)(2,1)S(1)} %head_terms.29), channel_id=1, source_target_pairs={{32,8},{40,16},{48,24},{56,0},{64,40},{72,48},{80,56},{88,32},{96,... | collective-permute-start | bytes 221192 | tf_op jit(solution)/shard_map/ppermute | solution.py:32
  620.9 10.0 %collective-permute-start.67 = (bf16[16,2304]{1,0:T(8,128)(2,1)S(1)}, bf16[16,2304]{1,0:T(8,128)(2,1)S(1)}, u32[]{:S(2)}, u32[]{:S(2)}) collective-permute-start(bf16[16,2304]{1,0:T(8,128)(2,1)S(1)} %head_terms.29), channel_id=1, source_target_pairs={{32,16},{40,24},{48,0},{56,8},{64,48},{72,56},{80,32},{88,40},{96,... | collective-permute-start | bytes 221192 | tf_op jit(solution)/shard_map/ppermute | solution.py:32
  635.6 24.7 %all-to-all-start.10 = ((bf16[16,4,2304]{2,1,0:T(4,128)(2,1)}), bf16[16,4,2304]{2,1,0:T(4,128)(2,1)S(1)}, u32[]{:S(2)}, u32[]{:S(2)}) async-start(bf16[16,4,2304]{2,1,0:T(4,128)(2,1)} %copy.99), calls=%async_computation.10 | async-start | bytes 589824 | tf_op jit(solution)/shard_map/all_to_all | solution.py:217
  (38 other events, 257.4 us)

commit v3 on v2

v3 whole, which is shorter than its diff:
```python
import jax
import jax.numpy as jnp
from jax import lax
from jax.experimental import pallas as pl
from jax.experimental.pallas import tpu as pltpu
from jax.sharding import Mesh, PartitionSpec as P

K_ACT = 256
BF = jnp.bfloat16
F32 = jnp.float32
FEAT = ("y2", "par", "zh", "core")
CHIPS = ("y2", "par", "zh")
QUADS = 4
PANEL_BY = 5
SWAP = [(0, 1), (1, 0)]


def neighbour_heads(shard):
    pairs = []
    for y in range(8):
        pairs.append((2 * y, 2 * ((y - 1) % 8)))
        pairs.append((2 * y + 1, 2 * ((y + 1) % 8) + 1))
    split = [(y * 2 + core) for y in range(8) for core in range(2)]
    assert len(split) == len(pairs)
    return lax.ppermute(shard, ("y2", "par", "core"), pairs)


def send_down(shard, turn, sections):
    places = {0: ((0, 0), (3, 1)), 1: ((2, 1), (1, 0))}[turn]
    pairs = []
    for section in range(1, sections):
        for i in range(QUADS):
            for core, (by, to_core) in enumerate(places):
                below = (section - 1) * QUADS + (i + by) % QUADS
                pairs.append(((section * QUADS + i) * 2 + core, below * 2 + to_core))
    return lax.ppermute(shard, ("section", "y2", "core"), pairs)


def grads_kernel(first_ref, second_ref, *refs):
    *outs, part_ref, rounded_ref, grads_ref = refs
    part = first_ref[...].astype(F32) + second_ref[...].astype(F32)
    part_ref[...] = part
    rounded = part.astype(BF)
    rounded_ref[...] = rounded
    wide = outs[0].shape[0]
    for k, ref in enumerate(outs):
        grads_ref[:, k * wide : (k + 1) * wide] = lax.dot_general(
            rounded, ref[...], (((1,), (1,)), ((), ())), preferred_element_type=F32
        )


def terms_kernel(core_ref, grads_ref, mix_ref, part_ref, scales_ref, *refs):
    *values, share_ref = refs
    core = core_ref[0]
    mine, other = grads_ref[core], grads_ref[1 - core]
    wide = values[0].shape[1]
    head = wide // 2
    swapped = []
    for k in range(len(values)):
        swapped.append(other[:, k * wide + head : (k + 1) * wide])
        swapped.append(other[:, k * wide : k * wide + head])
    grads = mine + jnp.concatenate(swapped, axis=1)
    mixed = mix_ref[0] * grads[0:1, :]
    for p in range(1, grads.shape[0]):
        mixed = mixed + mix_ref[p] * grads[p : p + 1, :]
    mixed = mixed.astype(BF)
    term = None
    for k, ref in enumerate(values):
        product = lax.dot_general(
            mixed[:, k * wide : (k + 1) * wide],
            ref[...],
            (((1,), (1,)), ((), ())),
            preferred_element_type=F32,
        )
        term = product if term is None else term + product
    share_ref[...] = (part_ref[...] * 0.5 + term * scales_ref[...]).astype(BF)


def keep(array):
    return pltpu.with_memory_space_constraint(array, pltpu.VMEM)


def whole():
    return pl.BlockSpec(memory_space=pltpu.VMEM)


def head_grads(arrived, outs):
    seq_len, model_width = arrived[0].shape
    heads_wide = sum(w.shape[0] for w in outs)
    return pl.pallas_call(
        grads_kernel,
        out_shape=(
            jax.ShapeDtypeStruct((seq_len, model_width), F32),
            jax.ShapeDtypeStruct((seq_len, model_width), BF),
            jax.ShapeDtypeStruct((seq_len, heads_wide), F32),
        ),
        in_specs=[whole()] * (2 + len(outs)),
        out_specs=(whole(),) * 3,
        compiler_params=pltpu.CompilerParams(vmem_limit_bytes=24 << 20),
        name="head_grads",
    )(*arrived, *outs)


def head_terms(core, grads, mix_wide, part, scales, values):
    return pl.pallas_call(
        terms_kernel,
        out_shape=jax.ShapeDtypeStruct(part.shape, BF),
        in_specs=[pl.BlockSpec(memory_space=pltpu.SMEM)] + [whole()] * (4 + len(values)),
        out_specs=whole(),
        compiler_params=pltpu.CompilerParams(vmem_limit_bytes=24 << 20),
        name="head_terms",
    )(core, grads, mix_wide, part, scales, *values)


def panel_route(dec_table, act_ids, entries_dev, feat_index, feat_count):
    feat_rows, model_width = dec_table.shape
    slot_count = 2 * entries_dev // feat_count
    ids_blocks = act_ids.reshape(feat_count, entries_dev)
    owner_ids = ids_blocks // feat_rows
    local_ids = ids_blocks % feat_rows
    owned_mask = owner_ids == feat_index
    entry_iota = jnp.arange(entries_dev, dtype=jnp.int32)
    before = (entry_iota[:, None] < entry_iota[None, :]).astype(BF)
    slot_rank = jnp.dot(owned_mask.astype(BF), before, preferred_element_type=F32).astype(jnp.int32)
    slot_iota = jnp.arange(slot_count, dtype=jnp.int32)
    selected = (
        owned_mask[:, None, :] & (slot_rank[:, None, :] == slot_iota[None, :, None])
    ).astype(jnp.int32)
    source_row = jnp.sum(selected * local_ids[:, None, :], axis=2)
    outgoing = jnp.take(dec_table, source_row.reshape(-1), axis=0).reshape(
        feat_count, slot_count, model_width
    )
    own_owner = lax.dynamic_index_in_dim(owner_ids, feat_index, 0, keepdims=False)
    earlier = (entry_iota[None, :] < entry_iota[:, None]).astype(jnp.int32)
    same_owner = (own_owner[:, None] == own_owner[None, :]).astype(jnp.int32)
    own_rank = jnp.sum(earlier * same_owner, axis=1)
    flat_index = own_owner * slot_count + own_rank
    return outgoing, flat_index


def per_device(
    decoders,
    encoders,
    out_proj,
    value_proj,
    attention,
    norm_scale,
    act_ids,
    act_values,
    target_ids,
    target_pos,
):
    sections = lax.axis_size("section")
    section_index = lax.axis_index("section")
    feat_index = lax.axis_index(FEAT)
    feat_count = lax.axis_size(FEAT)
    model_width = decoders.shape[2]
    half = model_width // 2
    feat_rows = decoders.shape[1]
    seq_len = attention.shape[2]
    head_width = out_proj.shape[1]
    entries_dev = act_values.shape[1]
    targets = target_ids.shape[0]

    own = (out_proj[0], value_proj[0])
    own_mix = attention[0, 0]
    beyond = tuple(lax.ppermute(a, "zh", SWAP) for a in own)
    near = tuple(neighbour_heads(a) for a in own)

    feat_iota = jnp.arange(feat_rows, dtype=jnp.int32)
    target_pick = (
        (target_ids - feat_index * feat_rows)[:, None] == feat_iota[None, :]
    ).astype(BF)
    enc_rows = jnp.dot(target_pick, encoders[0], preferred_element_type=F32).astype(BF)
    enc_send = jnp.broadcast_to(
        enc_rows[None, :, None, :], (QUADS, targets, 2, model_width)
    ).reshape(feat_count, model_width)
    near, own, own_mix, enc_send = lax.optimization_barrier((near, own, own_mix, enc_send))
    beyond_mix = lax.ppermute(own_mix, "zh", SWAP)
    near_mix = neighbour_heads(own_mix)
    far_mix = neighbour_heads(beyond_mix)
    enc_got = lax.all_to_all(enc_send, FEAT, split_axis=0, concat_axis=0, tiled=True)
    enc_row = jnp.sum(enc_got.astype(F32), axis=0)
    own_target = lax.axis_index(("par", "zh"))
    own_pos = lax.dynamic_index_in_dim(target_pos, own_target, 0, keepdims=False)
    positions = jnp.arange(seq_len, dtype=jnp.int32)
    start = jnp.where((positions == own_pos)[:, None], enc_row[None, :], 0.0)

    outgoing, flat_index = panel_route(
        decoders[0], act_ids[0], entries_dev, feat_index, feat_count
    )
    far = tuple(neighbour_heads(a) for a in beyond)
    far, outgoing = lax.optimization_barrier((far, outgoing))
    incoming = lax.all_to_all(outgoing, FEAT, split_axis=0, concat_axis=0, tiled=True)

    outs, values = [], []
    for out_head, value_head in (own, near, beyond, far):
        outs.append(jnp.concatenate([out_head, lax.ppermute(out_head, "core", SWAP)], axis=0))
        values.append(
            jnp.concatenate([value_head, lax.ppermute(value_head, "core", SWAP)], axis=1)
        )
    core_mix = jnp.stack([own_mix, near_mix, beyond_mix, far_mix])
    mixing = jnp.stack([core_mix, lax.ppermute(core_mix, "core", SWAP)], axis=1)
    mixing = mixing.reshape(-1, seq_len, seq_len)
    heads = mixing.shape[0]
    mix_wide = jnp.broadcast_to(
        mixing.transpose(1, 2, 0)[..., None], (seq_len, seq_len, heads, head_width)
    ).reshape(seq_len, seq_len, heads * head_width)
    scales = norm_scale[0][:, None]

    outs, values = [keep(w) for w in outs], [keep(w) for w in values]
    mix_wide = keep(mix_wide)
    core = lax.axis_index("core").reshape(1)
    quarter = (start * 0.25).astype(BF)
    arrived = (quarter, quarter)
    history = []
    for step in range(sections - 1):
        if step == PANEL_BY:
            arrived, incoming = lax.optimization_barrier((arrived, incoming))
        part, rounded, grad_part = head_grads(arrived, outs)
        history.append(rounded)
        grads = lax.all_gather(grad_part, "core", axis=0)
        share = head_terms(core, grads, mix_wide, part, scales, values)
        arrived = tuple(send_down(share, turn, sections) for turn in range(2))
    history.append((arrived[0].astype(F32) + arrived[1].astype(F32)).astype(BF))
    panel = jnp.take(incoming.reshape(-1, model_width), flat_index, axis=0)

    steps_each = sections // QUADS
    held = jnp.stack(history)
    first = lax.axis_index("y2") * steps_each
    held = lax.dynamic_slice_in_dim(held, first, steps_each, 0).transpose(1, 0, 2)
    this_half = lax.dynamic_slice_in_dim(held, core[0] * half, half, 2)
    other_half = lax.dynamic_slice_in_dim(held, (1 - core[0]) * half, half, 2)
    got_half = lax.ppermute(other_half, "core", SWAP)
    held = (this_half.astype(F32) + got_half.astype(F32)).astype(BF)
    got = lax.all_to_all(held, CHIPS, split_axis=0, concat_axis=0, tiled=True)
    got = lax.all_gather(got.reshape(-1, half), "core", axis=0)
    raw = sum(
        lax.dot_general(
            got[side],
            panel[:, side * half : (side + 1) * half],
            (((1,), (1,)), ((), ())),
            preferred_element_type=F32,
        )
        for side in range(2)
    )
    edges = raw.reshape(QUADS, targets, steps_each, entries_dev).transpose(0, 2, 1, 3)
    edges = edges.reshape(sections * targets, entries_dev) * act_values[0][None, :]
    padded = jnp.concatenate([jnp.zeros_like(edges), edges], axis=0)
    edges = lax.dynamic_slice_in_dim(
        padded, (sections - section_index) * targets, sections * targets, 0
    )
    return edges[None]


def solution(mesh):
    sections = mesh.shape["section"]
    fine = Mesh(mesh.devices.reshape(sections, 4, 2, 2, 2), ("section", *FEAT))
    in_specs = (
        P("section", FEAT, None),
        P("section", FEAT, None),
        P("section", FEAT, None),
        P("section", None, FEAT),
        P("section", FEAT, None, None),
        P("section", None),
        P("section", None),
        P("section", FEAT),
        P("section"),
        P("section"),
    )
    return jax.shard_map(
        per_device, mesh=fine, in_specs=in_specs, out_specs=P("section", None, FEAT), check_vma=False
    )
```

time: 680 us -> 649 us (0.954)
  the two profiles are of different devices: /device:TPU:197 before, /device:TPU:7 now
where the time goes in v3:
time: 649 us; the launch traced here: 639 us
  waiting for transfers between devices  245 us (38%)
  starting transfers between devices  212 us (33%)
  local copies, waits for them, and re-layouts  90.6 us (14%)
  Pallas kernels  42.2 us (7%)
  blocking collectives  32.8 us (5%)
  other arithmetic  13.1 us (2%)
    ppermute x30, waiting for transfers between devices, send_down(): return lax.ppermute(shard, ('section', 'y2', 'core'), pairs)  207 us
    ppermute x30, starting transfers between devices, send_down(): return lax.ppermute(shard, ('section', 'y2', 'core'), pairs)  68 us
    ppermute x4, starting transfers between devices, per_device(): lax.ppermute(value_head, 'core', SWAP)  60.2 us
    pallas_call x14, local copies, waits for them, and re-layouts, head_grads(): pl.pallas_call(grads_kernel, out_shape=(jax.ShapeDtypeStruct((seq_len, mo...  45.4 us
    pallas_call x15, Pallas kernels, head_terms(): pl.pallas_call(terms_kernel, out_shape=jax.ShapeDtypeStruct(part.shape, B...  39.7 us
    all_gather x15, blocking collectives, per_device(): grads = lax.all_gather(grad_part, 'core', axis=0)  29.2 us
    ppermute x6, waiting for transfers between devices, neighbour_heads(): return lax.ppermute(shard, ('y2', 'par', 'core'), pairs)  21.3 us
    unnamed x85, local copies, waits for them, and re-layouts  19.4 us
  transfers between devices with their start and end apart: 52, of which 33 were waited for; matrix products, arithmetic and copies ran while one was open for 10% of the time, Pallas kernels for 2%

profile of v3, /device:TPU:7, one launch (start us, length us, event | category | flops | bytes accessed | tf_op | source)
XLA Modules:
  0.0 638.8 jit_solution(16823728997661038615)
XLA Ops:
  0.0 10.8 %collective-permute-start.4 = (bf16[128,4608]{1,0:T(8,128)(2,1)}, bf16[128,4608]{1,0:T(8,128)(2,1)}, u32[]{:S(2)}, u32[]{:S(2)}) collective-permute-start(bf16[128,4608]{1,0:T(8,128)(2,1)} %bitcast.1), channel_id=1, source_target_pairs={{0,2},{2,0},{1,3},{3,1},{4,6},{6,4},{5,7},{7,5},{8,10},{10,8},{9,1... | collective-permute-start | bytes 3538952 | tf_op jit(solution)/shard_map/ppermute | solution.py:167
  10.8 3.2 collective-permute-start
  15.9 3.2 collective-permute-start.1
  31.1 11.7 %collective-permute-done.1 = bf16[4608,128]{1,0:T(8,128)(2,1)} collective-permute-done((bf16[4608,128]{1,0:T(8,128)(2,1)}, bf16[4608,128]{1,0:T(8,128)(2,1)}, u32[]{:S(2)}, u32[]{:S(2)}) %collective-permute-start.1) | collective-permute-done | bytes 1179680 | tf_op jit(solution)/shard_map/ppermute | solution.py:25
  42.7 3.0 collective-permute-start.3
  49.9 6.8 %all-to-all-start = ((bf16[32,2,2304]{2,1,0:T(2,128)(2,1)}), bf16[32,2,2304]{2,1,0:T(2,128)(2,1)}, u32[]{:S(2)}, u32[]{:S(2)}) async-start(bf16[32,2,2304]{2,1,0:T(2,128)(2,1)} %reshape.202), calls=%async_computation | async-start | bytes 589824 | tf_op jit(solution)/shard_map/all_to_all | solution.py:182
  56.7 7.3 %collective-permute-start.11 = (f32[16,16]{1,0:T(8,128)}, f32[16,16]{1,0:T(8,128)S(1)}, u32[]{:S(2)}, u32[]{:S(2)}) collective-permute-start(f32[16,16]{1,0:T(8,128)} %bitcast.140), channel_id=1, source_target_pairs={{0,2},{2,0},{1,3},{3,1},{4,6},{6,4},{5,7},{7,5},{8,10},{10,8},{9,1... | collective-permute-start | bytes 3080 | tf_op jit(solution)/shard_map/ppermute | solution.py:179
  64.1 2.8 constant_dynamic-update-slice_fusion.1
  66.9 2.9 constant_dynamic-update-slice_fusion.9
  69.8 3.1 collective-permute-start.10
  72.9 3.1 collective-permute-start.12
  78.3 52.4 %collective-permute-start.15 = (bf16[4608,128]{1,0:T(8,128)(2,1)}, bf16[4608,128]{1,0:T(8,128)(2,1)}, u32[]{:S(2)}, u32[]{:S(2)}) collective-permute-start(bf16[4608,128]{1,0:T(8,128)(2,1)} %collective-permute-done.1), channel_id=1, source_target_pairs={{0,1},{1,0},{2,3},{3,2},{4,5},{5,4},{6,7},{7,6},{8,9},{9,8},{10,11... | collective-permute-start | bytes 3538952 | tf_op jit(solution)/shard_map/ppermute | solution.py:200
  132.7 3.3 collective-permute-start.13
  143.5 3.0 reshape.203
  149.2 3.3 collective-permute-start.14
  152.5 9.3 %collective-permute-done.8 = bf16[4608,128]{1,0:T(8,128)(2,1)} collective-permute-done((bf16[4608,128]{1,0:T(8,128)(2,1)}, bf16[4608,128]{1,0:T(8,128)(2,1)}, u32[]{:S(2)}, u32[]{:S(2)}) %collective-permute-start.8) | collective-permute-done | bytes 1179680 | tf_op jit(solution)/shard_map/ppermute | solution.py:25
  163.8 10.5 %all-to-all-start.1 = ((bf16[32,8,4608]{2,1,0:T(8,128)(2,1)}), bf16[32,8,4608]{2,1,0:T(8,128)(2,1)}, u32[]{:S(2)}, u32[]{:S(2)}) async-start(bf16[32,8,4608]{2,1,0:T(8,128)(2,1)} %bitcast_select_fusion), calls=%async_computation.1 | async-start | bytes 4718592 | tf_op jit(solution)/shard_map/all_to_all | solution.py:194
  199.3 2.6 head_terms.15
  201.8 5.8 collective-permute-start.18
  210.2 27.7 %collective-permute-done.18 = bf16[16,4608]{1,0:T(8,128)(2,1)S(1)} collective-permute-done((bf16[16,4608]{1,0:T(8,128)(2,1)S(1)}, bf16[16,4608]{1,0:T(8,128)(2,1)S(1)}, u32[]{:S(2)}, u32[]{:S(2)}) %collective-permute-start.18) | collective-permute-done | bytes 147488 | tf_op jit(solution)/shard_map/ppermute | solution.py:36
  242.4 2.6 head_terms.16
  244.9 5.4 collective-permute-start.20
  252.2 2.6 collective-permute-done.20
  254.8 8.9 %collective-permute-done.21 = bf16[16,4608]{1,0:T(8,128)(2,1)S(1)} collective-permute-done((bf16[16,4608]{1,0:T(8,128)(2,1)S(1)}, bf16[16,4608]{1,0:T(8,128)(2,1)S(1)}, u32[]{:S(2)}, u32[]{:S(2)}) %collective-permute-start.21) | collective-permute-done | bytes 147488 | tf_op jit(solution)/shard_map/ppermute | solution.py:36
  270.8 4.6 collective-permute-start.22
  277.3 4.8 collective-permute-done.22
  282.1 7.1 %collective-permute-done.23 = bf16[16,4608]{1,0:T(8,128)(2,1)S(1)} collective-permute-done((bf16[16,4608]{1,0:T(8,128)(2,1)S(1)}, bf16[16,4608]{1,0:T(8,128)(2,1)S(1)}, u32[]{:S(2)}, u32[]{:S(2)}) %collective-permute-start.23) | collective-permute-done | bytes 147488 | tf_op jit(solution)/shard_map/ppermute | solution.py:36
  300.1 7.5 %collective-permute-done.24 = bf16[16,4608]{1,0:T(8,128)(2,1)S(1)} collective-permute-done((bf16[16,4608]{1,0:T(8,128)(2,1)S(1)}, bf16[16,4608]{1,0:T(8,128)(2,1)S(1)}, u32[]{:S(2)}, u32[]{:S(2)}) %collective-permute-start.24) | collective-permute-done | bytes 147488 | tf_op jit(solution)/shard_map/ppermute | solution.py:36
  307.6 6.8 %collective-permute-done.25 = bf16[16,4608]{1,0:T(8,128)(2,1)S(1)} collective-permute-done((bf16[16,4608]{1,0:T(8,128)(2,1)S(1)}, bf16[16,4608]{1,0:T(8,128)(2,1)S(1)}, u32[]{:S(2)}, u32[]{:S(2)}) %collective-permute-start.25) | collective-permute-done | bytes 147488 | tf_op jit(solution)/shard_map/ppermute | solution.py:36
  318.9 2.6 head_terms.19
  325.6 7.3 %collective-permute-done.26 = bf16[16,4608]{1,0:T(8,128)(2,1)S(1)} collective-permute-done((bf16[16,4608]{1,0:T(8,128)(2,1)S(1)}, bf16[16,4608]{1,0:T(8,128)(2,1)S(1)}, u32[]{:S(2)}, u32[]{:S(2)}) %collective-permute-start.26) | collective-permute-done | bytes 147488 | tf_op jit(solution)/shard_map/ppermute | solution.py:36
  333.5 4.9 collective-permute-done.27
  338.4 5.9 head_grads.25
  346.3 2.6 head_terms.20
  352.7 7.3 %collective-permute-done.28 = bf16[16,4608]{1,0:T(8,128)(2,1)S(1)} collective-permute-done((bf16[16,4608]{1,0:T(8,128)(2,1)S(1)}, bf16[16,4608]{1,0:T(8,128)(2,1)S(1)}, u32[]{:S(2)}, u32[]{:S(2)}) %collective-permute-start.28) | collective-permute-done | bytes 147488 | tf_op jit(solution)/shard_map/ppermute | solution.py:36
  360.0 6.1 collective-permute-done.29
  376.9 7.3 %collective-permute-done.30 = bf16[16,4608]{1,0:T(8,128)(2,1)S(1)} collective-permute-done((bf16[16,4608]{1,0:T(8,128)(2,1)S(1)}, bf16[16,4608]{1,0:T(8,128)(2,1)S(1)}, u32[]{:S(2)}, u32[]{:S(2)}) %collective-permute-start.30) | collective-permute-done | bytes 147488 | tf_op jit(solution)/shard_map/ppermute | solution.py:36
  384.3 5.6 collective-permute-done.31
  400.7 7.3 %collective-permute-done.32 = bf16[16,4608]{1,0:T(8,128)(2,1)S(1)} collective-permute-done((bf16[16,4608]{1,0:T(8,128)(2,1)S(1)}, bf16[16,4608]{1,0:T(8,128)(2,1)S(1)}, u32[]{:S(2)}, u32[]{:S(2)}) %collective-permute-start.32) | collective-permute-done | bytes 147488 | tf_op jit(solution)/shard_map/ppermute | solution.py:36
  408.0 6.0 collective-permute-done.33
  424.8 7.3 %collective-permute-done.34 = bf16[16,4608]{1,0:T(8,128)(2,1)S(1)} collective-permute-done((bf16[16,4608]{1,0:T(8,128)(2,1)S(1)}, bf16[16,4608]{1,0:T(8,128)(2,1)S(1)}, u32[]{:S(2)}, u32[]{:S(2)}) %collective-permute-start.34) | collective-permute-done | bytes 147488 | tf_op jit(solution)/shard_map/ppermute | solution.py:36
  432.1 6.2 collective-permute-done.35
  449.6 6.7 %collective-permute-done.36 = bf16[16,4608]{1,0:T(8,128)(2,1)S(1)} collective-permute-done((bf16[16,4608]{1,0:T(8,128)(2,1)S(1)}, bf16[16,4608]{1,0:T(8,128)(2,1)S(1)}, u32[]{:S(2)}, u32[]{:S(2)}) %collective-permute-start.36) | collective-permute-done | bytes 147488 | tf_op jit(solution)/shard_map/ppermute | solution.py:36
  456.4 6.3 collective-permute-done.37
  473.6 6.8 %collective-permute-done.38 = bf16[16,4608]{1,0:T(8,128)(2,1)S(1)} collective-permute-done((bf16[16,4608]{1,0:T(8,128)(2,1)S(1)}, bf16[16,4608]{1,0:T(8,128)(2,1)S(1)}, u32[]{:S(2)}, u32[]{:S(2)}) %collective-permute-start.38) | collective-permute-done | bytes 147488 | tf_op jit(solution)/shard_map/ppermute | solution.py:36
  480.4 6.3 collective-permute-done.39
  497.5 6.8 %collective-permute-done.40 = bf16[16,4608]{1,0:T(8,128)(2,1)S(1)} collective-permute-done((bf16[16,4608]{1,0:T(8,128)(2,1)S(1)}, bf16[16,4608]{1,0:T(8,128)(2,1)S(1)}, u32[]{:S(2)}, u32[]{:S(2)}) %collective-permute-start.40) | collective-permute-done | bytes 147488 | tf_op jit(solution)/shard_map/ppermute | solution.py:36
  504.3 6.5 %collective-permute-done.41 = bf16[16,4608]{1,0:T(8,128)(2,1)S(1)} collective-permute-done((bf16[16,4608]{1,0:T(8,128)(2,1)S(1)}, bf16[16,4608]{1,0:T(8,128)(2,1)S(1)}, u32[]{:S(2)}, u32[]{:S(2)}) %collective-permute-start.41) | collective-permute-done | bytes 147488 | tf_op jit(solution)/shard_map/ppermute | solution.py:36
  515.2 3.2 head_terms.27
  522.3 7.0 %collective-permute-done.42 = bf16[16,4608]{1,0:T(8,128)(2,1)} collective-permute-done((bf16[16,4608]{1,0:T(8,128)(2,1)}, bf16[16,4608]{1,0:T(8,128)(2,1)}, u32[]{:S(2)}, u32[]{:S(2)}) %collective-permute-start.42) | collective-permute-done | bytes 147488 | tf_op jit(solution)/shard_map/ppermute | solution.py:36
  529.3 6.3 collective-permute-done.43
  535.6 5.9 head_grads.17
  543.4 3.2 head_terms.28
  551.5 6.1 collective-permute-done.44
  557.6 6.5 %collective-permute-done.45 = bf16[16,4608]{1,0:T(8,128)(2,1)} collective-permute-done((bf16[16,4608]{1,0:T(8,128)(2,1)}, bf16[16,4608]{1,0:T(8,128)(2,1)}, u32[]{:S(2)}, u32[]{:S(2)}) %collective-permute-start.45) | collective-permute-done | bytes 147488 | tf_op jit(solution)/shard_map/ppermute | solution.py:36
  564.1 5.9 head_grads.16
  571.9 2.6 head_terms.29
  579.0 6.1 collective-permute-done.46
  585.1 5.1 collective-permute-done.47
  592.0 2.6 collective-permute-start.48
  595.4 4.4 gather_fusion.1
  601.8 14.7 %all-to-all-start.2 = ((bf16[16,4,2304]{2,1,0:T(4,128)(2,1)}), bf16[16,4,2304]{2,1,0:T(4,128)(2,1)}, u32[]{:S(2)}, u32[]{:S(2)}) async-start(bf16[16,4,2304]{2,1,0:T(4,128)(2,1)} %copy.102), calls=%async_computation.2 | async-start | bytes 589824 | tf_op jit(solution)/shard_map/all_to_all | solution.py:236
  616.7 15.9 %all-to-all-done.2 = bf16[16,4,2304]{2,1,0:T(4,128)(2,1)} async-done(((bf16[16,4,2304]{2,1,0:T(4,128)(2,1)}), bf16[16,4,2304]{2,1,0:T(4,128)(2,1)}, u32[]{:S(2)}, u32[]{:S(2)}) %all-to-all-start.2) | async-done | bytes 294944 | tf_op jit(solution)/shard_map/all_to_all | solution.py:236
  633.7 3.6 all_gather.123
  (222 shorter events, 196.7 us)
Async XLA Ops:
  0.0 27.4 %copy-start = (bf16[1,128,4608]{2,1,0:T(8,128)(2,1)S(1)}, bf16[1,128,4608]{2,1,0:T(8,128)(2,1)}, u32[]{:S(2)}) copy-start(bf16[1,128,4608]{2,1,0:T(8,128)(2,1)} %param.10) | copy-start | bytes 3538948
  0.0 25.4 %copy-start.37 = (s32[4]{0:T(128)S(1)}, s32[4]{0:T(128)}, u32[]{:S(2)}) copy-start(s32[4]{0:T(128)} %param.19) | copy-start | bytes 52
  0.0 27.3 %copy-start.36 = (f32[1,16]{1,0:T(1,128)S(1)}, f32[1,16]{1,0:T(1,128)}, u32[]{:S(2)}) copy-start(f32[1,16]{1,0:T(1,128)} %param.15) | copy-start | bytes 196
  0.0 69.8 %collective-permute-start.4 = (bf16[128,4608]{1,0:T(8,128)(2,1)}, bf16[128,4608]{1,0:T(8,128)(2,1)}, u32[]{:S(2)}, u32[]{:S(2)}) collective-permute-start(bf16[128,4608]{1,0:T(8,128)(2,1)} %bitcast.1), channel_id=1, source_target_pairs={{0,2},{2,0},{1,3},{3,1},{4,6},{6,4},{5,7},{7,5},{8,10},{10,8},{9,1... | collective-permute-start | bytes 3538952 | tf_op jit(solution)/shard_map/ppermute | solution.py:167
  10.8 20.3 %collective-permute-start = (bf16[128,4608]{1,0:T(8,128)(2,1)}, bf16[128,4608]{1,0:T(8,128)(2,1)}, u32[]{:S(2)}, u32[]{:S(2)}) collective-permute-start(bf16[128,4608]{1,0:T(8,128)(2,1)} %bitcast.1), channel_id=1, source_target_pairs={{0,28},{1,5},{4,0},{5,9},{8,4},{9,13},{12,8},{13,17},{16,12},{17,2... | collective-permute-start | bytes 3538952 | tf_op jit(solution)/shard_map/ppermute | solution.py:25
  14.0 118.7 %collective-permute-start.7 = (bf16[4608,128]{1,0:T(8,128)(2,1)}, bf16[4608,128]{1,0:T(8,128)(2,1)}, u32[]{:S(2)}, u32[]{:S(2)}) collective-permute-start(bf16[4608,128]{1,0:T(8,128)(2,1)} %bitcast.129), channel_id=1, source_target_pairs={{0,2},{2,0},{1,3},{3,1},{4,6},{6,4},{5,7},{7,5},{8,10},{10,8},{9,1... | collective-permute-start | bytes 3538952 | tf_op jit(solution)/shard_map/ppermute | solution.py:167
  15.9 26.8 %collective-permute-start.1 = (bf16[4608,128]{1,0:T(8,128)(2,1)}, bf16[4608,128]{1,0:T(8,128)(2,1)}, u32[]{:S(2)}, u32[]{:S(2)}) collective-permute-start(bf16[4608,128]{1,0:T(8,128)(2,1)} %bitcast.130), channel_id=1, source_target_pairs={{0,28},{1,5},{4,0},{5,9},{8,4},{9,13},{12,8},{13,17},{16,12},{17,2... | collective-permute-start | bytes 3538952 | tf_op jit(solution)/shard_map/ppermute | solution.py:25
  42.7 134.5 %collective-permute-start.3 = (bf16[128,4608]{1,0:T(8,128)(2,1)}, bf16[128,4608]{1,0:T(8,128)(2,1)}, u32[]{:S(2)}, u32[]{:S(2)}) collective-permute-start(bf16[128,4608]{1,0:T(8,128)(2,1)} %collective-permute-done), channel_id=1, source_target_pairs={{0,1},{1,0},{2,3},{3,2},{4,5},{5,4},{6,7},{7,6},{8,9},{9,8},{10,11... | collective-permute-start | bytes 3538952 | tf_op jit(solution)/shard_map/ppermute | solution.py:198
  45.7 135.3 %collective-permute-start.2 = (bf16[128,4608]{1,0:T(8,128)(2,1)}, bf16[128,4608]{1,0:T(8,128)(2,1)}, u32[]{:S(2)}, u32[]{:S(2)}) collective-permute-start(bf16[128,4608]{1,0:T(8,128)(2,1)} %bitcast.1), channel_id=1, source_target_pairs={{0,1},{1,0},{2,3},{3,2},{4,5},{5,4},{6,7},{7,6},{8,9},{9,8},{10,11... | collective-permute-start | bytes 3538952 | tf_op jit(solution)/shard_map/ppermute | solution.py:198
  49.9 93.7 %all-to-all-start = ((bf16[32,2,2304]{2,1,0:T(2,128)(2,1)}), bf16[32,2,2304]{2,1,0:T(2,128)(2,1)}, u32[]{:S(2)}, u32[]{:S(2)}) async-start(bf16[32,2,2304]{2,1,0:T(2,128)(2,1)} %reshape.202), calls=%async_computation | async-start | bytes 589824 | tf_op jit(solution)/shard_map/all_to_all | solution.py:182
  56.7 16.2 %collective-permute-start.11 = (f32[16,16]{1,0:T(8,128)}, f32[16,16]{1,0:T(8,128)S(1)}, u32[]{:S(2)}, u32[]{:S(2)}) collective-permute-start(f32[16,16]{1,0:T(8,128)} %bitcast.140), channel_id=1, source_target_pairs={{0,2},{2,0},{1,3},{3,1},{4,6},{6,4},{5,7},{7,5},{8,10},{10,8},{9,1... | collective-permute-start | bytes 3080 | tf_op jit(solution)/shard_map/ppermute | solution.py:179
  69.8 8.6 %collective-permute-start.10 = (f32[16,16]{1,0:T(8,128)S(1)}, f32[16,16]{1,0:T(8,128)S(1)}, u32[]{:S(2)}, u32[]{:S(2)}) collective-permute-start(f32[16,16]{1,0:T(8,128)S(1)} %bitcast.141), channel_id=1, source_target_pairs={{0,28},{1,5},{4,0},{5,9},{8,4},{9,13},{12,8},{13,17},{16,12},{17,2... | collective-permute-start | bytes 3080 | tf_op jit(solution)/shard_map/ppermute | solution.py:25
  72.9 57.9 %collective-permute-start.12 = (f32[16,16]{1,0:T(8,128)S(1)}, f32[16,16]{1,0:T(8,128)S(1)}, u32[]{:S(2)}, u32[]{:S(2)}) collective-permute-start(f32[16,16]{1,0:T(8,128)S(1)} %collective-permute-done.11), channel_id=1, source_target_pairs={{0,28},{1,5},{4,0},{5,9},{8,4},{9,13},{12,8},{13,17},{16,12},{17,2... | collective-permute-start | bytes 3080 | tf_op jit(solution)/shard_map/ppermute | solution.py:25
  78.3 110.1 %collective-permute-start.15 = (bf16[4608,128]{1,0:T(8,128)(2,1)}, bf16[4608,128]{1,0:T(8,128)(2,1)}, u32[]{:S(2)}, u32[]{:S(2)}) collective-permute-start(bf16[4608,128]{1,0:T(8,128)(2,1)} %collective-permute-done.1), channel_id=1, source_target_pairs={{0,1},{1,0},{2,3},{3,2},{4,5},{5,4},{6,7},{7,6},{8,9},{9,8},{10,11... | collective-permute-start | bytes 3538952 | tf_op jit(solution)/shard_map/ppermute | solution.py:200
  130.8 18.5 %collective-permute-start.6 = (bf16[128,4608]{1,0:T(8,128)(2,1)}, bf16[128,4608]{1,0:T(8,128)(2,1)}, u32[]{:S(2)}, u32[]{:S(2)}) collective-permute-start(bf16[128,4608]{1,0:T(8,128)(2,1)} %collective-permute-done.4), channel_id=1, source_target_pairs={{0,28},{1,5},{4,0},{5,9},{8,4},{9,13},{12,8},{13,17},{16,12},{17,2... | collective-permute-start | bytes 3538952 | tf_op jit(solution)/shard_map/ppermute | solution.py:25
  132.7 5.8 collective-permute-start.13
  138.5 23.4 %collective-permute-start.8 = (bf16[4608,128]{1,0:T(8,128)(2,1)}, bf16[4608,128]{1,0:T(8,128)(2,1)}, u32[]{:S(2)}, u32[]{:S(2)}) collective-permute-start(bf16[4608,128]{1,0:T(8,128)(2,1)} %collective-permute-done.7), channel_id=1, source_target_pairs={{0,28},{1,5},{4,0},{5,9},{8,4},{9,13},{12,8},{13,17},{16,12},{17,2... | collective-permute-start | bytes 3538952 | tf_op jit(solution)/shard_map/ppermute | solution.py:25
  149.2 41.6 %collective-permute-start.14 = (bf16[4608,128]{1,0:T(8,128)(2,1)}, bf16[4608,128]{1,0:T(8,128)(2,1)}, u32[]{:S(2)}, u32[]{:S(2)}) collective-permute-start(bf16[4608,128]{1,0:T(8,128)(2,1)} %bitcast.131), channel_id=1, source_target_pairs={{0,1},{1,0},{2,3},{3,2},{4,5},{5,4},{6,7},{7,6},{8,9},{9,8},{10,11... | collective-permute-start | bytes 3538952 | tf_op jit(solution)/shard_map/ppermute | solution.py:200
  161.9 22.8 %collective-permute-start.5 = (bf16[128,4608]{1,0:T(8,128)(2,1)}, bf16[128,4608]{1,0:T(8,128)(2,1)}, u32[]{:S(2)}, u32[]{:S(2)}) collective-permute-start(bf16[128,4608]{1,0:T(8,128)(2,1)} %collective-permute-done.4), channel_id=1, source_target_pairs={{0,1},{1,0},{2,3},{3,2},{4,5},{5,4},{6,7},{7,6},{8,9},{9,8},{10,11... | collective-permute-start | bytes 3538952 | tf_op jit(solution)/shard_map/ppermute | solution.py:198
  163.8 174.6 %all-to-all-start.1 = ((bf16[32,8,4608]{2,1,0:T(8,128)(2,1)}), bf16[32,8,4608]{2,1,0:T(8,128)(2,1)}, u32[]{:S(2)}, u32[]{:S(2)}) async-start(bf16[32,8,4608]{2,1,0:T(8,128)(2,1)} %bitcast_select_fusion), calls=%async_computation.1 | async-start | bytes 4718592 | tf_op jit(solution)/shard_map/all_to_all | solution.py:194
  177.3 16.0 %collective-permute-start.16 = (bf16[4608,128]{1,0:T(8,128)(2,1)}, bf16[4608,128]{1,0:T(8,128)(2,1)S(1)}, u32[]{:S(2)}, u32[]{:S(2)}) collective-permute-start(bf16[4608,128]{1,0:T(8,128)(2,1)} %collective-permute-done.7), channel_id=1, source_target_pairs={{0,1},{1,0},{2,3},{3,2},{4,5},{5,4},{6,7},{7,6},{8,9},{9,8},{10,11... | collective-permute-start | bytes 3538952 | tf_op jit(solution)/shard_map/ppermute | solution.py:200
  181.0 133.5 %copy-start.6 = (bf16[256,4608]{1,0:T(8,128)(2,1)}, bf16[256,4608]{1,0:T(8,128)(2,1)S(1)}, u32[]{:S(2)}) copy-start(bf16[256,4608]{1,0:T(8,128)(2,1)S(1)} %constant_dynamic-update-slice_fusion.2.refs_1_) | copy-start | bytes 7077892
  181.0 12.6 %collective-permute-start.9 = (bf16[128,4608]{1,0:T(8,128)(2,1)}, bf16[128,4608]{1,0:T(8,128)(2,1)S(1)}, u32[]{:S(2)}, u32[]{:S(2)}) collective-permute-start(bf16[128,4608]{1,0:T(8,128)(2,1)} %collective-permute-done.6), channel_id=1, source_target_pairs={{0,1},{1,0},{2,3},{3,2},{4,5},{5,4},{6,7},{7,6},{8,9},{9,8},{10,11... | collective-permute-start | bytes 3538952 | tf_op jit(solution)/shard_map/ppermute | solution.py:198
  184.7 14.3 %collective-permute-start.17 = (bf16[4608,128]{1,0:T(8,128)(2,1)}, bf16[4608,128]{1,0:T(8,128)(2,1)S(1)}, u32[]{:S(2)}, u32[]{:S(2)}) collective-permute-start(bf16[4608,128]{1,0:T(8,128)(2,1)} %collective-permute-done.8), channel_id=1, source_target_pairs={{0,1},{1,0},{2,3},{3,2},{4,5},{5,4},{6,7},{7,6},{8,9},{9,8},{10,11... | collective-permute-start | bytes 3538952 | tf_op jit(solution)/shard_map/ppermute | solution.py:200
  188.4 126.1 %copy-start.3 = (bf16[256,4608]{1,0:T(8,128)(2,1)}, bf16[256,4608]{1,0:T(8,128)(2,1)S(1)}, u32[]{:S(2)}) copy-start(bf16[256,4608]{1,0:T(8,128)(2,1)S(1)} %constant_dynamic-update-slice_fusion.4.refs_2_) | copy-start | bytes 7077892
  190.9 128.0 %copy-start.16 = (bf16[4608,256]{1,0:T(8,128)(2,1)}, bf16[4608,256]{1,0:T(8,128)(2,1)S(1)}, u32[]{:S(2)}) copy-start(bf16[4608,256]{1,0:T(8,128)(2,1)S(1)} %constant_dynamic-update-slice_fusion.10.refs_1_) | copy-start | bytes 7077892
  193.3 125.6 %copy-start.11 = (bf16[4608,256]{1,0:T(8,128)(2,1)}, bf16[4608,256]{1,0:T(8,128)(2,1)S(1)}, u32[]{:S(2)}) copy-start(bf16[4608,256]{1,0:T(8,128)(2,1)S(1)} %constant_dynamic-update-slice_fusion.8.refs_0_) | copy-start | bytes 7077892
  193.6 125.3 %copy-start.21 = (bf16[4608,256]{1,0:T(8,128)(2,1)}, bf16[4608,256]{1,0:T(8,128)(2,1)S(1)}, u32[]{:S(2)}) copy-start(bf16[4608,256]{1,0:T(8,128)(2,1)S(1)} %constant_dynamic-update-slice_fusion.12.refs_2_) | copy-start | bytes 7077892
  194.4 120.1 %copy-start.8 = (bf16[256,4608]{1,0:T(8,128)(2,1)}, bf16[256,4608]{1,0:T(8,128)(2,1)S(1)}, u32[]{:S(2)}) copy-start(bf16[256,4608]{1,0:T(8,128)(2,1)S(1)} %constant_dynamic-update-slice_fusion.6.refs_3_) | copy-start | bytes 7077892
  199.3 119.7 %copy-start.25 = (bf16[4608,256]{1,0:T(8,128)(2,1)}, bf16[4608,256]{1,0:T(8,128)(2,1)S(1)}, u32[]{:S(2)}) copy-start(bf16[4608,256]{1,0:T(8,128)(2,1)S(1)} %constant_dynamic-update-slice_fusion.14.refs_3_) | copy-start | bytes 7077892
  201.8 36.1 %collective-permute-start.18 = (bf16[16,4608]{1,0:T(8,128)(2,1)S(1)}, bf16[16,4608]{1,0:T(8,128)(2,1)S(1)}, u32[]{:S(2)}, u32[]{:S(2)}) collective-permute-start(bf16[16,4608]{1,0:T(8,128)(2,1)S(1)} %head_terms.15), channel_id=1, source_target_pairs={{32,0},{33,25},{40,8},{41,1},{48,16},{49,9},{56,24},{57,17},{64,32... | collective-permute-start | bytes 442376 | tf_op jit(solution)/shard_map/ppermute | solution.py:36
  207.6 30.3 %collective-permute-start.19 = (bf16[16,4608]{1,0:T(8,128)(2,1)S(1)}, bf16[16,4608]{1,0:T(8,128)(2,1)S(1)}, u32[]{:S(2)}, u32[]{:S(2)}) collective-permute-start(bf16[16,4608]{1,0:T(8,128)(2,1)S(1)} %head_terms.15), channel_id=1, source_target_pairs={{32,17},{33,8},{40,25},{41,16},{48,1},{49,24},{56,9},{57,0},{64,49... | collective-permute-start | bytes 442376 | tf_op jit(solution)/shard_map/ppermute | solution.py:36
  244.9 9.9 %collective-permute-start.20 = (bf16[16,4608]{1,0:T(8,128)(2,1)S(1)}, bf16[16,4608]{1,0:T(8,128)(2,1)S(1)}, u32[]{:S(2)}, u32[]{:S(2)}) collective-permute-start(bf16[16,4608]{1,0:T(8,128)(2,1)S(1)} %head_terms.16), channel_id=1, source_target_pairs={{32,0},{33,25},{40,8},{41,1},{48,16},{49,9},{56,24},{57,17},{64,32... | collective-permute-start | bytes 442376 | tf_op jit(solution)/shard_map/ppermute | solution.py:36
  250.3 13.5 %collective-permute-start.21 = (bf16[16,4608]{1,0:T(8,128)(2,1)S(1)}, bf16[16,4608]{1,0:T(8,128)(2,1)S(1)}, u32[]{:S(2)}, u32[]{:S(2)}) collective-permute-start(bf16[16,4608]{1,0:T(8,128)(2,1)S(1)} %head_terms.16), channel_id=1, source_target_pairs={{32,17},{33,8},{40,25},{41,16},{48,1},{49,24},{56,9},{57,0},{64,49... | collective-permute-start | bytes 442376 | tf_op jit(solution)/shard_map/ppermute | solution.py:36
  270.8 11.4 %collective-permute-start.22 = (bf16[16,4608]{1,0:T(8,128)(2,1)S(1)}, bf16[16,4608]{1,0:T(8,128)(2,1)S(1)}, u32[]{:S(2)}, u32[]{:S(2)}) collective-permute-start(bf16[16,4608]{1,0:T(8,128)(2,1)S(1)} %head_terms.17), channel_id=1, source_target_pairs={{32,0},{33,25},{40,8},{41,1},{48,16},{49,9},{56,24},{57,17},{64,32... | collective-permute-start | bytes 442376 | tf_op jit(solution)/shard_map/ppermute | solution.py:36
  275.4 13.9 %collective-permute-start.23 = (bf16[16,4608]{1,0:T(8,128)(2,1)S(1)}, bf16[16,4608]{1,0:T(8,128)(2,1)S(1)}, u32[]{:S(2)}, u32[]{:S(2)}) collective-permute-start(bf16[16,4608]{1,0:T(8,128)(2,1)S(1)} %head_terms.17), channel_id=1, source_target_pairs={{32,17},{33,8},{40,25},{41,16},{48,1},{49,24},{56,9},{57,0},{64,49... | collective-permute-start | bytes 442376 | tf_op jit(solution)/shard_map/ppermute | solution.py:36
  296.2 11.4 %collective-permute-start.24 = (bf16[16,4608]{1,0:T(8,128)(2,1)S(1)}, bf16[16,4608]{1,0:T(8,128)(2,1)S(1)}, u32[]{:S(2)}, u32[]{:S(2)}) collective-permute-start(bf16[16,4608]{1,0:T(8,128)(2,1)S(1)} %head_terms.18), channel_id=1, source_target_pairs={{32,0},{33,25},{40,8},{41,1},{48,16},{49,9},{56,24},{57,17},{64,32... | collective-permute-start | bytes 442376 | tf_op jit(solution)/shard_map/ppermute | solution.py:36
  298.2 16.3 %collective-permute-start.25 = (bf16[16,4608]{1,0:T(8,128)(2,1)S(1)}, bf16[16,4608]{1,0:T(8,128)(2,1)S(1)}, u32[]{:S(2)}, u32[]{:S(2)}) collective-permute-start(bf16[16,4608]{1,0:T(8,128)(2,1)S(1)} %head_terms.18), channel_id=1, source_target_pairs={{32,17},{33,8},{40,25},{41,16},{48,1},{49,24},{56,9},{57,0},{64,49... | collective-permute-start | bytes 442376 | tf_op jit(solution)/shard_map/ppermute | solution.py:36
  321.5 11.3 %collective-permute-start.26 = (bf16[16,4608]{1,0:T(8,128)(2,1)S(1)}, bf16[16,4608]{1,0:T(8,128)(2,1)S(1)}, u32[]{:S(2)}, u32[]{:S(2)}) collective-permute-start(bf16[16,4608]{1,0:T(8,128)(2,1)S(1)} %head_terms.19), channel_id=1, source_target_pairs={{32,0},{33,25},{40,8},{41,1},{48,16},{49,9},{56,24},{57,17},{64,32... | collective-permute-start | bytes 442376 | tf_op jit(solution)/shard_map/ppermute | solution.py:36
  323.4 15.0 %collective-permute-start.27 = (bf16[16,4608]{1,0:T(8,128)(2,1)S(1)}, bf16[16,4608]{1,0:T(8,128)(2,1)}, u32[]{:S(2)}, u32[]{:S(2)}) collective-permute-start(bf16[16,4608]{1,0:T(8,128)(2,1)S(1)} %head_terms.19), channel_id=1, source_target_pairs={{32,17},{33,8},{40,25},{41,16},{48,1},{49,24},{56,9},{57,0},{64,49... | collective-permute-start | bytes 442376 | tf_op jit(solution)/shard_map/ppermute | solution.py:36
  348.8 11.2 %collective-permute-start.28 = (bf16[16,4608]{1,0:T(8,128)(2,1)S(1)}, bf16[16,4608]{1,0:T(8,128)(2,1)S(1)}, u32[]{:S(2)}, u32[]{:S(2)}) collective-permute-start(bf16[16,4608]{1,0:T(8,128)(2,1)S(1)} %head_terms.20), channel_id=1, source_target_pairs={{32,0},{33,25},{40,8},{41,1},{48,16},{49,9},{56,24},{57,17},{64,32... | collective-permute-start | bytes 442376 | tf_op jit(solution)/shard_map/ppermute | solution.py:36
  350.8 15.3 %collective-permute-start.29 = (bf16[16,4608]{1,0:T(8,128)(2,1)S(1)}, bf16[16,4608]{1,0:T(8,128)(2,1)S(1)}, u32[]{:S(2)}, u32[]{:S(2)}) collective-permute-start(bf16[16,4608]{1,0:T(8,128)(2,1)S(1)} %head_terms.20), channel_id=1, source_target_pairs={{32,17},{33,8},{40,25},{41,16},{48,1},{49,24},{56,9},{57,0},{64,49... | collective-permute-start | bytes 442376 | tf_op jit(solution)/shard_map/ppermute | solution.py:36
  373.1 11.2 %collective-permute-start.30 = (bf16[16,4608]{1,0:T(8,128)(2,1)S(1)}, bf16[16,4608]{1,0:T(8,128)(2,1)S(1)}, u32[]{:S(2)}, u32[]{:S(2)}) collective-permute-start(bf16[16,4608]{1,0:T(8,128)(2,1)S(1)} %head_terms.21), channel_id=1, source_target_pairs={{32,0},{33,25},{40,8},{41,1},{48,16},{49,9},{56,24},{57,17},{64,32... | collective-permute-start | bytes 442376 | tf_op jit(solution)/shard_map/ppermute | solution.py:36
  375.0 14.9 %collective-permute-start.31 = (bf16[16,4608]{1,0:T(8,128)(2,1)S(1)}, bf16[16,4608]{1,0:T(8,128)(2,1)S(1)}, u32[]{:S(2)}, u32[]{:S(2)}) collective-permute-start(bf16[16,4608]{1,0:T(8,128)(2,1)S(1)} %head_terms.21), channel_id=1, source_target_pairs={{32,17},{33,8},{40,25},{41,16},{48,1},{49,24},{56,9},{57,0},{64,49... | collective-permute-start | bytes 442376 | tf_op jit(solution)/shard_map/ppermute | solution.py:36
  396.9 11.1 %collective-permute-start.32 = (bf16[16,4608]{1,0:T(8,128)(2,1)S(1)}, bf16[16,4608]{1,0:T(8,128)(2,1)S(1)}, u32[]{:S(2)}, u32[]{:S(2)}) collective-permute-start(bf16[16,4608]{1,0:T(8,128)(2,1)S(1)} %head_terms.22), channel_id=1, source_target_pairs={{32,0},{33,25},{40,8},{41,1},{48,16},{49,9},{56,24},{57,17},{64,32... | collective-permute-start | bytes 442376 | tf_op jit(solution)/shard_map/ppermute | solution.py:36
  398.8 15.2 %collective-permute-start.33 = (bf16[16,4608]{1,0:T(8,128)(2,1)S(1)}, bf16[16,4608]{1,0:T(8,128)(2,1)S(1)}, u32[]{:S(2)}, u32[]{:S(2)}) collective-permute-start(bf16[16,4608]{1,0:T(8,128)(2,1)S(1)} %head_terms.22), channel_id=1, source_target_pairs={{32,17},{33,8},{40,25},{41,16},{48,1},{49,24},{56,9},{57,0},{64,49... | collective-permute-start | bytes 442376 | tf_op jit(solution)/shard_map/ppermute | solution.py:36
  421.0 11.2 %collective-permute-start.34 = (bf16[16,4608]{1,0:T(8,128)(2,1)S(1)}, bf16[16,4608]{1,0:T(8,128)(2,1)S(1)}, u32[]{:S(2)}, u32[]{:S(2)}) collective-permute-start(bf16[16,4608]{1,0:T(8,128)(2,1)S(1)} %head_terms.23), channel_id=1, source_target_pairs={{32,0},{33,25},{40,8},{41,1},{48,16},{49,9},{56,24},{57,17},{64,32... | collective-permute-start | bytes 442376 | tf_op jit(solution)/shard_map/ppermute | solution.py:36
  422.9 15.5 %collective-permute-start.35 = (bf16[16,4608]{1,0:T(8,128)(2,1)S(1)}, bf16[16,4608]{1,0:T(8,128)(2,1)S(1)}, u32[]{:S(2)}, u32[]{:S(2)}) collective-permute-start(bf16[16,4608]{1,0:T(8,128)(2,1)S(1)} %head_terms.23), channel_id=1, source_target_pairs={{32,17},{33,8},{40,25},{41,16},{48,1},{49,24},{56,9},{57,0},{64,49... | collective-permute-start | bytes 442376 | tf_op jit(solution)/shard_map/ppermute | solution.py:36
  445.8 10.6 %collective-permute-start.36 = (bf16[16,4608]{1,0:T(8,128)(2,1)S(1)}, bf16[16,4608]{1,0:T(8,128)(2,1)S(1)}, u32[]{:S(2)}, u32[]{:S(2)}) collective-permute-start(bf16[16,4608]{1,0:T(8,128)(2,1)S(1)} %head_terms.24), channel_id=1, source_target_pairs={{32,0},{33,25},{40,8},{41,1},{48,16},{49,9},{56,24},{57,17},{64,32... | collective-permute-start | bytes 442376 | tf_op jit(solution)/shard_map/ppermute | solution.py:36
  447.7 15.0 %collective-permute-start.37 = (bf16[16,4608]{1,0:T(8,128)(2,1)S(1)}, bf16[16,4608]{1,0:T(8,128)(2,1)S(1)}, u32[]{:S(2)}, u32[]{:S(2)}) collective-permute-start(bf16[16,4608]{1,0:T(8,128)(2,1)S(1)} %head_terms.24), channel_id=1, source_target_pairs={{32,17},{33,8},{40,25},{41,16},{48,1},{49,24},{56,9},{57,0},{64,49... | collective-permute-start | bytes 442376 | tf_op jit(solution)/shard_map/ppermute | solution.py:36
  469.7 10.7 %collective-permute-start.38 = (bf16[16,4608]{1,0:T(8,128)(2,1)S(1)}, bf16[16,4608]{1,0:T(8,128)(2,1)S(1)}, u32[]{:S(2)}, u32[]{:S(2)}) collective-permute-start(bf16[16,4608]{1,0:T(8,128)(2,1)S(1)} %head_terms.25), channel_id=1, source_target_pairs={{32,0},{33,25},{40,8},{41,1},{48,16},{49,9},{56,24},{57,17},{64,32... | collective-permute-start | bytes 442376 | tf_op jit(solution)/shard_map/ppermute | solution.py:36
  471.6 15.0 %collective-permute-start.39 = (bf16[16,4608]{1,0:T(8,128)(2,1)S(1)}, bf16[16,4608]{1,0:T(8,128)(2,1)S(1)}, u32[]{:S(2)}, u32[]{:S(2)}) collective-permute-start(bf16[16,4608]{1,0:T(8,128)(2,1)S(1)} %head_terms.25), channel_id=1, source_target_pairs={{32,17},{33,8},{40,25},{41,16},{48,1},{49,24},{56,9},{57,0},{64,49... | collective-permute-start | bytes 442376 | tf_op jit(solution)/shard_map/ppermute | solution.py:36
  493.7 10.7 %collective-permute-start.40 = (bf16[16,4608]{1,0:T(8,128)(2,1)S(1)}, bf16[16,4608]{1,0:T(8,128)(2,1)S(1)}, u32[]{:S(2)}, u32[]{:S(2)}) collective-permute-start(bf16[16,4608]{1,0:T(8,128)(2,1)S(1)} %head_terms.26), channel_id=1, source_target_pairs={{32,0},{33,25},{40,8},{41,1},{48,16},{49,9},{56,24},{57,17},{64,32... | collective-permute-start | bytes 442376 | tf_op jit(solution)/shard_map/ppermute | solution.py:36
  495.6 15.2 %collective-permute-start.41 = (bf16[16,4608]{1,0:T(8,128)(2,1)S(1)}, bf16[16,4608]{1,0:T(8,128)(2,1)S(1)}, u32[]{:S(2)}, u32[]{:S(2)}) collective-permute-start(bf16[16,4608]{1,0:T(8,128)(2,1)S(1)} %head_terms.26), channel_id=1, source_target_pairs={{32,17},{33,8},{40,25},{41,16},{48,1},{49,24},{56,9},{57,0},{64,49... | collective-permute-start | bytes 442376 | tf_op jit(solution)/shard_map/ppermute | solution.py:36
  518.5 10.8 %collective-permute-start.42 = (bf16[16,4608]{1,0:T(8,128)(2,1)}, bf16[16,4608]{1,0:T(8,128)(2,1)}, u32[]{:S(2)}, u32[]{:S(2)}) collective-permute-start(bf16[16,4608]{1,0:T(8,128)(2,1)} %head_terms.27), channel_id=1, source_target_pairs={{32,0},{33,25},{40,8},{41,1},{48,16},{49,9},{56,24},{57,17},{64,32... | collective-permute-start | bytes 442376 | tf_op jit(solution)/shard_map/ppermute | solution.py:36
  520.4 15.2 %collective-permute-start.43 = (bf16[16,4608]{1,0:T(8,128)(2,1)}, bf16[16,4608]{1,0:T(8,128)(2,1)}, u32[]{:S(2)}, u32[]{:S(2)}) collective-permute-start(bf16[16,4608]{1,0:T(8,128)(2,1)} %head_terms.27), channel_id=1, source_target_pairs={{32,17},{33,8},{40,25},{41,16},{48,1},{49,24},{56,9},{57,0},{64,49... | collective-permute-start | bytes 442376 | tf_op jit(solution)/shard_map/ppermute | solution.py:36
  546.6 11.0 %collective-permute-start.44 = (bf16[16,4608]{1,0:T(8,128)(2,1)}, bf16[16,4608]{1,0:T(8,128)(2,1)}, u32[]{:S(2)}, u32[]{:S(2)}) collective-permute-start(bf16[16,4608]{1,0:T(8,128)(2,1)} %head_terms.28), channel_id=1, source_target_pairs={{32,0},{33,25},{40,8},{41,1},{48,16},{49,9},{56,24},{57,17},{64,32... | collective-permute-start | bytes 442376 | tf_op jit(solution)/shard_map/ppermute | solution.py:36
  548.5 15.6 %collective-permute-start.45 = (bf16[16,4608]{1,0:T(8,128)(2,1)}, bf16[16,4608]{1,0:T(8,128)(2,1)}, u32[]{:S(2)}, u32[]{:S(2)}) collective-permute-start(bf16[16,4608]{1,0:T(8,128)(2,1)} %head_terms.28), channel_id=1, source_target_pairs={{32,17},{33,8},{40,25},{41,16},{48,1},{49,24},{56,9},{57,0},{64,49... | collective-permute-start | bytes 442376 | tf_op jit(solution)/shard_map/ppermute | solution.py:36
  574.5 10.7 %collective-permute-start.46 = (bf16[16,4608]{1,0:T(8,128)(2,1)S(1)}, bf16[16,4608]{1,0:T(8,128)(2,1)S(1)}, u32[]{:S(2)}, u32[]{:S(2)}) collective-permute-start(bf16[16,4608]{1,0:T(8,128)(2,1)S(1)} %head_terms.29), channel_id=1, source_target_pairs={{32,0},{33,25},{40,8},{41,1},{48,16},{49,9},{56,24},{57,17},{64,32... | collective-permute-start | bytes 442376 | tf_op jit(solution)/shard_map/ppermute | solution.py:36
  576.4 13.8 %collective-permute-start.47 = (bf16[16,4608]{1,0:T(8,128)(2,1)S(1)}, bf16[16,4608]{1,0:T(8,128)(2,1)S(1)}, u32[]{:S(2)}, u32[]{:S(2)}) collective-permute-start(bf16[16,4608]{1,0:T(8,128)(2,1)S(1)} %head_terms.29), channel_id=1, source_target_pairs={{32,17},{33,8},{40,25},{41,16},{48,1},{49,24},{56,9},{57,0},{64,49... | collective-permute-start | bytes 442376 | tf_op jit(solution)/shard_map/ppermute | solution.py:36
  592.0 7.8 %collective-permute-start.48 = (bf16[16,4,2304]{2,0,1:T(8,128)(2,1)S(1)}, bf16[16,4,2304]{2,0,1:T(8,128)(2,1)S(1)}, u32[]{:S(2)}, u32[]{:S(2)}) collective-permute-start(bf16[16,4,2304]{2,0,1:T(8,128)(2,1)S(1)} %dynamic-slice_bitcast_fusion), channel_id=1, source_target_pairs={{0,1},{1,0},{2,3},{3,2},{4,5},{5,4},{6,7},{7,6},{8,9},{9,8},{10,11... | collective-permute-start | bytes 884744 | tf_op jit(solution)/shard_map/ppermute | solution.py:234
  601.8 30.8 %all-to-all-start.2 = ((bf16[16,4,2304]{2,1,0:T(4,128)(2,1)}), bf16[16,4,2304]{2,1,0:T(4,128)(2,1)}, u32[]{:S(2)}, u32[]{:S(2)}) async-start(bf16[16,4,2304]{2,1,0:T(4,128)(2,1)} %copy.102), calls=%async_computation.2 | async-start | bytes 589824 | tf_op jit(solution)/shard_map/all_to_all | solution.py:236
  616.5 22.1 %copy-start.1 = (bf16[1,128,4608]{2,1,0:T(8,128)(2,1)S(1)}, bf16[1,128,4608]{2,1,0:T(8,128)(2,1)}, u32[]{:S(2)}) copy-start(bf16[1,128,4608]{2,1,0:T(8,128)(2,1)} %param.10) | copy-start | bytes 3538948
  616.7 21.2 %copy-start.34 = (f32[1,128]{1,0:T(1,128)S(1)}, f32[1,128]{1,0:T(1,128)}, u32[]{:S(2)}) copy-start(f32[1,128]{1,0:T(1,128)} %param.17) | copy-start | bytes 1540
  (26 other events, 223.3 us)

commit v4 on v3

--- a/solution.py
+++ b/solution.py
@@ -42,10 +42,10 @@
     part_ref[...] = part
     rounded = part.astype(BF)
     rounded_ref[...] = rounded
-    wide = outs[0].shape[0]
+    wide = outs[0].shape[1]
     for k, ref in enumerate(outs):
-        grads_ref[:, k * wide : (k + 1) * wide] = lax.dot_general(
-            rounded, ref[...], (((1,), (1,)), ((), ())), preferred_element_type=F32
+        grads_ref[:, k * wide : (k + 1) * wide] = jnp.dot(
+            rounded, ref[...], preferred_element_type=F32
         )
 
 
@@ -53,12 +53,10 @@
     *values, share_ref = refs
     core = core_ref[0]
     mine, other = grads_ref[core], grads_ref[1 - core]
-    wide = values[0].shape[1]
-    head = wide // 2
+    head = values[0].shape[0] // 2
     swapped = []
     for k in range(len(values)):
-        swapped.append(other[:, k * wide + head : (k + 1) * wide])
-        swapped.append(other[:, k * wide : k * wide + head])
+        swapped.append(other[:, (k ^ 1) * head : ((k ^ 1) + 1) * head])
     grads = mine + jnp.concatenate(swapped, axis=1)
     mixed = mix_ref[0] * grads[0:1, :]
     for p in range(1, grads.shape[0]):
@@ -66,16 +64,21 @@
     mixed = mixed.astype(BF)
     term = None
     for k, ref in enumerate(values):
-        product = lax.dot_general(
-            mixed[:, k * wide : (k + 1) * wide],
-            ref[...],
-            (((1,), (1,)), ((), ())),
+        product = jnp.dot(
+            mixed[:, k * head : (k + 1) * head],
+            ref[head : 2 * head, :],
             preferred_element_type=F32,
         )
         term = product if term is None else term + product
     share_ref[...] = (part_ref[...] * 0.5 + term * scales_ref[...]).astype(BF)
 
 
+def turn_kernel(mine_ref, other_ref, turned_ref):
+    head = mine_ref.shape[0] // 2
+    turned_ref[:, :head] = mine_ref[:head, :].T
+    turned_ref[:, head:] = other_ref[:head, :].T
+
+
 def keep(array):
     return pltpu.with_memory_space_constraint(array, pltpu.VMEM)
 
@@ -84,9 +87,22 @@
     return pl.BlockSpec(memory_space=pltpu.VMEM)
 
 
+def prepare(mine):
+    other = lax.ppermute(mine, "core", SWAP)
+    turned = pl.pallas_call(
+        turn_kernel,
+        out_shape=jax.ShapeDtypeStruct((mine.shape[1], mine.shape[0]), BF),
+        in_specs=[whole()] * 2,
+        out_specs=whole(),
+        compiler_params=pltpu.CompilerParams(vmem_limit_bytes=24 << 20),
+        name="turn_heads",
+    )(keep(mine), keep(other))
+    return turned, mine, other
+
+
 def head_grads(arrived, outs):
     seq_len, model_width = arrived[0].shape
-    heads_wide = sum(w.shape[0] for w in outs)
+    heads_wide = sum(w.shape[1] for w in outs)
     return pl.pallas_call(
         grads_kernel,
         out_shape=(
@@ -162,10 +178,10 @@
     entries_dev = act_values.shape[1]
     targets = target_ids.shape[0]
 
-    own = (out_proj[0], value_proj[0])
+    own = jnp.concatenate([out_proj[0], value_proj[0].T], axis=0)
     own_mix = attention[0, 0]
-    beyond = tuple(lax.ppermute(a, "zh", SWAP) for a in own)
-    near = tuple(neighbour_heads(a) for a in own)
+    beyond = lax.ppermute(own, "zh", SWAP)
+    near = neighbour_heads(own)
 
     feat_iota = jnp.arange(feat_rows, dtype=jnp.int32)
     target_pick = (
@@ -175,30 +191,24 @@
     enc_send = jnp.broadcast_to(
         enc_rows[None, :, None, :], (QUADS, targets, 2, model_width)
     ).reshape(feat_count, model_width)
-    near, own, own_mix, enc_send = lax.optimization_barrier((near, own, own_mix, enc_send))
     beyond_mix = lax.ppermute(own_mix, "zh", SWAP)
     near_mix = neighbour_heads(own_mix)
+    enc_got = lax.all_to_all(enc_send, FEAT, split_axis=0, concat_axis=0, tiled=True)
+    outgoing, flat_index = panel_route(
+        decoders[0], act_ids[0], entries_dev, feat_index, feat_count
+    )
+    own, beyond, near, beyond_mix, near_mix, enc_got, outgoing = lax.optimization_barrier(
+        (own, beyond, near, beyond_mix, near_mix, enc_got, outgoing)
+    )
+    far = neighbour_heads(beyond)
     far_mix = neighbour_heads(beyond_mix)
-    enc_got = lax.all_to_all(enc_send, FEAT, split_axis=0, concat_axis=0, tiled=True)
     enc_row = jnp.sum(enc_got.astype(F32), axis=0)
     own_target = lax.axis_index(("par", "zh"))
     own_pos = lax.dynamic_index_in_dim(target_pos, own_target, 0, keepdims=False)
     positions = jnp.arange(seq_len, dtype=jnp.int32)
     start = jnp.where((positions == own_pos)[:, None], enc_row[None, :], 0.0)
 
-    outgoing, flat_index = panel_route(
-        decoders[0], act_ids[0], entries_dev, feat_index, feat_count
-    )
-    far = tuple(neighbour_heads(a) for a in beyond)
-    far, outgoing = lax.optimization_barrier((far, outgoing))
-    incoming = lax.all_to_all(outgoing, FEAT, split_axis=0, concat_axis=0, tiled=True)
-
-    outs, values = [], []
-    for out_head, value_head in (own, near, beyond, far):
-        outs.append(jnp.concatenate([out_head, lax.ppermute(out_head, "core", SWAP)], axis=0))
-        values.append(
-            jnp.concatenate([value_head, lax.ppermute(value_head, "core", SWAP)], axis=1)
-        )
+    groups = [prepare(head) for head in (own, near, beyond)]
     core_mix = jnp.stack([own_mix, near_mix, beyond_mix, far_mix])
     mixing = jnp.stack([core_mix, lax.ppermute(core_mix, "core", SWAP)], axis=1)
     mixing = mixing.reshape(-1, seq_len, seq_len)
@@ -206,24 +216,31 @@
     mix_wide = jnp.broadcast_to(
         mixing.transpose(1, 2, 0)[..., None], (seq_len, seq_len, heads, head_width)
     ).reshape(seq_len, seq_len, heads * head_width)
+    quarter = (start * 0.25).astype(BF)
+    far, groups, mix_wide, quarter, outgoing = lax.optimization_barrier(
+        (far, groups, mix_wide, quarter, outgoing)
+    )
+    incoming = lax.all_to_all(outgoing, FEAT, split_axis=0, concat_axis=0, tiled=True)
+    panel = jnp.take(incoming.reshape(-1, model_width), flat_index, axis=0)
+    groups.append(prepare(far))
+    outs = [group[0] for group in groups]
+    values = [head for group in groups for head in group[1:]]
     scales = norm_scale[0][:, None]
 
     outs, values = [keep(w) for w in outs], [keep(w) for w in values]
     mix_wide = keep(mix_wide)
     core = lax.axis_index("core").reshape(1)
-    quarter = (start * 0.25).astype(BF)
     arrived = (quarter, quarter)
     history = []
     for step in range(sections - 1):
         if step == PANEL_BY:
-            arrived, incoming = lax.optimization_barrier((arrived, incoming))
+            arrived, panel = lax.optimization_barrier((arrived, panel))
         part, rounded, grad_part = head_grads(arrived, outs)
         history.append(rounded)
         grads = lax.all_gather(grad_part, "core", axis=0)
         share = head_terms(core, grads, mix_wide, part, scales, values)
-        arrived = tuple(send_down(share, turn, sections) for turn in range(2))
+        arrived = tuple(send_down(share, turn, sections) for turn in (1, 0))
     history.append((arrived[0].astype(F32) + arrived[1].astype(F32)).astype(BF))
-    panel = jnp.take(incoming.reshape(-1, model_width), flat_index, axis=0)
 
     steps_each = sections // QUADS
     held = jnp.stack(history)

time: 649 us -> 713 us (1.099)
  waiting for transfers between devices: 245 us -> 330 us
  Pallas kernels: 42.2 us -> 120 us
  starting transfers between devices: 212 us -> 136 us
  local copies, waits for them, and re-layouts: 90.6 us -> 55.4 us
    all_to_all x1, waiting for transfers between devices: 0.01 us -> 79.3 us  [per_device(): lax.all_to_all(enc_send, FEAT, split_axis=0, concat_axis=0, tiled=True)]
    ppermute x10 -> x5, starting transfers between devices: 81.8 us -> 11 us  [the longest x4 9.05 us: prepare(): other = lax.ppermute(mine, 'core', SWAP)]
    pallas_call x15, Pallas kernels: 39.7 us -> 107 us  [head_terms(): pl.pallas_call(terms_kernel, out_shape=jax.ShapeDtypeStruct(part.shape, B...]
    pallas_call x14, local copies, waits for them, and re-layouts: 45.4 us -> 21.9 us  [head_grads(): pl.pallas_call(grads_kernel, out_shape=(jax.ShapeDtypeStruct((seq_len, mo...]
    pallas_call x0 -> x4, Pallas kernels: none -> 11.4 us  [prepare(): pl.pallas_call(turn_kernel, out_shape=jax.ShapeDtypeStruct((mine.shape[1]...]
    concatenate x8 -> x0, local copies, waits for them, and re-layouts: 9.8 us -> none  [the longest x4 5.38 us: per_device(): jnp.concatenate([value_head, lax.ppermute(value_head, 'core', SWAP)], axi...]
    unnamed x85 -> x47, local copies, waits for them, and re-layouts: 19.4 us -> 11.5 us
    ppermute x6 -> x4, starting transfers between devices: 16.8 us -> 12.6 us  [neighbour_heads(): return lax.ppermute(shard, ('y2', 'par', 'core'), pairs)]
  transfers between devices with their start and end apart: 52 -> 45, of which waited for: 33 -> 34; matrix products, arithmetic and copies ran while one was open for 10% -> 7% of each run, Pallas kernels for 2% -> 7%
where the time goes in v4:
time: 713 us; the launch traced here: 700 us
  waiting for transfers between devices  330 us (46%)
  starting transfers between devices  136 us (19%)
  Pallas kernels  120 us (17%)
  local copies, waits for them, and re-layouts  55.4 us (8%)
  blocking collectives  34.2 us (5%)
  other arithmetic  20 us (3%)
    ppermute x30, waiting for transfers between devices, send_down(): return lax.ppermute(shard, ('section', 'y2', 'core'), pairs)  205 us
    pallas_call x15, Pallas kernels, head_terms(): pl.pallas_call(terms_kernel, out_shape=jax.ShapeDtypeStruct(part.shape, B...  107 us
    all_to_all x1, waiting for transfers between devices, per_device(): lax.all_to_all(enc_send, FEAT, split_axis=0, concat_axis=0, tiled=True)  79.3 us
    ppermute x30, starting transfers between devices, send_down(): return lax.ppermute(shard, ('section', 'y2', 'core'), pairs)  69.6 us
    all_gather x15, blocking collectives, per_device(): grads = lax.all_gather(grad_part, 'core', axis=0)  30.8 us
    ppermute x4, waiting for transfers between devices, neighbour_heads(): return lax.ppermute(shard, ('y2', 'par', 'core'), pairs)  23.6 us
    pallas_call x14, local copies, waits for them, and re-layouts, head_grads(): pl.pallas_call(grads_kernel, out_shape=(jax.ShapeDtypeStruct((seq_len, mo...  21.9 us
    all_to_all x1, waiting for transfers between devices, per_device(): got = lax.all_to_all(held, CHIPS, split_axis=0, concat_axis=0, tiled=True)  15.9 us
  transfers between devices with their start and end apart: 45, of which 34 were waited for; matrix products, arithmetic and copies ran while one was open for 7% of the time, Pallas kernels for 7%

profile of v4, /device:TPU:7, one launch (start us, length us, event | category | flops | bytes accessed | tf_op | source)
XLA Modules:
  0.0 699.7 jit_solution(13628070988693179325)
XLA Ops:
  0.0 3.3 collective-permute-start.3
  3.3 10.6 %collective-permute-start.2 = (f32[16,16]{1,0:T(8,128)}, f32[16,16]{1,0:T(8,128)}, u32[]{:S(2)}, u32[]{:S(2)}) collective-permute-start(f32[16,16]{1,0:T(8,128)} %bitcast.143), channel_id=1, source_target_pairs={{0,2},{2,0},{1,3},{3,1},{4,6},{6,4},{5,7},{7,5},{8,10},{10,8},{9,1... | collective-permute-start | bytes 3080 | tf_op jit(solution)/shard_map/ppermute | solution.py:194
  18.2 3.2 collective-permute-start.1
  29.9 4.1 reduce
  35.8 12.2 %all-to-all-start = ((bf16[32,2,2304]{2,1,0:T(2,128)(2,1)}), bf16[32,2,2304]{2,1,0:T(2,128)(2,1)}, u32[]{:S(2)}, u32[]{:S(2)}) async-start(bf16[32,2,2304]{2,1,0:T(2,128)(2,1)} %reshape.199), calls=%async_computation | async-start | bytes 589824 | tf_op jit(solution)/shard_map/all_to_all | solution.py:196
  51.2 3.5 gather_fusion
  54.7 3.3 bitcast_select_fusion
  58.1 79.3 %all-to-all-done = bf16[32,2,2304]{2,1,0:T(2,128)(2,1)} async-done(((bf16[32,2,2304]{2,1,0:T(2,128)(2,1)}), bf16[32,2,2304]{2,1,0:T(2,128)(2,1)}, u32[]{:S(2)}, u32[]{:S(2)}) %all-to-all-start) | async-done | bytes 294944 | tf_op jit(solution)/shard_map/all_to_all | solution.py:196
  149.7 4.2 collective-permute-start.8
  154.0 23.6 %collective-permute-done.8 = f32[16,16]{1,0:T(8,128)S(1)} collective-permute-done((f32[16,16]{1,0:T(8,128)}, f32[16,16]{1,0:T(8,128)S(1)}, u32[]{:S(2)}, u32[]{:S(2)}) %collective-permute-start.8) | collective-permute-done | bytes 1056 | tf_op jit(solution)/shard_map/ppermute | solution.py:25
  193.5 3.0 turn_heads.6.refs_2_
  197.9 6.2 all-to-all-start.1
  206.6 4.3 collective-permute-done.10.other_ref.refs_7_
  217.2 7.2 %head_terms.15 = bf16[16,4608]{1,0:T(8,128)(2,1)S(1)} custom-call(s32[1]{0:T(128)} %bitcast.20.core_ref, f32[2,16,1024]{2,1,0:T(8,128)S(1)} %bitcast.118, f32[16,16,1024]{2,1,0:T(8,128)S(1)} %copy-done.13, f32[16,4608]{1,0:T(8,128)S(1)} %get-tuple-element.88.part_ref, f32[16,1]{1,0:T(8,128)S(1)} %copy.92.scales_ref, ...), custom_call_target="tpu_custom_call" | custom-call | tf_op jit(solution)/shard_map/head_terms/pallas_call | solution.py:121
  224.4 5.7 collective-permute-start.12
  232.7 35.4 %collective-permute-done.12 = bf16[16,4608]{1,0:T(8,128)(2,1)S(1)} collective-permute-done((bf16[16,4608]{1,0:T(8,128)(2,1)S(1)}, bf16[16,4608]{1,0:T(8,128)(2,1)S(1)}, u32[]{:S(2)}, u32[]{:S(2)}) %collective-permute-start.12) | collective-permute-done | bytes 147488 | tf_op jit(solution)/shard_map/ppermute | solution.py:36
  271.3 7.2 %head_terms.16 = bf16[16,4608]{1,0:T(8,128)(2,1)S(1)} custom-call(s32[1]{0:T(128)} %bitcast.20.core_ref, f32[2,16,1024]{2,1,0:T(8,128)S(1)} %bitcast.119, f32[16,16,1024]{2,1,0:T(8,128)S(1)} %copy-done.13, f32[16,4608]{1,0:T(8,128)S(1)} %get-tuple-element.164.part_ref, f32[16,1]{1,0:T(8,128)S(1)} %copy.92.scales_ref, ...), custom_call_target="tpu_custom_call" | custom-call | tf_op jit(solution)/shard_map/head_terms/pallas_call | solution.py:121
  278.4 4.6 collective-permute-start.14
  288.7 7.7 %collective-permute-done.13 = bf16[16,4608]{1,0:T(8,128)(2,1)S(1)} collective-permute-done((bf16[16,4608]{1,0:T(8,128)(2,1)S(1)}, bf16[16,4608]{1,0:T(8,128)(2,1)S(1)}, u32[]{:S(2)}, u32[]{:S(2)}) %collective-permute-start.13) | collective-permute-done | bytes 147488 | tf_op jit(solution)/shard_map/ppermute | solution.py:36
  299.6 7.2 %head_terms.17 = bf16[16,4608]{1,0:T(8,128)(2,1)S(1)} custom-call(s32[1]{0:T(128)} %bitcast.20.core_ref, f32[2,16,1024]{2,1,0:T(8,128)S(1)} %bitcast.120, f32[16,16,1024]{2,1,0:T(8,128)S(1)} %copy-done.13, f32[16,4608]{1,0:T(8,128)S(1)} %get-tuple-element.170.part_ref, f32[16,1]{1,0:T(8,128)S(1)} %copy.92.scales_ref, ...), custom_call_target="tpu_custom_call" | custom-call | tf_op jit(solution)/shard_map/head_terms/pallas_call | solution.py:121
  306.8 5.4 collective-permute-start.16
  316.7 11.1 %collective-permute-done.15 = bf16[16,4608]{1,0:T(8,128)(2,1)S(1)} collective-permute-done((bf16[16,4608]{1,0:T(8,128)(2,1)S(1)}, bf16[16,4608]{1,0:T(8,128)(2,1)S(1)}, u32[]{:S(2)}, u32[]{:S(2)}) %collective-permute-start.15) | collective-permute-done | bytes 147488 | tf_op jit(solution)/shard_map/ppermute | solution.py:36
  331.0 7.2 %head_terms.18 = bf16[16,4608]{1,0:T(8,128)(2,1)S(1)} custom-call(s32[1]{0:T(128)} %bitcast.20.core_ref, f32[2,16,1024]{2,1,0:T(8,128)S(1)} %bitcast.121, f32[16,16,1024]{2,1,0:T(8,128)S(1)} %copy-done.13, f32[16,4608]{1,0:T(8,128)S(1)} %get-tuple-element.158.part_ref, f32[16,1]{1,0:T(8,128)S(1)} %copy.92.scales_ref, ...), custom_call_target="tpu_custom_call" | custom-call | tf_op jit(solution)/shard_map/head_terms/pallas_call | solution.py:121
  342.8 5.3 collective-permute-done.18
  348.1 6.9 collective-permute-done.17
  358.3 7.2 %head_terms.19 = bf16[16,4608]{1,0:T(8,128)(2,1)S(1)} custom-call(s32[1]{0:T(128)} %bitcast.20.core_ref, f32[2,16,1024]{2,1,0:T(8,128)S(1)} %bitcast.122, f32[16,16,1024]{2,1,0:T(8,128)S(1)} %copy-done.13, f32[16,4608]{1,0:T(8,128)S(1)} %get-tuple-element.188.part_ref, f32[16,1]{1,0:T(8,128)S(1)} %copy.92.scales_ref, ...), custom_call_target="tpu_custom_call" | custom-call | tf_op jit(solution)/shard_map/head_terms/pallas_call | solution.py:121
  369.5 5.5 gather_fusion.1
  377.6 3.8 collective-permute-done.19
  381.5 4.5 head_grads.25
  388.7 7.3 %head_terms.20 = bf16[16,4608]{1,0:T(8,128)(2,1)S(1)} custom-call(s32[1]{0:T(128)} %bitcast.20.core_ref, f32[2,16,1024]{2,1,0:T(8,128)S(1)} %bitcast.123, f32[16,16,1024]{2,1,0:T(8,128)S(1)} %copy-done.14, f32[16,4608]{1,0:T(8,128)S(1)} %get-tuple-element.176.part_ref, f32[16,1]{1,0:T(8,128)S(1)} %copy.92.scales_ref, ...), custom_call_target="tpu_custom_call" | custom-call | tf_op jit(solution)/shard_map/head_terms/pallas_call | solution.py:121
  399.9 6.4 collective-permute-done.22
  406.3 6.2 collective-permute-done.21
  415.8 7.2 %head_terms.21 = bf16[16,4608]{1,0:T(8,128)(2,1)S(1)} custom-call(s32[1]{0:T(128)} %bitcast.20.core_ref, f32[2,16,1024]{2,1,0:T(8,128)S(1)} %bitcast.124, f32[16,16,1024]{2,1,0:T(8,128)S(1)} %copy-done.14, f32[16,4608]{1,0:T(8,128)S(1)} %get-tuple-element.152.part_ref, f32[16,1]{1,0:T(8,128)S(1)} %copy.92.scales_ref, ...), custom_call_target="tpu_custom_call" | custom-call | tf_op jit(solution)/shard_map/head_terms/pallas_call | solution.py:121
  426.8 6.0 collective-permute-done.24
  432.8 6.8 collective-permute-done.23
  442.9 7.2 %head_terms.22 = bf16[16,4608]{1,0:T(8,128)(2,1)S(1)} custom-call(s32[1]{0:T(128)} %bitcast.20.core_ref, f32[2,16,1024]{2,1,0:T(8,128)S(1)} %bitcast.125, f32[16,16,1024]{2,1,0:T(8,128)S(1)} %copy-done.14, f32[16,4608]{1,0:T(8,128)S(1)} %get-tuple-element.182.part_ref, f32[16,1]{1,0:T(8,128)S(1)} %copy.92.scales_ref, ...), custom_call_target="tpu_custom_call" | custom-call | tf_op jit(solution)/shard_map/head_terms/pallas_call | solution.py:121
  453.9 7.6 %collective-permute-done.26 = bf16[16,4608]{1,0:T(8,128)(2,1)S(1)} collective-permute-done((bf16[16,4608]{1,0:T(8,128)(2,1)S(1)}, bf16[16,4608]{1,0:T(8,128)(2,1)S(1)}, u32[]{:S(2)}, u32[]{:S(2)}) %collective-permute-start.26) | collective-permute-done | bytes 147488 | tf_op jit(solution)/shard_map/ppermute | solution.py:36
  461.5 4.9 collective-permute-done.25
  469.6 7.2 %head_terms.23 = bf16[16,4608]{1,0:T(8,128)(2,1)S(1)} custom-call(s32[1]{0:T(128)} %bitcast.20.core_ref, f32[2,16,1024]{2,1,0:T(8,128)S(1)} %bitcast.126, f32[16,16,1024]{2,1,0:T(8,128)S(1)} %copy-done.14, f32[16,4608]{1,0:T(8,128)S(1)} %get-tuple-element.224.part_ref, f32[16,1]{1,0:T(8,128)S(1)} %copy.92.scales_ref, ...), custom_call_target="tpu_custom_call" | custom-call | tf_op jit(solution)/shard_map/head_terms/pallas_call | solution.py:121
  476.8 3.1 collective-permute-start.28
  482.3 6.0 collective-permute-done.28
  488.3 6.8 collective-permute-done.27
  496.4 3.4 all-gather.9
  499.8 7.2 %head_terms.24 = bf16[16,4608]{1,0:T(8,128)(2,1)S(1)} custom-call(s32[1]{0:T(128)} %bitcast.20.core_ref, f32[2,16,1024]{2,1,0:T(8,128)S(1)} %bitcast.127, f32[16,16,1024]{2,1,0:T(8,128)S(1)} %copy-done.14, f32[16,4608]{1,0:T(8,128)S(1)} %get-tuple-element.194.part_ref, f32[16,1]{1,0:T(8,128)S(1)} %copy.92.scales_ref, ...), custom_call_target="tpu_custom_call" | custom-call | tf_op jit(solution)/shard_map/head_terms/pallas_call | solution.py:121
  510.8 6.8 collective-permute-done.30
  517.5 6.1 collective-permute-done.29
  526.9 7.2 %head_terms.25 = bf16[16,4608]{1,0:T(8,128)(2,1)S(1)} custom-call(s32[1]{0:T(128)} %bitcast.20.core_ref, f32[2,16,1024]{2,1,0:T(8,128)S(1)} %bitcast.128, f32[16,16,1024]{2,1,0:T(8,128)S(1)} %copy-done.14, f32[16,4608]{1,0:T(8,128)S(1)} %get-tuple-element.218.part_ref, f32[16,1]{1,0:T(8,128)S(1)} %copy.92.scales_ref, ...), custom_call_target="tpu_custom_call" | custom-call | tf_op jit(solution)/shard_map/head_terms/pallas_call | solution.py:121
  537.9 6.1 collective-permute-done.32
  544.0 6.8 collective-permute-done.31
  554.0 7.2 %head_terms.26 = bf16[16,4608]{1,0:T(8,128)(2,1)S(1)} custom-call(s32[1]{0:T(128)} %bitcast.20.core_ref, f32[2,16,1024]{2,1,0:T(8,128)S(1)} %bitcast.129, f32[16,16,1024]{2,1,0:T(8,128)S(1)} %copy-done.14, f32[16,4608]{1,0:T(8,128)S(1)} %get-tuple-element.200.part_ref, f32[16,1]{1,0:T(8,128)S(1)} %copy.92.scales_ref, ...), custom_call_target="tpu_custom_call" | custom-call | tf_op jit(solution)/shard_map/head_terms/pallas_call | solution.py:121
  565.1 7.0 %collective-permute-done.34 = bf16[16,4608]{1,0:T(8,128)(2,1)S(1)} collective-permute-done((bf16[16,4608]{1,0:T(8,128)(2,1)S(1)}, bf16[16,4608]{1,0:T(8,128)(2,1)S(1)}, u32[]{:S(2)}, u32[]{:S(2)}) %collective-permute-start.34) | collective-permute-done | bytes 147488 | tf_op jit(solution)/shard_map/ppermute | solution.py:36
  572.1 6.2 collective-permute-done.33
  581.5 7.2 %head_terms.27 = bf16[16,4608]{1,0:T(8,128)(2,1)S(1)} custom-call(s32[1]{0:T(128)} %bitcast.20.core_ref, f32[2,16,1024]{2,1,0:T(8,128)S(1)} %bitcast.130, f32[16,16,1024]{2,1,0:T(8,128)S(1)} %copy-done.14, f32[16,4608]{1,0:T(8,128)S(1)} %get-tuple-element.146.part_ref, f32[16,1]{1,0:T(8,128)S(1)} %copy.92.scales_ref, ...), custom_call_target="tpu_custom_call" | custom-call | tf_op jit(solution)/shard_map/head_terms/pallas_call | solution.py:121
  592.5 6.8 collective-permute-done.36
  599.3 6.8 collective-permute-done.35
  609.4 7.2 %head_terms.28 = bf16[16,4608]{1,0:T(8,128)(2,1)S(1)} custom-call(s32[1]{0:T(128)} %bitcast.20.core_ref, f32[2,16,1024]{2,1,0:T(8,128)S(1)} %bitcast.131, f32[16,16,1024]{2,1,0:T(8,128)S(1)} %copy-done.14, f32[16,4608]{1,0:T(8,128)S(1)} %get-tuple-element.212.part_ref, f32[16,1]{1,0:T(8,128)S(1)} %copy.92.scales_ref, ...), custom_call_target="tpu_custom_call" | custom-call | tf_op jit(solution)/shard_map/head_terms/pallas_call | solution.py:121
  620.6 6.6 collective-permute-done.38
  627.2 6.3 collective-permute-done.37
  636.8 7.2 %head_terms.29 = bf16[16,4608]{1,0:T(8,128)(2,1)S(1)} custom-call(s32[1]{0:T(128)} %bitcast.20.core_ref, f32[2,16,1024]{2,1,0:T(8,128)S(1)} %bitcast.117, f32[16,16,1024]{2,1,0:T(8,128)S(1)} %copy-done.14, f32[16,4608]{1,0:T(8,128)S(1)} %get-tuple-element.206.part_ref, f32[16,1]{1,0:T(8,128)S(1)} %copy.92.scales_ref, ...), custom_call_target="tpu_custom_call" | custom-call | tf_op jit(solution)/shard_map/head_terms/pallas_call | solution.py:121
  647.9 6.6 collective-permute-done.40
  654.6 6.7 collective-permute-done.39
  668.7 10.0 %all-to-all-start.2 = ((bf16[16,4,2304]{2,1,0:T(4,128)(2,1)}), bf16[16,4,2304]{2,1,0:T(4,128)(2,1)S(1)}, u32[]{:S(2)}, u32[]{:S(2)}) async-start(bf16[16,4,2304]{2,1,0:T(4,128)(2,1)} %copy.107), calls=%async_computation.2 | async-start | bytes 589824 | tf_op jit(solution)/shard_map/all_to_all | solution.py:253
  678.7 15.9 %all-to-all-done.2 = bf16[16,4,2304]{2,1,0:T(4,128)(2,1)S(1)} async-done(((bf16[16,4,2304]{2,1,0:T(4,128)(2,1)}), bf16[16,4,2304]{2,1,0:T(4,128)(2,1)S(1)}, u32[]{:S(2)}, u32[]{:S(2)}) %all-to-all-start.2) | async-done | bytes 294944 | tf_op jit(solution)/shard_map/all_to_all | solution.py:253
  694.7 3.5 all_gather.123
  (167 shorter events, 168.9 us)
Async XLA Ops:
  0.0 51.2 %copy-start = (bf16[1,128,4608]{2,1,0:T(8,128)(2,1)S(1)}, bf16[1,128,4608]{2,1,0:T(8,128)(2,1)}, u32[]{:S(2)}) copy-start(bf16[1,128,4608]{2,1,0:T(8,128)(2,1)} %param.10) | copy-start | bytes 3538948
  0.0 139.7 %collective-permute-start.3 = (f32[16,16]{1,0:T(8,128)}, f32[16,16]{1,0:T(8,128)}, u32[]{:S(2)}, u32[]{:S(2)}) collective-permute-start(f32[16,16]{1,0:T(8,128)} %bitcast.142), channel_id=1, source_target_pairs={{0,28},{1,5},{4,0},{5,9},{8,4},{9,13},{12,8},{13,17},{16,12},{17,2... | collective-permute-start | bytes 3080 | tf_op jit(solution)/shard_map/ppermute | solution.py:25
  3.3 136.4 %collective-permute-start.2 = (f32[16,16]{1,0:T(8,128)}, f32[16,16]{1,0:T(8,128)}, u32[]{:S(2)}, u32[]{:S(2)}) collective-permute-start(f32[16,16]{1,0:T(8,128)} %bitcast.143), channel_id=1, source_target_pairs={{0,2},{2,0},{1,3},{3,1},{4,6},{6,4},{5,7},{7,5},{8,10},{10,8},{9,1... | collective-permute-start | bytes 3080 | tf_op jit(solution)/shard_map/ppermute | solution.py:194
  18.2 29.7 %copy-start.16 = (s32[1,4096]{1,0:T(1,128)S(1)}, s32[1,4096]{1,0:T(1,128)}, u32[]{:S(2)}) copy-start(s32[1,4096]{1,0:T(1,128)} %param.16) | copy-start | bytes 49156
  18.2 121.5 %collective-permute-start.1 = (bf16[256,4608]{1,0:T(8,128)(2,1)S(1)}, bf16[256,4608]{1,0:T(8,128)(2,1)}, u32[]{:S(2)}, u32[]{:S(2)}) collective-permute-start(bf16[256,4608]{1,0:T(8,128)(2,1)S(1)} %pad_maximum_fusion.mine_ref.refs_0_), channel_id=1, source_target_pairs={{0,28},{1,5},{4,0},{5,9},{8,4},{9,13},{12,8},{13,17},{16,12},{17,2... | collective-permute-start | bytes 7077896 | tf_op jit(solution)/shard_map/ppermute | solution.py:25
  21.4 118.3 %collective-permute-start = (bf16[256,4608]{1,0:T(8,128)(2,1)S(1)}, bf16[256,4608]{1,0:T(8,128)(2,1)}, u32[]{:S(2)}, u32[]{:S(2)}) collective-permute-start(bf16[256,4608]{1,0:T(8,128)(2,1)S(1)} %pad_maximum_fusion.mine_ref.refs_0_), channel_id=1, source_target_pairs={{0,2},{2,0},{1,3},{3,1},{4,6},{6,4},{5,7},{7,5},{8,10},{10,8},{9,1... | collective-permute-start | bytes 7077896 | tf_op jit(solution)/shard_map/ppermute | solution.py:183
  35.8 101.6 %all-to-all-start = ((bf16[32,2,2304]{2,1,0:T(2,128)(2,1)}), bf16[32,2,2304]{2,1,0:T(2,128)(2,1)}, u32[]{:S(2)}, u32[]{:S(2)}) async-start(bf16[32,2,2304]{2,1,0:T(2,128)(2,1)} %reshape.199), calls=%async_computation | async-start | bytes 589824 | tf_op jit(solution)/shard_map/all_to_all | solution.py:196
  54.7 93.7 %copy-start.20 = (s32[4]{0:T(128)S(1)}, s32[4]{0:T(128)}, u32[]{:S(2)}) copy-start(s32[4]{0:T(128)} %param.19) | copy-start | bytes 52
  54.7 122.8 %copy-start.17 = (f32[1,1,16,16]{3,2,1,0:T(8,128)S(1)}, f32[1,1,16,16]{3,2,1,0:T(8,128)}, u32[]{:S(2)}) copy-start(f32[1,1,16,16]{3,2,1,0:T(8,128)} %param.14) | copy-start | bytes 3076
  139.8 45.5 %collective-permute-start.5 = (bf16[256,4608]{1,0:T(8,128)(2,1)S(1)}, bf16[256,4608]{1,0:T(8,128)(2,1)}, u32[]{:S(2)}, u32[]{:S(2)}) collective-permute-start(bf16[256,4608]{1,0:T(8,128)(2,1)S(1)} %pad_maximum_fusion.mine_ref.refs_0_), channel_id=1, source_target_pairs={{0,1},{1,0},{2,3},{3,2},{4,5},{5,4},{6,7},{7,6},{8,9},{9,8},{10,11... | collective-permute-start | bytes 7077896 | tf_op jit(solution)/shard_map/ppermute | solution.py:91
  142.1 46.9 %collective-permute-start.6 = (bf16[256,4608]{1,0:T(8,128)(2,1)}, bf16[256,4608]{1,0:T(8,128)(2,1)}, u32[]{:S(2)}, u32[]{:S(2)}) collective-permute-start(bf16[256,4608]{1,0:T(8,128)(2,1)} %collective-permute-done.1.mine_ref.refs_2_), channel_id=1, source_target_pairs={{0,1},{1,0},{2,3},{3,2},{4,5},{5,4},{6,7},{7,6},{8,9},{9,8},{10,11... | collective-permute-start | bytes 7077896 | tf_op jit(solution)/shard_map/ppermute | solution.py:91
  144.1 49.4 %collective-permute-start.7 = (bf16[256,4608]{1,0:T(8,128)(2,1)}, bf16[256,4608]{1,0:T(8,128)(2,1)}, u32[]{:S(2)}, u32[]{:S(2)}) collective-permute-start(bf16[256,4608]{1,0:T(8,128)(2,1)} %collective-permute-done.mine_ref.refs_4_), channel_id=1, source_target_pairs={{0,1},{1,0},{2,3},{3,2},{4,5},{5,4},{6,7},{7,6},{8,9},{9,8},{10,11... | collective-permute-start | bytes 7077896 | tf_op jit(solution)/shard_map/ppermute | solution.py:91
  146.4 51.5 %collective-permute-start.4 = (bf16[256,4608]{1,0:T(8,128)(2,1)}, bf16[256,4608]{1,0:T(8,128)(2,1)}, u32[]{:S(2)}, u32[]{:S(2)}) collective-permute-start(bf16[256,4608]{1,0:T(8,128)(2,1)} %collective-permute-done.mine_ref.refs_4_), channel_id=1, source_target_pairs={{0,28},{1,5},{4,0},{5,9},{8,4},{9,13},{12,8},{13,17},{16,12},{17,2... | collective-permute-start | bytes 7077896 | tf_op jit(solution)/shard_map/ppermute | solution.py:25
  149.7 27.8 %collective-permute-start.8 = (f32[16,16]{1,0:T(8,128)}, f32[16,16]{1,0:T(8,128)S(1)}, u32[]{:S(2)}, u32[]{:S(2)}) collective-permute-start(f32[16,16]{1,0:T(8,128)} %collective-permute-done.2), channel_id=1, source_target_pairs={{0,28},{1,5},{4,0},{5,9},{8,4},{9,13},{12,8},{13,17},{16,12},{17,2... | collective-permute-start | bytes 3080 | tf_op jit(solution)/shard_map/ppermute | solution.py:25
  178.3 3.1 collective-permute-start.9
  192.0 1.5 copy-start.5
  197.9 8.6 %copy-start.19 = (f32[1,16]{1,0:T(1,128)S(1)}, f32[1,16]{1,0:T(1,128)}, u32[]{:S(2)}) copy-start(f32[1,16]{1,0:T(1,128)} %param.15) | copy-start | bytes 196
  197.9 171.6 %all-to-all-start.1 = ((bf16[32,8,4608]{2,1,0:T(8,128)(2,1)}), bf16[32,8,4608]{2,1,0:T(8,128)(2,1)}, u32[]{:S(2)}, u32[]{:S(2)}) async-start(bf16[32,8,4608]{2,1,0:T(8,128)(2,1)} %bitcast_select_fusion), calls=%async_computation.1 | async-start | bytes 4718592 | tf_op jit(solution)/shard_map/all_to_all | solution.py:223
  204.1 6.8 collective-permute-start.10
  206.6 7.3 %copy-start.3 = (bf16[4608,256]{1,0:T(8,128)(2,1)S(1)}, bf16[4608,256]{1,0:T(8,128)(2,1)}, u32[]{:S(2)}) copy-start(bf16[4608,256]{1,0:T(8,128)(2,1)} %copy-done.2) | copy-start | bytes 7077892
  206.6 7.3 %copy-start.6 = (bf16[4608,256]{1,0:T(8,128)(2,1)S(1)}, bf16[4608,256]{1,0:T(8,128)(2,1)}, u32[]{:S(2)}) copy-start(bf16[4608,256]{1,0:T(8,128)(2,1)} %copy-done.5) | copy-start | bytes 7077892
  206.6 7.3 %copy-start.9 = (bf16[4608,256]{1,0:T(8,128)(2,1)S(1)}, bf16[4608,256]{1,0:T(8,128)(2,1)}, u32[]{:S(2)}) copy-start(bf16[4608,256]{1,0:T(8,128)(2,1)} %copy-done.8) | copy-start | bytes 7077892
  214.0 141.1 %copy-start.11 = (bf16[4608,256]{1,0:T(8,128)(2,1)}, bf16[4608,256]{1,0:T(8,128)(2,1)S(1)}, u32[]{:S(2)}) copy-start(bf16[4608,256]{1,0:T(8,128)(2,1)S(1)} %turn_heads.7.refs_3_) | copy-start | bytes 7077892
  214.0 3.2 copy-start.13
  224.4 43.7 %collective-permute-start.12 = (bf16[16,4608]{1,0:T(8,128)(2,1)S(1)}, bf16[16,4608]{1,0:T(8,128)(2,1)S(1)}, u32[]{:S(2)}, u32[]{:S(2)}) collective-permute-start(bf16[16,4608]{1,0:T(8,128)(2,1)S(1)} %head_terms.15), channel_id=1, source_target_pairs={{32,0},{33,25},{40,8},{41,1},{48,16},{49,9},{56,24},{57,17},{64,32... | collective-permute-start | bytes 442376 | tf_op jit(solution)/shard_map/ppermute | solution.py:36
  230.1 37.9 %collective-permute-start.11 = (bf16[16,4608]{1,0:T(8,128)(2,1)S(1)}, bf16[16,4608]{1,0:T(8,128)(2,1)S(1)}, u32[]{:S(2)}, u32[]{:S(2)}) collective-permute-start(bf16[16,4608]{1,0:T(8,128)(2,1)S(1)} %head_terms.15), channel_id=1, source_target_pairs={{32,17},{33,8},{40,25},{41,16},{48,1},{49,24},{56,9},{57,0},{64,49... | collective-permute-start | bytes 442376 | tf_op jit(solution)/shard_map/ppermute | solution.py:36
  278.4 10.3 %collective-permute-start.14 = (bf16[16,4608]{1,0:T(8,128)(2,1)S(1)}, bf16[16,4608]{1,0:T(8,128)(2,1)S(1)}, u32[]{:S(2)}, u32[]{:S(2)}) collective-permute-start(bf16[16,4608]{1,0:T(8,128)(2,1)S(1)} %head_terms.16), channel_id=1, source_target_pairs={{32,0},{33,25},{40,8},{41,1},{48,16},{49,9},{56,24},{57,17},{64,32... | collective-permute-start | bytes 442376 | tf_op jit(solution)/shard_map/ppermute | solution.py:36
  283.0 13.4 %collective-permute-start.13 = (bf16[16,4608]{1,0:T(8,128)(2,1)S(1)}, bf16[16,4608]{1,0:T(8,128)(2,1)S(1)}, u32[]{:S(2)}, u32[]{:S(2)}) collective-permute-start(bf16[16,4608]{1,0:T(8,128)(2,1)S(1)} %head_terms.16), channel_id=1, source_target_pairs={{32,17},{33,8},{40,25},{41,16},{48,1},{49,24},{56,9},{57,0},{64,49... | collective-permute-start | bytes 442376 | tf_op jit(solution)/shard_map/ppermute | solution.py:36
  306.8 9.9 %collective-permute-start.16 = (bf16[16,4608]{1,0:T(8,128)(2,1)S(1)}, bf16[16,4608]{1,0:T(8,128)(2,1)S(1)}, u32[]{:S(2)}, u32[]{:S(2)}) collective-permute-start(bf16[16,4608]{1,0:T(8,128)(2,1)S(1)} %head_terms.17), channel_id=1, source_target_pairs={{32,0},{33,25},{40,8},{41,1},{48,16},{49,9},{56,24},{57,17},{64,32... | collective-permute-start | bytes 442376 | tf_op jit(solution)/shard_map/ppermute | solution.py:36
  312.2 15.6 %collective-permute-start.15 = (bf16[16,4608]{1,0:T(8,128)(2,1)S(1)}, bf16[16,4608]{1,0:T(8,128)(2,1)S(1)}, u32[]{:S(2)}, u32[]{:S(2)}) collective-permute-start(bf16[16,4608]{1,0:T(8,128)(2,1)S(1)} %head_terms.17), channel_id=1, source_target_pairs={{32,17},{33,8},{40,25},{41,16},{48,1},{49,24},{56,9},{57,0},{64,49... | collective-permute-start | bytes 442376 | tf_op jit(solution)/shard_map/ppermute | solution.py:36
  338.2 9.9 %collective-permute-start.18 = (bf16[16,4608]{1,0:T(8,128)(2,1)S(1)}, bf16[16,4608]{1,0:T(8,128)(2,1)S(1)}, u32[]{:S(2)}, u32[]{:S(2)}) collective-permute-start(bf16[16,4608]{1,0:T(8,128)(2,1)S(1)} %head_terms.18), channel_id=1, source_target_pairs={{32,0},{33,25},{40,8},{41,1},{48,16},{49,9},{56,24},{57,17},{64,32... | collective-permute-start | bytes 442376 | tf_op jit(solution)/shard_map/ppermute | solution.py:36
  340.1 14.9 %collective-permute-start.17 = (bf16[16,4608]{1,0:T(8,128)(2,1)S(1)}, bf16[16,4608]{1,0:T(8,128)(2,1)S(1)}, u32[]{:S(2)}, u32[]{:S(2)}) collective-permute-start(bf16[16,4608]{1,0:T(8,128)(2,1)S(1)} %head_terms.18), channel_id=1, source_target_pairs={{32,17},{33,8},{40,25},{41,16},{48,1},{49,24},{56,9},{57,0},{64,49... | collective-permute-start | bytes 442376 | tf_op jit(solution)/shard_map/ppermute | solution.py:36
  365.4 12.2 %collective-permute-start.20 = (bf16[16,4608]{1,0:T(8,128)(2,1)S(1)}, bf16[16,4608]{1,0:T(8,128)(2,1)S(1)}, u32[]{:S(2)}, u32[]{:S(2)}) collective-permute-start(bf16[16,4608]{1,0:T(8,128)(2,1)S(1)} %head_terms.19), channel_id=1, source_target_pairs={{32,0},{33,25},{40,8},{41,1},{48,16},{49,9},{56,24},{57,17},{64,32... | collective-permute-start | bytes 442376 | tf_op jit(solution)/shard_map/ppermute | solution.py:36
  367.4 14.1 %collective-permute-start.19 = (bf16[16,4608]{1,0:T(8,128)(2,1)S(1)}, bf16[16,4608]{1,0:T(8,128)(2,1)S(1)}, u32[]{:S(2)}, u32[]{:S(2)}) collective-permute-start(bf16[16,4608]{1,0:T(8,128)(2,1)S(1)} %head_terms.19), channel_id=1, source_target_pairs={{32,17},{33,8},{40,25},{41,16},{48,1},{49,24},{56,9},{57,0},{64,49... | collective-permute-start | bytes 442376 | tf_op jit(solution)/shard_map/ppermute | solution.py:36
  375.0 6.5 copy-start.4
  381.4 7.3 %copy-start.14 = (f32[16,16,1024]{2,1,0:T(8,128)S(1)}, f32[16,16,1024]{2,1,0:T(8,128)}, u32[]{:S(2)}) copy-start(f32[16,16,1024]{2,1,0:T(8,128)} %reshape.163.mix_ref) | copy-start | bytes 3145732
  388.7 23.8 %copy-start.7 = (bf16[4608,256]{1,0:T(8,128)(2,1)S(1)}, bf16[4608,256]{1,0:T(8,128)(2,1)}, u32[]{:S(2)}) copy-start(bf16[4608,256]{1,0:T(8,128)(2,1)} %copy-done.5) | copy-start | bytes 7077892
  388.7 23.8 %copy-start.10 = (bf16[4608,256]{1,0:T(8,128)(2,1)S(1)}, bf16[4608,256]{1,0:T(8,128)(2,1)}, u32[]{:S(2)}) copy-start(bf16[4608,256]{1,0:T(8,128)(2,1)} %copy-done.8) | copy-start | bytes 7077892
  388.7 23.8 %copy-start.12 = (bf16[4608,256]{1,0:T(8,128)(2,1)S(1)}, bf16[4608,256]{1,0:T(8,128)(2,1)}, u32[]{:S(2)}) copy-start(bf16[4608,256]{1,0:T(8,128)(2,1)} %copy-done.11) | copy-start | bytes 7077892
  396.0 10.2 %collective-permute-start.22 = (bf16[16,4608]{1,0:T(8,128)(2,1)S(1)}, bf16[16,4608]{1,0:T(8,128)(2,1)S(1)}, u32[]{:S(2)}, u32[]{:S(2)}) collective-permute-start(bf16[16,4608]{1,0:T(8,128)(2,1)S(1)} %head_terms.20), channel_id=1, source_target_pairs={{32,0},{33,25},{40,8},{41,1},{48,16},{49,9},{56,24},{57,17},{64,32... | collective-permute-start | bytes 442376 | tf_op jit(solution)/shard_map/ppermute | solution.py:36
  397.9 14.6 %collective-permute-start.21 = (bf16[16,4608]{1,0:T(8,128)(2,1)S(1)}, bf16[16,4608]{1,0:T(8,128)(2,1)S(1)}, u32[]{:S(2)}, u32[]{:S(2)}) collective-permute-start(bf16[16,4608]{1,0:T(8,128)(2,1)S(1)} %head_terms.20), channel_id=1, source_target_pairs={{32,17},{33,8},{40,25},{41,16},{48,1},{49,24},{56,9},{57,0},{64,49... | collective-permute-start | bytes 442376 | tf_op jit(solution)/shard_map/ppermute | solution.py:36
  422.9 9.9 %collective-permute-start.24 = (bf16[16,4608]{1,0:T(8,128)(2,1)S(1)}, bf16[16,4608]{1,0:T(8,128)(2,1)S(1)}, u32[]{:S(2)}, u32[]{:S(2)}) collective-permute-start(bf16[16,4608]{1,0:T(8,128)(2,1)S(1)} %head_terms.21), channel_id=1, source_target_pairs={{32,0},{33,25},{40,8},{41,1},{48,16},{49,9},{56,24},{57,17},{64,32... | collective-permute-start | bytes 442376 | tf_op jit(solution)/shard_map/ppermute | solution.py:36
  424.8 14.8 %collective-permute-start.23 = (bf16[16,4608]{1,0:T(8,128)(2,1)S(1)}, bf16[16,4608]{1,0:T(8,128)(2,1)S(1)}, u32[]{:S(2)}, u32[]{:S(2)}) collective-permute-start(bf16[16,4608]{1,0:T(8,128)(2,1)S(1)} %head_terms.21), channel_id=1, source_target_pairs={{32,17},{33,8},{40,25},{41,16},{48,1},{49,24},{56,9},{57,0},{64,49... | collective-permute-start | bytes 442376 | tf_op jit(solution)/shard_map/ppermute | solution.py:36
  450.0 11.5 %collective-permute-start.26 = (bf16[16,4608]{1,0:T(8,128)(2,1)S(1)}, bf16[16,4608]{1,0:T(8,128)(2,1)S(1)}, u32[]{:S(2)}, u32[]{:S(2)}) collective-permute-start(bf16[16,4608]{1,0:T(8,128)(2,1)S(1)} %head_terms.22), channel_id=1, source_target_pairs={{32,0},{33,25},{40,8},{41,1},{48,16},{49,9},{56,24},{57,17},{64,32... | collective-permute-start | bytes 442376 | tf_op jit(solution)/shard_map/ppermute | solution.py:36
  451.9 14.5 %collective-permute-start.25 = (bf16[16,4608]{1,0:T(8,128)(2,1)S(1)}, bf16[16,4608]{1,0:T(8,128)(2,1)S(1)}, u32[]{:S(2)}, u32[]{:S(2)}) collective-permute-start(bf16[16,4608]{1,0:T(8,128)(2,1)S(1)} %head_terms.22), channel_id=1, source_target_pairs={{32,17},{33,8},{40,25},{41,16},{48,1},{49,24},{56,9},{57,0},{64,49... | collective-permute-start | bytes 442376 | tf_op jit(solution)/shard_map/ppermute | solution.py:36
  476.8 11.5 %collective-permute-start.28 = (bf16[16,4608]{1,0:T(8,128)(2,1)S(1)}, bf16[16,4608]{1,0:T(8,128)(2,1)S(1)}, u32[]{:S(2)}, u32[]{:S(2)}) collective-permute-start(bf16[16,4608]{1,0:T(8,128)(2,1)S(1)} %head_terms.23), channel_id=1, source_target_pairs={{32,0},{33,25},{40,8},{41,1},{48,16},{49,9},{56,24},{57,17},{64,32... | collective-permute-start | bytes 442376 | tf_op jit(solution)/shard_map/ppermute | solution.py:36
  479.9 15.1 %collective-permute-start.27 = (bf16[16,4608]{1,0:T(8,128)(2,1)S(1)}, bf16[16,4608]{1,0:T(8,128)(2,1)S(1)}, u32[]{:S(2)}, u32[]{:S(2)}) collective-permute-start(bf16[16,4608]{1,0:T(8,128)(2,1)S(1)} %head_terms.23), channel_id=1, source_target_pairs={{32,17},{33,8},{40,25},{41,16},{48,1},{49,24},{56,9},{57,0},{64,49... | collective-permute-start | bytes 442376 | tf_op jit(solution)/shard_map/ppermute | solution.py:36
  506.9 10.6 %collective-permute-start.30 = (bf16[16,4608]{1,0:T(8,128)(2,1)S(1)}, bf16[16,4608]{1,0:T(8,128)(2,1)S(1)}, u32[]{:S(2)}, u32[]{:S(2)}) collective-permute-start(bf16[16,4608]{1,0:T(8,128)(2,1)S(1)} %head_terms.24), channel_id=1, source_target_pairs={{32,0},{33,25},{40,8},{41,1},{48,16},{49,9},{56,24},{57,17},{64,32... | collective-permute-start | bytes 442376 | tf_op jit(solution)/shard_map/ppermute | solution.py:36
  508.8 14.8 %collective-permute-start.29 = (bf16[16,4608]{1,0:T(8,128)(2,1)S(1)}, bf16[16,4608]{1,0:T(8,128)(2,1)S(1)}, u32[]{:S(2)}, u32[]{:S(2)}) collective-permute-start(bf16[16,4608]{1,0:T(8,128)(2,1)S(1)} %head_terms.24), channel_id=1, source_target_pairs={{32,17},{33,8},{40,25},{41,16},{48,1},{49,24},{56,9},{57,0},{64,49... | collective-permute-start | bytes 442376 | tf_op jit(solution)/shard_map/ppermute | solution.py:36
  534.0 9.9 %collective-permute-start.32 = (bf16[16,4608]{1,0:T(8,128)(2,1)S(1)}, bf16[16,4608]{1,0:T(8,128)(2,1)S(1)}, u32[]{:S(2)}, u32[]{:S(2)}) collective-permute-start(bf16[16,4608]{1,0:T(8,128)(2,1)S(1)} %head_terms.25), channel_id=1, source_target_pairs={{32,0},{33,25},{40,8},{41,1},{48,16},{49,9},{56,24},{57,17},{64,32... | collective-permute-start | bytes 442376 | tf_op jit(solution)/shard_map/ppermute | solution.py:36
  536.0 14.9 %collective-permute-start.31 = (bf16[16,4608]{1,0:T(8,128)(2,1)S(1)}, bf16[16,4608]{1,0:T(8,128)(2,1)S(1)}, u32[]{:S(2)}, u32[]{:S(2)}) collective-permute-start(bf16[16,4608]{1,0:T(8,128)(2,1)S(1)} %head_terms.25), channel_id=1, source_target_pairs={{32,17},{33,8},{40,25},{41,16},{48,1},{49,24},{56,9},{57,0},{64,49... | collective-permute-start | bytes 442376 | tf_op jit(solution)/shard_map/ppermute | solution.py:36
  561.2 10.9 %collective-permute-start.34 = (bf16[16,4608]{1,0:T(8,128)(2,1)S(1)}, bf16[16,4608]{1,0:T(8,128)(2,1)S(1)}, u32[]{:S(2)}, u32[]{:S(2)}) collective-permute-start(bf16[16,4608]{1,0:T(8,128)(2,1)S(1)} %head_terms.26), channel_id=1, source_target_pairs={{32,0},{33,25},{40,8},{41,1},{48,16},{49,9},{56,24},{57,17},{64,32... | collective-permute-start | bytes 442376 | tf_op jit(solution)/shard_map/ppermute | solution.py:36
  563.1 15.1 %collective-permute-start.33 = (bf16[16,4608]{1,0:T(8,128)(2,1)S(1)}, bf16[16,4608]{1,0:T(8,128)(2,1)S(1)}, u32[]{:S(2)}, u32[]{:S(2)}) collective-permute-start(bf16[16,4608]{1,0:T(8,128)(2,1)S(1)} %head_terms.26), channel_id=1, source_target_pairs={{32,17},{33,8},{40,25},{41,16},{48,1},{49,24},{56,9},{57,0},{64,49... | collective-permute-start | bytes 442376 | tf_op jit(solution)/shard_map/ppermute | solution.py:36
  588.7 10.7 %collective-permute-start.36 = (bf16[16,4608]{1,0:T(8,128)(2,1)S(1)}, bf16[16,4608]{1,0:T(8,128)(2,1)S(1)}, u32[]{:S(2)}, u32[]{:S(2)}) collective-permute-start(bf16[16,4608]{1,0:T(8,128)(2,1)S(1)} %head_terms.27), channel_id=1, source_target_pairs={{32,0},{33,25},{40,8},{41,1},{48,16},{49,9},{56,24},{57,17},{64,32... | collective-permute-start | bytes 442376 | tf_op jit(solution)/shard_map/ppermute | solution.py:36
  590.6 15.6 %collective-permute-start.35 = (bf16[16,4608]{1,0:T(8,128)(2,1)S(1)}, bf16[16,4608]{1,0:T(8,128)(2,1)S(1)}, u32[]{:S(2)}, u32[]{:S(2)}) collective-permute-start(bf16[16,4608]{1,0:T(8,128)(2,1)S(1)} %head_terms.27), channel_id=1, source_target_pairs={{32,17},{33,8},{40,25},{41,16},{48,1},{49,24},{56,9},{57,0},{64,49... | collective-permute-start | bytes 442376 | tf_op jit(solution)/shard_map/ppermute | solution.py:36
  616.6 10.6 %collective-permute-start.38 = (bf16[16,4608]{1,0:T(8,128)(2,1)S(1)}, bf16[16,4608]{1,0:T(8,128)(2,1)S(1)}, u32[]{:S(2)}, u32[]{:S(2)}) collective-permute-start(bf16[16,4608]{1,0:T(8,128)(2,1)S(1)} %head_terms.28), channel_id=1, source_target_pairs={{32,0},{33,25},{40,8},{41,1},{48,16},{49,9},{56,24},{57,17},{64,32... | collective-permute-start | bytes 442376 | tf_op jit(solution)/shard_map/ppermute | solution.py:36
  618.5 15.0 %collective-permute-start.37 = (bf16[16,4608]{1,0:T(8,128)(2,1)S(1)}, bf16[16,4608]{1,0:T(8,128)(2,1)S(1)}, u32[]{:S(2)}, u32[]{:S(2)}) collective-permute-start(bf16[16,4608]{1,0:T(8,128)(2,1)S(1)} %head_terms.28), channel_id=1, source_target_pairs={{32,17},{33,8},{40,25},{41,16},{48,1},{49,24},{56,9},{57,0},{64,49... | collective-permute-start | bytes 442376 | tf_op jit(solution)/shard_map/ppermute | solution.py:36
  643.9 54.3 %copy-start.15 = (bf16[128,4608]{1,0:T(8,128)(2,1)S(1)}, bf16[128,4608]{1,0:T(8,128)(2,1)}, u32[]{:S(2)}) copy-start(bf16[128,4608]{1,0:T(8,128)(2,1)} %broadcast_select_fusion) | copy-start | bytes 3538948
  643.9 10.6 %collective-permute-start.40 = (bf16[16,4608]{1,0:T(8,128)(2,1)S(1)}, bf16[16,4608]{1,0:T(8,128)(2,1)S(1)}, u32[]{:S(2)}, u32[]{:S(2)}) collective-permute-start(bf16[16,4608]{1,0:T(8,128)(2,1)S(1)} %head_terms.29), channel_id=1, source_target_pairs={{32,0},{33,25},{40,8},{41,1},{48,16},{49,9},{56,24},{57,17},{64,32... | collective-permute-start | bytes 442376 | tf_op jit(solution)/shard_map/ppermute | solution.py:36
  646.0 15.3 %collective-permute-start.39 = (bf16[16,4608]{1,0:T(8,128)(2,1)S(1)}, bf16[16,4608]{1,0:T(8,128)(2,1)S(1)}, u32[]{:S(2)}, u32[]{:S(2)}) collective-permute-start(bf16[16,4608]{1,0:T(8,128)(2,1)S(1)} %head_terms.29), channel_id=1, source_target_pairs={{32,17},{33,8},{40,25},{41,16},{48,1},{49,24},{56,9},{57,0},{64,49... | collective-permute-start | bytes 442376 | tf_op jit(solution)/shard_map/ppermute | solution.py:36
  663.1 3.5 collective-permute-start.41
  666.6 33.0 %copy-start.1 = (bf16[1,128,4608]{2,1,0:T(8,128)(2,1)S(1)}, bf16[1,128,4608]{2,1,0:T(8,128)(2,1)}, u32[]{:S(2)}) copy-start(bf16[1,128,4608]{2,1,0:T(8,128)(2,1)} %param.10) | copy-start | bytes 3538948
  667.8 31.1 %copy-start.18 = (f32[1,128]{1,0:T(1,128)S(1)}, f32[1,128]{1,0:T(1,128)}, u32[]{:S(2)}) copy-start(f32[1,128]{1,0:T(1,128)} %param.17) | copy-start | bytes 1540
  668.7 25.9 %all-to-all-start.2 = ((bf16[16,4,2304]{2,1,0:T(4,128)(2,1)}), bf16[16,4,2304]{2,1,0:T(4,128)(2,1)S(1)}, u32[]{:S(2)}, u32[]{:S(2)}) async-start(bf16[16,4,2304]{2,1,0:T(4,128)(2,1)} %copy.107), calls=%async_computation.2 | async-start | bytes 589824 | tf_op jit(solution)/shard_map/all_to_all | solution.py:253
  (2 other events, 2.8 us)

commit v5 on v4

--- a/solution.py
+++ b/solution.py
@@ -53,9 +53,10 @@
     *values, share_ref = refs
     core = core_ref[0]
     mine, other = grads_ref[core], grads_ref[1 - core]
-    head = values[0].shape[0] // 2
+    wide = values[0].shape[0]
+    head = wide // 2
     swapped = []
-    for k in range(len(values)):
+    for k in range(2 * len(values)):
         swapped.append(other[:, (k ^ 1) * head : ((k ^ 1) + 1) * head])
     grads = mine + jnp.concatenate(swapped, axis=1)
     mixed = mix_ref[0] * grads[0:1, :]
@@ -65,18 +66,20 @@
     term = None
     for k, ref in enumerate(values):
         product = jnp.dot(
-            mixed[:, k * head : (k + 1) * head],
-            ref[head : 2 * head, :],
+            mixed[:, k * wide : (k + 1) * wide],
+            ref[...],
             preferred_element_type=F32,
         )
         term = product if term is None else term + product
     share_ref[...] = (part_ref[...] * 0.5 + term * scales_ref[...]).astype(BF)
 
 
-def turn_kernel(mine_ref, other_ref, turned_ref):
+def turn_kernel(mine_ref, other_ref, turned_ref, values_ref):
     head = mine_ref.shape[0] // 2
     turned_ref[:, :head] = mine_ref[:head, :].T
     turned_ref[:, head:] = other_ref[:head, :].T
+    values_ref[:head, :] = mine_ref[head:, :]
+    values_ref[head:, :] = other_ref[head:, :]
 
 
 def keep(array):
@@ -89,15 +92,18 @@
 
 def prepare(mine):
     other = lax.ppermute(mine, "core", SWAP)
-    turned = pl.pallas_call(
+    rows, model_width = mine.shape
+    return pl.pallas_call(
         turn_kernel,
-        out_shape=jax.ShapeDtypeStruct((mine.shape[1], mine.shape[0]), BF),
+        out_shape=(
+            jax.ShapeDtypeStruct((model_width, rows), BF),
+            jax.ShapeDtypeStruct((rows, model_width), BF),
+        ),
         in_specs=[whole()] * 2,
-        out_specs=whole(),
+        out_specs=(whole(),) * 2,
         compiler_params=pltpu.CompilerParams(vmem_limit_bytes=24 << 20),
         name="turn_heads",
-    )(keep(mine), keep(other))
-    return turned, mine, other
+    )(mine, other)
 
 
 def head_grads(arrived, outs):
@@ -191,17 +197,16 @@
     enc_send = jnp.broadcast_to(
         enc_rows[None, :, None, :], (QUADS, targets, 2, model_width)
     ).reshape(feat_count, model_width)
-    beyond_mix = lax.ppermute(own_mix, "zh", SWAP)
     near_mix = neighbour_heads(own_mix)
-    enc_got = lax.all_to_all(enc_send, FEAT, split_axis=0, concat_axis=0, tiled=True)
+    zh_mix = lax.ppermute(jnp.stack([own_mix, near_mix]), "zh", SWAP)
     outgoing, flat_index = panel_route(
         decoders[0], act_ids[0], entries_dev, feat_index, feat_count
     )
-    own, beyond, near, beyond_mix, near_mix, enc_got, outgoing = lax.optimization_barrier(
-        (own, beyond, near, beyond_mix, near_mix, enc_got, outgoing)
+    own, beyond, near, near_mix, zh_mix, outgoing, enc_send = lax.optimization_barrier(
+        (own, beyond, near, near_mix, zh_mix, outgoing, enc_send)
     )
     far = neighbour_heads(beyond)
-    far_mix = neighbour_heads(beyond_mix)
+    enc_got = lax.all_to_all(enc_send, FEAT, split_axis=0, concat_axis=0, tiled=True)
     enc_row = jnp.sum(enc_got.astype(F32), axis=0)
     own_target = lax.axis_index(("par", "zh"))
     own_pos = lax.dynamic_index_in_dim(target_pos, own_target, 0, keepdims=False)
@@ -209,7 +214,7 @@
     start = jnp.where((positions == own_pos)[:, None], enc_row[None, :], 0.0)
 
     groups = [prepare(head) for head in (own, near, beyond)]
-    core_mix = jnp.stack([own_mix, near_mix, beyond_mix, far_mix])
+    core_mix = jnp.stack([own_mix, near_mix, zh_mix[0], zh_mix[1]])
     mixing = jnp.stack([core_mix, lax.ppermute(core_mix, "core", SWAP)], axis=1)
     mixing = mixing.reshape(-1, seq_len, seq_len)
     heads = mixing.shape[0]
@@ -224,7 +229,7 @@
     panel = jnp.take(incoming.reshape(-1, model_width), flat_index, axis=0)
     groups.append(prepare(far))
     outs = [group[0] for group in groups]
-    values = [head for group in groups for head in group[1:]]
+    values = [group[1] for group in groups]
     scales = norm_scale[0][:, None]
 
     outs, values = [keep(w) for w in outs], [keep(w) for w in values]

time: 713 us -> 629 us (0.88)
  Pallas kernels: 120 us -> 34.2 us
  starting transfers between devices: 136 us -> 196 us
  waiting for transfers between devices: 330 us -> 282 us
    pallas_call x15, Pallas kernels: 107 us -> 20.8 us  [head_terms(): pl.pallas_call(terms_kernel, out_shape=jax.ShapeDtypeStruct(part.shape, B...]
    all_to_all x1, waiting for transfers between devices: 79.3 us -> 18.6 us  [per_device(): lax.all_to_all(enc_send, FEAT, split_axis=0, concat_axis=0, tiled=True)]
    all_to_all x1, starting transfers between devices: 12.2 us -> 62.2 us  [per_device(): lax.all_to_all(enc_send, FEAT, split_axis=0, concat_axis=0, tiled=True)]
    ppermute x1, waiting for transfers between devices: 0.01 us -> 20.2 us  [per_device(): zh_mix = lax.ppermute(jnp.stack([own_mix, near_mix]), 'zh', SWAP)]
    ppermute x4 -> x3, waiting for transfers between devices: 23.6 us -> 7.06 us  [neighbour_heads(): return lax.ppermute(shard, ('y2', 'par', 'core'), pairs)]
    ppermute x30, waiting for transfers between devices: 205 us -> 214 us  [send_down(): return lax.ppermute(shard, ('section', 'y2', 'core'), pairs)]
    ppermute x1, starting transfers between devices: 1.92 us -> 10.6 us  [per_device(): beyond = lax.ppermute(own, 'zh', SWAP)]
    unnamed x47 -> x68, local copies, waits for them, and re-layouts: 11.5 us -> 17.5 us
  transfers between devices with their start and end apart: 45 -> 44, of which waited for: 34 -> 35; matrix products, arithmetic and copies ran while one was open for 7% -> 6% of each run, Pallas kernels for 7% -> 3%
where the time goes in v5:
time: 629 us; the launch traced here: 619 us
  waiting for transfers between devices  282 us (45%)
  starting transfers between devices  196 us (31%)
  local copies, waits for them, and re-layouts  54.8 us (9%)
  blocking collectives  34.3 us (5%)
  Pallas kernels  34.2 us (5%)
  other arithmetic  15.5 us (2%)
    ppermute x30, waiting for transfers between devices, send_down(): return lax.ppermute(shard, ('section', 'y2', 'core'), pairs)  214 us
    ppermute x30, starting transfers between devices, send_down(): return lax.ppermute(shard, ('section', 'y2', 'core'), pairs)  68.7 us
    all_to_all x1, starting transfers between devices, per_device(): lax.all_to_all(enc_send, FEAT, split_axis=0, concat_axis=0, tiled=True)  62.2 us
    all_gather x15, blocking collectives, per_device(): grads = lax.all_gather(grad_part, 'core', axis=0)  30.5 us
    pallas_call x14, local copies, waits for them, and re-layouts, head_grads(): pl.pallas_call(grads_kernel, out_shape=(jax.ShapeDtypeStruct((seq_len, mo...  21.3 us
    pallas_call x15, Pallas kernels, head_terms(): pl.pallas_call(terms_kernel, out_shape=jax.ShapeDtypeStruct(part.shape, B...  20.8 us
    ppermute x1, waiting for transfers between devices, per_device(): zh_mix = lax.ppermute(jnp.stack([own_mix, near_mix]), 'zh', SWAP)  20.2 us
    all_to_all x1, waiting for transfers between devices, per_device(): lax.all_to_all(enc_send, FEAT, split_axis=0, concat_axis=0, tiled=True)  18.6 us
  transfers between devices with their start and end apart: 44, of which 35 were waited for; matrix products, arithmetic and copies ran while one was open for 6% of the time, Pallas kernels for 3%

profile of v5, /device:TPU:7, one launch (start us, length us, event | category | flops | bytes accessed | tf_op | source)
XLA Modules:
  0.0 619.4 jit_solution(12015539274153708866)
XLA Ops:
  1.7 2.8 pad_maximum_fusion.mine_ref
  4.5 3.2 collective-permute-start.1
  7.7 10.6 %collective-permute-start = (bf16[256,4608]{1,0:T(8,128)(2,1)}, bf16[256,4608]{1,0:T(8,128)(2,1)}, u32[]{:S(2)}, u32[]{:S(2)}) collective-permute-start(bf16[256,4608]{1,0:T(8,128)(2,1)} %pad_maximum_fusion.mine_ref), channel_id=1, source_target_pairs={{0,2},{2,0},{1,3},{3,1},{4,6},{6,4},{5,7},{7,5},{8,10},{10,8},{9,1... | collective-permute-start | bytes 7077896 | tf_op jit(solution)/shard_map/ppermute | solution.py:189
  18.4 3.2 collective-permute-start.2
  22.6 3.5 gather_fusion
  26.1 3.4 bitcast_select_fusion
  29.5 7.1 %collective-permute-done.2 = f32[16,16]{1,0:T(8,128)S(1)} collective-permute-done((f32[16,16]{1,0:T(8,128)S(1)}, f32[16,16]{1,0:T(8,128)S(1)}, u32[]{:S(2)}, u32[]{:S(2)}) %collective-permute-start.2) | collective-permute-done | bytes 1056 | tf_op jit(solution)/shard_map/ppermute | solution.py:25
  36.6 10.6 %collective-permute-start.3 = (f32[2,16,16]{2,1,0:T(8,128)S(1)}, f32[2,16,16]{2,1,0:T(8,128)S(1)}, u32[]{:S(2)}, u32[]{:S(2)}) collective-permute-start(f32[2,16,16]{2,1,0:T(8,128)S(1)} %pad_maximum_fusion.3), channel_id=1, source_target_pairs={{0,2},{2,0},{1,3},{3,1},{4,6},{6,4},{5,7},{7,5},{8,10},{10,8},{9,1... | collective-permute-start | bytes 6152 | tf_op jit(solution)/shard_map/ppermute | solution.py:201
  47.8 20.2 %collective-permute-done.3 = f32[2,16,16]{2,1,0:T(8,128)S(1)} collective-permute-done((f32[2,16,16]{2,1,0:T(8,128)S(1)}, f32[2,16,16]{2,1,0:T(8,128)S(1)}, u32[]{:S(2)}, u32[]{:S(2)}) %collective-permute-start.3) | collective-permute-done | bytes 2080 | tf_op jit(solution)/shard_map/ppermute | solution.py:201
  68.0 5.3 collective-permute-start.5
  75.3 2.4 collective-permute-start.7
  77.7 3.2 collective-permute-start.4
  83.1 62.2 %all-to-all-start = ((bf16[32,2,2304]{2,1,0:T(2,128)(2,1)}), bf16[32,2,2304]{2,1,0:T(2,128)(2,1)}, u32[]{:S(2)}, u32[]{:S(2)}) async-start(bf16[32,2,2304]{2,1,0:T(2,128)(2,1)} %reshape.202), calls=%async_computation | async-start | bytes 589824 | tf_op jit(solution)/shard_map/all_to_all | solution.py:209
  146.0 2.2 collective-permute-start.8
  151.9 18.6 %all-to-all-done = bf16[32,2,2304]{2,1,0:T(2,128)(2,1)} async-done(((bf16[32,2,2304]{2,1,0:T(2,128)(2,1)}), bf16[32,2,2304]{2,1,0:T(2,128)(2,1)}, u32[]{:S(2)}, u32[]{:S(2)}) %all-to-all-start) | async-done | bytes 294944 | tf_op jit(solution)/shard_map/all_to_all | solution.py:209
  170.5 3.0 reshape.203
  178.9 2.5 turn_heads.4
  182.8 3.2 turn_heads.5
  188.9 3.2 turn_heads.6
  195.0 7.5 %all-to-all-start.1 = ((bf16[32,8,4608]{2,1,0:T(8,128)(2,1)}), bf16[32,8,4608]{2,1,0:T(8,128)(2,1)}, u32[]{:S(2)}, u32[]{:S(2)}) async-start(bf16[32,8,4608]{2,1,0:T(8,128)(2,1)} %bitcast_select_fusion), calls=%async_computation.1 | async-start | bytes 4718592 | tf_op jit(solution)/shard_map/all_to_all | solution.py:228
  202.5 2.2 collective-permute-start.9
  204.8 4.5 collective-permute-done.9.other_ref
  209.3 3.2 turn_heads.7
  214.9 2.6 all-gather
  218.8 5.7 collective-permute-start.11
  227.1 40.3 %collective-permute-done.11 = bf16[16,4608]{1,0:T(8,128)(2,1)S(1)} collective-permute-done((bf16[16,4608]{1,0:T(8,128)(2,1)S(1)}, bf16[16,4608]{1,0:T(8,128)(2,1)S(1)}, u32[]{:S(2)}, u32[]{:S(2)}) %collective-permute-start.11) | collective-permute-done | bytes 147488 | tf_op jit(solution)/shard_map/ppermute | solution.py:36
  272.0 4.5 collective-permute-start.13
  278.6 3.3 collective-permute-done.13
  281.9 8.0 %collective-permute-done.12 = bf16[16,4608]{1,0:T(8,128)(2,1)S(1)} collective-permute-done((bf16[16,4608]{1,0:T(8,128)(2,1)S(1)}, bf16[16,4608]{1,0:T(8,128)(2,1)S(1)}, u32[]{:S(2)}, u32[]{:S(2)}) %collective-permute-start.12) | collective-permute-done | bytes 147488 | tf_op jit(solution)/shard_map/ppermute | solution.py:36
  294.4 6.1 collective-permute-start.15
  304.3 12.3 %collective-permute-done.14 = bf16[16,4608]{1,0:T(8,128)(2,1)S(1)} collective-permute-done((bf16[16,4608]{1,0:T(8,128)(2,1)S(1)}, bf16[16,4608]{1,0:T(8,128)(2,1)S(1)}, u32[]{:S(2)}, u32[]{:S(2)}) %collective-permute-start.14) | collective-permute-done | bytes 147488 | tf_op jit(solution)/shard_map/ppermute | solution.py:36
  325.0 6.5 %collective-permute-done.17 = bf16[16,4608]{1,0:T(8,128)(2,1)S(1)} collective-permute-done((bf16[16,4608]{1,0:T(8,128)(2,1)S(1)}, bf16[16,4608]{1,0:T(8,128)(2,1)S(1)}, u32[]{:S(2)}, u32[]{:S(2)}) %collective-permute-start.17) | collective-permute-done | bytes 147488 | tf_op jit(solution)/shard_map/ppermute | solution.py:36
  331.5 5.5 collective-permute-done.16
  344.2 2.1 collective-permute-start.18
  346.3 5.4 gather_fusion.1
  351.7 2.6 broadcast_select_fusion
  354.3 6.2 %collective-permute-done.18 = bf16[16,4608]{1,0:T(8,128)(2,1)} collective-permute-done((bf16[16,4608]{1,0:T(8,128)(2,1)}, bf16[16,4608]{1,0:T(8,128)(2,1)}, u32[]{:S(2)}, u32[]{:S(2)}) %collective-permute-start.18) | collective-permute-done | bytes 147488 | tf_op jit(solution)/shard_map/ppermute | solution.py:36
  360.6 4.0 head_grads.25
  372.0 6.1 collective-permute-done.21
  378.1 6.2 %collective-permute-done.20 = bf16[16,4608]{1,0:T(8,128)(2,1)S(1)} collective-permute-done((bf16[16,4608]{1,0:T(8,128)(2,1)S(1)}, bf16[16,4608]{1,0:T(8,128)(2,1)S(1)}, u32[]{:S(2)}, u32[]{:S(2)}) %collective-permute-start.20) | collective-permute-done | bytes 147488 | tf_op jit(solution)/shard_map/ppermute | solution.py:36
  392.7 6.0 collective-permute-done.23
  398.8 6.4 %collective-permute-done.22 = bf16[16,4608]{1,0:T(8,128)(2,1)S(1)} collective-permute-done((bf16[16,4608]{1,0:T(8,128)(2,1)S(1)}, bf16[16,4608]{1,0:T(8,128)(2,1)S(1)}, u32[]{:S(2)}, u32[]{:S(2)}) %collective-permute-start.22) | collective-permute-done | bytes 147488 | tf_op jit(solution)/shard_map/ppermute | solution.py:36
  413.7 6.0 collective-permute-done.25
  419.8 6.6 %collective-permute-done.24 = bf16[16,4608]{1,0:T(8,128)(2,1)S(1)} collective-permute-done((bf16[16,4608]{1,0:T(8,128)(2,1)S(1)}, bf16[16,4608]{1,0:T(8,128)(2,1)S(1)}, u32[]{:S(2)}, u32[]{:S(2)}) %collective-permute-start.24) | collective-permute-done | bytes 147488 | tf_op jit(solution)/shard_map/ppermute | solution.py:36
  427.7 2.8 all-gather.8
  433.8 2.1 collective-permute-start.26
  436.0 6.1 collective-permute-done.27
  442.0 6.8 %collective-permute-done.26 = bf16[16,4608]{1,0:T(8,128)(2,1)S(1)} collective-permute-done((bf16[16,4608]{1,0:T(8,128)(2,1)S(1)}, bf16[16,4608]{1,0:T(8,128)(2,1)S(1)}, u32[]{:S(2)}, u32[]{:S(2)}) %collective-permute-start.26) | collective-permute-done | bytes 147488 | tf_op jit(solution)/shard_map/ppermute | solution.py:36
  457.2 6.0 collective-permute-done.29
  463.2 7.2 %collective-permute-done.28 = bf16[16,4608]{1,0:T(8,128)(2,1)S(1)} collective-permute-done((bf16[16,4608]{1,0:T(8,128)(2,1)S(1)}, bf16[16,4608]{1,0:T(8,128)(2,1)S(1)}, u32[]{:S(2)}, u32[]{:S(2)}) %collective-permute-start.28) | collective-permute-done | bytes 147488 | tf_op jit(solution)/shard_map/ppermute | solution.py:36
  478.9 6.0 collective-permute-done.31
  485.0 7.5 %collective-permute-done.30 = bf16[16,4608]{1,0:T(8,128)(2,1)S(1)} collective-permute-done((bf16[16,4608]{1,0:T(8,128)(2,1)S(1)}, bf16[16,4608]{1,0:T(8,128)(2,1)S(1)}, u32[]{:S(2)}, u32[]{:S(2)}) %collective-permute-start.30) | collective-permute-done | bytes 147488 | tf_op jit(solution)/shard_map/ppermute | solution.py:36
  500.8 6.0 collective-permute-done.33
  506.9 7.4 %collective-permute-done.32 = bf16[16,4608]{1,0:T(8,128)(2,1)S(1)} collective-permute-done((bf16[16,4608]{1,0:T(8,128)(2,1)S(1)}, bf16[16,4608]{1,0:T(8,128)(2,1)S(1)}, u32[]{:S(2)}, u32[]{:S(2)}) %collective-permute-start.32) | collective-permute-done | bytes 147488 | tf_op jit(solution)/shard_map/ppermute | solution.py:36
  522.7 6.0 collective-permute-done.35
  528.7 7.6 %collective-permute-done.34 = bf16[16,4608]{1,0:T(8,128)(2,1)S(1)} collective-permute-done((bf16[16,4608]{1,0:T(8,128)(2,1)S(1)}, bf16[16,4608]{1,0:T(8,128)(2,1)S(1)}, u32[]{:S(2)}, u32[]{:S(2)}) %collective-permute-start.34) | collective-permute-done | bytes 147488 | tf_op jit(solution)/shard_map/ppermute | solution.py:36
  544.7 6.0 collective-permute-done.37
  550.7 6.9 %collective-permute-done.36 = bf16[16,4608]{1,0:T(8,128)(2,1)S(1)} collective-permute-done((bf16[16,4608]{1,0:T(8,128)(2,1)S(1)}, bf16[16,4608]{1,0:T(8,128)(2,1)S(1)}, u32[]{:S(2)}, u32[]{:S(2)}) %collective-permute-start.36) | collective-permute-done | bytes 147488 | tf_op jit(solution)/shard_map/ppermute | solution.py:36
  559.0 2.2 all-gather.14
  566.5 6.2 %collective-permute-done.39 = bf16[16,4608]{1,0:T(8,128)(2,1)S(1)} collective-permute-done((bf16[16,4608]{1,0:T(8,128)(2,1)S(1)}, bf16[16,4608]{1,0:T(8,128)(2,1)S(1)}, u32[]{:S(2)}, u32[]{:S(2)}) %collective-permute-start.39) | collective-permute-done | bytes 147488 | tf_op jit(solution)/shard_map/ppermute | solution.py:36
  572.7 6.9 %collective-permute-done.38 = bf16[16,4608]{1,0:T(8,128)(2,1)S(1)} collective-permute-done((bf16[16,4608]{1,0:T(8,128)(2,1)S(1)}, bf16[16,4608]{1,0:T(8,128)(2,1)S(1)}, u32[]{:S(2)}, u32[]{:S(2)}) %collective-permute-start.38) | collective-permute-done | bytes 147488 | tf_op jit(solution)/shard_map/ppermute | solution.py:36
  587.0 11.2 %all-to-all-start.2 = ((bf16[16,4,2304]{2,1,0:T(4,128)(2,1)}), bf16[16,4,2304]{2,1,0:T(4,128)(2,1)S(1)}, u32[]{:S(2)}, u32[]{:S(2)}) async-start(bf16[16,4,2304]{2,1,0:T(4,128)(2,1)} %copy.107), calls=%async_computation.2 | async-start | bytes 589824 | tf_op jit(solution)/shard_map/all_to_all | solution.py:258
  598.2 15.5 %all-to-all-done.2 = bf16[16,4,2304]{2,1,0:T(4,128)(2,1)S(1)} async-done(((bf16[16,4,2304]{2,1,0:T(4,128)(2,1)}), bf16[16,4,2304]{2,1,0:T(4,128)(2,1)S(1)}, u32[]{:S(2)}, u32[]{:S(2)}) %all-to-all-start.2) | async-done | bytes 294944 | tf_op jit(solution)/shard_map/all_to_all | solution.py:258
  613.8 3.8 all_gather.123
  (187 shorter events, 147.5 us)
Async XLA Ops:
  0.0 22.6 %copy-start = (bf16[1,128,4608]{2,1,0:T(8,128)(2,1)S(1)}, bf16[1,128,4608]{2,1,0:T(8,128)(2,1)}, u32[]{:S(2)}) copy-start(bf16[1,128,4608]{2,1,0:T(8,128)(2,1)} %param.10) | copy-start | bytes 3538948
  1.7 16.7 %copy-start.27 = (f32[1,1,16,16]{3,2,1,0:T(8,128)S(1)}, f32[1,1,16,16]{3,2,1,0:T(8,128)}, u32[]{:S(2)}) copy-start(f32[1,1,16,16]{3,2,1,0:T(8,128)} %param.14) | copy-start | bytes 3076
  1.7 19.9 %copy-start.26 = (s32[1,4096]{1,0:T(1,128)S(1)}, s32[1,4096]{1,0:T(1,128)}, u32[]{:S(2)}) copy-start(s32[1,4096]{1,0:T(1,128)} %param.16) | copy-start | bytes 49156
  4.5 63.5 %collective-permute-start.1 = (bf16[256,4608]{1,0:T(8,128)(2,1)}, bf16[256,4608]{1,0:T(8,128)(2,1)}, u32[]{:S(2)}, u32[]{:S(2)}) collective-permute-start(bf16[256,4608]{1,0:T(8,128)(2,1)} %pad_maximum_fusion.mine_ref), channel_id=1, source_target_pairs={{0,28},{1,5},{4,0},{5,9},{8,4},{9,13},{12,8},{13,17},{16,12},{17,2... | collective-permute-start | bytes 7077896 | tf_op jit(solution)/shard_map/ppermute | solution.py:25
  7.7 60.3 %collective-permute-start = (bf16[256,4608]{1,0:T(8,128)(2,1)}, bf16[256,4608]{1,0:T(8,128)(2,1)}, u32[]{:S(2)}, u32[]{:S(2)}) collective-permute-start(bf16[256,4608]{1,0:T(8,128)(2,1)} %pad_maximum_fusion.mine_ref), channel_id=1, source_target_pairs={{0,2},{2,0},{1,3},{3,1},{4,6},{6,4},{5,7},{7,5},{8,10},{10,8},{9,1... | collective-permute-start | bytes 7077896 | tf_op jit(solution)/shard_map/ppermute | solution.py:189
  18.4 18.2 %collective-permute-start.2 = (f32[16,16]{1,0:T(8,128)S(1)}, f32[16,16]{1,0:T(8,128)S(1)}, u32[]{:S(2)}, u32[]{:S(2)}) collective-permute-start(f32[16,16]{1,0:T(8,128)S(1)} %bitcast.138), channel_id=1, source_target_pairs={{0,28},{1,5},{4,0},{5,9},{8,4},{9,13},{12,8},{13,17},{16,12},{17,2... | collective-permute-start | bytes 3080 | tf_op jit(solution)/shard_map/ppermute | solution.py:25
  26.1 21.1 %copy-start.25 = (bf16[1,128,4608]{2,1,0:T(8,128)(2,1)S(1)}, bf16[1,128,4608]{2,1,0:T(8,128)(2,1)}, u32[]{:S(2)}) copy-start(bf16[1,128,4608]{2,1,0:T(8,128)(2,1)} %param.11) | copy-start | bytes 3538948
  29.5 115.8 %copy-start.31 = (s32[4]{0:T(128)S(1)}, s32[4]{0:T(128)}, u32[]{:S(2)}) copy-start(s32[4]{0:T(128)} %param.19) | copy-start | bytes 52
  36.6 31.5 %collective-permute-start.3 = (f32[2,16,16]{2,1,0:T(8,128)S(1)}, f32[2,16,16]{2,1,0:T(8,128)S(1)}, u32[]{:S(2)}, u32[]{:S(2)}) collective-permute-start(f32[2,16,16]{2,1,0:T(8,128)S(1)} %pad_maximum_fusion.3), channel_id=1, source_target_pairs={{0,2},{2,0},{1,3},{3,1},{4,6},{6,4},{5,7},{7,5},{8,10},{10,8},{9,1... | collective-permute-start | bytes 6152 | tf_op jit(solution)/shard_map/ppermute | solution.py:201
  68.0 107.9 %collective-permute-start.5 = (bf16[256,4608]{1,0:T(8,128)(2,1)}, bf16[256,4608]{1,0:T(8,128)(2,1)S(1)}, u32[]{:S(2)}, u32[]{:S(2)}) collective-permute-start(bf16[256,4608]{1,0:T(8,128)(2,1)} %pad_maximum_fusion.mine_ref), channel_id=1, source_target_pairs={{0,1},{1,0},{2,3},{3,2},{4,5},{5,4},{6,7},{7,6},{8,9},{9,8},{10,11... | collective-permute-start | bytes 7077896 | tf_op jit(solution)/shard_map/ppermute | solution.py:94
  73.4 109.4 %collective-permute-start.6 = (bf16[256,4608]{1,0:T(8,128)(2,1)}, bf16[256,4608]{1,0:T(8,128)(2,1)}, u32[]{:S(2)}, u32[]{:S(2)}) collective-permute-start(bf16[256,4608]{1,0:T(8,128)(2,1)} %collective-permute-done.1.mine_ref), channel_id=1, source_target_pairs={{0,1},{1,0},{2,3},{3,2},{4,5},{5,4},{6,7},{7,6},{8,9},{9,8},{10,11... | collective-permute-start | bytes 7077896 | tf_op jit(solution)/shard_map/ppermute | solution.py:94
  75.3 113.5 %collective-permute-start.7 = (bf16[256,4608]{1,0:T(8,128)(2,1)}, bf16[256,4608]{1,0:T(8,128)(2,1)}, u32[]{:S(2)}, u32[]{:S(2)}) collective-permute-start(bf16[256,4608]{1,0:T(8,128)(2,1)} %collective-permute-done.mine_ref), channel_id=1, source_target_pairs={{0,1},{1,0},{2,3},{3,2},{4,5},{5,4},{6,7},{7,6},{8,9},{9,8},{10,11... | collective-permute-start | bytes 7077896 | tf_op jit(solution)/shard_map/ppermute | solution.py:94
  77.7 117.2 %collective-permute-start.4 = (bf16[256,4608]{1,0:T(8,128)(2,1)}, bf16[256,4608]{1,0:T(8,128)(2,1)}, u32[]{:S(2)}, u32[]{:S(2)}) collective-permute-start(bf16[256,4608]{1,0:T(8,128)(2,1)} %collective-permute-done.mine_ref), channel_id=1, source_target_pairs={{0,28},{1,5},{4,0},{5,9},{8,4},{9,13},{12,8},{13,17},{16,12},{17,2... | collective-permute-start | bytes 7077896 | tf_op jit(solution)/shard_map/ppermute | solution.py:25
  83.1 87.4 %all-to-all-start = ((bf16[32,2,2304]{2,1,0:T(2,128)(2,1)}), bf16[32,2,2304]{2,1,0:T(2,128)(2,1)}, u32[]{:S(2)}, u32[]{:S(2)}) async-start(bf16[32,2,2304]{2,1,0:T(2,128)(2,1)} %reshape.202), calls=%async_computation | async-start | bytes 589824 | tf_op jit(solution)/shard_map/all_to_all | solution.py:209
  146.0 3.1 collective-permute-start.8
  195.0 9.7 %copy-start.29 = (f32[1,16]{1,0:T(1,128)S(1)}, f32[1,16]{1,0:T(1,128)}, u32[]{:S(2)}) copy-start(f32[1,16]{1,0:T(1,128)} %param.15) | copy-start | bytes 196
  195.0 151.3 %all-to-all-start.1 = ((bf16[32,8,4608]{2,1,0:T(8,128)(2,1)}), bf16[32,8,4608]{2,1,0:T(8,128)(2,1)}, u32[]{:S(2)}, u32[]{:S(2)}) async-start(bf16[32,8,4608]{2,1,0:T(8,128)(2,1)} %bitcast_select_fusion), calls=%async_computation.1 | async-start | bytes 4718592 | tf_op jit(solution)/shard_map/all_to_all | solution.py:228
  202.5 6.8 %collective-permute-start.9 = (bf16[256,4608]{1,0:T(8,128)(2,1)}, bf16[256,4608]{1,0:T(8,128)(2,1)}, u32[]{:S(2)}, u32[]{:S(2)}) collective-permute-start(bf16[256,4608]{1,0:T(8,128)(2,1)} %collective-permute-done.4.mine_ref), channel_id=1, source_target_pairs={{0,1},{1,0},{2,3},{3,2},{4,5},{5,4},{6,7},{7,6},{8,9},{9,8},{10,11... | collective-permute-start | bytes 7077896 | tf_op jit(solution)/shard_map/ppermute | solution.py:94
  204.8 7.7 %copy-start.3 = (bf16[4608,256]{1,0:T(8,128)(2,1)S(1)}, bf16[4608,256]{1,0:T(8,128)(2,1)}, u32[]{:S(2)}) copy-start(bf16[4608,256]{1,0:T(8,128)(2,1)} %copy-done.2) | copy-start | bytes 7077892
  204.8 7.7 %copy-start.6 = (bf16[4608,256]{1,0:T(8,128)(2,1)S(1)}, bf16[4608,256]{1,0:T(8,128)(2,1)}, u32[]{:S(2)}) copy-start(bf16[4608,256]{1,0:T(8,128)(2,1)} %copy-done.5) | copy-start | bytes 7077892
  212.4 124.6 %copy-start.8 = (bf16[4608,256]{1,0:T(8,128)(2,1)}, bf16[4608,256]{1,0:T(8,128)(2,1)S(1)}, u32[]{:S(2)}) copy-start(bf16[4608,256]{1,0:T(8,128)(2,1)S(1)} %get-tuple-element.96.refs_3_) | copy-start | bytes 7077892
  212.4 127.8 %copy-start.19 = (bf16[256,4608]{1,0:T(8,128)(2,1)}, bf16[256,4608]{1,0:T(8,128)(2,1)S(1)}, u32[]{:S(2)}) copy-start(bf16[256,4608]{1,0:T(8,128)(2,1)S(1)} %get-tuple-element.104.refs_3_) | copy-start | bytes 7077892
  218.8 48.6 %collective-permute-start.11 = (bf16[16,4608]{1,0:T(8,128)(2,1)S(1)}, bf16[16,4608]{1,0:T(8,128)(2,1)S(1)}, u32[]{:S(2)}, u32[]{:S(2)}) collective-permute-start(bf16[16,4608]{1,0:T(8,128)(2,1)S(1)} %head_terms.15), channel_id=1, source_target_pairs={{32,0},{33,25},{40,8},{41,1},{48,16},{49,9},{56,24},{57,17},{64,32... | collective-permute-start | bytes 442376 | tf_op jit(solution)/shard_map/ppermute | solution.py:36
  224.5 42.9 %collective-permute-start.10 = (bf16[16,4608]{1,0:T(8,128)(2,1)S(1)}, bf16[16,4608]{1,0:T(8,128)(2,1)S(1)}, u32[]{:S(2)}, u32[]{:S(2)}) collective-permute-start(bf16[16,4608]{1,0:T(8,128)(2,1)S(1)} %head_terms.15), channel_id=1, source_target_pairs={{32,17},{33,8},{40,25},{41,16},{48,1},{49,24},{56,9},{57,0},{64,49... | collective-permute-start | bytes 442376 | tf_op jit(solution)/shard_map/ppermute | solution.py:36
  272.0 9.9 %collective-permute-start.13 = (bf16[16,4608]{1,0:T(8,128)(2,1)S(1)}, bf16[16,4608]{1,0:T(8,128)(2,1)S(1)}, u32[]{:S(2)}, u32[]{:S(2)}) collective-permute-start(bf16[16,4608]{1,0:T(8,128)(2,1)S(1)} %head_terms.16), channel_id=1, source_target_pairs={{32,0},{33,25},{40,8},{41,1},{48,16},{49,9},{56,24},{57,17},{64,32... | collective-permute-start | bytes 442376 | tf_op jit(solution)/shard_map/ppermute | solution.py:36
  276.4 13.4 %collective-permute-start.12 = (bf16[16,4608]{1,0:T(8,128)(2,1)S(1)}, bf16[16,4608]{1,0:T(8,128)(2,1)S(1)}, u32[]{:S(2)}, u32[]{:S(2)}) collective-permute-start(bf16[16,4608]{1,0:T(8,128)(2,1)S(1)} %head_terms.16), channel_id=1, source_target_pairs={{32,17},{33,8},{40,25},{41,16},{48,1},{49,24},{56,9},{57,0},{64,49... | collective-permute-start | bytes 442376 | tf_op jit(solution)/shard_map/ppermute | solution.py:36
  294.4 9.9 %collective-permute-start.15 = (bf16[16,4608]{1,0:T(8,128)(2,1)S(1)}, bf16[16,4608]{1,0:T(8,128)(2,1)S(1)}, u32[]{:S(2)}, u32[]{:S(2)}) collective-permute-start(bf16[16,4608]{1,0:T(8,128)(2,1)S(1)} %head_terms.17), channel_id=1, source_target_pairs={{32,0},{33,25},{40,8},{41,1},{48,16},{49,9},{56,24},{57,17},{64,32... | collective-permute-start | bytes 442376 | tf_op jit(solution)/shard_map/ppermute | solution.py:36
  300.5 16.1 %collective-permute-start.14 = (bf16[16,4608]{1,0:T(8,128)(2,1)S(1)}, bf16[16,4608]{1,0:T(8,128)(2,1)S(1)}, u32[]{:S(2)}, u32[]{:S(2)}) collective-permute-start(bf16[16,4608]{1,0:T(8,128)(2,1)S(1)} %head_terms.17), channel_id=1, source_target_pairs={{32,17},{33,8},{40,25},{41,16},{48,1},{49,24},{56,9},{57,0},{64,49... | collective-permute-start | bytes 442376 | tf_op jit(solution)/shard_map/ppermute | solution.py:36
  321.1 10.3 %collective-permute-start.17 = (bf16[16,4608]{1,0:T(8,128)(2,1)S(1)}, bf16[16,4608]{1,0:T(8,128)(2,1)S(1)}, u32[]{:S(2)}, u32[]{:S(2)}) collective-permute-start(bf16[16,4608]{1,0:T(8,128)(2,1)S(1)} %head_terms.18), channel_id=1, source_target_pairs={{32,0},{33,25},{40,8},{41,1},{48,16},{49,9},{56,24},{57,17},{64,32... | collective-permute-start | bytes 442376 | tf_op jit(solution)/shard_map/ppermute | solution.py:36
  323.0 14.0 %collective-permute-start.16 = (bf16[16,4608]{1,0:T(8,128)(2,1)S(1)}, bf16[16,4608]{1,0:T(8,128)(2,1)S(1)}, u32[]{:S(2)}, u32[]{:S(2)}) collective-permute-start(bf16[16,4608]{1,0:T(8,128)(2,1)S(1)} %head_terms.18), channel_id=1, source_target_pairs={{32,17},{33,8},{40,25},{41,16},{48,1},{49,24},{56,9},{57,0},{64,49... | collective-permute-start | bytes 442376 | tf_op jit(solution)/shard_map/ppermute | solution.py:36
  342.3 12.1 %collective-permute-start.19 = (bf16[16,4608]{1,0:T(8,128)(2,1)}, bf16[16,4608]{1,0:T(8,128)(2,1)}, u32[]{:S(2)}, u32[]{:S(2)}) collective-permute-start(bf16[16,4608]{1,0:T(8,128)(2,1)} %head_terms.19), channel_id=1, source_target_pairs={{32,0},{33,25},{40,8},{41,1},{48,16},{49,9},{56,24},{57,17},{64,32... | collective-permute-start | bytes 442376 | tf_op jit(solution)/shard_map/ppermute | solution.py:36
  344.2 16.4 %collective-permute-start.18 = (bf16[16,4608]{1,0:T(8,128)(2,1)}, bf16[16,4608]{1,0:T(8,128)(2,1)}, u32[]{:S(2)}, u32[]{:S(2)}) collective-permute-start(bf16[16,4608]{1,0:T(8,128)(2,1)} %head_terms.19), channel_id=1, source_target_pairs={{32,17},{33,8},{40,25},{41,16},{48,1},{49,24},{56,9},{57,0},{64,49... | collective-permute-start | bytes 442376 | tf_op jit(solution)/shard_map/ppermute | solution.py:36
  351.7 8.9 %copy-start.4 = (bf16[4608,256]{1,0:T(8,128)(2,1)S(1)}, bf16[4608,256]{1,0:T(8,128)(2,1)}, u32[]{:S(2)}) copy-start(bf16[4608,256]{1,0:T(8,128)(2,1)} %copy-done.2) | copy-start | bytes 7077892
  360.6 6.0 copy-start.12
  360.6 6.0 copy-start.15
  360.6 6.0 copy-start.18
  360.6 6.0 copy-start.20
  366.6 17.7 %copy-start.7 = (bf16[4608,256]{1,0:T(8,128)(2,1)S(1)}, bf16[4608,256]{1,0:T(8,128)(2,1)}, u32[]{:S(2)}) copy-start(bf16[4608,256]{1,0:T(8,128)(2,1)} %copy-done.5) | copy-start | bytes 7077892
  366.6 17.7 %copy-start.9 = (bf16[4608,256]{1,0:T(8,128)(2,1)S(1)}, bf16[4608,256]{1,0:T(8,128)(2,1)}, u32[]{:S(2)}) copy-start(bf16[4608,256]{1,0:T(8,128)(2,1)} %copy-done.8) | copy-start | bytes 7077892
  368.0 10.1 %collective-permute-start.21 = (bf16[16,4608]{1,0:T(8,128)(2,1)S(1)}, bf16[16,4608]{1,0:T(8,128)(2,1)S(1)}, u32[]{:S(2)}, u32[]{:S(2)}) collective-permute-start(bf16[16,4608]{1,0:T(8,128)(2,1)S(1)} %head_terms.20), channel_id=1, source_target_pairs={{32,0},{33,25},{40,8},{41,1},{48,16},{49,9},{56,24},{57,17},{64,32... | collective-permute-start | bytes 442376 | tf_op jit(solution)/shard_map/ppermute | solution.py:36
  370.1 14.3 %collective-permute-start.20 = (bf16[16,4608]{1,0:T(8,128)(2,1)S(1)}, bf16[16,4608]{1,0:T(8,128)(2,1)S(1)}, u32[]{:S(2)}, u32[]{:S(2)}) collective-permute-start(bf16[16,4608]{1,0:T(8,128)(2,1)S(1)} %head_terms.20), channel_id=1, source_target_pairs={{32,17},{33,8},{40,25},{41,16},{48,1},{49,24},{56,9},{57,0},{64,49... | collective-permute-start | bytes 442376 | tf_op jit(solution)/shard_map/ppermute | solution.py:36
  388.9 9.9 %collective-permute-start.23 = (bf16[16,4608]{1,0:T(8,128)(2,1)S(1)}, bf16[16,4608]{1,0:T(8,128)(2,1)S(1)}, u32[]{:S(2)}, u32[]{:S(2)}) collective-permute-start(bf16[16,4608]{1,0:T(8,128)(2,1)S(1)} %head_terms.21), channel_id=1, source_target_pairs={{32,0},{33,25},{40,8},{41,1},{48,16},{49,9},{56,24},{57,17},{64,32... | collective-permute-start | bytes 442376 | tf_op jit(solution)/shard_map/ppermute | solution.py:36
  390.8 14.3 %collective-permute-start.22 = (bf16[16,4608]{1,0:T(8,128)(2,1)S(1)}, bf16[16,4608]{1,0:T(8,128)(2,1)S(1)}, u32[]{:S(2)}, u32[]{:S(2)}) collective-permute-start(bf16[16,4608]{1,0:T(8,128)(2,1)S(1)} %head_terms.21), channel_id=1, source_target_pairs={{32,17},{33,8},{40,25},{41,16},{48,1},{49,24},{56,9},{57,0},{64,49... | collective-permute-start | bytes 442376 | tf_op jit(solution)/shard_map/ppermute | solution.py:36
  409.9 9.9 %collective-permute-start.25 = (bf16[16,4608]{1,0:T(8,128)(2,1)S(1)}, bf16[16,4608]{1,0:T(8,128)(2,1)S(1)}, u32[]{:S(2)}, u32[]{:S(2)}) collective-permute-start(bf16[16,4608]{1,0:T(8,128)(2,1)S(1)} %head_terms.22), channel_id=1, source_target_pairs={{32,0},{33,25},{40,8},{41,1},{48,16},{49,9},{56,24},{57,17},{64,32... | collective-permute-start | bytes 442376 | tf_op jit(solution)/shard_map/ppermute | solution.py:36
  411.8 14.6 %collective-permute-start.24 = (bf16[16,4608]{1,0:T(8,128)(2,1)S(1)}, bf16[16,4608]{1,0:T(8,128)(2,1)S(1)}, u32[]{:S(2)}, u32[]{:S(2)}) collective-permute-start(bf16[16,4608]{1,0:T(8,128)(2,1)S(1)} %head_terms.22), channel_id=1, source_target_pairs={{32,17},{33,8},{40,25},{41,16},{48,1},{49,24},{56,9},{57,0},{64,49... | collective-permute-start | bytes 442376 | tf_op jit(solution)/shard_map/ppermute | solution.py:36
  431.9 10.1 %collective-permute-start.27 = (bf16[16,4608]{1,0:T(8,128)(2,1)S(1)}, bf16[16,4608]{1,0:T(8,128)(2,1)S(1)}, u32[]{:S(2)}, u32[]{:S(2)}) collective-permute-start(bf16[16,4608]{1,0:T(8,128)(2,1)S(1)} %head_terms.23), channel_id=1, source_target_pairs={{32,0},{33,25},{40,8},{41,1},{48,16},{49,9},{56,24},{57,17},{64,32... | collective-permute-start | bytes 442376 | tf_op jit(solution)/shard_map/ppermute | solution.py:36
  433.8 15.0 %collective-permute-start.26 = (bf16[16,4608]{1,0:T(8,128)(2,1)S(1)}, bf16[16,4608]{1,0:T(8,128)(2,1)S(1)}, u32[]{:S(2)}, u32[]{:S(2)}) collective-permute-start(bf16[16,4608]{1,0:T(8,128)(2,1)S(1)} %head_terms.23), channel_id=1, source_target_pairs={{32,17},{33,8},{40,25},{41,16},{48,1},{49,24},{56,9},{57,0},{64,49... | collective-permute-start | bytes 442376 | tf_op jit(solution)/shard_map/ppermute | solution.py:36
  453.4 9.9 %collective-permute-start.29 = (bf16[16,4608]{1,0:T(8,128)(2,1)S(1)}, bf16[16,4608]{1,0:T(8,128)(2,1)S(1)}, u32[]{:S(2)}, u32[]{:S(2)}) collective-permute-start(bf16[16,4608]{1,0:T(8,128)(2,1)S(1)} %head_terms.24), channel_id=1, source_target_pairs={{32,0},{33,25},{40,8},{41,1},{48,16},{49,9},{56,24},{57,17},{64,32... | collective-permute-start | bytes 442376 | tf_op jit(solution)/shard_map/ppermute | solution.py:36
  455.3 15.2 %collective-permute-start.28 = (bf16[16,4608]{1,0:T(8,128)(2,1)S(1)}, bf16[16,4608]{1,0:T(8,128)(2,1)S(1)}, u32[]{:S(2)}, u32[]{:S(2)}) collective-permute-start(bf16[16,4608]{1,0:T(8,128)(2,1)S(1)} %head_terms.24), channel_id=1, source_target_pairs={{32,17},{33,8},{40,25},{41,16},{48,1},{49,24},{56,9},{57,0},{64,49... | collective-permute-start | bytes 442376 | tf_op jit(solution)/shard_map/ppermute | solution.py:36
  475.1 9.9 %collective-permute-start.31 = (bf16[16,4608]{1,0:T(8,128)(2,1)S(1)}, bf16[16,4608]{1,0:T(8,128)(2,1)S(1)}, u32[]{:S(2)}, u32[]{:S(2)}) collective-permute-start(bf16[16,4608]{1,0:T(8,128)(2,1)S(1)} %head_terms.25), channel_id=1, source_target_pairs={{32,0},{33,25},{40,8},{41,1},{48,16},{49,9},{56,24},{57,17},{64,32... | collective-permute-start | bytes 442376 | tf_op jit(solution)/shard_map/ppermute | solution.py:36
  477.0 15.4 %collective-permute-start.30 = (bf16[16,4608]{1,0:T(8,128)(2,1)S(1)}, bf16[16,4608]{1,0:T(8,128)(2,1)S(1)}, u32[]{:S(2)}, u32[]{:S(2)}) collective-permute-start(bf16[16,4608]{1,0:T(8,128)(2,1)S(1)} %head_terms.25), channel_id=1, source_target_pairs={{32,17},{33,8},{40,25},{41,16},{48,1},{49,24},{56,9},{57,0},{64,49... | collective-permute-start | bytes 442376 | tf_op jit(solution)/shard_map/ppermute | solution.py:36
  497.0 9.9 %collective-permute-start.33 = (bf16[16,4608]{1,0:T(8,128)(2,1)S(1)}, bf16[16,4608]{1,0:T(8,128)(2,1)S(1)}, u32[]{:S(2)}, u32[]{:S(2)}) collective-permute-start(bf16[16,4608]{1,0:T(8,128)(2,1)S(1)} %head_terms.26), channel_id=1, source_target_pairs={{32,0},{33,25},{40,8},{41,1},{48,16},{49,9},{56,24},{57,17},{64,32... | collective-permute-start | bytes 442376 | tf_op jit(solution)/shard_map/ppermute | solution.py:36
  498.9 15.3 %collective-permute-start.32 = (bf16[16,4608]{1,0:T(8,128)(2,1)S(1)}, bf16[16,4608]{1,0:T(8,128)(2,1)S(1)}, u32[]{:S(2)}, u32[]{:S(2)}) collective-permute-start(bf16[16,4608]{1,0:T(8,128)(2,1)S(1)} %head_terms.26), channel_id=1, source_target_pairs={{32,17},{33,8},{40,25},{41,16},{48,1},{49,24},{56,9},{57,0},{64,49... | collective-permute-start | bytes 442376 | tf_op jit(solution)/shard_map/ppermute | solution.py:36
  518.8 9.9 %collective-permute-start.35 = (bf16[16,4608]{1,0:T(8,128)(2,1)S(1)}, bf16[16,4608]{1,0:T(8,128)(2,1)S(1)}, u32[]{:S(2)}, u32[]{:S(2)}) collective-permute-start(bf16[16,4608]{1,0:T(8,128)(2,1)S(1)} %head_terms.27), channel_id=1, source_target_pairs={{32,0},{33,25},{40,8},{41,1},{48,16},{49,9},{56,24},{57,17},{64,32... | collective-permute-start | bytes 442376 | tf_op jit(solution)/shard_map/ppermute | solution.py:36
  520.8 15.5 %collective-permute-start.34 = (bf16[16,4608]{1,0:T(8,128)(2,1)S(1)}, bf16[16,4608]{1,0:T(8,128)(2,1)S(1)}, u32[]{:S(2)}, u32[]{:S(2)}) collective-permute-start(bf16[16,4608]{1,0:T(8,128)(2,1)S(1)} %head_terms.27), channel_id=1, source_target_pairs={{32,17},{33,8},{40,25},{41,16},{48,1},{49,24},{56,9},{57,0},{64,49... | collective-permute-start | bytes 442376 | tf_op jit(solution)/shard_map/ppermute | solution.py:36
  540.8 9.9 %collective-permute-start.37 = (bf16[16,4608]{1,0:T(8,128)(2,1)S(1)}, bf16[16,4608]{1,0:T(8,128)(2,1)S(1)}, u32[]{:S(2)}, u32[]{:S(2)}) collective-permute-start(bf16[16,4608]{1,0:T(8,128)(2,1)S(1)} %head_terms.28), channel_id=1, source_target_pairs={{32,0},{33,25},{40,8},{41,1},{48,16},{49,9},{56,24},{57,17},{64,32... | collective-permute-start | bytes 442376 | tf_op jit(solution)/shard_map/ppermute | solution.py:36
  542.8 14.9 %collective-permute-start.36 = (bf16[16,4608]{1,0:T(8,128)(2,1)S(1)}, bf16[16,4608]{1,0:T(8,128)(2,1)S(1)}, u32[]{:S(2)}, u32[]{:S(2)}) collective-permute-start(bf16[16,4608]{1,0:T(8,128)(2,1)S(1)} %head_terms.28), channel_id=1, source_target_pairs={{32,17},{33,8},{40,25},{41,16},{48,1},{49,24},{56,9},{57,0},{64,49... | collective-permute-start | bytes 442376 | tf_op jit(solution)/shard_map/ppermute | solution.py:36
  562.5 55.1 %copy-start.24 = (bf16[128,4608]{1,0:T(8,128)(2,1)S(1)}, bf16[128,4608]{1,0:T(8,128)(2,1)}, u32[]{:S(2)}) copy-start(bf16[128,4608]{1,0:T(8,128)(2,1)} %broadcast_select_fusion) | copy-start | bytes 3538948
  562.5 10.2 %collective-permute-start.39 = (bf16[16,4608]{1,0:T(8,128)(2,1)S(1)}, bf16[16,4608]{1,0:T(8,128)(2,1)S(1)}, u32[]{:S(2)}, u32[]{:S(2)}) collective-permute-start(bf16[16,4608]{1,0:T(8,128)(2,1)S(1)} %head_terms.29), channel_id=1, source_target_pairs={{32,0},{33,25},{40,8},{41,1},{48,16},{49,9},{56,24},{57,17},{64,32... | collective-permute-start | bytes 442376 | tf_op jit(solution)/shard_map/ppermute | solution.py:36
  564.5 15.1 %collective-permute-start.38 = (bf16[16,4608]{1,0:T(8,128)(2,1)S(1)}, bf16[16,4608]{1,0:T(8,128)(2,1)S(1)}, u32[]{:S(2)}, u32[]{:S(2)}) collective-permute-start(bf16[16,4608]{1,0:T(8,128)(2,1)S(1)} %head_terms.29), channel_id=1, source_target_pairs={{32,17},{33,8},{40,25},{41,16},{48,1},{49,24},{56,9},{57,0},{64,49... | collective-permute-start | bytes 442376 | tf_op jit(solution)/shard_map/ppermute | solution.py:36
  581.4 3.5 collective-permute-start.40
  584.9 34.0 %copy-start.1 = (bf16[1,128,4608]{2,1,0:T(8,128)(2,1)S(1)}, bf16[1,128,4608]{2,1,0:T(8,128)(2,1)}, u32[]{:S(2)}) copy-start(bf16[1,128,4608]{2,1,0:T(8,128)(2,1)} %param.10) | copy-start | bytes 3538948
  586.1 32.2 %copy-start.28 = (f32[1,128]{1,0:T(1,128)S(1)}, f32[1,128]{1,0:T(1,128)}, u32[]{:S(2)}) copy-start(f32[1,128]{1,0:T(1,128)} %param.17) | copy-start | bytes 1540
  587.0 26.7 %all-to-all-start.2 = ((bf16[16,4,2304]{2,1,0:T(4,128)(2,1)}), bf16[16,4,2304]{2,1,0:T(4,128)(2,1)S(1)}, u32[]{:S(2)}, u32[]{:S(2)}) async-start(bf16[16,4,2304]{2,1,0:T(4,128)(2,1)} %copy.107), calls=%async_computation.2 | async-start | bytes 589824 | tf_op jit(solution)/shard_map/all_to_all | solution.py:258
  (12 other events, 26.4 us)

commit v6 on v5

--- a/solution.py
+++ b/solution.py
@@ -187,7 +187,6 @@
     own = jnp.concatenate([out_proj[0], value_proj[0].T], axis=0)
     own_mix = attention[0, 0]
     beyond = lax.ppermute(own, "zh", SWAP)
-    near = neighbour_heads(own)
 
     feat_iota = jnp.arange(feat_rows, dtype=jnp.int32)
     target_pick = (
@@ -198,12 +197,14 @@
         enc_rows[None, :, None, :], (QUADS, targets, 2, model_width)
     ).reshape(feat_count, model_width)
     near_mix = neighbour_heads(own_mix)
+    own, near_mix = lax.optimization_barrier((own, near_mix))
+    near = neighbour_heads(own)
     zh_mix = lax.ppermute(jnp.stack([own_mix, near_mix]), "zh", SWAP)
     outgoing, flat_index = panel_route(
         decoders[0], act_ids[0], entries_dev, feat_index, feat_count
     )
-    own, beyond, near, near_mix, zh_mix, outgoing, enc_send = lax.optimization_barrier(
-        (own, beyond, near, near_mix, zh_mix, outgoing, enc_send)
+    beyond, outgoing, near_mix, zh_mix = lax.optimization_barrier(
+        (beyond, outgoing, near_mix, zh_mix)
     )
     far = neighbour_heads(beyond)
     enc_got = lax.all_to_all(enc_send, FEAT, split_axis=0, concat_axis=0, tiled=True)
@@ -222,8 +223,8 @@
         mixing.transpose(1, 2, 0)[..., None], (seq_len, seq_len, heads, head_width)
     ).reshape(seq_len, seq_len, heads * head_width)
     quarter = (start * 0.25).astype(BF)
-    far, groups, mix_wide, quarter, outgoing = lax.optimization_barrier(
-        (far, groups, mix_wide, quarter, outgoing)
+    far, groups, mix_wide, outgoing = lax.optimization_barrier(
+        (far, groups, mix_wide, outgoing)
     )
     incoming = lax.all_to_all(outgoing, FEAT, split_axis=0, concat_axis=0, tiled=True)
     panel = jnp.take(incoming.reshape(-1, model_width), flat_index, axis=0)

time: 629 us -> 609 us (0.968)
  waiting for transfers between devices: 282 us -> 255 us
    all_to_all x1, waiting for transfers between devices: 18.6 us -> 0.52 us  [per_device(): lax.all_to_all(enc_send, FEAT, split_axis=0, concat_axis=0, tiled=True)]
    ppermute x1, starting transfers between devices: 10.6 us -> 2.05 us  [per_device(): zh_mix = lax.ppermute(jnp.stack([own_mix, near_mix]), 'zh', SWAP)]
    ppermute x1, waiting for transfers between devices: 20.2 us -> 28.1 us  [per_device(): zh_mix = lax.ppermute(jnp.stack([own_mix, near_mix]), 'zh', SWAP)]
    ppermute x3, waiting for transfers between devices: 7.06 us -> 0.01 us  [neighbour_heads(): return lax.ppermute(shard, ('y2', 'par', 'core'), pairs)]
    unnamed x68 -> x74, local copies, waits for them, and re-layouts: 17.5 us -> 16.6 us
  transfers between devices with their start and end apart: 44 -> 44, of which waited for: 35 -> 32; matrix products, arithmetic and copies ran while one was open for 6% -> 7% of each run, Pallas kernels for 3% -> 3%
where the time goes in v6:
time: 609 us; the launch traced here: 598 us
  waiting for transfers between devices  255 us (42%)
  starting transfers between devices  196 us (32%)
  local copies, waits for them, and re-layouts  54.4 us (9%)
  blocking collectives  36.4 us (6%)
  Pallas kernels  34.3 us (6%)
  other arithmetic  18.9 us (3%)
    ppermute x30, waiting for transfers between devices, send_down(): return lax.ppermute(shard, ('section', 'y2', 'core'), pairs)  210 us
    ppermute x30, starting transfers between devices, send_down(): return lax.ppermute(shard, ('section', 'y2', 'core'), pairs)  67.4 us
    all_to_all x1, starting transfers between devices, per_device(): lax.all_to_all(enc_send, FEAT, split_axis=0, concat_axis=0, tiled=True)  62.2 us
    all_gather x15, blocking collectives, per_device(): grads = lax.all_gather(grad_part, 'core', axis=0)  32.6 us
    ppermute x1, waiting for transfers between devices, per_device(): zh_mix = lax.ppermute(jnp.stack([own_mix, near_mix]), 'zh', SWAP)  28.1 us
    pallas_call x14, local copies, waits for them, and re-layouts, head_grads(): pl.pallas_call(grads_kernel, out_shape=(jax.ShapeDtypeStruct((seq_len, mo...  21.3 us
    pallas_call x15, Pallas kernels, head_terms(): pl.pallas_call(terms_kernel, out_shape=jax.ShapeDtypeStruct(part.shape, B...  20.8 us
    unnamed x74, local copies, waits for them, and re-layouts  16.6 us
  transfers between devices with their start and end apart: 44, of which 32 were waited for; matrix products, arithmetic and copies ran while one was open for 7% of the time, Pallas kernels for 3%

profile of v6, /device:TPU:7, one launch (start us, length us, event | category | flops | bytes accessed | tf_op | source)
XLA Modules:
  0.0 598.0 jit_solution(7812724458077137880)
XLA Ops:
  0.0 3.3 collective-permute-start.1
  3.3 2.4 copy.89
  7.5 10.6 %collective-permute-start = (bf16[256,4608]{1,0:T(8,128)(2,1)S(1)}, bf16[256,4608]{1,0:T(8,128)(2,1)}, u32[]{:S(2)}, u32[]{:S(2)}) collective-permute-start(bf16[256,4608]{1,0:T(8,128)(2,1)S(1)} %pad_maximum_fusion.mine_ref), channel_id=1, source_target_pairs={{0,2},{2,0},{1,3},{3,1},{4,6},{6,4},{5,7},{7,5},{8,10},{10,8},{9,1... | collective-permute-start | bytes 7077896 | tf_op jit(solution)/shard_map/ppermute | solution.py:189
  18.8 3.2 collective-permute-start.5
  24.8 3.6 gather_fusion
  28.3 5.1 collective-permute-start.4
  36.2 3.3 bitcast_select_fusion
  39.6 28.1 %collective-permute-done.2 = f32[2,16,16]{2,1,0:T(8,128)S(1)} collective-permute-done((f32[2,16,16]{2,1,0:T(8,128)S(1)}, f32[2,16,16]{2,1,0:T(8,128)S(1)}, u32[]{:S(2)}, u32[]{:S(2)}) %collective-permute-start.2) | collective-permute-done | bytes 2080 | tf_op jit(solution)/shard_map/ppermute | solution.py:202
  67.6 5.3 collective-permute-start.7
  74.9 3.3 collective-permute-start.3
  79.6 2.4 reduce.1
  82.8 62.2 %all-to-all-start = ((bf16[32,2,2304]{2,1,0:T(2,128)(2,1)}), bf16[32,2,2304]{2,1,0:T(2,128)(2,1)}, u32[]{:S(2)}, u32[]{:S(2)}) async-start(bf16[32,2,2304]{2,1,0:T(2,128)(2,1)} %reshape.200), calls=%async_computation | async-start | bytes 589824 | tf_op jit(solution)/shard_map/all_to_all | solution.py:210
  145.7 2.2 collective-permute-start.8
  149.6 2.5 turn_heads.4
  155.1 3.2 turn_heads.6
  161.2 3.2 turn_heads.5
  167.8 11.7 %all-to-all-start.1 = ((bf16[32,8,4608]{2,1,0:T(8,128)(2,1)}), bf16[32,8,4608]{2,1,0:T(8,128)(2,1)}, u32[]{:S(2)}, u32[]{:S(2)}) async-start(bf16[32,8,4608]{2,1,0:T(8,128)(2,1)} %bitcast_select_fusion), calls=%async_computation.1 | async-start | bytes 4718592 | tf_op jit(solution)/shard_map/all_to_all | solution.py:229
  179.5 2.4 collective-permute-start.9
  183.3 2.3 reshape.201
  186.3 3.3 turn_heads.7
  196.0 5.8 collective-permute-start.11
  204.4 40.0 %collective-permute-done.11 = bf16[16,4608]{1,0:T(8,128)(2,1)S(1)} collective-permute-done((bf16[16,4608]{1,0:T(8,128)(2,1)S(1)}, bf16[16,4608]{1,0:T(8,128)(2,1)S(1)}, u32[]{:S(2)}, u32[]{:S(2)}) %collective-permute-start.11) | collective-permute-done | bytes 147488 | tf_op jit(solution)/shard_map/ppermute | solution.py:36
  249.0 3.8 collective-permute-start.13
  255.6 3.3 collective-permute-done.13
  258.9 7.3 %collective-permute-done.12 = bf16[16,4608]{1,0:T(8,128)(2,1)S(1)} collective-permute-done((bf16[16,4608]{1,0:T(8,128)(2,1)S(1)}, bf16[16,4608]{1,0:T(8,128)(2,1)S(1)}, u32[]{:S(2)}, u32[]{:S(2)}) %collective-permute-start.12) | collective-permute-done | bytes 147488 | tf_op jit(solution)/shard_map/ppermute | solution.py:36
  270.8 5.6 collective-permute-start.15
  280.7 11.4 %collective-permute-done.14 = bf16[16,4608]{1,0:T(8,128)(2,1)S(1)} collective-permute-done((bf16[16,4608]{1,0:T(8,128)(2,1)S(1)}, bf16[16,4608]{1,0:T(8,128)(2,1)S(1)}, u32[]{:S(2)}, u32[]{:S(2)}) %collective-permute-start.14) | collective-permute-done | bytes 147488 | tf_op jit(solution)/shard_map/ppermute | solution.py:36
  301.2 5.3 collective-permute-done.17
  306.5 7.0 %collective-permute-done.16 = bf16[16,4608]{1,0:T(8,128)(2,1)S(1)} collective-permute-done((bf16[16,4608]{1,0:T(8,128)(2,1)S(1)}, bf16[16,4608]{1,0:T(8,128)(2,1)S(1)}, u32[]{:S(2)}, u32[]{:S(2)}) %collective-permute-start.16) | collective-permute-done | bytes 147488 | tf_op jit(solution)/shard_map/ppermute | solution.py:36
  314.8 2.1 all-gather.4
  322.8 5.5 gather_fusion.1
  328.2 2.6 broadcast_select_fusion
  330.8 4.4 collective-permute-done.18
  335.3 4.0 head_grads.25
  339.3 2.9 all-gather.5
  343.6 2.0 collective-permute-start.21
  347.5 6.1 %collective-permute-done.21 = bf16[16,4608]{1,0:T(8,128)(2,1)S(1)} collective-permute-done((bf16[16,4608]{1,0:T(8,128)(2,1)S(1)}, bf16[16,4608]{1,0:T(8,128)(2,1)S(1)}, u32[]{:S(2)}, u32[]{:S(2)}) %collective-permute-start.21) | collective-permute-done | bytes 147488 | tf_op jit(solution)/shard_map/ppermute | solution.py:36
  353.6 6.8 %collective-permute-done.20 = bf16[16,4608]{1,0:T(8,128)(2,1)S(1)} collective-permute-done((bf16[16,4608]{1,0:T(8,128)(2,1)S(1)}, bf16[16,4608]{1,0:T(8,128)(2,1)S(1)}, u32[]{:S(2)}, u32[]{:S(2)}) %collective-permute-start.20) | collective-permute-done | bytes 147488 | tf_op jit(solution)/shard_map/ppermute | solution.py:36
  368.9 6.0 %collective-permute-done.23 = bf16[16,4608]{1,0:T(8,128)(2,1)S(1)} collective-permute-done((bf16[16,4608]{1,0:T(8,128)(2,1)S(1)}, bf16[16,4608]{1,0:T(8,128)(2,1)S(1)}, u32[]{:S(2)}, u32[]{:S(2)}) %collective-permute-start.23) | collective-permute-done | bytes 147488 | tf_op jit(solution)/shard_map/ppermute | solution.py:36
  374.9 6.9 %collective-permute-done.22 = bf16[16,4608]{1,0:T(8,128)(2,1)S(1)} collective-permute-done((bf16[16,4608]{1,0:T(8,128)(2,1)S(1)}, bf16[16,4608]{1,0:T(8,128)(2,1)S(1)}, u32[]{:S(2)}, u32[]{:S(2)}) %collective-permute-start.22) | collective-permute-done | bytes 147488 | tf_op jit(solution)/shard_map/ppermute | solution.py:36
  383.1 2.5 all-gather.7
  390.9 6.0 %collective-permute-done.25 = bf16[16,4608]{1,0:T(8,128)(2,1)S(1)} collective-permute-done((bf16[16,4608]{1,0:T(8,128)(2,1)S(1)}, bf16[16,4608]{1,0:T(8,128)(2,1)S(1)}, u32[]{:S(2)}, u32[]{:S(2)}) %collective-permute-start.25) | collective-permute-done | bytes 147488 | tf_op jit(solution)/shard_map/ppermute | solution.py:36
  396.9 6.9 %collective-permute-done.24 = bf16[16,4608]{1,0:T(8,128)(2,1)S(1)} collective-permute-done((bf16[16,4608]{1,0:T(8,128)(2,1)S(1)}, bf16[16,4608]{1,0:T(8,128)(2,1)S(1)}, u32[]{:S(2)}, u32[]{:S(2)}) %collective-permute-start.24) | collective-permute-done | bytes 147488 | tf_op jit(solution)/shard_map/ppermute | solution.py:36
  405.2 2.8 all-gather.8
  413.2 6.4 %collective-permute-done.27 = bf16[16,4608]{1,0:T(8,128)(2,1)S(1)} collective-permute-done((bf16[16,4608]{1,0:T(8,128)(2,1)S(1)}, bf16[16,4608]{1,0:T(8,128)(2,1)S(1)}, u32[]{:S(2)}, u32[]{:S(2)}) %collective-permute-start.27) | collective-permute-done | bytes 147488 | tf_op jit(solution)/shard_map/ppermute | solution.py:36
  419.6 6.8 %collective-permute-done.26 = bf16[16,4608]{1,0:T(8,128)(2,1)S(1)} collective-permute-done((bf16[16,4608]{1,0:T(8,128)(2,1)S(1)}, bf16[16,4608]{1,0:T(8,128)(2,1)S(1)}, u32[]{:S(2)}, u32[]{:S(2)}) %collective-permute-start.26) | collective-permute-done | bytes 147488 | tf_op jit(solution)/shard_map/ppermute | solution.py:36
  434.7 6.0 %collective-permute-done.29 = bf16[16,4608]{1,0:T(8,128)(2,1)S(1)} collective-permute-done((bf16[16,4608]{1,0:T(8,128)(2,1)S(1)}, bf16[16,4608]{1,0:T(8,128)(2,1)S(1)}, u32[]{:S(2)}, u32[]{:S(2)}) %collective-permute-start.29) | collective-permute-done | bytes 147488 | tf_op jit(solution)/shard_map/ppermute | solution.py:36
  440.8 7.1 %collective-permute-done.28 = bf16[16,4608]{1,0:T(8,128)(2,1)S(1)} collective-permute-done((bf16[16,4608]{1,0:T(8,128)(2,1)S(1)}, bf16[16,4608]{1,0:T(8,128)(2,1)S(1)}, u32[]{:S(2)}, u32[]{:S(2)}) %collective-permute-start.28) | collective-permute-done | bytes 147488 | tf_op jit(solution)/shard_map/ppermute | solution.py:36
  456.3 6.2 %collective-permute-done.31 = bf16[16,4608]{1,0:T(8,128)(2,1)S(1)} collective-permute-done((bf16[16,4608]{1,0:T(8,128)(2,1)S(1)}, bf16[16,4608]{1,0:T(8,128)(2,1)S(1)}, u32[]{:S(2)}, u32[]{:S(2)}) %collective-permute-start.31) | collective-permute-done | bytes 147488 | tf_op jit(solution)/shard_map/ppermute | solution.py:36
  462.5 6.7 %collective-permute-done.30 = bf16[16,4608]{1,0:T(8,128)(2,1)S(1)} collective-permute-done((bf16[16,4608]{1,0:T(8,128)(2,1)S(1)}, bf16[16,4608]{1,0:T(8,128)(2,1)S(1)}, u32[]{:S(2)}, u32[]{:S(2)}) %collective-permute-start.30) | collective-permute-done | bytes 147488 | tf_op jit(solution)/shard_map/ppermute | solution.py:36
  477.7 6.7 %collective-permute-done.33 = bf16[16,4608]{1,0:T(8,128)(2,1)S(1)} collective-permute-done((bf16[16,4608]{1,0:T(8,128)(2,1)S(1)}, bf16[16,4608]{1,0:T(8,128)(2,1)S(1)}, u32[]{:S(2)}, u32[]{:S(2)}) %collective-permute-start.33) | collective-permute-done | bytes 147488 | tf_op jit(solution)/shard_map/ppermute | solution.py:36
  484.4 6.0 %collective-permute-done.32 = bf16[16,4608]{1,0:T(8,128)(2,1)S(1)} collective-permute-done((bf16[16,4608]{1,0:T(8,128)(2,1)S(1)}, bf16[16,4608]{1,0:T(8,128)(2,1)S(1)}, u32[]{:S(2)}, u32[]{:S(2)}) %collective-permute-start.32) | collective-permute-done | bytes 147488 | tf_op jit(solution)/shard_map/ppermute | solution.py:36
  491.7 2.6 all-gather.12
  499.6 6.4 %collective-permute-done.35 = bf16[16,4608]{1,0:T(8,128)(2,1)S(1)} collective-permute-done((bf16[16,4608]{1,0:T(8,128)(2,1)S(1)}, bf16[16,4608]{1,0:T(8,128)(2,1)S(1)}, u32[]{:S(2)}, u32[]{:S(2)}) %collective-permute-start.35) | collective-permute-done | bytes 147488 | tf_op jit(solution)/shard_map/ppermute | solution.py:36
  506.0 6.6 %collective-permute-done.34 = bf16[16,4608]{1,0:T(8,128)(2,1)S(1)} collective-permute-done((bf16[16,4608]{1,0:T(8,128)(2,1)S(1)}, bf16[16,4608]{1,0:T(8,128)(2,1)S(1)}, u32[]{:S(2)}, u32[]{:S(2)}) %collective-permute-start.34) | collective-permute-done | bytes 147488 | tf_op jit(solution)/shard_map/ppermute | solution.py:36
  513.9 2.3 all-gather.13
  519.6 2.1 collective-permute-start.36
  521.7 6.5 %collective-permute-done.37 = bf16[16,4608]{1,0:T(8,128)(2,1)S(1)} collective-permute-done((bf16[16,4608]{1,0:T(8,128)(2,1)S(1)}, bf16[16,4608]{1,0:T(8,128)(2,1)S(1)}, u32[]{:S(2)}, u32[]{:S(2)}) %collective-permute-start.37) | collective-permute-done | bytes 147488 | tf_op jit(solution)/shard_map/ppermute | solution.py:36
  528.1 6.4 %collective-permute-done.36 = bf16[16,4608]{1,0:T(8,128)(2,1)S(1)} collective-permute-done((bf16[16,4608]{1,0:T(8,128)(2,1)S(1)}, bf16[16,4608]{1,0:T(8,128)(2,1)S(1)}, u32[]{:S(2)}, u32[]{:S(2)}) %collective-permute-start.36) | collective-permute-done | bytes 147488 | tf_op jit(solution)/shard_map/ppermute | solution.py:36
  543.1 6.0 %collective-permute-done.39 = bf16[16,4608]{1,0:T(8,128)(2,1)S(1)} collective-permute-done((bf16[16,4608]{1,0:T(8,128)(2,1)S(1)}, bf16[16,4608]{1,0:T(8,128)(2,1)S(1)}, u32[]{:S(2)}, u32[]{:S(2)}) %collective-permute-start.39) | collective-permute-done | bytes 147488 | tf_op jit(solution)/shard_map/ppermute | solution.py:36
  549.1 6.8 %collective-permute-done.38 = bf16[16,4608]{1,0:T(8,128)(2,1)S(1)} collective-permute-done((bf16[16,4608]{1,0:T(8,128)(2,1)S(1)}, bf16[16,4608]{1,0:T(8,128)(2,1)S(1)}, u32[]{:S(2)}, u32[]{:S(2)}) %collective-permute-start.38) | collective-permute-done | bytes 147488 | tf_op jit(solution)/shard_map/ppermute | solution.py:36
  563.3 13.7 %all-to-all-start.2 = ((bf16[16,4,2304]{2,1,0:T(4,128)(2,1)}), bf16[16,4,2304]{2,1,0:T(4,128)(2,1)S(1)}, u32[]{:S(2)}, u32[]{:S(2)}) async-start(bf16[16,4,2304]{2,1,0:T(4,128)(2,1)} %copy.107), calls=%async_computation.2 | async-start | bytes 589824 | tf_op jit(solution)/shard_map/all_to_all | solution.py:259
  577.1 15.5 %all-to-all-done.2 = bf16[16,4,2304]{2,1,0:T(4,128)(2,1)S(1)} async-done(((bf16[16,4,2304]{2,1,0:T(4,128)(2,1)}), bf16[16,4,2304]{2,1,0:T(4,128)(2,1)S(1)}, u32[]{:S(2)}, u32[]{:S(2)}) %all-to-all-start.2) | async-done | bytes 294944 | tf_op jit(solution)/shard_map/all_to_all | solution.py:259
  592.7 3.8 all_gather.123
  (193 shorter events, 145.5 us)
Async XLA Ops:
  0.0 24.7 %copy-start = (bf16[1,128,4608]{2,1,0:T(8,128)(2,1)S(1)}, bf16[1,128,4608]{2,1,0:T(8,128)(2,1)}, u32[]{:S(2)}) copy-start(bf16[1,128,4608]{2,1,0:T(8,128)(2,1)} %param.10) | copy-start | bytes 3538948
  0.0 18.8 %collective-permute-start.1 = (f32[16,16]{1,0:T(8,128)}, f32[16,16]{1,0:T(8,128)}, u32[]{:S(2)}, u32[]{:S(2)}) collective-permute-start(f32[16,16]{1,0:T(8,128)} %bitcast.136), channel_id=1, source_target_pairs={{0,28},{1,5},{4,0},{5,9},{8,4},{9,13},{12,8},{13,17},{16,12},{17,2... | collective-permute-start | bytes 3080 | tf_op jit(solution)/shard_map/ppermute | solution.py:25
  5.7 12.5 %copy-start.27 = (s32[1,4096]{1,0:T(1,128)S(1)}, s32[1,4096]{1,0:T(1,128)}, u32[]{:S(2)}) copy-start(s32[1,4096]{1,0:T(1,128)} %param.16) | copy-start | bytes 49156
  7.5 20.8 %copy-start.23 = (bf16[256,4608]{1,0:T(8,128)(2,1)}, bf16[256,4608]{1,0:T(8,128)(2,1)S(1)}, u32[]{:S(2)}) copy-start(bf16[256,4608]{1,0:T(8,128)(2,1)S(1)} %pad_maximum_fusion.mine_ref) | copy-start | bytes 7077892
  7.5 60.1 %collective-permute-start = (bf16[256,4608]{1,0:T(8,128)(2,1)S(1)}, bf16[256,4608]{1,0:T(8,128)(2,1)}, u32[]{:S(2)}, u32[]{:S(2)}) collective-permute-start(bf16[256,4608]{1,0:T(8,128)(2,1)S(1)} %pad_maximum_fusion.mine_ref), channel_id=1, source_target_pairs={{0,2},{2,0},{1,3},{3,1},{4,6},{6,4},{5,7},{7,5},{8,10},{10,8},{9,1... | collective-permute-start | bytes 7077896 | tf_op jit(solution)/shard_map/ppermute | solution.py:189
  18.8 54.1 %collective-permute-start.5 = (bf16[256,4608]{1,0:T(8,128)(2,1)S(1)}, bf16[256,4608]{1,0:T(8,128)(2,1)}, u32[]{:S(2)}, u32[]{:S(2)}) collective-permute-start(bf16[256,4608]{1,0:T(8,128)(2,1)S(1)} %pad_maximum_fusion.mine_ref), channel_id=1, source_target_pairs={{0,28},{1,5},{4,0},{5,9},{8,4},{9,13},{12,8},{13,17},{16,12},{17,2... | collective-permute-start | bytes 7077896 | tf_op jit(solution)/shard_map/ppermute | solution.py:25
  28.3 119.5 %collective-permute-start.4 = (bf16[256,4608]{1,0:T(8,128)(2,1)S(1)}, bf16[256,4608]{1,0:T(8,128)(2,1)}, u32[]{:S(2)}, u32[]{:S(2)}) collective-permute-start(bf16[256,4608]{1,0:T(8,128)(2,1)S(1)} %pad_maximum_fusion.mine_ref), channel_id=1, source_target_pairs={{0,1},{1,0},{2,3},{3,2},{4,5},{5,4},{6,7},{7,6},{8,9},{9,8},{10,11... | collective-permute-start | bytes 7077896 | tf_op jit(solution)/shard_map/ppermute | solution.py:94
  34.2 44.0 %copy-start.33 = (s32[4]{0:T(128)S(1)}, s32[4]{0:T(128)}, u32[]{:S(2)}) copy-start(s32[4]{0:T(128)} %param.18) | copy-start | bytes 52
  34.2 44.1 %copy-start.26 = (bf16[1,128,4608]{2,1,0:T(8,128)(2,1)S(1)}, bf16[1,128,4608]{2,1,0:T(8,128)(2,1)}, u32[]{:S(2)}) copy-start(bf16[1,128,4608]{2,1,0:T(8,128)(2,1)} %param.11) | copy-start | bytes 3538948
  34.2 33.5 %collective-permute-start.2 = (f32[2,16,16]{2,1,0:T(8,128)S(1)}, f32[2,16,16]{2,1,0:T(8,128)S(1)}, u32[]{:S(2)}, u32[]{:S(2)}) collective-permute-start(f32[2,16,16]{2,1,0:T(8,128)S(1)} %pad_maximum_fusion.3), channel_id=1, source_target_pairs={{0,2},{2,0},{1,3},{3,1},{4,6},{6,4},{5,7},{7,5},{8,10},{10,8},{9,1... | collective-permute-start | bytes 6152 | tf_op jit(solution)/shard_map/ppermute | solution.py:202
  39.6 105.4 %copy-start.28 = (f32[1,1,16,16]{3,2,1,0:T(8,128)S(1)}, f32[1,1,16,16]{3,2,1,0:T(8,128)}, u32[]{:S(2)}) copy-start(f32[1,1,16,16]{3,2,1,0:T(8,128)} %param.14) | copy-start | bytes 3076
  67.6 87.5 %collective-permute-start.7 = (bf16[256,4608]{1,0:T(8,128)(2,1)}, bf16[256,4608]{1,0:T(8,128)(2,1)}, u32[]{:S(2)}, u32[]{:S(2)}) collective-permute-start(bf16[256,4608]{1,0:T(8,128)(2,1)} %collective-permute-done.mine_ref), channel_id=1, source_target_pairs={{0,1},{1,0},{2,3},{3,2},{4,5},{5,4},{6,7},{7,6},{8,9},{9,8},{10,11... | collective-permute-start | bytes 7077896 | tf_op jit(solution)/shard_map/ppermute | solution.py:94
  73.0 88.2 %collective-permute-start.6 = (bf16[256,4608]{1,0:T(8,128)(2,1)}, bf16[256,4608]{1,0:T(8,128)(2,1)}, u32[]{:S(2)}, u32[]{:S(2)}) collective-permute-start(bf16[256,4608]{1,0:T(8,128)(2,1)} %collective-permute-done.5.mine_ref), channel_id=1, source_target_pairs={{0,1},{1,0},{2,3},{3,2},{4,5},{5,4},{6,7},{7,6},{8,9},{9,8},{10,11... | collective-permute-start | bytes 7077896 | tf_op jit(solution)/shard_map/ppermute | solution.py:94
  74.9 92.3 %collective-permute-start.3 = (bf16[256,4608]{1,0:T(8,128)(2,1)}, bf16[256,4608]{1,0:T(8,128)(2,1)}, u32[]{:S(2)}, u32[]{:S(2)}) collective-permute-start(bf16[256,4608]{1,0:T(8,128)(2,1)} %collective-permute-done.mine_ref), channel_id=1, source_target_pairs={{0,28},{1,5},{4,0},{5,9},{8,4},{9,13},{12,8},{13,17},{16,12},{17,2... | collective-permute-start | bytes 7077896 | tf_op jit(solution)/shard_map/ppermute | solution.py:25
  78.5 66.4 %copy-start.30 = (f32[2,16,16]{2,1,0:T(8,128)S(1)}, f32[2,16,16]{2,1,0:T(8,128)}, u32[]{:S(2)}) copy-start(f32[2,16,16]{2,1,0:T(8,128)} %copy-done.29) | copy-start | bytes 6148
  82.8 85.0 %all-to-all-start = ((bf16[32,2,2304]{2,1,0:T(2,128)(2,1)}), bf16[32,2,2304]{2,1,0:T(2,128)(2,1)}, u32[]{:S(2)}, u32[]{:S(2)}) async-start(bf16[32,2,2304]{2,1,0:T(2,128)(2,1)} %reshape.200), calls=%async_computation | async-start | bytes 589824 | tf_op jit(solution)/shard_map/all_to_all | solution.py:210
  145.7 7.8 %collective-permute-start.8 = (f32[4,16,16]{2,1,0:T(8,128)S(1)}, f32[4,16,16]{2,1,0:T(8,128)S(1)}, u32[]{:S(2)}, u32[]{:S(2)}) collective-permute-start(f32[4,16,16]{2,1,0:T(8,128)S(1)} %get-tuple-element.234), channel_id=1, source_target_pairs={{0,1},{1,0},{2,3},{3,2},{4,5},{5,4},{6,7},{7,6},{8,9},{9,8},{10,11... | collective-permute-start | bytes 12296 | tf_op jit(solution)/shard_map/ppermute | solution.py:219
  167.3 14.7 %copy-start.32 = (f32[1,16]{1,0:T(1,128)S(1)}, f32[1,16]{1,0:T(1,128)}, u32[]{:S(2)}) copy-start(f32[1,16]{1,0:T(1,128)} %param.15) | copy-start | bytes 196
  167.3 14.7 %copy-start.34 = (s32[4]{0:T(128)S(1)}, s32[4]{0:T(128)}, u32[]{:S(2)}) copy-start(s32[4]{0:T(128)} %param.19) | copy-start | bytes 52
  167.8 155.0 %all-to-all-start.1 = ((bf16[32,8,4608]{2,1,0:T(8,128)(2,1)}), bf16[32,8,4608]{2,1,0:T(8,128)(2,1)}, u32[]{:S(2)}, u32[]{:S(2)}) async-start(bf16[32,8,4608]{2,1,0:T(8,128)(2,1)} %bitcast_select_fusion), calls=%async_computation.1 | async-start | bytes 4718592 | tf_op jit(solution)/shard_map/all_to_all | solution.py:229
  179.5 6.8 %collective-permute-start.9 = (bf16[256,4608]{1,0:T(8,128)(2,1)}, bf16[256,4608]{1,0:T(8,128)(2,1)}, u32[]{:S(2)}, u32[]{:S(2)}) collective-permute-start(bf16[256,4608]{1,0:T(8,128)(2,1)} %collective-permute-done.3.mine_ref), channel_id=1, source_target_pairs={{0,1},{1,0},{2,3},{3,2},{4,5},{5,4},{6,7},{7,6},{8,9},{9,8},{10,11... | collective-permute-start | bytes 7077896 | tf_op jit(solution)/shard_map/ppermute | solution.py:94
  189.7 123.8 %copy-start.8 = (bf16[4608,256]{1,0:T(8,128)(2,1)}, bf16[4608,256]{1,0:T(8,128)(2,1)S(1)}, u32[]{:S(2)}) copy-start(bf16[4608,256]{1,0:T(8,128)(2,1)S(1)} %get-tuple-element.92.refs_3_) | copy-start | bytes 7077892
  189.7 127.2 %copy-start.19 = (bf16[256,4608]{1,0:T(8,128)(2,1)}, bf16[256,4608]{1,0:T(8,128)(2,1)S(1)}, u32[]{:S(2)}) copy-start(bf16[256,4608]{1,0:T(8,128)(2,1)S(1)} %get-tuple-element.100.refs_3_) | copy-start | bytes 7077892
  196.0 48.4 %collective-permute-start.11 = (bf16[16,4608]{1,0:T(8,128)(2,1)S(1)}, bf16[16,4608]{1,0:T(8,128)(2,1)S(1)}, u32[]{:S(2)}, u32[]{:S(2)}) collective-permute-start(bf16[16,4608]{1,0:T(8,128)(2,1)S(1)} %head_terms.15), channel_id=1, source_target_pairs={{32,0},{33,25},{40,8},{41,1},{48,16},{49,9},{56,24},{57,17},{64,32... | collective-permute-start | bytes 442376 | tf_op jit(solution)/shard_map/ppermute | solution.py:36
  201.8 42.6 %collective-permute-start.10 = (bf16[16,4608]{1,0:T(8,128)(2,1)S(1)}, bf16[16,4608]{1,0:T(8,128)(2,1)S(1)}, u32[]{:S(2)}, u32[]{:S(2)}) collective-permute-start(bf16[16,4608]{1,0:T(8,128)(2,1)S(1)} %head_terms.15), channel_id=1, source_target_pairs={{32,17},{33,8},{40,25},{41,16},{48,1},{49,24},{56,9},{57,0},{64,49... | collective-permute-start | bytes 442376 | tf_op jit(solution)/shard_map/ppermute | solution.py:36
  249.0 9.9 %collective-permute-start.13 = (bf16[16,4608]{1,0:T(8,128)(2,1)S(1)}, bf16[16,4608]{1,0:T(8,128)(2,1)S(1)}, u32[]{:S(2)}, u32[]{:S(2)}) collective-permute-start(bf16[16,4608]{1,0:T(8,128)(2,1)S(1)} %head_terms.16), channel_id=1, source_target_pairs={{32,0},{33,25},{40,8},{41,1},{48,16},{49,9},{56,24},{57,17},{64,32... | collective-permute-start | bytes 442376 | tf_op jit(solution)/shard_map/ppermute | solution.py:36
  252.8 13.4 %collective-permute-start.12 = (bf16[16,4608]{1,0:T(8,128)(2,1)S(1)}, bf16[16,4608]{1,0:T(8,128)(2,1)S(1)}, u32[]{:S(2)}, u32[]{:S(2)}) collective-permute-start(bf16[16,4608]{1,0:T(8,128)(2,1)S(1)} %head_terms.16), channel_id=1, source_target_pairs={{32,17},{33,8},{40,25},{41,16},{48,1},{49,24},{56,9},{57,0},{64,49... | collective-permute-start | bytes 442376 | tf_op jit(solution)/shard_map/ppermute | solution.py:36
  270.8 9.9 %collective-permute-start.15 = (bf16[16,4608]{1,0:T(8,128)(2,1)S(1)}, bf16[16,4608]{1,0:T(8,128)(2,1)S(1)}, u32[]{:S(2)}, u32[]{:S(2)}) collective-permute-start(bf16[16,4608]{1,0:T(8,128)(2,1)S(1)} %head_terms.17), channel_id=1, source_target_pairs={{32,0},{33,25},{40,8},{41,1},{48,16},{49,9},{56,24},{57,17},{64,32... | collective-permute-start | bytes 442376 | tf_op jit(solution)/shard_map/ppermute | solution.py:36
  276.4 15.6 %collective-permute-start.14 = (bf16[16,4608]{1,0:T(8,128)(2,1)S(1)}, bf16[16,4608]{1,0:T(8,128)(2,1)S(1)}, u32[]{:S(2)}, u32[]{:S(2)}) collective-permute-start(bf16[16,4608]{1,0:T(8,128)(2,1)S(1)} %head_terms.17), channel_id=1, source_target_pairs={{32,17},{33,8},{40,25},{41,16},{48,1},{49,24},{56,9},{57,0},{64,49... | collective-permute-start | bytes 442376 | tf_op jit(solution)/shard_map/ppermute | solution.py:36
  296.6 9.9 %collective-permute-start.17 = (bf16[16,4608]{1,0:T(8,128)(2,1)S(1)}, bf16[16,4608]{1,0:T(8,128)(2,1)S(1)}, u32[]{:S(2)}, u32[]{:S(2)}) collective-permute-start(bf16[16,4608]{1,0:T(8,128)(2,1)S(1)} %head_terms.18), channel_id=1, source_target_pairs={{32,0},{33,25},{40,8},{41,1},{48,16},{49,9},{56,24},{57,17},{64,32... | collective-permute-start | bytes 442376 | tf_op jit(solution)/shard_map/ppermute | solution.py:36
  298.5 14.9 %collective-permute-start.16 = (bf16[16,4608]{1,0:T(8,128)(2,1)S(1)}, bf16[16,4608]{1,0:T(8,128)(2,1)S(1)}, u32[]{:S(2)}, u32[]{:S(2)}) collective-permute-start(bf16[16,4608]{1,0:T(8,128)(2,1)S(1)} %head_terms.18), channel_id=1, source_target_pairs={{32,17},{33,8},{40,25},{41,16},{48,1},{49,24},{56,9},{57,0},{64,49... | collective-permute-start | bytes 442376 | tf_op jit(solution)/shard_map/ppermute | solution.py:36
  318.9 11.9 %collective-permute-start.19 = (bf16[16,4608]{1,0:T(8,128)(2,1)}, bf16[16,4608]{1,0:T(8,128)(2,1)}, u32[]{:S(2)}, u32[]{:S(2)}) collective-permute-start(bf16[16,4608]{1,0:T(8,128)(2,1)} %head_terms.19), channel_id=1, source_target_pairs={{32,0},{33,25},{40,8},{41,1},{48,16},{49,9},{56,24},{57,17},{64,32... | collective-permute-start | bytes 442376 | tf_op jit(solution)/shard_map/ppermute | solution.py:36
  320.8 14.5 %collective-permute-start.18 = (bf16[16,4608]{1,0:T(8,128)(2,1)}, bf16[16,4608]{1,0:T(8,128)(2,1)}, u32[]{:S(2)}, u32[]{:S(2)}) collective-permute-start(bf16[16,4608]{1,0:T(8,128)(2,1)} %head_terms.19), channel_id=1, source_target_pairs={{32,17},{33,8},{40,25},{41,16},{48,1},{49,24},{56,9},{57,0},{64,49... | collective-permute-start | bytes 442376 | tf_op jit(solution)/shard_map/ppermute | solution.py:36
  322.7 19.4 %copy-start.22 = (f32[16,16,1024]{2,1,0:T(8,128)S(1)}, f32[16,16,1024]{2,1,0:T(8,128)}, u32[]{:S(2)}) copy-start(f32[16,16,1024]{2,1,0:T(8,128)} %reshape.164.mix_ref) | copy-start | bytes 3145732
  328.2 7.0 %copy-start.4 = (bf16[4608,256]{1,0:T(8,128)(2,1)S(1)}, bf16[4608,256]{1,0:T(8,128)(2,1)}, u32[]{:S(2)}) copy-start(bf16[4608,256]{1,0:T(8,128)(2,1)} %copy-done.2) | copy-start | bytes 7077892
  335.3 6.9 %copy-start.15 = (bf16[256,4608]{1,0:T(8,128)(2,1)S(1)}, bf16[256,4608]{1,0:T(8,128)(2,1)}, u32[]{:S(2)}) copy-start(bf16[256,4608]{1,0:T(8,128)(2,1)} %copy-done.13) | copy-start | bytes 7077892
  335.3 6.9 %copy-start.18 = (bf16[256,4608]{1,0:T(8,128)(2,1)S(1)}, bf16[256,4608]{1,0:T(8,128)(2,1)}, u32[]{:S(2)}) copy-start(bf16[256,4608]{1,0:T(8,128)(2,1)} %copy-done.16) | copy-start | bytes 7077892
  342.2 18.2 %copy-start.7 = (bf16[4608,256]{1,0:T(8,128)(2,1)S(1)}, bf16[4608,256]{1,0:T(8,128)(2,1)}, u32[]{:S(2)}) copy-start(bf16[4608,256]{1,0:T(8,128)(2,1)} %copy-done.5) | copy-start | bytes 7077892
  342.2 18.2 %copy-start.9 = (bf16[4608,256]{1,0:T(8,128)(2,1)S(1)}, bf16[4608,256]{1,0:T(8,128)(2,1)}, u32[]{:S(2)}) copy-start(bf16[4608,256]{1,0:T(8,128)(2,1)} %copy-done.8) | copy-start | bytes 7077892
  343.6 10.1 %collective-permute-start.21 = (bf16[16,4608]{1,0:T(8,128)(2,1)S(1)}, bf16[16,4608]{1,0:T(8,128)(2,1)S(1)}, u32[]{:S(2)}, u32[]{:S(2)}) collective-permute-start(bf16[16,4608]{1,0:T(8,128)(2,1)S(1)} %head_terms.20), channel_id=1, source_target_pairs={{32,0},{33,25},{40,8},{41,1},{48,16},{49,9},{56,24},{57,17},{64,32... | collective-permute-start | bytes 442376 | tf_op jit(solution)/shard_map/ppermute | solution.py:36
  345.6 14.8 %collective-permute-start.20 = (bf16[16,4608]{1,0:T(8,128)(2,1)S(1)}, bf16[16,4608]{1,0:T(8,128)(2,1)S(1)}, u32[]{:S(2)}, u32[]{:S(2)}) collective-permute-start(bf16[16,4608]{1,0:T(8,128)(2,1)S(1)} %head_terms.20), channel_id=1, source_target_pairs={{32,17},{33,8},{40,25},{41,16},{48,1},{49,24},{56,9},{57,0},{64,49... | collective-permute-start | bytes 442376 | tf_op jit(solution)/shard_map/ppermute | solution.py:36
  365.0 9.9 %collective-permute-start.23 = (bf16[16,4608]{1,0:T(8,128)(2,1)S(1)}, bf16[16,4608]{1,0:T(8,128)(2,1)S(1)}, u32[]{:S(2)}, u32[]{:S(2)}) collective-permute-start(bf16[16,4608]{1,0:T(8,128)(2,1)S(1)} %head_terms.21), channel_id=1, source_target_pairs={{32,0},{33,25},{40,8},{41,1},{48,16},{49,9},{56,24},{57,17},{64,32... | collective-permute-start | bytes 442376 | tf_op jit(solution)/shard_map/ppermute | solution.py:36
  366.9 14.9 %collective-permute-start.22 = (bf16[16,4608]{1,0:T(8,128)(2,1)S(1)}, bf16[16,4608]{1,0:T(8,128)(2,1)S(1)}, u32[]{:S(2)}, u32[]{:S(2)}) collective-permute-start(bf16[16,4608]{1,0:T(8,128)(2,1)S(1)} %head_terms.21), channel_id=1, source_target_pairs={{32,17},{33,8},{40,25},{41,16},{48,1},{49,24},{56,9},{57,0},{64,49... | collective-permute-start | bytes 442376 | tf_op jit(solution)/shard_map/ppermute | solution.py:36
  387.0 9.9 %collective-permute-start.25 = (bf16[16,4608]{1,0:T(8,128)(2,1)S(1)}, bf16[16,4608]{1,0:T(8,128)(2,1)S(1)}, u32[]{:S(2)}, u32[]{:S(2)}) collective-permute-start(bf16[16,4608]{1,0:T(8,128)(2,1)S(1)} %head_terms.22), channel_id=1, source_target_pairs={{32,0},{33,25},{40,8},{41,1},{48,16},{49,9},{56,24},{57,17},{64,32... | collective-permute-start | bytes 442376 | tf_op jit(solution)/shard_map/ppermute | solution.py:36
  388.9 14.9 %collective-permute-start.24 = (bf16[16,4608]{1,0:T(8,128)(2,1)S(1)}, bf16[16,4608]{1,0:T(8,128)(2,1)S(1)}, u32[]{:S(2)}, u32[]{:S(2)}) collective-permute-start(bf16[16,4608]{1,0:T(8,128)(2,1)S(1)} %head_terms.22), channel_id=1, source_target_pairs={{32,17},{33,8},{40,25},{41,16},{48,1},{49,24},{56,9},{57,0},{64,49... | collective-permute-start | bytes 442376 | tf_op jit(solution)/shard_map/ppermute | solution.py:36
  409.3 10.2 %collective-permute-start.27 = (bf16[16,4608]{1,0:T(8,128)(2,1)S(1)}, bf16[16,4608]{1,0:T(8,128)(2,1)S(1)}, u32[]{:S(2)}, u32[]{:S(2)}) collective-permute-start(bf16[16,4608]{1,0:T(8,128)(2,1)S(1)} %head_terms.23), channel_id=1, source_target_pairs={{32,0},{33,25},{40,8},{41,1},{48,16},{49,9},{56,24},{57,17},{64,32... | collective-permute-start | bytes 442376 | tf_op jit(solution)/shard_map/ppermute | solution.py:36
  411.3 15.0 %collective-permute-start.26 = (bf16[16,4608]{1,0:T(8,128)(2,1)S(1)}, bf16[16,4608]{1,0:T(8,128)(2,1)S(1)}, u32[]{:S(2)}, u32[]{:S(2)}) collective-permute-start(bf16[16,4608]{1,0:T(8,128)(2,1)S(1)} %head_terms.23), channel_id=1, source_target_pairs={{32,17},{33,8},{40,25},{41,16},{48,1},{49,24},{56,9},{57,0},{64,49... | collective-permute-start | bytes 442376 | tf_op jit(solution)/shard_map/ppermute | solution.py:36
  430.9 9.9 %collective-permute-start.29 = (bf16[16,4608]{1,0:T(8,128)(2,1)S(1)}, bf16[16,4608]{1,0:T(8,128)(2,1)S(1)}, u32[]{:S(2)}, u32[]{:S(2)}) collective-permute-start(bf16[16,4608]{1,0:T(8,128)(2,1)S(1)} %head_terms.24), channel_id=1, source_target_pairs={{32,0},{33,25},{40,8},{41,1},{48,16},{49,9},{56,24},{57,17},{64,32... | collective-permute-start | bytes 442376 | tf_op jit(solution)/shard_map/ppermute | solution.py:36
  432.8 15.0 %collective-permute-start.28 = (bf16[16,4608]{1,0:T(8,128)(2,1)S(1)}, bf16[16,4608]{1,0:T(8,128)(2,1)S(1)}, u32[]{:S(2)}, u32[]{:S(2)}) collective-permute-start(bf16[16,4608]{1,0:T(8,128)(2,1)S(1)} %head_terms.24), channel_id=1, source_target_pairs={{32,17},{33,8},{40,25},{41,16},{48,1},{49,24},{56,9},{57,0},{64,49... | collective-permute-start | bytes 442376 | tf_op jit(solution)/shard_map/ppermute | solution.py:36
  452.4 10.1 %collective-permute-start.31 = (bf16[16,4608]{1,0:T(8,128)(2,1)S(1)}, bf16[16,4608]{1,0:T(8,128)(2,1)S(1)}, u32[]{:S(2)}, u32[]{:S(2)}) collective-permute-start(bf16[16,4608]{1,0:T(8,128)(2,1)S(1)} %head_terms.25), channel_id=1, source_target_pairs={{32,0},{33,25},{40,8},{41,1},{48,16},{49,9},{56,24},{57,17},{64,32... | collective-permute-start | bytes 442376 | tf_op jit(solution)/shard_map/ppermute | solution.py:36
  454.3 14.8 %collective-permute-start.30 = (bf16[16,4608]{1,0:T(8,128)(2,1)S(1)}, bf16[16,4608]{1,0:T(8,128)(2,1)S(1)}, u32[]{:S(2)}, u32[]{:S(2)}) collective-permute-start(bf16[16,4608]{1,0:T(8,128)(2,1)S(1)} %head_terms.25), channel_id=1, source_target_pairs={{32,17},{33,8},{40,25},{41,16},{48,1},{49,24},{56,9},{57,0},{64,49... | collective-permute-start | bytes 442376 | tf_op jit(solution)/shard_map/ppermute | solution.py:36
  473.8 10.6 %collective-permute-start.33 = (bf16[16,4608]{1,0:T(8,128)(2,1)S(1)}, bf16[16,4608]{1,0:T(8,128)(2,1)S(1)}, u32[]{:S(2)}, u32[]{:S(2)}) collective-permute-start(bf16[16,4608]{1,0:T(8,128)(2,1)S(1)} %head_terms.26), channel_id=1, source_target_pairs={{32,0},{33,25},{40,8},{41,1},{48,16},{49,9},{56,24},{57,17},{64,32... | collective-permute-start | bytes 442376 | tf_op jit(solution)/shard_map/ppermute | solution.py:36
  475.8 14.7 %collective-permute-start.32 = (bf16[16,4608]{1,0:T(8,128)(2,1)S(1)}, bf16[16,4608]{1,0:T(8,128)(2,1)S(1)}, u32[]{:S(2)}, u32[]{:S(2)}) collective-permute-start(bf16[16,4608]{1,0:T(8,128)(2,1)S(1)} %head_terms.26), channel_id=1, source_target_pairs={{32,17},{33,8},{40,25},{41,16},{48,1},{49,24},{56,9},{57,0},{64,49... | collective-permute-start | bytes 442376 | tf_op jit(solution)/shard_map/ppermute | solution.py:36
  495.7 10.3 %collective-permute-start.35 = (bf16[16,4608]{1,0:T(8,128)(2,1)S(1)}, bf16[16,4608]{1,0:T(8,128)(2,1)S(1)}, u32[]{:S(2)}, u32[]{:S(2)}) collective-permute-start(bf16[16,4608]{1,0:T(8,128)(2,1)S(1)} %head_terms.27), channel_id=1, source_target_pairs={{32,0},{33,25},{40,8},{41,1},{48,16},{49,9},{56,24},{57,17},{64,32... | collective-permute-start | bytes 442376 | tf_op jit(solution)/shard_map/ppermute | solution.py:36
  497.7 15.0 %collective-permute-start.34 = (bf16[16,4608]{1,0:T(8,128)(2,1)S(1)}, bf16[16,4608]{1,0:T(8,128)(2,1)S(1)}, u32[]{:S(2)}, u32[]{:S(2)}) collective-permute-start(bf16[16,4608]{1,0:T(8,128)(2,1)S(1)} %head_terms.27), channel_id=1, source_target_pairs={{32,17},{33,8},{40,25},{41,16},{48,1},{49,24},{56,9},{57,0},{64,49... | collective-permute-start | bytes 442376 | tf_op jit(solution)/shard_map/ppermute | solution.py:36
  517.6 10.5 %collective-permute-start.37 = (bf16[16,4608]{1,0:T(8,128)(2,1)S(1)}, bf16[16,4608]{1,0:T(8,128)(2,1)S(1)}, u32[]{:S(2)}, u32[]{:S(2)}) collective-permute-start(bf16[16,4608]{1,0:T(8,128)(2,1)S(1)} %head_terms.28), channel_id=1, source_target_pairs={{32,0},{33,25},{40,8},{41,1},{48,16},{49,9},{56,24},{57,17},{64,32... | collective-permute-start | bytes 442376 | tf_op jit(solution)/shard_map/ppermute | solution.py:36
  519.6 15.0 %collective-permute-start.36 = (bf16[16,4608]{1,0:T(8,128)(2,1)S(1)}, bf16[16,4608]{1,0:T(8,128)(2,1)S(1)}, u32[]{:S(2)}, u32[]{:S(2)}) collective-permute-start(bf16[16,4608]{1,0:T(8,128)(2,1)S(1)} %head_terms.28), channel_id=1, source_target_pairs={{32,17},{33,8},{40,25},{41,16},{48,1},{49,24},{56,9},{57,0},{64,49... | collective-permute-start | bytes 442376 | tf_op jit(solution)/shard_map/ppermute | solution.py:36
  539.1 57.4 %copy-start.25 = (bf16[128,4608]{1,0:T(8,128)(2,1)S(1)}, bf16[128,4608]{1,0:T(8,128)(2,1)}, u32[]{:S(2)}) copy-start(bf16[128,4608]{1,0:T(8,128)(2,1)} %broadcast_select_fusion) | copy-start | bytes 3538948
  539.1 10.0 %collective-permute-start.39 = (bf16[16,4608]{1,0:T(8,128)(2,1)S(1)}, bf16[16,4608]{1,0:T(8,128)(2,1)S(1)}, u32[]{:S(2)}, u32[]{:S(2)}) collective-permute-start(bf16[16,4608]{1,0:T(8,128)(2,1)S(1)} %head_terms.29), channel_id=1, source_target_pairs={{32,0},{33,25},{40,8},{41,1},{48,16},{49,9},{56,24},{57,17},{64,32... | collective-permute-start | bytes 442376 | tf_op jit(solution)/shard_map/ppermute | solution.py:36
  541.1 14.8 %collective-permute-start.38 = (bf16[16,4608]{1,0:T(8,128)(2,1)S(1)}, bf16[16,4608]{1,0:T(8,128)(2,1)S(1)}, u32[]{:S(2)}, u32[]{:S(2)}) collective-permute-start(bf16[16,4608]{1,0:T(8,128)(2,1)S(1)} %head_terms.29), channel_id=1, source_target_pairs={{32,17},{33,8},{40,25},{41,16},{48,1},{49,24},{56,9},{57,0},{64,49... | collective-permute-start | bytes 442376 | tf_op jit(solution)/shard_map/ppermute | solution.py:36
  557.8 3.5 collective-permute-start.40
  561.2 36.6 %copy-start.1 = (bf16[1,128,4608]{2,1,0:T(8,128)(2,1)S(1)}, bf16[1,128,4608]{2,1,0:T(8,128)(2,1)}, u32[]{:S(2)}) copy-start(bf16[1,128,4608]{2,1,0:T(8,128)(2,1)} %param.10) | copy-start | bytes 3538948
  562.4 34.7 %copy-start.31 = (f32[1,128]{1,0:T(1,128)S(1)}, f32[1,128]{1,0:T(1,128)}, u32[]{:S(2)}) copy-start(f32[1,128]{1,0:T(1,128)} %param.17) | copy-start | bytes 1540
  563.3 29.3 %all-to-all-start.2 = ((bf16[16,4,2304]{2,1,0:T(4,128)(2,1)}), bf16[16,4,2304]{2,1,0:T(4,128)(2,1)S(1)}, u32[]{:S(2)}, u32[]{:S(2)}) async-start(bf16[16,4,2304]{2,1,0:T(4,128)(2,1)} %copy.107), calls=%async_computation.2 | async-start | bytes 589824 | tf_op jit(solution)/shard_map/all_to_all | solution.py:259
  (15 other events, 51.1 us)

commit v7 on v6

--- a/solution.py
+++ b/solution.py
@@ -197,17 +197,18 @@
         enc_rows[None, :, None, :], (QUADS, targets, 2, model_width)
     ).reshape(feat_count, model_width)
     near_mix = neighbour_heads(own_mix)
-    own, near_mix = lax.optimization_barrier((own, near_mix))
+    own, near_mix, enc_send = lax.optimization_barrier((own, near_mix, enc_send))
     near = neighbour_heads(own)
     zh_mix = lax.ppermute(jnp.stack([own_mix, near_mix]), "zh", SWAP)
     outgoing, flat_index = panel_route(
         decoders[0], act_ids[0], entries_dev, feat_index, feat_count
     )
-    beyond, outgoing, near_mix, zh_mix = lax.optimization_barrier(
-        (beyond, outgoing, near_mix, zh_mix)
+    enc_got = lax.all_to_all(enc_send, FEAT, split_axis=0, concat_axis=0, tiled=True)
+    beyond, outgoing, near_mix, zh_mix, enc_got = lax.optimization_barrier(
+        (beyond, outgoing, near_mix, zh_mix, enc_got)
     )
     far = neighbour_heads(beyond)
-    enc_got = lax.all_to_all(enc_send, FEAT, split_axis=0, concat_axis=0, tiled=True)
+    incoming = lax.all_to_all(outgoing, FEAT, split_axis=0, concat_axis=0, tiled=True)
     enc_row = jnp.sum(enc_got.astype(F32), axis=0)
     own_target = lax.axis_index(("par", "zh"))
     own_pos = lax.dynamic_index_in_dim(target_pos, own_target, 0, keepdims=False)
@@ -223,10 +224,7 @@
         mixing.transpose(1, 2, 0)[..., None], (seq_len, seq_len, heads, head_width)
     ).reshape(seq_len, seq_len, heads * head_width)
     quarter = (start * 0.25).astype(BF)
-    far, groups, mix_wide, outgoing = lax.optimization_barrier(
-        (far, groups, mix_wide, outgoing)
-    )
-    incoming = lax.all_to_all(outgoing, FEAT, split_axis=0, concat_axis=0, tiled=True)
+    far, groups, mix_wide = lax.optimization_barrier((far, groups, mix_wide))
     panel = jnp.take(incoming.reshape(-1, model_width), flat_index, axis=0)
     groups.append(prepare(far))
     outs = [group[0] for group in groups]

time: 609 us -> 590 us (0.969)
  the two profiles are of different devices: /device:TPU:7 before, /device:TPU:71 now
where the time goes in v7:
time: 590 us; the launch traced here: 579 us
  waiting for transfers between devices  304 us (52%)
  starting transfers between devices  133 us (23%)
  local copies, waits for them, and re-layouts  53.7 us (9%)
  blocking collectives  35.9 us (6%)
  Pallas kernels  34.7 us (6%)
  other arithmetic  14.9 us (3%)
    ppermute x30, waiting for transfers between devices, send_down(): return lax.ppermute(shard, ('section', 'y2', 'core'), pairs)  190 us
    all_to_all x1, waiting for transfers between devices, per_device(): lax.all_to_all(enc_send, FEAT, split_axis=0, concat_axis=0, tiled=True)  78.4 us
    ppermute x30, starting transfers between devices, send_down(): return lax.ppermute(shard, ('section', 'y2', 'core'), pairs)  67.1 us
    all_gather x15, blocking collectives, per_device(): grads = lax.all_gather(grad_part, 'core', axis=0)  32.3 us
    pallas_call x14, local copies, waits for them, and re-layouts, head_grads(): pl.pallas_call(grads_kernel, out_shape=(jax.ShapeDtypeStruct((seq_len, mo...  22.2 us
    pallas_call x15, Pallas kernels, head_terms(): pl.pallas_call(terms_kernel, out_shape=jax.ShapeDtypeStruct(part.shape, B...  21.3 us
    ppermute x3, waiting for transfers between devices, neighbour_heads(): return lax.ppermute(shard, ('y2', 'par', 'core'), pairs)  16.2 us
    all_to_all x1, waiting for transfers between devices, per_device(): got = lax.all_to_all(held, CHIPS, split_axis=0, concat_axis=0, tiled=True)  15.8 us
  transfers between devices with their start and end apart: 44, of which 34 were waited for; matrix products, arithmetic and copies ran while one was open for 6% of the time, Pallas kernels for 3%

profile of v7, /device:TPU:71, one launch (start us, length us, event | category | flops | bytes accessed | tf_op | source)
XLA Modules:
  0.0 578.6 jit_solution(17262801837382632001)
XLA Ops:
  0.0 3.3 collective-permute-start.1
  4.9 2.9 pad_maximum_fusion.mine_ref
  7.9 9.7 %collective-permute-start = (bf16[256,4608]{1,0:T(8,128)(2,1)}, bf16[256,4608]{1,0:T(8,128)(2,1)}, u32[]{:S(2)}, u32[]{:S(2)}) collective-permute-start(bf16[256,4608]{1,0:T(8,128)(2,1)} %pad_maximum_fusion.mine_ref), channel_id=1, source_target_pairs={{0,2},{2,0},{1,3},{3,1},{4,6},{6,4},{5,7},{7,5},{8,10},{10,8},{9,1... | collective-permute-start | bytes 7077896 | tf_op jit(solution)/shard_map/ppermute | solution.py:189
  18.9 3.2 collective-permute-start.5
  23.1 3.4 gather_fusion
  26.5 5.1 collective-permute-start.4
  33.7 3.7 all-to-all-start
  38.1 7.2 %collective-permute-start.2 = (f32[2,16,16]{2,1,0:T(8,128)S(1)}, f32[2,16,16]{2,1,0:T(8,128)S(1)}, u32[]{:S(2)}, u32[]{:S(2)}) collective-permute-start(f32[2,16,16]{2,1,0:T(8,128)S(1)} %pad_maximum_fusion.3), channel_id=1, source_target_pairs={{0,2},{2,0},{1,3},{3,1},{4,6},{6,4},{5,7},{7,5},{8,10},{10,8},{9,1... | collective-permute-start | bytes 6152 | tf_op jit(solution)/shard_map/ppermute | solution.py:202
  45.3 3.3 bitcast_select_fusion
  48.6 78.4 %all-to-all-done = bf16[32,2,2304]{2,1,0:T(2,128)(2,1)S(1)} async-done(((bf16[32,2,2304]{2,1,0:T(2,128)(2,1)}), bf16[32,2,2304]{2,1,0:T(2,128)(2,1)S(1)}, u32[]{:S(2)}, u32[]{:S(2)}) %all-to-all-start) | async-done | bytes 294944 | tf_op jit(solution)/shard_map/all_to_all | solution.py:206
  128.0 2.5 collective-permute-start.7
  132.4 3.2 collective-permute-start.3
  135.7 12.0 %all-to-all-start.1 = ((bf16[32,8,4608]{2,1,0:T(8,128)(2,1)}), bf16[32,8,4608]{2,1,0:T(8,128)(2,1)}, u32[]{:S(2)}, u32[]{:S(2)}) async-start(bf16[32,8,4608]{2,1,0:T(8,128)(2,1)} %bitcast_select_fusion), calls=%async_computation.1 | async-start | bytes 4718592 | tf_op jit(solution)/shard_map/all_to_all | solution.py:211
  148.4 2.2 collective-permute-start.8
  153.7 2.5 turn_heads.4
  160.5 3.2 turn_heads.6
  166.5 3.2 turn_heads.5
  172.5 16.2 %collective-permute-done.3.mine_ref = bf16[256,4608]{1,0:T(8,128)(2,1)} collective-permute-done((bf16[256,4608]{1,0:T(8,128)(2,1)}, bf16[256,4608]{1,0:T(8,128)(2,1)}, u32[]{:S(2)}, u32[]{:S(2)}) %collective-permute-start.3) | collective-permute-done | bytes 2359328 | tf_op jit(solution)/shard_map/ppermute | solution.py:25
  188.7 2.3 collective-permute-start.9
  195.5 3.2 turn_heads.7
  204.9 5.6 collective-permute-start.11
  210.5 2.1 collective-permute-start.10
  213.3 3.7 collective-permute-done.11
  217.0 7.6 %collective-permute-done.10 = bf16[16,4608]{1,0:T(8,128)(2,1)S(1)} collective-permute-done((bf16[16,4608]{1,0:T(8,128)(2,1)S(1)}, bf16[16,4608]{1,0:T(8,128)(2,1)S(1)}, u32[]{:S(2)}, u32[]{:S(2)}) %collective-permute-start.10) | collective-permute-done | bytes 147488 | tf_op jit(solution)/shard_map/ppermute | solution.py:36
  229.2 5.9 %collective-permute-start.13 = (bf16[16,4608]{1,0:T(8,128)(2,1)S(1)}, bf16[16,4608]{1,0:T(8,128)(2,1)S(1)}, u32[]{:S(2)}, u32[]{:S(2)}) collective-permute-start(bf16[16,4608]{1,0:T(8,128)(2,1)S(1)} %head_terms.16), channel_id=1, source_target_pairs={{32,0},{33,25},{40,8},{41,1},{48,16},{49,9},{56,24},{57,17},{64,32... | collective-permute-start | bytes 442376 | tf_op jit(solution)/shard_map/ppermute | solution.py:36
  239.1 12.9 %collective-permute-done.12 = bf16[16,4608]{1,0:T(8,128)(2,1)S(1)} collective-permute-done((bf16[16,4608]{1,0:T(8,128)(2,1)S(1)}, bf16[16,4608]{1,0:T(8,128)(2,1)S(1)}, u32[]{:S(2)}, u32[]{:S(2)}) %collective-permute-start.12) | collective-permute-done | bytes 147488 | tf_op jit(solution)/shard_map/ppermute | solution.py:36
  260.5 6.0 %collective-permute-done.15 = bf16[16,4608]{1,0:T(8,128)(2,1)S(1)} collective-permute-done((bf16[16,4608]{1,0:T(8,128)(2,1)S(1)}, bf16[16,4608]{1,0:T(8,128)(2,1)S(1)}, u32[]{:S(2)}, u32[]{:S(2)}) %collective-permute-start.15) | collective-permute-done | bytes 147488 | tf_op jit(solution)/shard_map/ppermute | solution.py:36
  266.5 6.4 %collective-permute-done.14 = bf16[16,4608]{1,0:T(8,128)(2,1)S(1)} collective-permute-done((bf16[16,4608]{1,0:T(8,128)(2,1)S(1)}, bf16[16,4608]{1,0:T(8,128)(2,1)S(1)}, u32[]{:S(2)}, u32[]{:S(2)}) %collective-permute-start.14) | collective-permute-done | bytes 147488 | tf_op jit(solution)/shard_map/ppermute | solution.py:36
  280.1 2.9 collective-permute-start.16
  283.0 5.4 gather_fusion.1
  288.4 7.6 %collective-permute-done.16 = bf16[16,4608]{1,0:T(8,128)(2,1)} collective-permute-done((bf16[16,4608]{1,0:T(8,128)(2,1)}, bf16[16,4608]{1,0:T(8,128)(2,1)}, u32[]{:S(2)}, u32[]{:S(2)}) %collective-permute-start.16) | collective-permute-done | bytes 147488 | tf_op jit(solution)/shard_map/ppermute | solution.py:36
  296.1 4.7 head_grads.26
  304.2 2.2 collective-permute-start.19
  306.4 2.1 collective-permute-start.18
  309.8 6.0 %collective-permute-done.19 = bf16[16,4608]{1,0:T(8,128)(2,1)S(1)} collective-permute-done((bf16[16,4608]{1,0:T(8,128)(2,1)S(1)}, bf16[16,4608]{1,0:T(8,128)(2,1)S(1)}, u32[]{:S(2)}, u32[]{:S(2)}) %collective-permute-start.19) | collective-permute-done | bytes 147488 | tf_op jit(solution)/shard_map/ppermute | solution.py:36
  315.7 6.9 %collective-permute-done.18 = bf16[16,4608]{1,0:T(8,128)(2,1)S(1)} collective-permute-done((bf16[16,4608]{1,0:T(8,128)(2,1)S(1)}, bf16[16,4608]{1,0:T(8,128)(2,1)S(1)}, u32[]{:S(2)}, u32[]{:S(2)}) %collective-permute-start.18) | collective-permute-done | bytes 147488 | tf_op jit(solution)/shard_map/ppermute | solution.py:36
  331.1 7.3 %collective-permute-done.21 = bf16[16,4608]{1,0:T(8,128)(2,1)S(1)} collective-permute-done((bf16[16,4608]{1,0:T(8,128)(2,1)S(1)}, bf16[16,4608]{1,0:T(8,128)(2,1)S(1)}, u32[]{:S(2)}, u32[]{:S(2)}) %collective-permute-start.21) | collective-permute-done | bytes 147488 | tf_op jit(solution)/shard_map/ppermute | solution.py:36
  338.5 5.4 collective-permute-done.20
  352.3 6.0 %collective-permute-done.23 = bf16[16,4608]{1,0:T(8,128)(2,1)S(1)} collective-permute-done((bf16[16,4608]{1,0:T(8,128)(2,1)S(1)}, bf16[16,4608]{1,0:T(8,128)(2,1)S(1)}, u32[]{:S(2)}, u32[]{:S(2)}) %collective-permute-start.23) | collective-permute-done | bytes 147488 | tf_op jit(solution)/shard_map/ppermute | solution.py:36
  358.4 6.9 %collective-permute-done.22 = bf16[16,4608]{1,0:T(8,128)(2,1)S(1)} collective-permute-done((bf16[16,4608]{1,0:T(8,128)(2,1)S(1)}, bf16[16,4608]{1,0:T(8,128)(2,1)S(1)}, u32[]{:S(2)}, u32[]{:S(2)}) %collective-permute-start.22) | collective-permute-done | bytes 147488 | tf_op jit(solution)/shard_map/ppermute | solution.py:36
  373.8 6.0 %collective-permute-done.25 = bf16[16,4608]{1,0:T(8,128)(2,1)S(1)} collective-permute-done((bf16[16,4608]{1,0:T(8,128)(2,1)S(1)}, bf16[16,4608]{1,0:T(8,128)(2,1)S(1)}, u32[]{:S(2)}, u32[]{:S(2)}) %collective-permute-start.25) | collective-permute-done | bytes 147488 | tf_op jit(solution)/shard_map/ppermute | solution.py:36
  379.8 6.2 %collective-permute-done.24 = bf16[16,4608]{1,0:T(8,128)(2,1)S(1)} collective-permute-done((bf16[16,4608]{1,0:T(8,128)(2,1)S(1)}, bf16[16,4608]{1,0:T(8,128)(2,1)S(1)}, u32[]{:S(2)}, u32[]{:S(2)}) %collective-permute-start.24) | collective-permute-done | bytes 147488 | tf_op jit(solution)/shard_map/ppermute | solution.py:36
  387.3 2.6 all-gather.8
  395.2 6.0 %collective-permute-done.27 = bf16[16,4608]{1,0:T(8,128)(2,1)S(1)} collective-permute-done((bf16[16,4608]{1,0:T(8,128)(2,1)S(1)}, bf16[16,4608]{1,0:T(8,128)(2,1)S(1)}, u32[]{:S(2)}, u32[]{:S(2)}) %collective-permute-start.27) | collective-permute-done | bytes 147488 | tf_op jit(solution)/shard_map/ppermute | solution.py:36
  401.3 6.6 %collective-permute-done.26 = bf16[16,4608]{1,0:T(8,128)(2,1)S(1)} collective-permute-done((bf16[16,4608]{1,0:T(8,128)(2,1)S(1)}, bf16[16,4608]{1,0:T(8,128)(2,1)S(1)}, u32[]{:S(2)}, u32[]{:S(2)}) %collective-permute-start.26) | collective-permute-done | bytes 147488 | tf_op jit(solution)/shard_map/ppermute | solution.py:36
  409.3 3.0 all-gather.9
  417.5 6.0 %collective-permute-done.29 = bf16[16,4608]{1,0:T(8,128)(2,1)S(1)} collective-permute-done((bf16[16,4608]{1,0:T(8,128)(2,1)S(1)}, bf16[16,4608]{1,0:T(8,128)(2,1)S(1)}, u32[]{:S(2)}, u32[]{:S(2)}) %collective-permute-start.29) | collective-permute-done | bytes 147488 | tf_op jit(solution)/shard_map/ppermute | solution.py:36
  423.6 6.8 %collective-permute-done.28 = bf16[16,4608]{1,0:T(8,128)(2,1)S(1)} collective-permute-done((bf16[16,4608]{1,0:T(8,128)(2,1)S(1)}, bf16[16,4608]{1,0:T(8,128)(2,1)S(1)}, u32[]{:S(2)}, u32[]{:S(2)}) %collective-permute-start.28) | collective-permute-done | bytes 147488 | tf_op jit(solution)/shard_map/ppermute | solution.py:36
  431.7 2.9 all-gather.10
  439.9 6.0 %collective-permute-done.31 = bf16[16,4608]{1,0:T(8,128)(2,1)S(1)} collective-permute-done((bf16[16,4608]{1,0:T(8,128)(2,1)S(1)}, bf16[16,4608]{1,0:T(8,128)(2,1)S(1)}, u32[]{:S(2)}, u32[]{:S(2)}) %collective-permute-start.31) | collective-permute-done | bytes 147488 | tf_op jit(solution)/shard_map/ppermute | solution.py:36
  445.9 7.8 %collective-permute-done.30 = bf16[16,4608]{1,0:T(8,128)(2,1)S(1)} collective-permute-done((bf16[16,4608]{1,0:T(8,128)(2,1)S(1)}, bf16[16,4608]{1,0:T(8,128)(2,1)S(1)}, u32[]{:S(2)}, u32[]{:S(2)}) %collective-permute-start.30) | collective-permute-done | bytes 147488 | tf_op jit(solution)/shard_map/ppermute | solution.py:36
  462.3 6.0 %collective-permute-done.33 = bf16[16,4608]{1,0:T(8,128)(2,1)S(1)} collective-permute-done((bf16[16,4608]{1,0:T(8,128)(2,1)S(1)}, bf16[16,4608]{1,0:T(8,128)(2,1)S(1)}, u32[]{:S(2)}, u32[]{:S(2)}) %collective-permute-start.33) | collective-permute-done | bytes 147488 | tf_op jit(solution)/shard_map/ppermute | solution.py:36
  468.3 7.5 %collective-permute-done.32 = bf16[16,4608]{1,0:T(8,128)(2,1)S(1)} collective-permute-done((bf16[16,4608]{1,0:T(8,128)(2,1)S(1)}, bf16[16,4608]{1,0:T(8,128)(2,1)S(1)}, u32[]{:S(2)}, u32[]{:S(2)}) %collective-permute-start.32) | collective-permute-done | bytes 147488 | tf_op jit(solution)/shard_map/ppermute | solution.py:36
  480.4 2.1 collective-permute-start.35
  484.4 5.9 %collective-permute-done.35 = bf16[16,4608]{1,0:T(8,128)(2,1)S(1)} collective-permute-done((bf16[16,4608]{1,0:T(8,128)(2,1)S(1)}, bf16[16,4608]{1,0:T(8,128)(2,1)S(1)}, u32[]{:S(2)}, u32[]{:S(2)}) %collective-permute-start.35) | collective-permute-done | bytes 147488 | tf_op jit(solution)/shard_map/ppermute | solution.py:36
  490.3 10.0 %collective-permute-done.34 = bf16[16,4608]{1,0:T(8,128)(2,1)S(1)} collective-permute-done((bf16[16,4608]{1,0:T(8,128)(2,1)S(1)}, bf16[16,4608]{1,0:T(8,128)(2,1)S(1)}, u32[]{:S(2)}, u32[]{:S(2)}) %collective-permute-start.34) | collective-permute-done | bytes 147488 | tf_op jit(solution)/shard_map/ppermute | solution.py:36
  508.7 6.8 %collective-permute-done.37 = bf16[16,4608]{1,0:T(8,128)(2,1)S(1)} collective-permute-done((bf16[16,4608]{1,0:T(8,128)(2,1)S(1)}, bf16[16,4608]{1,0:T(8,128)(2,1)S(1)}, u32[]{:S(2)}, u32[]{:S(2)}) %collective-permute-start.37) | collective-permute-done | bytes 147488 | tf_op jit(solution)/shard_map/ppermute | solution.py:36
  515.5 5.2 collective-permute-done.36
  522.0 2.5 all-gather.14
  529.9 6.0 %collective-permute-done.39 = bf16[16,4608]{1,0:T(8,128)(2,1)S(1)} collective-permute-done((bf16[16,4608]{1,0:T(8,128)(2,1)S(1)}, bf16[16,4608]{1,0:T(8,128)(2,1)S(1)}, u32[]{:S(2)}, u32[]{:S(2)}) %collective-permute-start.39) | collective-permute-done | bytes 147488 | tf_op jit(solution)/shard_map/ppermute | solution.py:36
  536.0 6.4 %collective-permute-done.38 = bf16[16,4608]{1,0:T(8,128)(2,1)S(1)} collective-permute-done((bf16[16,4608]{1,0:T(8,128)(2,1)S(1)}, bf16[16,4608]{1,0:T(8,128)(2,1)S(1)}, u32[]{:S(2)}, u32[]{:S(2)}) %collective-permute-start.38) | collective-permute-done | bytes 147488 | tf_op jit(solution)/shard_map/ppermute | solution.py:36
  549.7 7.5 %all-to-all-start.2 = ((bf16[16,4,2304]{2,1,0:T(4,128)(2,1)}), bf16[16,4,2304]{2,1,0:T(4,128)(2,1)S(1)}, u32[]{:S(2)}, u32[]{:S(2)}) async-start(bf16[16,4,2304]{2,1,0:T(4,128)(2,1)} %copy.107), calls=%async_computation.2 | async-start | bytes 589824 | tf_op jit(solution)/shard_map/all_to_all | solution.py:257
  557.3 15.8 %all-to-all-done.2 = bf16[16,4,2304]{2,1,0:T(4,128)(2,1)S(1)} async-done(((bf16[16,4,2304]{2,1,0:T(4,128)(2,1)}), bf16[16,4,2304]{2,1,0:T(4,128)(2,1)S(1)}, u32[]{:S(2)}, u32[]{:S(2)}) %all-to-all-start.2) | async-done | bytes 294944 | tf_op jit(solution)/shard_map/all_to_all | solution.py:257
  573.2 3.6 all_gather.123
  (186 shorter events, 147.3 us)
Async XLA Ops:
  0.0 23.0 %copy-start = (bf16[1,128,4608]{2,1,0:T(8,128)(2,1)S(1)}, bf16[1,128,4608]{2,1,0:T(8,128)(2,1)}, u32[]{:S(2)}) copy-start(bf16[1,128,4608]{2,1,0:T(8,128)(2,1)} %param.10) | copy-start | bytes 3538948
  0.0 18.9 %collective-permute-start.1 = (f32[16,16]{1,0:T(8,128)}, f32[16,16]{1,0:T(8,128)}, u32[]{:S(2)}, u32[]{:S(2)}) collective-permute-start(f32[16,16]{1,0:T(8,128)} %bitcast.142), channel_id=1, source_target_pairs={{0,28},{1,5},{4,0},{5,9},{8,4},{9,13},{12,8},{13,17},{16,12},{17,2... | collective-permute-start | bytes 3080 | tf_op jit(solution)/shard_map/ppermute | solution.py:25
  4.9 13.4 %copy-start.25 = (bf16[1,128,4608]{2,1,0:T(8,128)(2,1)S(1)}, bf16[1,128,4608]{2,1,0:T(8,128)(2,1)}, u32[]{:S(2)}) copy-start(bf16[1,128,4608]{2,1,0:T(8,128)(2,1)} %param.11) | copy-start | bytes 3538948
  4.9 13.7 %copy-start.26 = (s32[1,4096]{1,0:T(1,128)S(1)}, s32[1,4096]{1,0:T(1,128)}, u32[]{:S(2)}) copy-start(s32[1,4096]{1,0:T(1,128)} %param.16) | copy-start | bytes 49156
  7.9 120.2 %collective-permute-start = (bf16[256,4608]{1,0:T(8,128)(2,1)}, bf16[256,4608]{1,0:T(8,128)(2,1)}, u32[]{:S(2)}, u32[]{:S(2)}) collective-permute-start(bf16[256,4608]{1,0:T(8,128)(2,1)} %pad_maximum_fusion.mine_ref), channel_id=1, source_target_pairs={{0,2},{2,0},{1,3},{3,1},{4,6},{6,4},{5,7},{7,5},{8,10},{10,8},{9,1... | collective-permute-start | bytes 7077896 | tf_op jit(solution)/shard_map/ppermute | solution.py:189
  18.9 111.6 %collective-permute-start.5 = (bf16[256,4608]{1,0:T(8,128)(2,1)}, bf16[256,4608]{1,0:T(8,128)(2,1)}, u32[]{:S(2)}, u32[]{:S(2)}) collective-permute-start(bf16[256,4608]{1,0:T(8,128)(2,1)} %pad_maximum_fusion.mine_ref), channel_id=1, source_target_pairs={{0,28},{1,5},{4,0},{5,9},{8,4},{9,13},{12,8},{13,17},{16,12},{17,2... | collective-permute-start | bytes 7077896 | tf_op jit(solution)/shard_map/ppermute | solution.py:25
  23.0 14.4 %copy-start.27 = (f32[1,1,16,16]{3,2,1,0:T(8,128)S(1)}, f32[1,1,16,16]{3,2,1,0:T(8,128)}, u32[]{:S(2)}) copy-start(f32[1,1,16,16]{3,2,1,0:T(8,128)} %param.14) | copy-start | bytes 3076
  26.5 124.1 %collective-permute-start.4 = (bf16[256,4608]{1,0:T(8,128)(2,1)}, bf16[256,4608]{1,0:T(8,128)(2,1)S(1)}, u32[]{:S(2)}, u32[]{:S(2)}) collective-permute-start(bf16[256,4608]{1,0:T(8,128)(2,1)} %pad_maximum_fusion.mine_ref), channel_id=1, source_target_pairs={{0,1},{1,0},{2,3},{3,2},{4,5},{5,4},{6,7},{7,6},{8,9},{9,8},{10,11... | collective-permute-start | bytes 7077896 | tf_op jit(solution)/shard_map/ppermute | solution.py:94
  33.7 93.3 %all-to-all-start = ((bf16[32,2,2304]{2,1,0:T(2,128)(2,1)}), bf16[32,2,2304]{2,1,0:T(2,128)(2,1)S(1)}, u32[]{:S(2)}, u32[]{:S(2)}) async-start(bf16[32,2,2304]{2,1,0:T(2,128)(2,1)} %reshape.201), calls=%async_computation | async-start | bytes 589824 | tf_op jit(solution)/shard_map/all_to_all | solution.py:206
  38.1 89.9 %collective-permute-start.2 = (f32[2,16,16]{2,1,0:T(8,128)S(1)}, f32[2,16,16]{2,1,0:T(8,128)S(1)}, u32[]{:S(2)}, u32[]{:S(2)}) collective-permute-start(f32[2,16,16]{2,1,0:T(8,128)S(1)} %pad_maximum_fusion.3), channel_id=1, source_target_pairs={{0,2},{2,0},{1,3},{3,1},{4,6},{6,4},{5,7},{7,5},{8,10},{10,8},{9,1... | collective-permute-start | bytes 6152 | tf_op jit(solution)/shard_map/ppermute | solution.py:202
  128.0 32.5 %collective-permute-start.7 = (bf16[256,4608]{1,0:T(8,128)(2,1)}, bf16[256,4608]{1,0:T(8,128)(2,1)}, u32[]{:S(2)}, u32[]{:S(2)}) collective-permute-start(bf16[256,4608]{1,0:T(8,128)(2,1)} %collective-permute-done.mine_ref), channel_id=1, source_target_pairs={{0,1},{1,0},{2,3},{3,2},{4,5},{5,4},{6,7},{7,6},{8,9},{9,8},{10,11... | collective-permute-start | bytes 7077896 | tf_op jit(solution)/shard_map/ppermute | solution.py:94
  130.5 36.0 %collective-permute-start.6 = (bf16[256,4608]{1,0:T(8,128)(2,1)}, bf16[256,4608]{1,0:T(8,128)(2,1)}, u32[]{:S(2)}, u32[]{:S(2)}) collective-permute-start(bf16[256,4608]{1,0:T(8,128)(2,1)} %collective-permute-done.5.mine_ref), channel_id=1, source_target_pairs={{0,1},{1,0},{2,3},{3,2},{4,5},{5,4},{6,7},{7,6},{8,9},{9,8},{10,11... | collective-permute-start | bytes 7077896 | tf_op jit(solution)/shard_map/ppermute | solution.py:94
  132.4 56.2 %collective-permute-start.3 = (bf16[256,4608]{1,0:T(8,128)(2,1)}, bf16[256,4608]{1,0:T(8,128)(2,1)}, u32[]{:S(2)}, u32[]{:S(2)}) collective-permute-start(bf16[256,4608]{1,0:T(8,128)(2,1)} %collective-permute-done.mine_ref), channel_id=1, source_target_pairs={{0,28},{1,5},{4,0},{5,9},{8,4},{9,13},{12,8},{13,17},{16,12},{17,2... | collective-permute-start | bytes 7077896 | tf_op jit(solution)/shard_map/ppermute | solution.py:25
  135.7 147.3 %all-to-all-start.1 = ((bf16[32,8,4608]{2,1,0:T(8,128)(2,1)}), bf16[32,8,4608]{2,1,0:T(8,128)(2,1)}, u32[]{:S(2)}, u32[]{:S(2)}) async-start(bf16[32,8,4608]{2,1,0:T(8,128)(2,1)} %bitcast_select_fusion), calls=%async_computation.1 | async-start | bytes 4718592 | tf_op jit(solution)/shard_map/all_to_all | solution.py:211
  148.4 9.2 %collective-permute-start.8 = (f32[4,16,16]{2,1,0:T(8,128)S(1)}, f32[4,16,16]{2,1,0:T(8,128)S(1)}, u32[]{:S(2)}, u32[]{:S(2)}) collective-permute-start(f32[4,16,16]{2,1,0:T(8,128)S(1)} %get-tuple-element.236), channel_id=1, source_target_pairs={{0,1},{1,0},{2,3},{3,2},{4,5},{5,4},{6,7},{7,6},{8,9},{9,8},{10,11... | collective-permute-start | bytes 12296 | tf_op jit(solution)/shard_map/ppermute | solution.py:220
  166.5 24.6 %copy-start.29 = (f32[1,16]{1,0:T(1,128)S(1)}, f32[1,16]{1,0:T(1,128)}, u32[]{:S(2)}) copy-start(f32[1,16]{1,0:T(1,128)} %param.15) | copy-start | bytes 196
  166.5 24.7 %copy-start.30 = (s32[4]{0:T(128)S(1)}, s32[4]{0:T(128)}, u32[]{:S(2)}) copy-start(s32[4]{0:T(128)} %param.19) | copy-start | bytes 52
  188.7 6.8 %collective-permute-start.9 = (bf16[256,4608]{1,0:T(8,128)(2,1)}, bf16[256,4608]{1,0:T(8,128)(2,1)}, u32[]{:S(2)}, u32[]{:S(2)}) collective-permute-start(bf16[256,4608]{1,0:T(8,128)(2,1)} %collective-permute-done.3.mine_ref), channel_id=1, source_target_pairs={{0,1},{1,0},{2,3},{3,2},{4,5},{5,4},{6,7},{7,6},{8,9},{9,8},{10,11... | collective-permute-start | bytes 7077896 | tf_op jit(solution)/shard_map/ppermute | solution.py:94
  193.6 5.1 copy-start.3
  198.7 74.2 %copy-start.8 = (bf16[4608,256]{1,0:T(8,128)(2,1)}, bf16[4608,256]{1,0:T(8,128)(2,1)S(1)}, u32[]{:S(2)}) copy-start(bf16[4608,256]{1,0:T(8,128)(2,1)S(1)} %get-tuple-element.94.refs_3_) | copy-start | bytes 7077892
  198.7 77.4 %copy-start.19 = (bf16[256,4608]{1,0:T(8,128)(2,1)}, bf16[256,4608]{1,0:T(8,128)(2,1)S(1)}, u32[]{:S(2)}) copy-start(bf16[256,4608]{1,0:T(8,128)(2,1)S(1)} %get-tuple-element.102.refs_3_) | copy-start | bytes 7077892
  204.9 12.1 %collective-permute-start.11 = (bf16[16,4608]{1,0:T(8,128)(2,1)S(1)}, bf16[16,4608]{1,0:T(8,128)(2,1)S(1)}, u32[]{:S(2)}, u32[]{:S(2)}) collective-permute-start(bf16[16,4608]{1,0:T(8,128)(2,1)S(1)} %head_terms.15), channel_id=1, source_target_pairs={{32,0},{33,25},{40,8},{41,1},{48,16},{49,9},{56,24},{57,17},{64,32... | collective-permute-start | bytes 442376 | tf_op jit(solution)/shard_map/ppermute | solution.py:36
  210.5 14.1 %collective-permute-start.10 = (bf16[16,4608]{1,0:T(8,128)(2,1)S(1)}, bf16[16,4608]{1,0:T(8,128)(2,1)S(1)}, u32[]{:S(2)}, u32[]{:S(2)}) collective-permute-start(bf16[16,4608]{1,0:T(8,128)(2,1)S(1)} %head_terms.15), channel_id=1, source_target_pairs={{32,17},{33,8},{40,25},{41,16},{48,1},{49,24},{56,9},{57,0},{64,49... | collective-permute-start | bytes 442376 | tf_op jit(solution)/shard_map/ppermute | solution.py:36
  229.2 9.9 %collective-permute-start.13 = (bf16[16,4608]{1,0:T(8,128)(2,1)S(1)}, bf16[16,4608]{1,0:T(8,128)(2,1)S(1)}, u32[]{:S(2)}, u32[]{:S(2)}) collective-permute-start(bf16[16,4608]{1,0:T(8,128)(2,1)S(1)} %head_terms.16), channel_id=1, source_target_pairs={{32,0},{33,25},{40,8},{41,1},{48,16},{49,9},{56,24},{57,17},{64,32... | collective-permute-start | bytes 442376 | tf_op jit(solution)/shard_map/ppermute | solution.py:36
  235.1 16.9 %collective-permute-start.12 = (bf16[16,4608]{1,0:T(8,128)(2,1)S(1)}, bf16[16,4608]{1,0:T(8,128)(2,1)S(1)}, u32[]{:S(2)}, u32[]{:S(2)}) collective-permute-start(bf16[16,4608]{1,0:T(8,128)(2,1)S(1)} %head_terms.16), channel_id=1, source_target_pairs={{32,17},{33,8},{40,25},{41,16},{48,1},{49,24},{56,9},{57,0},{64,49... | collective-permute-start | bytes 442376 | tf_op jit(solution)/shard_map/ppermute | solution.py:36
  256.6 9.9 %collective-permute-start.15 = (bf16[16,4608]{1,0:T(8,128)(2,1)S(1)}, bf16[16,4608]{1,0:T(8,128)(2,1)S(1)}, u32[]{:S(2)}, u32[]{:S(2)}) collective-permute-start(bf16[16,4608]{1,0:T(8,128)(2,1)S(1)} %head_terms.17), channel_id=1, source_target_pairs={{32,0},{33,25},{40,8},{41,1},{48,16},{49,9},{56,24},{57,17},{64,32... | collective-permute-start | bytes 442376 | tf_op jit(solution)/shard_map/ppermute | solution.py:36
  258.5 14.4 %collective-permute-start.14 = (bf16[16,4608]{1,0:T(8,128)(2,1)S(1)}, bf16[16,4608]{1,0:T(8,128)(2,1)S(1)}, u32[]{:S(2)}, u32[]{:S(2)}) collective-permute-start(bf16[16,4608]{1,0:T(8,128)(2,1)S(1)} %head_terms.17), channel_id=1, source_target_pairs={{32,17},{33,8},{40,25},{41,16},{48,1},{49,24},{56,9},{57,0},{64,49... | collective-permute-start | bytes 442376 | tf_op jit(solution)/shard_map/ppermute | solution.py:36
  278.2 10.2 %collective-permute-start.17 = (bf16[16,4608]{1,0:T(8,128)(2,1)}, bf16[16,4608]{1,0:T(8,128)(2,1)}, u32[]{:S(2)}, u32[]{:S(2)}) collective-permute-start(bf16[16,4608]{1,0:T(8,128)(2,1)} %head_terms.18), channel_id=1, source_target_pairs={{32,0},{33,25},{40,8},{41,1},{48,16},{49,9},{56,24},{57,17},{64,32... | collective-permute-start | bytes 442376 | tf_op jit(solution)/shard_map/ppermute | solution.py:36
  280.1 16.0 %collective-permute-start.16 = (bf16[16,4608]{1,0:T(8,128)(2,1)}, bf16[16,4608]{1,0:T(8,128)(2,1)}, u32[]{:S(2)}, u32[]{:S(2)}) collective-permute-start(bf16[16,4608]{1,0:T(8,128)(2,1)} %head_terms.18), channel_id=1, source_target_pairs={{32,17},{33,8},{40,25},{41,16},{48,1},{49,24},{56,9},{57,0},{64,49... | collective-permute-start | bytes 442376 | tf_op jit(solution)/shard_map/ppermute | solution.py:36
  296.1 6.7 %copy-start.12 = (bf16[256,4608]{1,0:T(8,128)(2,1)S(1)}, bf16[256,4608]{1,0:T(8,128)(2,1)}, u32[]{:S(2)}) copy-start(bf16[256,4608]{1,0:T(8,128)(2,1)} %copy-done.10) | copy-start | bytes 7077892
  296.1 6.7 %copy-start.15 = (bf16[256,4608]{1,0:T(8,128)(2,1)S(1)}, bf16[256,4608]{1,0:T(8,128)(2,1)}, u32[]{:S(2)}) copy-start(bf16[256,4608]{1,0:T(8,128)(2,1)} %copy-done.13) | copy-start | bytes 7077892
  296.1 6.7 %copy-start.18 = (bf16[256,4608]{1,0:T(8,128)(2,1)S(1)}, bf16[256,4608]{1,0:T(8,128)(2,1)}, u32[]{:S(2)}) copy-start(bf16[256,4608]{1,0:T(8,128)(2,1)} %copy-done.16) | copy-start | bytes 7077892
  296.1 6.7 %copy-start.20 = (bf16[256,4608]{1,0:T(8,128)(2,1)S(1)}, bf16[256,4608]{1,0:T(8,128)(2,1)}, u32[]{:S(2)}) copy-start(bf16[256,4608]{1,0:T(8,128)(2,1)} %copy-done.19) | copy-start | bytes 7077892
  302.8 5.8 copy-start.23
  302.8 19.8 %copy-start.7 = (bf16[4608,256]{1,0:T(8,128)(2,1)S(1)}, bf16[4608,256]{1,0:T(8,128)(2,1)}, u32[]{:S(2)}) copy-start(bf16[4608,256]{1,0:T(8,128)(2,1)} %copy-done.5) | copy-start | bytes 7077892
  302.8 19.8 %copy-start.9 = (bf16[4608,256]{1,0:T(8,128)(2,1)S(1)}, bf16[4608,256]{1,0:T(8,128)(2,1)}, u32[]{:S(2)}) copy-start(bf16[4608,256]{1,0:T(8,128)(2,1)} %copy-done.8) | copy-start | bytes 7077892
  304.2 18.4 %copy-start.4 = (bf16[4608,256]{1,0:T(8,128)(2,1)S(1)}, bf16[4608,256]{1,0:T(8,128)(2,1)}, u32[]{:S(2)}) copy-start(bf16[4608,256]{1,0:T(8,128)(2,1)} %copy-done.2) | copy-start | bytes 7077892
  304.2 11.5 %collective-permute-start.19 = (bf16[16,4608]{1,0:T(8,128)(2,1)S(1)}, bf16[16,4608]{1,0:T(8,128)(2,1)S(1)}, u32[]{:S(2)}, u32[]{:S(2)}) collective-permute-start(bf16[16,4608]{1,0:T(8,128)(2,1)S(1)} %head_terms.19), channel_id=1, source_target_pairs={{32,0},{33,25},{40,8},{41,1},{48,16},{49,9},{56,24},{57,17},{64,32... | collective-permute-start | bytes 442376 | tf_op jit(solution)/shard_map/ppermute | solution.py:36
  306.4 16.2 %collective-permute-start.18 = (bf16[16,4608]{1,0:T(8,128)(2,1)S(1)}, bf16[16,4608]{1,0:T(8,128)(2,1)S(1)}, u32[]{:S(2)}, u32[]{:S(2)}) collective-permute-start(bf16[16,4608]{1,0:T(8,128)(2,1)S(1)} %head_terms.19), channel_id=1, source_target_pairs={{32,17},{33,8},{40,25},{41,16},{48,1},{49,24},{56,9},{57,0},{64,49... | collective-permute-start | bytes 442376 | tf_op jit(solution)/shard_map/ppermute | solution.py:36
  327.3 11.2 %collective-permute-start.21 = (bf16[16,4608]{1,0:T(8,128)(2,1)S(1)}, bf16[16,4608]{1,0:T(8,128)(2,1)S(1)}, u32[]{:S(2)}, u32[]{:S(2)}) collective-permute-start(bf16[16,4608]{1,0:T(8,128)(2,1)S(1)} %head_terms.20), channel_id=1, source_target_pairs={{32,0},{33,25},{40,8},{41,1},{48,16},{49,9},{56,24},{57,17},{64,32... | collective-permute-start | bytes 442376 | tf_op jit(solution)/shard_map/ppermute | solution.py:36
  329.2 14.6 %collective-permute-start.20 = (bf16[16,4608]{1,0:T(8,128)(2,1)S(1)}, bf16[16,4608]{1,0:T(8,128)(2,1)S(1)}, u32[]{:S(2)}, u32[]{:S(2)}) collective-permute-start(bf16[16,4608]{1,0:T(8,128)(2,1)S(1)} %head_terms.20), channel_id=1, source_target_pairs={{32,17},{33,8},{40,25},{41,16},{48,1},{49,24},{56,9},{57,0},{64,49... | collective-permute-start | bytes 442376 | tf_op jit(solution)/shard_map/ppermute | solution.py:36
  348.5 9.9 %collective-permute-start.23 = (bf16[16,4608]{1,0:T(8,128)(2,1)S(1)}, bf16[16,4608]{1,0:T(8,128)(2,1)S(1)}, u32[]{:S(2)}, u32[]{:S(2)}) collective-permute-start(bf16[16,4608]{1,0:T(8,128)(2,1)S(1)} %head_terms.21), channel_id=1, source_target_pairs={{32,0},{33,25},{40,8},{41,1},{48,16},{49,9},{56,24},{57,17},{64,32... | collective-permute-start | bytes 442376 | tf_op jit(solution)/shard_map/ppermute | solution.py:36
  350.4 14.9 %collective-permute-start.22 = (bf16[16,4608]{1,0:T(8,128)(2,1)S(1)}, bf16[16,4608]{1,0:T(8,128)(2,1)S(1)}, u32[]{:S(2)}, u32[]{:S(2)}) collective-permute-start(bf16[16,4608]{1,0:T(8,128)(2,1)S(1)} %head_terms.21), channel_id=1, source_target_pairs={{32,17},{33,8},{40,25},{41,16},{48,1},{49,24},{56,9},{57,0},{64,49... | collective-permute-start | bytes 442376 | tf_op jit(solution)/shard_map/ppermute | solution.py:36
  369.9 9.9 %collective-permute-start.25 = (bf16[16,4608]{1,0:T(8,128)(2,1)S(1)}, bf16[16,4608]{1,0:T(8,128)(2,1)S(1)}, u32[]{:S(2)}, u32[]{:S(2)}) collective-permute-start(bf16[16,4608]{1,0:T(8,128)(2,1)S(1)} %head_terms.22), channel_id=1, source_target_pairs={{32,0},{33,25},{40,8},{41,1},{48,16},{49,9},{56,24},{57,17},{64,32... | collective-permute-start | bytes 442376 | tf_op jit(solution)/shard_map/ppermute | solution.py:36
  371.8 14.2 %collective-permute-start.24 = (bf16[16,4608]{1,0:T(8,128)(2,1)S(1)}, bf16[16,4608]{1,0:T(8,128)(2,1)S(1)}, u32[]{:S(2)}, u32[]{:S(2)}) collective-permute-start(bf16[16,4608]{1,0:T(8,128)(2,1)S(1)} %head_terms.22), channel_id=1, source_target_pairs={{32,17},{33,8},{40,25},{41,16},{48,1},{49,24},{56,9},{57,0},{64,49... | collective-permute-start | bytes 442376 | tf_op jit(solution)/shard_map/ppermute | solution.py:36
  391.4 9.9 %collective-permute-start.27 = (bf16[16,4608]{1,0:T(8,128)(2,1)S(1)}, bf16[16,4608]{1,0:T(8,128)(2,1)S(1)}, u32[]{:S(2)}, u32[]{:S(2)}) collective-permute-start(bf16[16,4608]{1,0:T(8,128)(2,1)S(1)} %head_terms.23), channel_id=1, source_target_pairs={{32,0},{33,25},{40,8},{41,1},{48,16},{49,9},{56,24},{57,17},{64,32... | collective-permute-start | bytes 442376 | tf_op jit(solution)/shard_map/ppermute | solution.py:36
  393.3 14.6 %collective-permute-start.26 = (bf16[16,4608]{1,0:T(8,128)(2,1)S(1)}, bf16[16,4608]{1,0:T(8,128)(2,1)S(1)}, u32[]{:S(2)}, u32[]{:S(2)}) collective-permute-start(bf16[16,4608]{1,0:T(8,128)(2,1)S(1)} %head_terms.23), channel_id=1, source_target_pairs={{32,17},{33,8},{40,25},{41,16},{48,1},{49,24},{56,9},{57,0},{64,49... | collective-permute-start | bytes 442376 | tf_op jit(solution)/shard_map/ppermute | solution.py:36
  413.7 9.9 %collective-permute-start.29 = (bf16[16,4608]{1,0:T(8,128)(2,1)S(1)}, bf16[16,4608]{1,0:T(8,128)(2,1)S(1)}, u32[]{:S(2)}, u32[]{:S(2)}) collective-permute-start(bf16[16,4608]{1,0:T(8,128)(2,1)S(1)} %head_terms.24), channel_id=1, source_target_pairs={{32,0},{33,25},{40,8},{41,1},{48,16},{49,9},{56,24},{57,17},{64,32... | collective-permute-start | bytes 442376 | tf_op jit(solution)/shard_map/ppermute | solution.py:36
  415.6 14.8 %collective-permute-start.28 = (bf16[16,4608]{1,0:T(8,128)(2,1)S(1)}, bf16[16,4608]{1,0:T(8,128)(2,1)S(1)}, u32[]{:S(2)}, u32[]{:S(2)}) collective-permute-start(bf16[16,4608]{1,0:T(8,128)(2,1)S(1)} %head_terms.24), channel_id=1, source_target_pairs={{32,17},{33,8},{40,25},{41,16},{48,1},{49,24},{56,9},{57,0},{64,49... | collective-permute-start | bytes 442376 | tf_op jit(solution)/shard_map/ppermute | solution.py:36
  436.0 9.9 %collective-permute-start.31 = (bf16[16,4608]{1,0:T(8,128)(2,1)S(1)}, bf16[16,4608]{1,0:T(8,128)(2,1)S(1)}, u32[]{:S(2)}, u32[]{:S(2)}) collective-permute-start(bf16[16,4608]{1,0:T(8,128)(2,1)S(1)} %head_terms.25), channel_id=1, source_target_pairs={{32,0},{33,25},{40,8},{41,1},{48,16},{49,9},{56,24},{57,17},{64,32... | collective-permute-start | bytes 442376 | tf_op jit(solution)/shard_map/ppermute | solution.py:36
  438.0 15.8 %collective-permute-start.30 = (bf16[16,4608]{1,0:T(8,128)(2,1)S(1)}, bf16[16,4608]{1,0:T(8,128)(2,1)S(1)}, u32[]{:S(2)}, u32[]{:S(2)}) collective-permute-start(bf16[16,4608]{1,0:T(8,128)(2,1)S(1)} %head_terms.25), channel_id=1, source_target_pairs={{32,17},{33,8},{40,25},{41,16},{48,1},{49,24},{56,9},{57,0},{64,49... | collective-permute-start | bytes 442376 | tf_op jit(solution)/shard_map/ppermute | solution.py:36
  458.4 9.9 %collective-permute-start.33 = (bf16[16,4608]{1,0:T(8,128)(2,1)S(1)}, bf16[16,4608]{1,0:T(8,128)(2,1)S(1)}, u32[]{:S(2)}, u32[]{:S(2)}) collective-permute-start(bf16[16,4608]{1,0:T(8,128)(2,1)S(1)} %head_terms.26), channel_id=1, source_target_pairs={{32,0},{33,25},{40,8},{41,1},{48,16},{49,9},{56,24},{57,17},{64,32... | collective-permute-start | bytes 442376 | tf_op jit(solution)/shard_map/ppermute | solution.py:36
  460.3 15.5 %collective-permute-start.32 = (bf16[16,4608]{1,0:T(8,128)(2,1)S(1)}, bf16[16,4608]{1,0:T(8,128)(2,1)S(1)}, u32[]{:S(2)}, u32[]{:S(2)}) collective-permute-start(bf16[16,4608]{1,0:T(8,128)(2,1)S(1)} %head_terms.26), channel_id=1, source_target_pairs={{32,17},{33,8},{40,25},{41,16},{48,1},{49,24},{56,9},{57,0},{64,49... | collective-permute-start | bytes 442376 | tf_op jit(solution)/shard_map/ppermute | solution.py:36
  480.4 9.9 %collective-permute-start.35 = (bf16[16,4608]{1,0:T(8,128)(2,1)S(1)}, bf16[16,4608]{1,0:T(8,128)(2,1)S(1)}, u32[]{:S(2)}, u32[]{:S(2)}) collective-permute-start(bf16[16,4608]{1,0:T(8,128)(2,1)S(1)} %head_terms.27), channel_id=1, source_target_pairs={{32,0},{33,25},{40,8},{41,1},{48,16},{49,9},{56,24},{57,17},{64,32... | collective-permute-start | bytes 442376 | tf_op jit(solution)/shard_map/ppermute | solution.py:36
  482.5 17.8 %collective-permute-start.34 = (bf16[16,4608]{1,0:T(8,128)(2,1)S(1)}, bf16[16,4608]{1,0:T(8,128)(2,1)S(1)}, u32[]{:S(2)}, u32[]{:S(2)}) collective-permute-start(bf16[16,4608]{1,0:T(8,128)(2,1)S(1)} %head_terms.27), channel_id=1, source_target_pairs={{32,17},{33,8},{40,25},{41,16},{48,1},{49,24},{56,9},{57,0},{64,49... | collective-permute-start | bytes 442376 | tf_op jit(solution)/shard_map/ppermute | solution.py:36
  504.9 10.6 %collective-permute-start.37 = (bf16[16,4608]{1,0:T(8,128)(2,1)S(1)}, bf16[16,4608]{1,0:T(8,128)(2,1)S(1)}, u32[]{:S(2)}, u32[]{:S(2)}) collective-permute-start(bf16[16,4608]{1,0:T(8,128)(2,1)S(1)} %head_terms.28), channel_id=1, source_target_pairs={{32,0},{33,25},{40,8},{41,1},{48,16},{49,9},{56,24},{57,17},{64,32... | collective-permute-start | bytes 442376 | tf_op jit(solution)/shard_map/ppermute | solution.py:36
  506.8 13.9 %collective-permute-start.36 = (bf16[16,4608]{1,0:T(8,128)(2,1)S(1)}, bf16[16,4608]{1,0:T(8,128)(2,1)S(1)}, u32[]{:S(2)}, u32[]{:S(2)}) collective-permute-start(bf16[16,4608]{1,0:T(8,128)(2,1)S(1)} %head_terms.28), channel_id=1, source_target_pairs={{32,17},{33,8},{40,25},{41,16},{48,1},{49,24},{56,9},{57,0},{64,49... | collective-permute-start | bytes 442376 | tf_op jit(solution)/shard_map/ppermute | solution.py:36
  525.9 50.8 %copy-start.24 = (bf16[128,4608]{1,0:T(8,128)(2,1)S(1)}, bf16[128,4608]{1,0:T(8,128)(2,1)}, u32[]{:S(2)}) copy-start(bf16[128,4608]{1,0:T(8,128)(2,1)} %broadcast_select_fusion) | copy-start | bytes 3538948
  525.9 10.0 %collective-permute-start.39 = (bf16[16,4608]{1,0:T(8,128)(2,1)S(1)}, bf16[16,4608]{1,0:T(8,128)(2,1)S(1)}, u32[]{:S(2)}, u32[]{:S(2)}) collective-permute-start(bf16[16,4608]{1,0:T(8,128)(2,1)S(1)} %head_terms.29), channel_id=1, source_target_pairs={{32,0},{33,25},{40,8},{41,1},{48,16},{49,9},{56,24},{57,17},{64,32... | collective-permute-start | bytes 442376 | tf_op jit(solution)/shard_map/ppermute | solution.py:36
  528.0 14.4 %collective-permute-start.38 = (bf16[16,4608]{1,0:T(8,128)(2,1)S(1)}, bf16[16,4608]{1,0:T(8,128)(2,1)S(1)}, u32[]{:S(2)}, u32[]{:S(2)}) collective-permute-start(bf16[16,4608]{1,0:T(8,128)(2,1)S(1)} %head_terms.29), channel_id=1, source_target_pairs={{32,17},{33,8},{40,25},{41,16},{48,1},{49,24},{56,9},{57,0},{64,49... | collective-permute-start | bytes 442376 | tf_op jit(solution)/shard_map/ppermute | solution.py:36
  544.2 3.5 collective-permute-start.40
  547.6 30.5 %copy-start.1 = (bf16[1,128,4608]{2,1,0:T(8,128)(2,1)S(1)}, bf16[1,128,4608]{2,1,0:T(8,128)(2,1)}, u32[]{:S(2)}) copy-start(bf16[1,128,4608]{2,1,0:T(8,128)(2,1)} %param.10) | copy-start | bytes 3538948
  548.9 28.6 %copy-start.28 = (f32[1,128]{1,0:T(1,128)S(1)}, f32[1,128]{1,0:T(1,128)}, u32[]{:S(2)}) copy-start(f32[1,128]{1,0:T(1,128)} %param.17) | copy-start | bytes 1540
  549.7 23.3 %all-to-all-start.2 = ((bf16[16,4,2304]{2,1,0:T(4,128)(2,1)}), bf16[16,4,2304]{2,1,0:T(4,128)(2,1)S(1)}, u32[]{:S(2)}, u32[]{:S(2)}) async-start(bf16[16,4,2304]{2,1,0:T(4,128)(2,1)} %copy.107), calls=%async_computation.2 | async-start | bytes 589824 | tf_op jit(solution)/shard_map/all_to_all | solution.py:257
  (11 other events, 27.5 us)
